TPU v7x, 256 devices: a whole 4x4x8 slice. The times are simulated.
256 devices in a mesh: dp: 16 (over z, y_lo), mp: 16 (over y_hi, x, core).
Axes of the slice: x: 4, y: 4 (y_hi: 2, y_lo: 2; y = y_hi * 2 + y_lo), z: 8, core: 2. Of those that a mesh axis runs over, the one named last changes fastest.
Arguments:
- img_emb: bfloat16 [8192, 1536], P('dp')
- txt_emb: bfloat16 [8192, 1536], P(('dp', 'mp'))
- img_feat_t: bfloat16 [1536, 8192], P('mp', 'dp'), may hold values from -6 to 6
- txt_feat_t: bfloat16 [1536, 8192], P('mp', 'dp'), may hold values from -6 to 6
- logit_scale: float32 [1], replicated, may hold values from 8 to 16
- logit_bias: float32 [1], replicated
Outputs:
- row_loss: float32 [8192], P('dp')
- img_head_grad: float32 [1536, 1536], P('mp')
- txt_head_grad: float32 [1536, 1536], P('mp')
All inputs are finite; a program needn't handle non-finite values.
Results may differ from a plain program's by a relative error of at most 0.0061.
Values may be sent and summed in bfloat16 or wider, within the bound.
No kernel may reach another device: no remote copies, remote signals or barrier semaphores. Data moves between devices by JAX's collectives and lax.ppermute only.
A program may use at most 64 MiB of HBM per device.

v0:
```python
import jax
import jax.numpy as jnp
from jax import lax
from jax.sharding import PartitionSpec as P


def shifted(value, axis, steps):
    count = lax.axis_size(axis)
    pairs = [(source, (source + steps) % count) for source in range(count)]
    return lax.ppermute(value, axis, pairs)


def normalize(raw):
    values = raw.astype(jnp.float32)
    inverse = lax.rsqrt(jnp.sum(values * values, axis=1, keepdims=True) + 1e-06)
    return (values * inverse, inverse)


def through_norm(upstream, normed, inverse):
    return (upstream - normed * jnp.sum(normed * upstream, axis=1, keepdims=True)) * inverse


def score_block(block, images, text_ids, image_ids, scale, bias):
    logits = (
        scale
        * lax.dot_general(
            block, images, (((1,), (1,)), ((), ())), preferred_element_type=jnp.float32
        )
        + bias
    )
    signs = jnp.where(text_ids[:, None] == image_ids[None, :], 1.0, -1.0).astype(jnp.float32)
    losses = jnp.sum(jax.nn.softplus(-signs * logits), axis=0)
    slopes = (scale * -signs * jax.nn.sigmoid(-signs * logits)).astype(jnp.bfloat16)
    return (losses, slopes)


def pass_partial(partial_value):
    return shifted(partial_value, "dp", 1)


def shards(img_emb, txt_emb, img_feat_t, txt_feat_t, logit_scale, logit_bias):
    rows = img_emb.shape[0]
    width = img_emb.shape[1]
    sub = txt_emb.shape[0]
    cycle_size = lax.axis_size("dp")
    dp_index = lax.axis_index("dp")
    mp_index = lax.axis_index("mp")
    normed_img, inv_img = normalize(img_emb)
    normed_txt, inv_txt = normalize(txt_emb)
    images = normed_img.astype(jnp.bfloat16)
    texts = normed_txt.astype(jnp.bfloat16)
    scale = logit_scale[0]
    bias = logit_bias[0]
    image_ids = dp_index * rows + jnp.arange(rows, dtype=jnp.int32)
    local_ids = mp_index * sub + jnp.arange(sub, dtype=jnp.int32)

    def visit(step, block, partial_value, losses, slope_store, block_store):
        anchor = (dp_index - step) % cycle_size
        block_losses, slopes = score_block(
            block, images, anchor * rows + local_ids, image_ids, scale, bias
        )
        partial_value = partial_value + jnp.dot(slopes, images, preferred_element_type=jnp.float32)
        slope_store = lax.dynamic_update_slice_in_dim(slope_store, slopes, step * sub, 0)
        block_store = lax.dynamic_update_slice_in_dim(block_store, block, step * sub, 0)
        return (partial_value, losses + block_losses, slope_store, block_store)

    def turn(step, state):
        block, partial_value, losses, slope_store, block_store = state
        partial_value, losses, slope_store, block_store = visit(
            step, block, partial_value, losses, slope_store, block_store
        )
        moved = shifted(block, "dp", 1)
        return (moved, pass_partial(partial_value), losses, slope_store, block_store)

    state = (
        texts,
        jnp.zeros((sub, width), jnp.float32),
        jnp.zeros((rows,), jnp.float32),
        jnp.zeros((cycle_size * sub, rows), jnp.bfloat16),
        jnp.zeros((cycle_size * sub, width), jnp.bfloat16),
    )
    block, partial_value, losses, slope_store, block_store = lax.fori_loop(
        0, cycle_size - 1, turn, state
    )
    partial_value, losses, slope_store, block_store = visit(
        cycle_size - 1, block, partial_value, losses, slope_store, block_store
    )
    text_grad = pass_partial(partial_value)
    image_part = lax.dot_general(
        slope_store, block_store, (((0,), (0,)), ((), ())), preferred_element_type=jnp.float32
    )
    image_grad, losses = lax.psum((image_part, losses), "mp")
    d_img = through_norm(image_grad, normed_img, inv_img).astype(jnp.bfloat16)
    d_txt = through_norm(text_grad, normed_txt, inv_txt).astype(jnp.bfloat16)
    d_txt_rows = lax.all_gather(d_txt, "mp", axis=0, tiled=True)
    img_weight = jnp.dot(img_feat_t, d_img, preferred_element_type=jnp.float32)
    txt_weight = jnp.dot(txt_feat_t, d_txt_rows, preferred_element_type=jnp.float32)
    img_weight, txt_weight = lax.psum((img_weight, txt_weight), "dp")
    return (losses, img_weight, txt_weight)


def solution(mesh):
    in_specs = (P("dp", None), P(("dp", "mp"), None), P("mp", "dp"), P("mp", "dp"), P(), P())
    out_specs = (P("dp"), P("mp", None), P("mp", None))
    return jax.shard_map(shards, mesh=mesh, in_specs=in_specs, out_specs=out_specs, check_vma=False)
```

profile of v0, /device:TPU:2, one launch (start us, length us, event | category | flops | bytes accessed | tf_op | source)
XLA Modules:
  0.0 582.5 jit_solution(3059086581060058864)
XLA Ops:
  9.7 1.8 fusion.14
  14.8 204.7 %while.24 = (s32[]{:T(128)}, bf16[32,1536]{1,0:T(8,128)(2,1)S(1)}, f32[32,1536]{1,0:T(8,128)}, f32[512]{0:T(512)S(1)}, bf16[512,512]{1,0:T(8,128)(2,1)}, /*index...) while((s32[]{:T(128)}, bf16[32,1536]{1,0:T(8,128)(2,1)S(1)}, ...), condition=%wide.region_4.5_spmd.clone, body=%wide.region_2.4_spmd.clone.sunk | while | flops 101221456 | bytes 5457362 | solution.py:82
  14.8 1.7 collective-permute-start
  16.4 1.9 fusion.46
  18.4 2.7 convolution_add_fusion.3
  21.0 1.8 collective-permute-start.1
  24.8 6.8 %collective-permute-done.1 = f32[32,1536]{1,0:T(8,128)} collective-permute-done((f32[32,1536]{1,0:T(8,128)}, f32[32,1536]{1,0:T(8,128)}, u32[]{:S(2)}, u32[]{:S(2)}) %collective-permute-start.1) | collective-permute-done | bytes 196640 | tf_op jit(solution)/shard_map/while/body/eval_jaxpr/ppermute | solution.py:10
  31.8 1.9 fusion.46
  33.7 2.7 convolution_add_fusion.3
  38.7 6.2 %collective-permute-done.1 = f32[32,1536]{1,0:T(8,128)} collective-permute-done((f32[32,1536]{1,0:T(8,128)}, f32[32,1536]{1,0:T(8,128)}, u32[]{:S(2)}, u32[]{:S(2)}) %collective-permute-start.1) | collective-permute-done | bytes 196640 | tf_op jit(solution)/shard_map/while/body/eval_jaxpr/ppermute | solution.py:10
  45.0 1.9 fusion.46
  46.9 2.7 convolution_add_fusion.3
  51.7 6.0 %collective-permute-done.1 = f32[32,1536]{1,0:T(8,128)} collective-permute-done((f32[32,1536]{1,0:T(8,128)}, f32[32,1536]{1,0:T(8,128)}, u32[]{:S(2)}, u32[]{:S(2)}) %collective-permute-start.1) | collective-permute-done | bytes 196640 | tf_op jit(solution)/shard_map/while/body/eval_jaxpr/ppermute | solution.py:10
  57.9 1.9 fusion.46
  59.8 2.7 convolution_add_fusion.3
  64.8 5.8 collective-permute-done.1
  70.7 1.9 fusion.46
  72.6 2.7 convolution_add_fusion.3
  75.3 1.6 collective-permute-start.1
  78.9 4.5 collective-permute-done.1
  83.6 1.9 fusion.46
  85.5 2.7 convolution_add_fusion.3
  91.3 4.9 collective-permute-done.1
  96.4 1.9 fusion.46
  98.3 2.7 convolution_add_fusion.3
  101.0 2.4 collective-permute-start.1
  105.4 3.7 collective-permute-done.1
  110.6 1.9 fusion.46
  112.5 2.7 convolution_add_fusion.3
  115.2 1.8 collective-permute-start.1
  119.0 5.0 collective-permute-done.1
  124.1 1.9 fusion.46
  126.0 2.7 convolution_add_fusion.3
  128.7 3.3 collective-permute-start.1
  133.9 3.4 collective-permute-done.1
  138.6 1.9 fusion.46
  140.6 2.7 convolution_add_fusion.3
  143.2 1.7 collective-permute-start.1
  146.9 4.9 collective-permute-done.1
  153.0 1.9 fusion.46
  154.9 2.7 convolution_add_fusion.3
  159.9 7.4 %collective-permute-done.1 = f32[32,1536]{1,0:T(8,128)} collective-permute-done((f32[32,1536]{1,0:T(8,128)}, f32[32,1536]{1,0:T(8,128)}, u32[]{:S(2)}, u32[]{:S(2)}) %collective-permute-start.1) | collective-permute-done | bytes 196640 | tf_op jit(solution)/shard_map/while/body/eval_jaxpr/ppermute | solution.py:10
  167.4 1.9 fusion.46
  169.3 2.7 convolution_add_fusion.3
  174.1 6.8 %collective-permute-done.1 = f32[32,1536]{1,0:T(8,128)} collective-permute-done((f32[32,1536]{1,0:T(8,128)}, f32[32,1536]{1,0:T(8,128)}, u32[]{:S(2)}, u32[]{:S(2)}) %collective-permute-start.1) | collective-permute-done | bytes 196640 | tf_op jit(solution)/shard_map/while/body/eval_jaxpr/ppermute | solution.py:10
  181.1 1.9 fusion.46
  183.0 2.7 convolution_add_fusion.3
  187.7 6.0 %collective-permute-done.1 = f32[32,1536]{1,0:T(8,128)} collective-permute-done((f32[32,1536]{1,0:T(8,128)}, f32[32,1536]{1,0:T(8,128)}, u32[]{:S(2)}, u32[]{:S(2)}) %collective-permute-start.1) | collective-permute-done | bytes 196640 | tf_op jit(solution)/shard_map/while/body/eval_jaxpr/ppermute | solution.py:10
  193.9 1.9 fusion.46
  195.8 2.7 convolution_add_fusion.3
  200.6 6.0 %collective-permute-done.1 = f32[32,1536]{1,0:T(8,128)} collective-permute-done((f32[32,1536]{1,0:T(8,128)}, f32[32,1536]{1,0:T(8,128)}, u32[]{:S(2)}, u32[]{:S(2)}) %collective-permute-start.1) | collective-permute-done | bytes 196640 | tf_op jit(solution)/shard_map/while/body/eval_jaxpr/ppermute | solution.py:10
  206.7 1.9 fusion.46
  208.7 2.7 convolution_add_fusion.3
  213.4 6.0 %collective-permute-done.1 = f32[32,1536]{1,0:T(8,128)} collective-permute-done((f32[32,1536]{1,0:T(8,128)}, f32[32,1536]{1,0:T(8,128)}, u32[]{:S(2)}, u32[]{:S(2)}) %collective-permute-start.1) | collective-permute-done | bytes 196640 | tf_op jit(solution)/shard_map/while/body/eval_jaxpr/ppermute | solution.py:10
  221.5 3.7 fusion.27
  226.7 7.8 %collective-permute-done.2 = f32[32,1536]{1,0:T(8,128)S(1)} collective-permute-done((f32[32,1536]{1,0:T(8,128)S(1)}, f32[32,1536]{1,0:T(8,128)S(1)}, u32[]{:S(2)}, u32[]{:S(2)}) %collective-permute-start.2) | collective-permute-done | bytes 196640 | tf_op jit(solution)/shard_map/ppermute | solution.py:10
  235.5 133.8 %all-reduce.4.cloned.1.call-done = f32[512,1536]{1,0:T(8,128)} async-done(((f32[512,1536]{1,0:T(8,128)}), f32[512,1536]{1,0:T(8,128)}) %all-reduce.4.cloned.1.call-update) | async-done | bytes 3145744 | tf_op jit(solution)/shard_map/psum | solution.py:92
  369.4 2.6 fusion.10
  372.2 1.7 convolution_bitcast_fusion.1
  373.9 56.4 %all-gather.2.cloned.1.call-done = bf16[512,1536]{1,0:T(8,128)(2,1)} async-done(((bf16[32,1536]{1,0:T(8,128)(2,1)}), bf16[512,1536]{1,0:T(8,128)(2,1)}) %all-gather.2.cloned.1.call-update) | async-done | bytes 1572880 | tf_op jit(solution)/shard_map/all_gather | solution.py:95
  430.3 2.6 convolution_bitcast_fusion
  432.9 30.9 %psum.28 = f32[512]{0:T(512)} all-reduce(f32[512]{0:T(512)S(1)} %add.218), channel_id=1, replica_groups=mesh['dp'=16,'mp'=16] {'mp'}, use_global_device_ids=true, to_apply=%region_6.7 | all-reduce | flops 512 | bytes 4096 | tf_op jit(solution)/shard_map/psum | solution.py:92
  463.8 109.3 %all-reduce.6.cloned.1.call-done = (f32[96,1536]{1,0:T(8,128)}, f32[96,1536]{1,0:T(8,128)}) async-done(((f32[96,1536]{1,0:T(8,128)}, f32[96,1536]{1,0:T(8,128)}), (f32[96,1536]{1,0:T(8,128)}, f32[96,1536]{1,0:T(8,128)})) %all-reduce.6.cloned.1.call-update) | async-done | bytes 1179664 | tf_op jit(solution)/shard_map/psum | solution.py:98
  573.2 2.0 copy.36
  (170 shorter events, 47.3 us)
Async XLA Ops:
  7.2 364.8 %copy-start = (bf16[96,512]{1,0:T(8,128)(2,1)S(1)}, bf16[96,512]{1,0:T(8,128)(2,1)}, u32[]{:S(2)}) copy-start(bf16[96,512]{1,0:T(8,128)(2,1)} %param.10) | copy-start | bytes 294916
  7.2 4.4 copy-start.4
  7.2 4.4 copy-start.1
  7.2 362.2 %all-reduce.4.cloned.1.call-start = ((), (), s32[]{:S(2)}) async-start(), calls=%async_computation | async-start | bytes 6291456 | tf_op jit(solution)/shard_map/psum | solution.py:92
  14.8 10.0 %collective-permute-start = (bf16[32,1536]{1,0:T(8,128)(2,1)S(1)}, bf16[32,1536]{1,0:T(8,128)(2,1)S(1)}, u32[]{:S(2)}, u32[]{:S(2)}) collective-permute-start(bf16[32,1536]{1,0:T(8,128)(2,1)S(1)} %copy.18), channel_id=1, source_target_pairs={{0,16},{16,32},{32,48},{48,64},{64,80},{80,96},{96,112},{112,128},... | collective-permute-start | bytes 294920 | tf_op jit(solution)/shard_map/while/body/eval_jaxpr/ppermute | solution.py:10
  21.0 10.6 %collective-permute-start.1 = (f32[32,1536]{1,0:T(8,128)}, f32[32,1536]{1,0:T(8,128)}, u32[]{:S(2)}, u32[]{:S(2)}) collective-permute-start(f32[32,1536]{1,0:T(8,128)} %convolution_add_fusion.3), channel_id=1, source_target_pairs={{0,16},{16,32},{32,48},{48,64},{64,80},{80,96},{96,112},{112,128},... | collective-permute-start | bytes 589832 | tf_op jit(solution)/shard_map/while/body/eval_jaxpr/ppermute | solution.py:10
  31.6 7.1 %collective-permute-start = (bf16[32,1536]{1,0:T(8,128)(2,1)S(1)}, bf16[32,1536]{1,0:T(8,128)(2,1)S(1)}, u32[]{:S(2)}, u32[]{:S(2)}) collective-permute-start(bf16[32,1536]{1,0:T(8,128)(2,1)S(1)} %copy.18), channel_id=1, source_target_pairs={{0,16},{16,32},{32,48},{48,64},{64,80},{80,96},{96,112},{112,128},... | collective-permute-start | bytes 294920 | tf_op jit(solution)/shard_map/while/body/eval_jaxpr/ppermute | solution.py:10
  36.3 8.5 %collective-permute-start.1 = (f32[32,1536]{1,0:T(8,128)}, f32[32,1536]{1,0:T(8,128)}, u32[]{:S(2)}, u32[]{:S(2)}) collective-permute-start(f32[32,1536]{1,0:T(8,128)} %convolution_add_fusion.3), channel_id=1, source_target_pairs={{0,16},{16,32},{32,48},{48,64},{64,80},{80,96},{96,112},{112,128},... | collective-permute-start | bytes 589832 | tf_op jit(solution)/shard_map/while/body/eval_jaxpr/ppermute | solution.py:10
  44.9 6.8 %collective-permute-start = (bf16[32,1536]{1,0:T(8,128)(2,1)S(1)}, bf16[32,1536]{1,0:T(8,128)(2,1)S(1)}, u32[]{:S(2)}, u32[]{:S(2)}) collective-permute-start(bf16[32,1536]{1,0:T(8,128)(2,1)S(1)} %copy.18), channel_id=1, source_target_pairs={{0,16},{16,32},{32,48},{48,64},{64,80},{80,96},{96,112},{112,128},... | collective-permute-start | bytes 294920 | tf_op jit(solution)/shard_map/while/body/eval_jaxpr/ppermute | solution.py:10
  49.6 8.1 %collective-permute-start.1 = (f32[32,1536]{1,0:T(8,128)}, f32[32,1536]{1,0:T(8,128)}, u32[]{:S(2)}, u32[]{:S(2)}) collective-permute-start(f32[32,1536]{1,0:T(8,128)} %convolution_add_fusion.3), channel_id=1, source_target_pairs={{0,16},{16,32},{32,48},{48,64},{64,80},{80,96},{96,112},{112,128},... | collective-permute-start | bytes 589832 | tf_op jit(solution)/shard_map/while/body/eval_jaxpr/ppermute | solution.py:10
  57.7 7.1 %collective-permute-start = (bf16[32,1536]{1,0:T(8,128)(2,1)S(1)}, bf16[32,1536]{1,0:T(8,128)(2,1)S(1)}, u32[]{:S(2)}, u32[]{:S(2)}) collective-permute-start(bf16[32,1536]{1,0:T(8,128)(2,1)S(1)} %copy.18), channel_id=1, source_target_pairs={{0,16},{16,32},{32,48},{48,64},{64,80},{80,96},{96,112},{112,128},... | collective-permute-start | bytes 294920 | tf_op jit(solution)/shard_map/while/body/eval_jaxpr/ppermute | solution.py:10
  62.5 8.1 %collective-permute-start.1 = (f32[32,1536]{1,0:T(8,128)}, f32[32,1536]{1,0:T(8,128)}, u32[]{:S(2)}, u32[]{:S(2)}) collective-permute-start(f32[32,1536]{1,0:T(8,128)} %convolution_add_fusion.3), channel_id=1, source_target_pairs={{0,16},{16,32},{32,48},{48,64},{64,80},{80,96},{96,112},{112,128},... | collective-permute-start | bytes 589832 | tf_op jit(solution)/shard_map/while/body/eval_jaxpr/ppermute | solution.py:10
  70.6 8.3 %collective-permute-start = (bf16[32,1536]{1,0:T(8,128)(2,1)S(1)}, bf16[32,1536]{1,0:T(8,128)(2,1)S(1)}, u32[]{:S(2)}, u32[]{:S(2)}) collective-permute-start(bf16[32,1536]{1,0:T(8,128)(2,1)S(1)} %copy.18), channel_id=1, source_target_pairs={{0,16},{16,32},{32,48},{48,64},{64,80},{80,96},{96,112},{112,128},... | collective-permute-start | bytes 294920 | tf_op jit(solution)/shard_map/while/body/eval_jaxpr/ppermute | solution.py:10
  75.3 8.1 %collective-permute-start.1 = (f32[32,1536]{1,0:T(8,128)}, f32[32,1536]{1,0:T(8,128)}, u32[]{:S(2)}, u32[]{:S(2)}) collective-permute-start(f32[32,1536]{1,0:T(8,128)} %convolution_add_fusion.3), channel_id=1, source_target_pairs={{0,16},{16,32},{32,48},{48,64},{64,80},{80,96},{96,112},{112,128},... | collective-permute-start | bytes 589832 | tf_op jit(solution)/shard_map/while/body/eval_jaxpr/ppermute | solution.py:10
  83.4 7.9 %collective-permute-start = (bf16[32,1536]{1,0:T(8,128)(2,1)S(1)}, bf16[32,1536]{1,0:T(8,128)(2,1)S(1)}, u32[]{:S(2)}, u32[]{:S(2)}) collective-permute-start(bf16[32,1536]{1,0:T(8,128)(2,1)S(1)} %copy.18), channel_id=1, source_target_pairs={{0,16},{16,32},{32,48},{48,64},{64,80},{80,96},{96,112},{112,128},... | collective-permute-start | bytes 294920 | tf_op jit(solution)/shard_map/while/body/eval_jaxpr/ppermute | solution.py:10
  88.2 8.1 %collective-permute-start.1 = (f32[32,1536]{1,0:T(8,128)}, f32[32,1536]{1,0:T(8,128)}, u32[]{:S(2)}, u32[]{:S(2)}) collective-permute-start(f32[32,1536]{1,0:T(8,128)} %convolution_add_fusion.3), channel_id=1, source_target_pairs={{0,16},{16,32},{32,48},{48,64},{64,80},{80,96},{96,112},{112,128},... | collective-permute-start | bytes 589832 | tf_op jit(solution)/shard_map/while/body/eval_jaxpr/ppermute | solution.py:10
  96.3 9.2 %collective-permute-start = (bf16[32,1536]{1,0:T(8,128)(2,1)S(1)}, bf16[32,1536]{1,0:T(8,128)(2,1)S(1)}, u32[]{:S(2)}, u32[]{:S(2)}) collective-permute-start(bf16[32,1536]{1,0:T(8,128)(2,1)S(1)} %copy.18), channel_id=1, source_target_pairs={{0,16},{16,32},{32,48},{48,64},{64,80},{80,96},{96,112},{112,128},... | collective-permute-start | bytes 294920 | tf_op jit(solution)/shard_map/while/body/eval_jaxpr/ppermute | solution.py:10
  101.0 8.1 %collective-permute-start.1 = (f32[32,1536]{1,0:T(8,128)}, f32[32,1536]{1,0:T(8,128)}, u32[]{:S(2)}, u32[]{:S(2)}) collective-permute-start(f32[32,1536]{1,0:T(8,128)} %convolution_add_fusion.3), channel_id=1, source_target_pairs={{0,16},{16,32},{32,48},{48,64},{64,80},{80,96},{96,112},{112,128},... | collective-permute-start | bytes 589832 | tf_op jit(solution)/shard_map/while/body/eval_jaxpr/ppermute | solution.py:10
  109.1 9.9 %collective-permute-start = (bf16[32,1536]{1,0:T(8,128)(2,1)S(1)}, bf16[32,1536]{1,0:T(8,128)(2,1)S(1)}, u32[]{:S(2)}, u32[]{:S(2)}) collective-permute-start(bf16[32,1536]{1,0:T(8,128)(2,1)S(1)} %copy.18), channel_id=1, source_target_pairs={{0,16},{16,32},{32,48},{48,64},{64,80},{80,96},{96,112},{112,128},... | collective-permute-start | bytes 294920 | tf_op jit(solution)/shard_map/while/body/eval_jaxpr/ppermute | solution.py:10
  115.2 8.8 %collective-permute-start.1 = (f32[32,1536]{1,0:T(8,128)}, f32[32,1536]{1,0:T(8,128)}, u32[]{:S(2)}, u32[]{:S(2)}) collective-permute-start(f32[32,1536]{1,0:T(8,128)} %convolution_add_fusion.3), channel_id=1, source_target_pairs={{0,16},{16,32},{32,48},{48,64},{64,80},{80,96},{96,112},{112,128},... | collective-permute-start | bytes 589832 | tf_op jit(solution)/shard_map/while/body/eval_jaxpr/ppermute | solution.py:10
  123.9 10.0 %collective-permute-start = (bf16[32,1536]{1,0:T(8,128)(2,1)S(1)}, bf16[32,1536]{1,0:T(8,128)(2,1)S(1)}, u32[]{:S(2)}, u32[]{:S(2)}) collective-permute-start(bf16[32,1536]{1,0:T(8,128)(2,1)S(1)} %copy.18), channel_id=1, source_target_pairs={{0,16},{16,32},{32,48},{48,64},{64,80},{80,96},{96,112},{112,128},... | collective-permute-start | bytes 294920 | tf_op jit(solution)/shard_map/while/body/eval_jaxpr/ppermute | solution.py:10
  128.7 8.7 %collective-permute-start.1 = (f32[32,1536]{1,0:T(8,128)}, f32[32,1536]{1,0:T(8,128)}, u32[]{:S(2)}, u32[]{:S(2)}) collective-permute-start(f32[32,1536]{1,0:T(8,128)} %convolution_add_fusion.3), channel_id=1, source_target_pairs={{0,16},{16,32},{32,48},{48,64},{64,80},{80,96},{96,112},{112,128},... | collective-permute-start | bytes 589832 | tf_op jit(solution)/shard_map/while/body/eval_jaxpr/ppermute | solution.py:10
  137.4 9.5 %collective-permute-start = (bf16[32,1536]{1,0:T(8,128)(2,1)S(1)}, bf16[32,1536]{1,0:T(8,128)(2,1)S(1)}, u32[]{:S(2)}, u32[]{:S(2)}) collective-permute-start(bf16[32,1536]{1,0:T(8,128)(2,1)S(1)} %copy.18), channel_id=1, source_target_pairs={{0,16},{16,32},{32,48},{48,64},{64,80},{80,96},{96,112},{112,128},... | collective-permute-start | bytes 294920 | tf_op jit(solution)/shard_map/while/body/eval_jaxpr/ppermute | solution.py:10
  143.2 8.6 %collective-permute-start.1 = (f32[32,1536]{1,0:T(8,128)}, f32[32,1536]{1,0:T(8,128)}, u32[]{:S(2)}, u32[]{:S(2)}) collective-permute-start(f32[32,1536]{1,0:T(8,128)} %convolution_add_fusion.3), channel_id=1, source_target_pairs={{0,16},{16,32},{32,48},{48,64},{64,80},{80,96},{96,112},{112,128},... | collective-permute-start | bytes 589832 | tf_op jit(solution)/shard_map/while/body/eval_jaxpr/ppermute | solution.py:10
  151.8 8.0 %collective-permute-start = (bf16[32,1536]{1,0:T(8,128)(2,1)S(1)}, bf16[32,1536]{1,0:T(8,128)(2,1)S(1)}, u32[]{:S(2)}, u32[]{:S(2)}) collective-permute-start(bf16[32,1536]{1,0:T(8,128)(2,1)S(1)} %copy.18), channel_id=1, source_target_pairs={{0,16},{16,32},{32,48},{48,64},{64,80},{80,96},{96,112},{112,128},... | collective-permute-start | bytes 294920 | tf_op jit(solution)/shard_map/while/body/eval_jaxpr/ppermute | solution.py:10
  157.6 9.7 %collective-permute-start.1 = (f32[32,1536]{1,0:T(8,128)}, f32[32,1536]{1,0:T(8,128)}, u32[]{:S(2)}, u32[]{:S(2)}) collective-permute-start(f32[32,1536]{1,0:T(8,128)} %convolution_add_fusion.3), channel_id=1, source_target_pairs={{0,16},{16,32},{32,48},{48,64},{64,80},{80,96},{96,112},{112,128},... | collective-permute-start | bytes 589832 | tf_op jit(solution)/shard_map/while/body/eval_jaxpr/ppermute | solution.py:10
  167.3 6.8 %collective-permute-start = (bf16[32,1536]{1,0:T(8,128)(2,1)S(1)}, bf16[32,1536]{1,0:T(8,128)(2,1)S(1)}, u32[]{:S(2)}, u32[]{:S(2)}) collective-permute-start(bf16[32,1536]{1,0:T(8,128)(2,1)S(1)} %copy.18), channel_id=1, source_target_pairs={{0,16},{16,32},{32,48},{48,64},{64,80},{80,96},{96,112},{112,128},... | collective-permute-start | bytes 294920 | tf_op jit(solution)/shard_map/while/body/eval_jaxpr/ppermute | solution.py:10
  172.0 8.9 %collective-permute-start.1 = (f32[32,1536]{1,0:T(8,128)}, f32[32,1536]{1,0:T(8,128)}, u32[]{:S(2)}, u32[]{:S(2)}) collective-permute-start(f32[32,1536]{1,0:T(8,128)} %convolution_add_fusion.3), channel_id=1, source_target_pairs={{0,16},{16,32},{32,48},{48,64},{64,80},{80,96},{96,112},{112,128},... | collective-permute-start | bytes 589832 | tf_op jit(solution)/shard_map/while/body/eval_jaxpr/ppermute | solution.py:10
  180.9 6.8 %collective-permute-start = (bf16[32,1536]{1,0:T(8,128)(2,1)S(1)}, bf16[32,1536]{1,0:T(8,128)(2,1)S(1)}, u32[]{:S(2)}, u32[]{:S(2)}) collective-permute-start(bf16[32,1536]{1,0:T(8,128)(2,1)S(1)} %copy.18), channel_id=1, source_target_pairs={{0,16},{16,32},{32,48},{48,64},{64,80},{80,96},{96,112},{112,128},... | collective-permute-start | bytes 294920 | tf_op jit(solution)/shard_map/while/body/eval_jaxpr/ppermute | solution.py:10
  185.6 8.1 %collective-permute-start.1 = (f32[32,1536]{1,0:T(8,128)}, f32[32,1536]{1,0:T(8,128)}, u32[]{:S(2)}, u32[]{:S(2)}) collective-permute-start(f32[32,1536]{1,0:T(8,128)} %convolution_add_fusion.3), channel_id=1, source_target_pairs={{0,16},{16,32},{32,48},{48,64},{64,80},{80,96},{96,112},{112,128},... | collective-permute-start | bytes 589832 | tf_op jit(solution)/shard_map/while/body/eval_jaxpr/ppermute | solution.py:10
  193.8 6.8 %collective-permute-start = (bf16[32,1536]{1,0:T(8,128)(2,1)S(1)}, bf16[32,1536]{1,0:T(8,128)(2,1)S(1)}, u32[]{:S(2)}, u32[]{:S(2)}) collective-permute-start(bf16[32,1536]{1,0:T(8,128)(2,1)S(1)} %copy.18), channel_id=1, source_target_pairs={{0,16},{16,32},{32,48},{48,64},{64,80},{80,96},{96,112},{112,128},... | collective-permute-start | bytes 294920 | tf_op jit(solution)/shard_map/while/body/eval_jaxpr/ppermute | solution.py:10
  198.5 8.1 %collective-permute-start.1 = (f32[32,1536]{1,0:T(8,128)}, f32[32,1536]{1,0:T(8,128)}, u32[]{:S(2)}, u32[]{:S(2)}) collective-permute-start(f32[32,1536]{1,0:T(8,128)} %convolution_add_fusion.3), channel_id=1, source_target_pairs={{0,16},{16,32},{32,48},{48,64},{64,80},{80,96},{96,112},{112,128},... | collective-permute-start | bytes 589832 | tf_op jit(solution)/shard_map/while/body/eval_jaxpr/ppermute | solution.py:10
  206.6 6.8 %collective-permute-start = (bf16[32,1536]{1,0:T(8,128)(2,1)S(1)}, bf16[32,1536]{1,0:T(8,128)(2,1)S(1)}, u32[]{:S(2)}, u32[]{:S(2)}) collective-permute-start(bf16[32,1536]{1,0:T(8,128)(2,1)S(1)} %copy.18), channel_id=1, source_target_pairs={{0,16},{16,32},{32,48},{48,64},{64,80},{80,96},{96,112},{112,128},... | collective-permute-start | bytes 294920 | tf_op jit(solution)/shard_map/while/body/eval_jaxpr/ppermute | solution.py:10
  211.3 8.1 %collective-permute-start.1 = (f32[32,1536]{1,0:T(8,128)}, f32[32,1536]{1,0:T(8,128)}, u32[]{:S(2)}, u32[]{:S(2)}) collective-permute-start(f32[32,1536]{1,0:T(8,128)} %convolution_add_fusion.3), channel_id=1, source_target_pairs={{0,16},{16,32},{32,48},{48,64},{64,80},{80,96},{96,112},{112,128},... | collective-permute-start | bytes 589832 | tf_op jit(solution)/shard_map/while/body/eval_jaxpr/ppermute | solution.py:10
  220.1 1.4 copy-start.3
  225.3 9.2 %copy-start.5 = (bf16[32,1536]{1,0:T(8,128)(2,1)S(1)}, bf16[32,1536]{1,0:T(8,128)(2,1)}, u32[]{:S(2)}) copy-start(bf16[32,1536]{1,0:T(8,128)(2,1)} %param.9) | copy-start | bytes 294916
  225.3 205.0 %all-gather.2.cloned.1.call-start = ((), (), s32[]{:S(2)}) async-start(), calls=%async_computation.1 | async-start | bytes 1671168 | tf_op jit(solution)/shard_map/all_gather | solution.py:95
  226.7 7.8 %collective-permute-start.2 = (f32[32,1536]{1,0:T(8,128)S(1)}, f32[32,1536]{1,0:T(8,128)S(1)}, u32[]{:S(2)}, u32[]{:S(2)}) collective-permute-start(f32[32,1536]{1,0:T(8,128)S(1)} %convolution_add_fusion.1), channel_id=1, source_target_pairs={{0,16},{16,32},{32,48},{48,64},{64,80},{80,96},{96,112},{112,128},... | collective-permute-start | bytes 589832 | tf_op jit(solution)/shard_map/ppermute | solution.py:10
  235.5 337.7 %all-reduce.6.cloned.1.call-start = ((), (), s32[]{:S(2)}) async-start(), calls=%async_computation.2 | async-start | bytes 2359296 | tf_op jit(solution)/shard_map/psum | solution.py:98
  369.4 2.8 copy-start.2
  372.2 58.1 %copy-start.7 = (bf16[96,512]{1,0:T(8,128)(2,1)S(1)}, bf16[96,512]{1,0:T(8,128)(2,1)}, u32[]{:S(2)}) copy-start(bf16[96,512]{1,0:T(8,128)(2,1)} %param.11) | copy-start | bytes 294916
  573.2 2.0 copy-start.6
Sparse Core Ops, SparseCore 0:
  225.4 143.9 all-reduce.3
  372.7 57.5 all-gather.1
  433.5 139.5 all-reduce.5
where the time goes:
time: 584 us; the launch traced here: 582 us
  waiting for transfers between devices  391 us (67%)
  matrix products  79 us (14%)
  blocking collectives  30.9 us (5%)
  other arithmetic  28 us (5%)
  starting transfers between devices  21.3 us (4%)
  local copies, waits for them, and re-layouts  16.3 us (3%)
  between operations  15.3 us (3%)
    psum x1, waiting for transfers between devices, shards(): image_grad, losses = lax.psum((image_part, losses), 'mp')  134 us
    psum x1, waiting for transfers between devices, shards(): img_weight, txt_weight = lax.psum((img_weight, txt_weight), 'dp')  109 us
    ppermute x31, waiting for transfers between devices, shifted(): return lax.ppermute(value, axis, pairs)  91.6 us
    all_gather x1, waiting for transfers between devices, shards(): d_txt_rows = lax.all_gather(d_txt, 'mp', axis=0, tiled=True)  56.4 us
    dot_general x16, matrix products, visit(): jnp.dot(slopes, images, preferred_element_type=jnp.float32)  41.5 us
    psum x1, blocking collectives, shards(): image_grad, losses = lax.psum((image_part, losses), 'mp')  30.9 us
    dot_general x16, matrix products, score_block(): lax.dot_general(block, images, (((1,), (1,)), ((), ())), preferred_elemen...  29.4 us
    ppermute x31, starting transfers between devices, shifted(): return lax.ppermute(value, axis, pairs)  21.2 us
  transfers between devices with their start and end apart: 34, of which 24 were waited for; matrix products, arithmetic and copies ran while one was open for 18% of the time, Pallas kernels for 0%

commit v1 on v0

v1 whole, which is shorter than its diff:
```python
import jax
import jax.numpy as jnp
from jax import lax
from jax.sharding import PartitionSpec as P

F32 = jnp.float32
BF16 = jnp.bfloat16
CHIPS = 8
LANES = 128


def normalize(raw):
    values = raw.astype(F32)
    inverse = lax.rsqrt(jnp.sum(values * values, axis=1, keepdims=True) + 1e-06)
    return (values * inverse, inverse)


def through_norm(upstream, normed, inverse):
    return (upstream - normed * jnp.sum(normed * upstream, axis=1, keepdims=True)) * inverse


def move_dp(value, turn):
    return lax.ppermute(value, "dp", [(d, turn(d)) for d in range(16)])


def swap_core(value):
    return lax.ppermute(value, "mp", [(m, m ^ 1) for m in range(16)])


def same_core():
    return [[2 * chip + core for chip in range(CHIPS)] for core in range(2)]


def scatter_chips(value):
    return lax.all_to_all(value, "mp", 0, 0, tiled=True, axis_index_groups=same_core())


def gather_chips(value):
    return scatter_chips(jnp.concatenate([value] * CHIPS, axis=0))


def gather_texts(block, dp_index):
    along = [0, 1, -1, 2, -2, 3, -3, 4]
    own = [block] + [
        move_dp(block, lambda d, k=k: (d + 2 * k) % 16) for k in along[1:]
    ]
    other = [move_dp(value, lambda d: d ^ 1) for value in own]
    owners = [(dp_index - 2 * k) % 16 for k in along]
    owners += [owner ^ 1 for owner in owners]
    return jnp.concatenate(own + other, axis=0), owners


def split_pair(value):
    high = lax.reduce_precision(value, 8, 7)
    return high, value - high


def with_loss(matrix, losses):
    high, low = split_pair(losses)
    lane = lax.broadcasted_iota(jnp.int32, (matrix.shape[0], LANES), 1)
    extra = jnp.where(lane == 0, high[:, None], jnp.where(lane == 1, low[:, None], 0.0))
    return jnp.concatenate([matrix.astype(BF16), extra.astype(BF16)], axis=1)


def take_loss(extra):
    return extra[:, 0].astype(F32) + extra[:, 1].astype(F32)


def to_pieces(weight):
    rows, width = weight.shape
    pieces = weight.reshape(4, rows // 4, 4, width // 4).transpose(0, 2, 1, 3)
    return pieces.reshape(4 * rows, width // 4)


def from_pieces(pieces, rows, width):
    blocks = pieces.reshape(4, 4, rows // 4, width // 4).transpose(0, 2, 1, 3)
    return blocks.reshape(rows, width)


def sum_batch(weight):
    rows, width = weight.shape
    parts = lax.all_to_all(to_pieces(weight.astype(BF16)), "dp", 0, 0, tiled=True)
    own = jnp.sum(parts.reshape(16, rows // 4, width // 4).astype(F32), axis=0).astype(BF16)
    spread = jnp.broadcast_to(own[None], (16,) + own.shape)
    return from_pieces(lax.all_to_all(spread, "dp", 0, 0), rows, width).astype(F32)


def shards(img_emb, txt_emb, img_feat_t, txt_feat_t, logit_scale, logit_bias):
    rows, width = img_emb.shape
    sub = txt_emb.shape[0]
    half = rows // 2
    dp_index = lax.axis_index("dp")
    mp_index = lax.axis_index("mp")
    core = mp_index % 2
    chip = mp_index // 2
    scale = logit_scale[0]
    bias = logit_bias[0]

    normed_txt, inv_txt = normalize(txt_emb)
    texts, owners = gather_texts(normed_txt.astype(BF16), dp_index)
    normed_img, inv_img = normalize(img_emb)
    images = normed_img.astype(BF16)

    text_ids = jnp.concatenate(
        [owner * rows + mp_index * sub + jnp.arange(sub, dtype=jnp.int32) for owner in owners]
    )
    image_ids = dp_index * rows + jnp.arange(rows, dtype=jnp.int32)
    logits = scale * lax.dot_general(
        texts, images, (((1,), (1,)), ((), ())), preferred_element_type=F32
    ) + bias
    signs = jnp.where(text_ids[:, None] == image_ids[None, :], 1.0, -1.0).astype(F32)
    losses = jnp.sum(jax.nn.softplus(-signs * logits), axis=0)
    slopes = (scale * -signs * jax.nn.sigmoid(-signs * logits)).astype(BF16)

    text_part = jnp.dot(slopes, images, preferred_element_type=F32).astype(BF16)
    order = jnp.stack(owners)
    text_part = jnp.concatenate(
        [
            lax.dynamic_slice_in_dim(
                text_part, jnp.argmax(order == d).astype(jnp.int32) * sub, sub, 0
            )
            for d in range(16)
        ],
        axis=0,
    )
    text_pieces = lax.all_to_all(text_part, "dp", 0, 0, tiled=True)

    image_part = lax.dot_general(
        slopes, texts, (((0,), (0,)), ((), ())), preferred_element_type=F32
    )
    own_start, other_start = core * half, (1 - core) * half
    kept = lax.dynamic_slice_in_dim(image_part, own_start, half, 0)
    sent = lax.dynamic_slice_in_dim(image_part, other_start, half, 0)
    kept_loss = lax.dynamic_slice_in_dim(losses, own_start, half, 0)
    sent_loss = lax.dynamic_slice_in_dim(losses, other_start, half, 0)
    came = swap_core(with_loss(sent, sent_loss))
    both = kept + came[:, :width].astype(F32)
    both_loss = kept_loss + take_loss(came[:, width:])
    pieces = scatter_chips(with_loss(both, both_loss))
    summed = jnp.sum(pieces.reshape(CHIPS, half // CHIPS, -1).astype(F32), axis=0)
    image_grad = summed[:, :width]
    image_loss = summed[:, width] + summed[:, width + 1]
    row_start = own_start + chip * (half // CHIPS)
    d_img = through_norm(
        image_grad,
        lax.dynamic_slice_in_dim(normed_img, row_start, half // CHIPS, 0),
        lax.dynamic_slice_in_dim(inv_img, row_start, half // CHIPS, 0),
    )
    own_half = gather_chips(with_loss(d_img, image_loss))
    other_half = swap_core(own_half)
    img_weight = jnp.dot(
        lax.dynamic_slice_in_dim(img_feat_t, own_start, half, 1),
        own_half[:, :width],
        preferred_element_type=F32,
    ) + jnp.dot(
        lax.dynamic_slice_in_dim(img_feat_t, other_start, half, 1),
        other_half[:, :width],
        preferred_element_type=F32,
    )
    own_loss, other_loss = take_loss(own_half[:, width:]), take_loss(other_half[:, width:])
    row_loss = jnp.where(
        core == 0,
        jnp.concatenate([own_loss, other_loss]),
        jnp.concatenate([other_loss, own_loss]),
    )

    text_grad = jnp.sum(text_pieces.reshape(16, sub, width).astype(F32), axis=0)
    d_txt = through_norm(text_grad, normed_txt, inv_txt).astype(BF16)
    own_txt = gather_chips(d_txt)
    other_txt = swap_core(own_txt)
    by_core = txt_feat_t.reshape(-1, CHIPS, 2, sub)
    even, odd = by_core[:, :, 0].reshape(-1, half), by_core[:, :, 1].reshape(-1, half)
    txt_weight = jnp.dot(
        jnp.where(core == 0, even, odd), own_txt, preferred_element_type=F32
    ) + jnp.dot(jnp.where(core == 0, odd, even), other_txt, preferred_element_type=F32)

    total = sum_batch(jnp.concatenate([img_weight, txt_weight], axis=0))
    out_rows = img_weight.shape[0]
    return (row_loss, total[:out_rows], total[out_rows:])


def solution(mesh):
    in_specs = (P("dp", None), P(("dp", "mp"), None), P("mp", "dp"), P("mp", "dp"), P(), P())
    out_specs = (P("dp"), P("mp", None), P("mp", None))
    return jax.shard_map(shards, mesh=mesh, in_specs=in_specs, out_specs=out_specs, check_vma=False)
```

time: 584 us -> 233 us (0.40)
  waiting for transfers between devices: 391 us -> 79.1 us
  matrix products: 79 us -> 6.76 us
  starting transfers between devices: 21.3 us -> 53.2 us
  local copies, waits for them, and re-layouts: 16.3 us -> 25.5 us
    psum x2 -> x0, waiting for transfers between devices: 243 us -> none  [the longest x1 134 us: shards(): image_grad, losses = lax.psum((image_part, losses), 'mp')]
    ppermute x31 -> x18, waiting for transfers between devices: 91.6 us -> 4.63 us  [the longest x15 2.43 us: move_dp(): return lax.ppermute(value, 'dp', [(d, turn(d)) for d in range(16)])]
    all_to_all x0 -> x5, waiting for transfers between devices: none -> 74.5 us  [the longest x1 33.3 us: shards(): text_pieces = lax.all_to_all(text_part, 'dp', 0, 0, tiled=True)]
    dot_general x35 -> x7, matrix products: 79 us -> 6.76 us  [the longest x1 3.27 us: shards(): lax.dot_general(texts, images, (((1,), (1,)), ((), ())), preferred_elemen...]
    all_gather x1 -> x0, waiting for transfers between devices: 56.4 us -> none  [shards(): d_txt_rows = lax.all_gather(d_txt, 'mp', axis=0, tiled=True)]
    psum x1 -> x0, blocking collectives: 30.9 us -> none  [shards(): image_grad, losses = lax.psum((image_part, losses), 'mp')]
    all_to_all x0 -> x1, blocking collectives: none -> 29.4 us  [sum_batch(): lax.all_to_all(to_pieces(weight.astype(BF16)), 'dp', 0, 0, tiled=True)]
    all_to_all x0 -> x5, starting transfers between devices: none -> 25.4 us  [the longest x3 17 us: scatter_chips(): lax.all_to_all(value, 'mp', 0, 0, tiled=True, axis_index_groups=same_core())]
  transfers between devices with their start and end apart: 34 -> 23, of which waited for: 24 -> 11; matrix products, arithmetic and copies ran while one was open for 18% -> 18% of each run, Pallas kernels for 0% -> 0%
where the time goes in v1:
time: 233 us; the launch traced here: 232 us
  waiting for transfers between devices  79.1 us (34%)
  starting transfers between devices  53.2 us (23%)
  blocking collectives  29.4 us (13%)
  local copies, waits for them, and re-layouts  25.5 us (11%)
  other arithmetic  24.8 us (11%)
  between operations  13.2 us (6%)
  matrix products  6.76 us (3%)
    all_to_all x1, waiting for transfers between devices, shards(): text_pieces = lax.all_to_all(text_part, 'dp', 0, 0, tiled=True)  33.3 us
    all_to_all x1, blocking collectives, sum_batch(): lax.all_to_all(to_pieces(weight.astype(BF16)), 'dp', 0, 0, tiled=True)  29.4 us
    ppermute x15, starting transfers between devices, move_dp(): return lax.ppermute(value, 'dp', [(d, turn(d)) for d in range(16)])  27.8 us
    all_to_all x3, waiting for transfers between devices, scatter_chips(): lax.all_to_all(value, 'mp', 0, 0, tiled=True, axis_index_groups=same_core())  23.9 us
    unnamed x56, local copies, waits for them, and re-layouts  20.7 us
    all_to_all x1, waiting for transfers between devices, sum_batch(): lax.all_to_all(spread, 'dp', 0, 0)  17.3 us
    all_to_all x3, starting transfers between devices, scatter_chips(): lax.all_to_all(value, 'mp', 0, 0, tiled=True, axis_index_groups=same_core())  17 us
    another operation x16, other arithmetic, shards(): jnp.argmax(order == d).astype(jnp.int32) * sub  10.4 us
  transfers between devices with their start and end apart: 23, of which 11 were waited for; matrix products, arithmetic and copies ran while one was open for 18% of the time, Pallas kernels for 0%

profile of v1, /device:TPU:2, one launch (start us, length us, event | category | flops | bytes accessed | tf_op | source)
XLA Modules:
  0.0 232.0 jit_solution(10770122461954758687)
XLA Ops:
  0.6 1.1 fusion.18
  1.7 1.6 constant_dynamic-update-slice_fusion.15
  3.3 1.9 collective-permute-start
  5.2 3.9 %collective-permute-start.1 = (bf16[32,1536]{1,0:T(8,128)(2,1)S(1)}, bf16[32,1536]{1,0:T(8,128)(2,1)S(1)}, u32[]{:S(2)}, u32[]{:S(2)}) collective-permute-start(bf16[32,1536]{1,0:T(8,128)(2,1)S(1)} %get-tuple-element.40), channel_id=1, source_target_pairs={{0,224},{16,240},{32,0},{48,16},{64,32},{80,48},{96,64},{112,80},{... | collective-permute-start | bytes 294920 | tf_op jit(solution)/shard_map/ppermute | solution.py:23
  9.2 4.1 %collective-permute-start.3 = (bf16[32,1536]{1,0:T(8,128)(2,1)S(1)}, bf16[32,1536]{1,0:T(8,128)(2,1)S(1)}, u32[]{:S(2)}, u32[]{:S(2)}) collective-permute-start(bf16[32,1536]{1,0:T(8,128)(2,1)S(1)} %get-tuple-element.40), channel_id=1, source_target_pairs={{0,192},{16,208},{32,224},{48,240},{64,0},{80,16},{96,32},{112,48}... | collective-permute-start | bytes 294920 | tf_op jit(solution)/shard_map/ppermute | solution.py:23
  13.3 0.7 collective-permute-start.4
  14.1 0.7 compare_reduce_fusion.15
  15.4 0.7 compare_reduce_fusion.14
  16.7 0.7 compare_reduce_fusion.13
  18.0 0.7 compare_reduce_fusion.12
  19.3 0.7 compare_reduce_fusion.11
  20.6 0.7 compare_reduce_fusion.10
  21.9 0.7 compare_reduce_fusion.9
  23.2 0.7 compare_reduce_fusion.8
  24.5 0.7 compare_reduce_fusion.7
  25.9 0.7 compare_reduce_fusion.6
  27.2 0.7 compare_reduce_fusion.5
  28.5 0.7 compare_reduce_fusion.4
  29.8 0.7 compare_reduce_fusion.3
  31.1 0.7 compare_reduce_fusion.2
  32.4 0.7 compare_reduce_fusion.1
  33.7 0.7 compare_reduce_fusion
  35.7 1.8 fusion
  38.6 4.4 %collective-permute-start.5 = (bf16[32,1536]{1,0:T(8,128)(2,1)S(1)}, bf16[32,1536]{1,0:T(8,128)(2,1)S(1)}, u32[]{:S(2)}, u32[]{:S(2)}) collective-permute-start(bf16[32,1536]{1,0:T(8,128)(2,1)S(1)} %get-tuple-element.40), channel_id=1, source_target_pairs={{0,160},{16,176},{32,192},{48,208},{64,224},{80,240},{96,0},{112,1... | collective-permute-start | bytes 294920 | tf_op jit(solution)/shard_map/ppermute | solution.py:23
  43.7 4.6 %collective-permute-start.6 = (bf16[32,1536]{1,0:T(8,128)(2,1)S(1)}, bf16[32,1536]{1,0:T(8,128)(2,1)S(1)}, u32[]{:S(2)}, u32[]{:S(2)}) collective-permute-start(bf16[32,1536]{1,0:T(8,128)(2,1)S(1)} %get-tuple-element.40), channel_id=1, source_target_pairs={{0,128},{16,144},{32,160},{48,176},{64,192},{80,208},{96,224},{112... | collective-permute-start | bytes 294920 | tf_op jit(solution)/shard_map/ppermute | solution.py:23
  48.9 1.6 collective-permute-start.7
  50.4 0.7 constant_dynamic-update-slice_fusion.12
  52.2 1.6 collective-permute-start.9
  55.5 1.6 collective-permute-start.11
  58.8 1.6 collective-permute-start.13
  63.8 1.2 collective-permute-done.12
  67.7 3.3 %fusion.5 = (f32[512]{0:T(512)S(1)}, f32[512,512]{1,0:T(8,128)S(1)}) fusion(f32[]{:T(128)} %bitcast.49, bf16[512,1536]{1,0:T(8,128)(2,1)} %constant_dynamic-update-slice_fusion, f32[512]{0:T(512)S(1)} %add_rsqrt_fusion, bf16[512,1536]{1,0:T(8,128)(2,1)S(1)} %copy-done.1, f32[]{:T(128)} %bitcast.47, s32[512]{0:T(512)S(1)} %iota_add_fusion, ...), kind=kOutput, calls=%fused_computation.17 | convolution fusion | flops 811073024 | bytes 4202504 | tf_op jit(solution)/shard_map/dot_general | solution.py:108
  71.1 1.1 fusion.25
  72.7 1.3 convolution_convert_fusion
  74.3 0.8 collective-permute-done.15
  76.0 1.0 pad_maximum_fusion.1
  77.0 7.2 %all-to-all-start = ((bf16[8,32,1664]{2,1,0:T(8,128)(2,1)}), bf16[8,32,1664]{2,1,0:T(8,128)(2,1)S(1)}, u32[]{:S(2)}, u32[]{:S(2)}) async-start(bf16[8,32,1664]{2,1,0:T(8,128)(2,1)} %bitcast.2), calls=%async_computation | async-start | bytes 1703936 | tf_op jit(solution)/shard_map/all_to_all | solution.py:35
  84.2 1.5 constant_dynamic-update-slice_fusion.27
  85.7 1.5 constant_dynamic-update-slice_fusion.26
  87.2 1.5 constant_dynamic-update-slice_fusion.25
  88.8 1.5 constant_dynamic-update-slice_fusion.24
  90.3 8.5 %all-to-all-done = bf16[8,32,1664]{2,1,0:T(8,128)(2,1)S(1)} async-done(((bf16[8,32,1664]{2,1,0:T(8,128)(2,1)}), bf16[8,32,1664]{2,1,0:T(8,128)(2,1)S(1)}, u32[]{:S(2)}, u32[]{:S(2)}) %all-to-all-start) | async-done | bytes 852000 | tf_op jit(solution)/shard_map/all_to_all | solution.py:35
  98.8 0.9 copy-done.2
  99.7 4.8 %all-to-all-start.2 = ((bf16[16,32,1536]{2,1,0:T(8,128)(2,1)}), bf16[16,32,1536]{2,1,0:T(8,128)(2,1)S(1)}, u32[]{:S(2)}, u32[]{:S(2)}) async-start(bf16[16,32,1536]{2,1,0:T(8,128)(2,1)} %bitcast.59), calls=%async_computation.2 | async-start | bytes 3145728 | tf_op jit(solution)/shard_map/all_to_all | solution.py:126
  104.5 1.9 convert_multiply_fusion
  106.5 1.3 convert_reduce_fusion.1
  108.0 1.1 multiply_reduce_fusion
  109.1 1.0 multiply_convert_fusion.1
  110.3 33.3 %all-to-all-done.2 = bf16[16,32,1536]{2,1,0:T(8,128)(2,1)S(1)} async-done(((bf16[16,32,1536]{2,1,0:T(8,128)(2,1)}), bf16[16,32,1536]{2,1,0:T(8,128)(2,1)S(1)}, u32[]{:S(2)}, u32[]{:S(2)}) %all-to-all-start.2) | async-done | bytes 1572896 | tf_op jit(solution)/shard_map/all_to_all | solution.py:126
  143.6 5.1 %all-to-all-start.1 = ((bf16[8,32,1664]{2,1,0:T(8,128)(2,1)}), bf16[8,32,1664]{2,1,0:T(8,128)(2,1)S(1)}, u32[]{:S(2)}, u32[]{:S(2)}) async-start(bf16[8,32,1664]{2,1,0:T(8,128)(2,1)} %bitcast.60), calls=%async_computation.1 | async-start | bytes 1703936 | tf_op jit(solution)/shard_map/all_to_all | solution.py:35
  149.2 0.7 constant_dynamic-update-slice_fusion.47
  149.9 0.7 constant_dynamic-update-slice_fusion.46
  150.6 0.7 constant_dynamic-update-slice_fusion.45
  153.8 0.6 constant_dynamic-update-slice_fusion.40
  154.5 5.1 %all-to-all-done.1 = bf16[8,32,1664]{2,1,0:T(8,128)(2,1)S(1)} async-done(((bf16[8,32,1664]{2,1,0:T(8,128)(2,1)}), bf16[8,32,1664]{2,1,0:T(8,128)(2,1)S(1)}, u32[]{:S(2)}, u32[]{:S(2)}) %all-to-all-start.1) | async-done | bytes 852000 | tf_op jit(solution)/shard_map/all_to_all | solution.py:35
  159.6 4.6 %all-to-all-start.3 = ((bf16[8,32,1536]{2,1,0:T(8,128)(2,1)}), bf16[8,32,1536]{2,1,0:T(8,128)(2,1)S(1)}, u32[]{:S(2)}, u32[]{:S(2)}) async-start(bf16[8,32,1536]{2,1,0:T(8,128)(2,1)} %bitcast.24), calls=%async_computation.3 | async-start | bytes 1572864 | tf_op jit(solution)/shard_map/all_to_all | solution.py:35
  164.3 10.3 %all-to-all-done.3 = bf16[8,32,1536]{2,1,0:T(8,128)(2,1)S(1)} async-done(((bf16[8,32,1536]{2,1,0:T(8,128)(2,1)}), bf16[8,32,1536]{2,1,0:T(8,128)(2,1)S(1)}, u32[]{:S(2)}, u32[]{:S(2)}) %all-to-all-start.3) | async-done | bytes 786464 | tf_op jit(solution)/shard_map/all_to_all | solution.py:35
  175.5 1.4 collective-permute-done.17
  177.5 29.4 %all_to_all.56 = bf16[16,48,384]{2,1,0:T(8,128)(2,1)S(1)} all-to-all(bf16[16,48,384]{2,1,0:T(8,128)(2,1)S(1)} %bitcast.56), channel_id=1, replica_groups=mesh['dp'=16,'mp'=16] {'dp'}, dimensions={0} | all-to-all | bytes 1179648 | tf_op jit(solution)/shard_map/all_to_all | solution.py:82
  207.0 0.9 broadcast_in_dim.93
  207.9 3.6 %all-to-all-start.5 = ((bf16[16,48,384]{2,1,0:T(8,128)(2,1)}), bf16[16,48,384]{2,1,0:T(8,128)(2,1)S(1)}, u32[]{:S(2)}, u32[]{:S(2)}) async-start(bf16[16,48,384]{2,1,0:T(8,128)(2,1)} %broadcast_in_dim.93), calls=%async_computation.5 | async-start | bytes 1179648 | tf_op jit(solution)/shard_map/all_to_all | solution.py:85
  212.4 17.3 %all-to-all-done.5 = bf16[16,48,384]{2,1,0:T(8,128)(2,1)S(1)} async-done(((bf16[16,48,384]{2,1,0:T(8,128)(2,1)}), bf16[16,48,384]{2,1,0:T(8,128)(2,1)S(1)}, u32[]{:S(2)}, u32[]{:S(2)}) %all-to-all-start.5) | async-done | bytes 589856 | tf_op jit(solution)/shard_map/all_to_all | solution.py:85
  230.1 0.9 copy.16
  231.2 0.9 copy.17
  (122 shorter events, 20.4 us)
Async XLA Ops:
  0.6 174.1 %copy-start = (bf16[96,512]{1,0:T(8,128)(2,1)S(1)}, bf16[96,512]{1,0:T(8,128)(2,1)}, u32[]{:S(2)}) copy-start(bf16[96,512]{1,0:T(8,128)(2,1)} %param.8) | copy-start | bytes 294916
  3.3 35.3 %collective-permute-start = (bf16[32,1536]{1,0:T(8,128)(2,1)S(1)}, bf16[32,1536]{1,0:T(8,128)(2,1)S(1)}, u32[]{:S(2)}, u32[]{:S(2)}) collective-permute-start(bf16[32,1536]{1,0:T(8,128)(2,1)S(1)} %get-tuple-element.40), channel_id=1, source_target_pairs={{0,32},{16,48},{32,64},{48,80},{64,96},{80,112},{96,128},{112,144}... | collective-permute-start | bytes 294920 | tf_op jit(solution)/shard_map/ppermute | solution.py:23
  5.2 38.4 %collective-permute-start.1 = (bf16[32,1536]{1,0:T(8,128)(2,1)S(1)}, bf16[32,1536]{1,0:T(8,128)(2,1)S(1)}, u32[]{:S(2)}, u32[]{:S(2)}) collective-permute-start(bf16[32,1536]{1,0:T(8,128)(2,1)S(1)} %get-tuple-element.40), channel_id=1, source_target_pairs={{0,224},{16,240},{32,0},{48,16},{64,32},{80,48},{96,64},{112,80},{... | collective-permute-start | bytes 294920 | tf_op jit(solution)/shard_map/ppermute | solution.py:23
  9.2 39.7 %collective-permute-start.2 = (bf16[32,1536]{1,0:T(8,128)(2,1)S(1)}, bf16[32,1536]{1,0:T(8,128)(2,1)S(1)}, u32[]{:S(2)}, u32[]{:S(2)}) collective-permute-start(bf16[32,1536]{1,0:T(8,128)(2,1)S(1)} %get-tuple-element.40), channel_id=1, source_target_pairs={{0,64},{16,80},{32,96},{48,112},{64,128},{80,144},{96,160},{112,17... | collective-permute-start | bytes 294920 | tf_op jit(solution)/shard_map/ppermute | solution.py:23
  9.2 41.9 %collective-permute-start.3 = (bf16[32,1536]{1,0:T(8,128)(2,1)S(1)}, bf16[32,1536]{1,0:T(8,128)(2,1)S(1)}, u32[]{:S(2)}, u32[]{:S(2)}) collective-permute-start(bf16[32,1536]{1,0:T(8,128)(2,1)S(1)} %get-tuple-element.40), channel_id=1, source_target_pairs={{0,192},{16,208},{32,224},{48,240},{64,0},{80,16},{96,32},{112,48}... | collective-permute-start | bytes 294920 | tf_op jit(solution)/shard_map/ppermute | solution.py:23
  13.3 38.9 %collective-permute-start.4 = (bf16[32,1536]{1,0:T(8,128)(2,1)S(1)}, bf16[32,1536]{1,0:T(8,128)(2,1)S(1)}, u32[]{:S(2)}, u32[]{:S(2)}) collective-permute-start(bf16[32,1536]{1,0:T(8,128)(2,1)S(1)} %get-tuple-element.40), channel_id=1, source_target_pairs={{0,96},{16,112},{32,128},{48,144},{64,160},{80,176},{96,192},{112,... | collective-permute-start | bytes 294920 | tf_op jit(solution)/shard_map/ppermute | solution.py:23
  37.4 30.3 %copy-start.1 = (bf16[512,1536]{1,0:T(8,128)(2,1)S(1)}, bf16[512,1536]{1,0:T(8,128)(2,1)}, u32[]{:S(2)}) copy-start(bf16[512,1536]{1,0:T(8,128)(2,1)} %param.6) | copy-start | bytes 4718596
  38.6 15.8 %collective-permute-start.5 = (bf16[32,1536]{1,0:T(8,128)(2,1)S(1)}, bf16[32,1536]{1,0:T(8,128)(2,1)S(1)}, u32[]{:S(2)}, u32[]{:S(2)}) collective-permute-start(bf16[32,1536]{1,0:T(8,128)(2,1)S(1)} %get-tuple-element.40), channel_id=1, source_target_pairs={{0,160},{16,176},{32,192},{48,208},{64,224},{80,240},{96,0},{112,1... | collective-permute-start | bytes 294920 | tf_op jit(solution)/shard_map/ppermute | solution.py:23
  43.7 11.9 %collective-permute-start.6 = (bf16[32,1536]{1,0:T(8,128)(2,1)S(1)}, bf16[32,1536]{1,0:T(8,128)(2,1)S(1)}, u32[]{:S(2)}, u32[]{:S(2)}) collective-permute-start(bf16[32,1536]{1,0:T(8,128)(2,1)S(1)} %get-tuple-element.40), channel_id=1, source_target_pairs={{0,128},{16,144},{32,160},{48,176},{64,192},{80,208},{96,224},{112... | collective-permute-start | bytes 294920 | tf_op jit(solution)/shard_map/ppermute | solution.py:23
  48.9 8.9 %collective-permute-start.7 = (bf16[32,1536]{1,0:T(8,128)(2,1)S(1)}, bf16[32,1536]{1,0:T(8,128)(2,1)S(1)}, u32[]{:S(2)}, u32[]{:S(2)}) collective-permute-start(bf16[32,1536]{1,0:T(8,128)(2,1)S(1)} %get-tuple-element.40), channel_id=1, source_target_pairs={{0,16},{16,0},{32,48},{48,32},{64,80},{80,64},{96,112},{112,96},{1... | collective-permute-start | bytes 294920 | tf_op jit(solution)/shard_map/ppermute | solution.py:23
  51.1 7.7 %collective-permute-start.8 = (bf16[32,1536]{1,0:T(8,128)(2,1)S(1)}, bf16[32,1536]{1,0:T(8,128)(2,1)S(1)}, u32[]{:S(2)}, u32[]{:S(2)}) collective-permute-start(bf16[32,1536]{1,0:T(8,128)(2,1)S(1)} %collective-permute-done), channel_id=1, source_target_pairs={{0,16},{16,0},{32,48},{48,32},{64,80},{80,64},{96,112},{112,96},{1... | collective-permute-start | bytes 294920 | tf_op jit(solution)/shard_map/ppermute | solution.py:23
  52.2 8.8 %collective-permute-start.9 = (bf16[32,1536]{1,0:T(8,128)(2,1)S(1)}, bf16[32,1536]{1,0:T(8,128)(2,1)S(1)}, u32[]{:S(2)}, u32[]{:S(2)}) collective-permute-start(bf16[32,1536]{1,0:T(8,128)(2,1)S(1)} %collective-permute-done.1), channel_id=1, source_target_pairs={{0,16},{16,0},{32,48},{48,32},{64,80},{80,64},{96,112},{112,96},{1... | collective-permute-start | bytes 294920 | tf_op jit(solution)/shard_map/ppermute | solution.py:23
  54.4 7.7 %collective-permute-start.10 = (bf16[32,1536]{1,0:T(8,128)(2,1)S(1)}, bf16[32,1536]{1,0:T(8,128)(2,1)S(1)}, u32[]{:S(2)}, u32[]{:S(2)}) collective-permute-start(bf16[32,1536]{1,0:T(8,128)(2,1)S(1)} %collective-permute-done.2), channel_id=1, source_target_pairs={{0,16},{16,0},{32,48},{48,32},{64,80},{80,64},{96,112},{112,96},{1... | collective-permute-start | bytes 294920 | tf_op jit(solution)/shard_map/ppermute | solution.py:23
  55.5 7.6 %collective-permute-start.11 = (bf16[32,1536]{1,0:T(8,128)(2,1)S(1)}, bf16[32,1536]{1,0:T(8,128)(2,1)S(1)}, u32[]{:S(2)}, u32[]{:S(2)}) collective-permute-start(bf16[32,1536]{1,0:T(8,128)(2,1)S(1)} %collective-permute-done.3), channel_id=1, source_target_pairs={{0,16},{16,0},{32,48},{48,32},{64,80},{80,64},{96,112},{112,96},{1... | collective-permute-start | bytes 294920 | tf_op jit(solution)/shard_map/ppermute | solution.py:23
  57.7 7.3 %collective-permute-start.12 = (bf16[32,1536]{1,0:T(8,128)(2,1)S(1)}, bf16[32,1536]{1,0:T(8,128)(2,1)S(1)}, u32[]{:S(2)}, u32[]{:S(2)}) collective-permute-start(bf16[32,1536]{1,0:T(8,128)(2,1)S(1)} %collective-permute-done.4), channel_id=1, source_target_pairs={{0,16},{16,0},{32,48},{48,32},{64,80},{80,64},{96,112},{112,96},{1... | collective-permute-start | bytes 294920 | tf_op jit(solution)/shard_map/ppermute | solution.py:23
  58.8 7.2 %collective-permute-start.13 = (bf16[32,1536]{1,0:T(8,128)(2,1)S(1)}, bf16[32,1536]{1,0:T(8,128)(2,1)S(1)}, u32[]{:S(2)}, u32[]{:S(2)}) collective-permute-start(bf16[32,1536]{1,0:T(8,128)(2,1)S(1)} %collective-permute-done.5), channel_id=1, source_target_pairs={{0,16},{16,0},{32,48},{48,32},{64,80},{80,64},{96,112},{112,96},{1... | collective-permute-start | bytes 294920 | tf_op jit(solution)/shard_map/ppermute | solution.py:23
  61.0 6.1 %collective-permute-start.14 = (bf16[32,1536]{1,0:T(8,128)(2,1)S(1)}, bf16[32,1536]{1,0:T(8,128)(2,1)S(1)}, u32[]{:S(2)}, u32[]{:S(2)}) collective-permute-start(bf16[32,1536]{1,0:T(8,128)(2,1)S(1)} %collective-permute-done.6), channel_id=1, source_target_pairs={{0,16},{16,0},{32,48},{48,32},{64,80},{80,64},{96,112},{112,96},{1... | collective-permute-start | bytes 294920 | tf_op jit(solution)/shard_map/ppermute | solution.py:23
  67.7 3.4 %copy-start.8 = (bf16[512,1536]{1,0:T(8,128)(2,1)S(1)}, bf16[512,1536]{1,0:T(8,128)(2,1)}, u32[]{:S(2)}) copy-start(bf16[512,1536]{1,0:T(8,128)(2,1)} %constant_dynamic-update-slice_fusion) | copy-start | bytes 4718596
  72.6 2.5 %collective-permute-start.15 = (bf16[256,1664]{1,0:T(8,128)(2,1)S(1)}, bf16[256,1664]{1,0:T(8,128)(2,1)S(1)}, u32[]{:S(2)}, u32[]{:S(2)}) collective-permute-start(bf16[256,1664]{1,0:T(8,128)(2,1)S(1)} %pad_maximum_fusion), channel_id=1, source_target_pairs={{0,1},{1,0},{2,3},{3,2},{4,5},{5,4},{6,7},{7,6},{8,9},{9,8},{10,11... | collective-permute-start | bytes 2555912 | tf_op jit(solution)/shard_map/ppermute | solution.py:27
  73.9 2.0 copy-start.4
  74.2 1.4 copy-start.3
  77.0 21.8 %all-to-all-start = ((bf16[8,32,1664]{2,1,0:T(8,128)(2,1)}), bf16[8,32,1664]{2,1,0:T(8,128)(2,1)S(1)}, u32[]{:S(2)}, u32[]{:S(2)}) async-start(bf16[8,32,1664]{2,1,0:T(8,128)(2,1)} %bitcast.2), calls=%async_computation | async-start | bytes 1703936 | tf_op jit(solution)/shard_map/all_to_all | solution.py:35
  98.8 0.9 copy-start.2
  99.7 44.0 %all-to-all-start.2 = ((bf16[16,32,1536]{2,1,0:T(8,128)(2,1)}), bf16[16,32,1536]{2,1,0:T(8,128)(2,1)S(1)}, u32[]{:S(2)}, u32[]{:S(2)}) async-start(bf16[16,32,1536]{2,1,0:T(8,128)(2,1)} %bitcast.59), calls=%async_computation.2 | async-start | bytes 3145728 | tf_op jit(solution)/shard_map/all_to_all | solution.py:126
  110.3 33.3 %copy-start.6 = (bf16[256,1664]{1,0:T(8,128)(2,1)}, bf16[256,1664]{1,0:T(8,128)(2,1)S(1)}, u32[]{:S(2)}) copy-start(bf16[256,1664]{1,0:T(8,128)(2,1)S(1)} %constant_dynamic-update-slice_fusion.16) | copy-start | bytes 2555908
  143.6 5.3 %copy-start.5 = (bf16[32,1536]{1,0:T(8,128)(2,1)S(1)}, bf16[32,1536]{1,0:T(8,128)(2,1)}, u32[]{:S(2)}) copy-start(bf16[32,1536]{1,0:T(8,128)(2,1)} %param.7) | copy-start | bytes 294916
  143.6 15.9 %all-to-all-start.1 = ((bf16[8,32,1664]{2,1,0:T(8,128)(2,1)}), bf16[8,32,1664]{2,1,0:T(8,128)(2,1)S(1)}, u32[]{:S(2)}, u32[]{:S(2)}) async-start(bf16[8,32,1664]{2,1,0:T(8,128)(2,1)} %bitcast.60), calls=%async_computation.1 | async-start | bytes 1703936 | tf_op jit(solution)/shard_map/all_to_all | solution.py:35
  149.9 14.3 %copy-start.7 = (bf16[96,512]{1,0:T(8,128)(2,1)S(1)}, bf16[96,512]{1,0:T(8,128)(2,1)}, u32[]{:S(2)}) copy-start(bf16[96,512]{1,0:T(8,128)(2,1)} %param.9) | copy-start | bytes 294916
  159.6 15.1 %all-to-all-start.3 = ((bf16[8,32,1536]{2,1,0:T(8,128)(2,1)}), bf16[8,32,1536]{2,1,0:T(8,128)(2,1)S(1)}, u32[]{:S(2)}, u32[]{:S(2)}) async-start(bf16[8,32,1536]{2,1,0:T(8,128)(2,1)} %bitcast.24), calls=%async_computation.3 | async-start | bytes 1572864 | tf_op jit(solution)/shard_map/all_to_all | solution.py:35
  164.2 10.8 %collective-permute-start.16 = (bf16[256,1664]{1,0:T(8,128)(2,1)S(1)}, bf16[256,1664]{1,0:T(8,128)(2,1)S(1)}, u32[]{:S(2)}, u32[]{:S(2)}) collective-permute-start(bf16[256,1664]{1,0:T(8,128)(2,1)S(1)} %bitcast.50), channel_id=1, source_target_pairs={{0,1},{1,0},{2,3},{3,2},{4,5},{5,4},{6,7},{7,6},{8,9},{9,8},{10,11... | collective-permute-start | bytes 2555912 | tf_op jit(solution)/shard_map/ppermute | solution.py:27
  174.7 2.3 collective-permute-start.17
  207.9 21.8 %all-to-all-start.5 = ((bf16[16,48,384]{2,1,0:T(8,128)(2,1)}), bf16[16,48,384]{2,1,0:T(8,128)(2,1)S(1)}, u32[]{:S(2)}, u32[]{:S(2)}) async-start(bf16[16,48,384]{2,1,0:T(8,128)(2,1)} %broadcast_in_dim.93), calls=%async_computation.5 | async-start | bytes 1179648 | tf_op jit(solution)/shard_map/all_to_all | solution.py:85

commit v2 on v0

v2 whole, which is shorter than its diff:
```python
import jax
import jax.numpy as jnp
from jax import lax
from jax.experimental import pallas as pl
from jax.experimental.pallas import tpu as pltpu
from jax.sharding import PartitionSpec as P

F32 = jnp.float32
BF16 = jnp.bfloat16
LANES = 128
ALONG = (0, 1, -1, 2, -2, 3, -3, 4)
VMEM = pl.BlockSpec(memory_space=pltpu.VMEM)
SMEM = pl.BlockSpec(memory_space=pltpu.SMEM)


def local(kernel, outs, operands, specs=None, scratch=()):
    single = not isinstance(outs, list)
    shapes = [jax.ShapeDtypeStruct(*out) for out in ([outs] if single else outs)]
    result = pl.pallas_call(
        kernel,
        out_shape=shapes,
        in_specs=specs or [VMEM] * len(operands),
        out_specs=[VMEM] * len(shapes),
        scratch_shapes=list(scratch),
        compiler_params=pltpu.CompilerParams(vmem_limit_bytes=40 * 2**20),
    )(*operands)
    return result[0] if single else result


def normalize(raw):
    values = raw.astype(F32)
    inverse = lax.rsqrt(jnp.sum(values * values, axis=1, keepdims=True) + 1e-06)
    return (values * inverse, inverse)


def through_norm(upstream, normed, inverse):
    return (upstream - normed * jnp.sum(normed * upstream, axis=1, keepdims=True)) * inverse


def along_z(value, steps):
    return lax.ppermute(value, "dp", [(d, (d + 2 * steps) % 16) for d in range(16)])


def swap_y(value):
    return lax.ppermute(value, "dp", [(d, d ^ 1) for d in range(16)])


def swap_core(value):
    return lax.ppermute(value, "mp", [(m, m ^ 1) for m in range(16)])


def normalize_kernel(raw_ref, out_ref):
    out_ref[...] = normalize(raw_ref[...])[0].astype(BF16)


def loss_columns(losses):
    high = losses.astype(BF16)
    low = (losses - high.astype(F32)).astype(BF16)
    lane = lax.broadcasted_iota(jnp.int32, (losses.shape[0], LANES), 1)
    zero = jnp.zeros((), BF16)
    return jnp.where(lane == 0, high, jnp.where(lane == 1, low, zero))


def column_loss(extra):
    values = extra.astype(F32)
    return values[:, 0:1] + values[:, 1:2]


def tile_kernel(*refs):
    numbers, places, text_ids = refs[0], refs[1], refs[2]
    blocks, near, far = refs[3:11], refs[11], refs[12]
    keep_ref, keep_loss, send_ref = refs[13], refs[14], refs[15]
    text_outs, texts, slopes = refs[16:24], refs[24], refs[25]
    sub, width = blocks[0].shape
    for i, block in enumerate(blocks):
        texts[pl.ds(i * sub, sub), :] = block[...]
    scale, bias = numbers[0], numbers[1]
    rows = near.shape[0] // 2
    for part, source in enumerate((near, far)):
        for y in range(2):
            own = pl.ds(y * rows, rows)
            logits = scale * lax.dot_general(
                source[own, :], texts[...], (((1,), (1,)), ((), ())), preferred_element_type=F32
            ) + bias
            ids = places[2 * part + y] + lax.broadcasted_iota(jnp.int32, logits.shape, 0)
            match = ids == text_ids[...]
            u = jnp.where(match, -logits, logits)
            e = jnp.exp(-jnp.abs(u))
            w = 1.0 + e
            grown = jnp.where(w == 1.0, e, jnp.log(w) * (e / jnp.where(w == 1.0, 1.0, w - 1.0)))
            losses = jnp.sum(jnp.maximum(u, 0.0) + grown, axis=1, keepdims=True)
            slope = jnp.where(match, -scale, scale) * (jnp.where(u >= 0.0, 1.0, e) / w)
            slope = slope.astype(BF16)
            slopes[pl.ds((2 * part + y) * rows, rows), :] = slope
            grad = jnp.dot(slope, texts[...], preferred_element_type=F32)
            if part == 0:
                keep_ref[own, :] = grad
                keep_loss[own, :] = losses
            else:
                send_ref[own, pl.ds(0, width)] = grad.astype(BF16)
                send_ref[own, pl.ds(width, LANES)] = loss_columns(losses)
    across = (((0,), (0,)), ((), ()))
    text_grad = lax.dot_general(
        slopes[pl.ds(0, 2 * rows), :], near[...], across, preferred_element_type=F32
    ) + lax.dot_general(
        slopes[pl.ds(2 * rows, 2 * rows), :], far[...], across, preferred_element_type=F32
    )
    for i, out in enumerate(text_outs):
        out[...] = text_grad[i * sub : (i + 1) * sub].astype(BF16)


def join_kernel(keep_ref, keep_loss, came_ref, out_ref):
    width = keep_ref.shape[1]
    out_ref[:, pl.ds(0, width)] = (
        keep_ref[...] + came_ref[:, pl.ds(0, width)].astype(F32)
    ).astype(BF16)
    out_ref[:, pl.ds(width, LANES)] = loss_columns(
        keep_loss[...] + column_loss(came_ref[:, pl.ds(width, LANES)])
    )


def grad_kernel(*refs):
    pieces, blocks = refs[0], refs[1:9]
    raw_img, raw_txt, out_ref = refs[9], refs[10], refs[11]
    rows, width = raw_img.shape
    image_grad = pieces[0, :, pl.ds(0, width)].astype(F32)
    losses = column_loss(pieces[0, :, pl.ds(width, LANES)])
    for i in range(1, pieces.shape[0]):
        image_grad += pieces[i, :, pl.ds(0, width)].astype(F32)
        losses += column_loss(pieces[i, :, pl.ds(width, LANES)])
    text_grad = blocks[0][...].astype(F32)
    for block in blocks[1:]:
        text_grad += block[...].astype(F32)
    d_img = through_norm(image_grad, *normalize(raw_img[...])).astype(BF16)
    d_txt = through_norm(text_grad, *normalize(raw_txt[...])).astype(BF16)
    extra = loss_columns(losses)
    for i in range(out_ref.shape[0]):
        out_ref[i, pl.ds(0, rows), pl.ds(0, width)] = d_img
        out_ref[i, pl.ds(0, rows), pl.ds(width, LANES)] = extra
        out_ref[i, pl.ds(rows, rows), pl.ds(0, width)] = d_txt
        out_ref[i, pl.ds(rows, rows), pl.ds(width, LANES)] = jnp.zeros_like(extra)


def weight_kernel(img_ref, txt_ref, grads_ref, keep_ref, send_ref):
    count, rows = img_ref.shape[0] // 2, grads_ref.shape[1] // 2
    width = keep_ref.shape[1]
    for kind, feats in enumerate((img_ref, txt_ref)):
        grads = jnp.concatenate(
            [
                grads_ref[j, pl.ds(kind * rows, rows), pl.ds(0, width)]
                for j in range(grads_ref.shape[0])
            ],
            axis=0,
        )
        both = jnp.dot(feats[...], grads, preferred_element_type=F32)
        keep_ref[pl.ds(kind * count, count), :] = both[:count]
        send_ref[pl.ds(kind * count, count), :] = both[count:].astype(BF16)


def cut_kernel(keep_ref, came_ref, out_ref):
    rows, cols = out_ref.shape[1:]
    for r in range(4):
        for c in range(4):
            place = (pl.ds(r * rows, rows), pl.ds(c * cols, cols))
            out_ref[4 * r + c] = (keep_ref[place] + came_ref[place].astype(F32)).astype(BF16)


def spread_kernel(parts_ref, out_ref):
    total = parts_ref[0].astype(F32)
    for i in range(1, parts_ref.shape[0]):
        total += parts_ref[i].astype(F32)
    total = total.astype(BF16)
    for i in range(out_ref.shape[0]):
        out_ref[i] = total


def paste_kernel(parts_ref, img_ref, txt_ref):
    rows, cols = parts_ref.shape[1:]
    for r in range(4):
        out = (img_ref, txt_ref)[r // 2]
        for c in range(4):
            out[pl.ds((r % 2) * rows, rows), pl.ds(c * cols, cols)] = parts_ref[4 * r + c].astype(F32)


def shards(img_emb, txt_emb, img_feat_t, txt_feat_t, logit_scale, logit_bias):
    rows, width = img_emb.shape
    sub = txt_emb.shape[0]
    half = rows // 2
    feats = img_feat_t.shape[0]
    dp_index = lax.axis_index("dp").astype(jnp.int32)
    mp_index = lax.axis_index("mp").astype(jnp.int32)
    core, chip = mp_index % 2, mp_index // 2
    z, y = dp_index // 2, dp_index % 2

    texts = local(normalize_kernel, ((sub, width), BF16), [txt_emb])
    blocks = [texts] + [along_z(texts, steps) for steps in ALONG[1:]]

    own = lax.dynamic_slice_in_dim(img_emb, core * half, half, 0)
    partner = swap_y(own)
    near_raw = jnp.where(
        y == 0, jnp.concatenate([own, partner]), jnp.concatenate([partner, own])
    )
    far_raw = swap_core(near_raw)
    near = local(normalize_kernel, ((rows, width), BF16), [near_raw])
    far = local(normalize_kernel, ((rows, width), BF16), [far_raw])

    owners = jnp.stack([2 * ((z - steps) % 8) + y for steps in ALONG])
    text_ids = owners[:, None] * rows + mp_index * sub + jnp.arange(sub, dtype=jnp.int32)[None]
    places = jnp.stack(
        [(2 * z + s) * rows + c * half for c in (core, 1 - core) for s in range(2)]
    ).astype(jnp.int32)
    numbers = jnp.concatenate([logit_scale, logit_bias])
    outs = local(
        tile_kernel,
        [((rows, width), F32), ((rows, 1), F32), ((rows, width + LANES), BF16)]
        + [((sub, width), BF16)] * 8,
        [numbers, places, text_ids.astype(jnp.int32).reshape(1, 8 * sub), *blocks, near, far],
        [SMEM, SMEM] + [VMEM] * 11,
        [pltpu.VMEM((8 * sub, width), BF16), pltpu.VMEM((2 * rows, 8 * sub), BF16)],
    )
    keep, keep_loss, send, text_parts = outs[0], outs[1], outs[2], outs[3:]
    text_came = [text_parts[0]] + [
        along_z(part, -steps) for part, steps in zip(text_parts[1:], ALONG[1:], strict=True)
    ]
    joined = local(
        join_kernel, ((rows, width + LANES), BF16), [keep, keep_loss, swap_core(send)]
    )
    plane = [
        [(2 * s + t) * 16 + 2 * k + c for t in range(2) for k in range(8)]
        for s in range(8)
        for c in range(2)
    ]
    pieces = lax.all_to_all(
        joined.reshape(16, sub, width + LANES), ("dp", "mp"), 0, 0, tiled=True,
        axis_index_groups=plane,
    )
    raw_img = lax.dynamic_slice_in_dim(img_emb, core * half + chip * sub, sub, 0)
    spread = local(
        grad_kernel, ((8, 2 * sub, width + LANES), BF16), [pieces, *text_came, raw_img, txt_emb]
    )
    same_core = [[2 * k + c for k in range(8)] for c in range(2)]
    grads = lax.all_to_all(spread, "mp", 0, 0, tiled=True, axis_index_groups=same_core)

    both_img = jnp.concatenate([img_feat_t, swap_core(img_feat_t)])
    both_txt = jnp.concatenate([txt_feat_t, swap_core(txt_feat_t)])
    img_part = lax.dynamic_slice_in_dim(both_img, core * half, half, 1)
    txt_part = both_txt.reshape(2 * feats, 8, 2, sub)
    txt_part = jnp.where(core == 0, txt_part[:, :, 0], txt_part[:, :, 1]).reshape(2 * feats, half)
    kept, sent = local(
        weight_kernel,
        [((2 * feats, width), F32), ((2 * feats, width), BF16)],
        [img_part, txt_part, grads],
    )
    shape = (16, feats // 2, width // 4)
    cut = local(cut_kernel, (shape, BF16), [kept, swap_core(sent)])
    parts = lax.all_to_all(cut, "dp", 0, 0, tiled=True)
    summed = local(spread_kernel, (shape, BF16), [parts])
    weights = lax.all_to_all(summed, "dp", 0, 0, tiled=True)
    img_weight, txt_weight = local(paste_kernel, [((feats, width), F32)] * 2, [weights])

    extra = grads[:, :sub, width : width + 2].astype(F32)
    own_loss = (extra[:, :, 0] + extra[:, :, 1]).reshape(half)
    other_loss = swap_core(own_loss)
    row_loss = jnp.where(
        core == 0,
        jnp.concatenate([own_loss, other_loss]),
        jnp.concatenate([other_loss, own_loss]),
    )
    return (row_loss, img_weight, txt_weight)


def solution(mesh):
    in_specs = (P("dp", None), P(("dp", "mp"), None), P("mp", "dp"), P("mp", "dp"), P(), P())
    out_specs = (P("dp"), P("mp", None), P("mp", None))
    return jax.shard_map(shards, mesh=mesh, in_specs=in_specs, out_specs=out_specs, check_vma=False)
```

time: 584 us -> 188 us (0.32)
  waiting for transfers between devices: 391 us -> 68.9 us
  matrix products: 79 us -> 0 us
  starting transfers between devices: 21.3 us -> 54.9 us
  other arithmetic: 28 us -> 5.86 us
  between operations: 15.3 us -> 2.35 us
  Pallas kernels: 0 us -> 12.3 us
    psum x2 -> x0, waiting for transfers between devices: 243 us -> none  [the longest x1 134 us: shards(): image_grad, losses = lax.psum((image_part, losses), 'mp')]
    dot_general x35 -> x0, matrix products: 79 us -> none  [the longest x16 41.5 us: visit(): jnp.dot(slopes, images, preferred_element_type=jnp.float32)]
    ppermute x31 -> x21, waiting for transfers between devices: 91.6 us -> 34.4 us  [the longest x1 17.8 us: swap_y(): return lax.ppermute(value, 'dp', [(d, d ^ 1) for d in range(16)])]
    all_gather x1 -> x0, waiting for transfers between devices: 56.4 us -> none  [shards(): d_txt_rows = lax.all_gather(d_txt, 'mp', axis=0, tiled=True)]
    all_to_all x0 -> x3, waiting for transfers between devices: none -> 34.4 us  [the longest x1 17.3 us: shards(): lax.all_to_all(spread, 'mp', 0, 0, tiled=True, axis_index_groups=same_core)]
    psum x1 -> x0, blocking collectives: 30.9 us -> none  [shards(): image_grad, losses = lax.psum((image_part, losses), 'mp')]
    all_to_all x0 -> x1, blocking collectives: none -> 26.6 us  [shards(): parts = lax.all_to_all(cut, 'dp', 0, 0, tiled=True)]
    dynamic_update_slice x16 -> x0, other arithmetic: 20.9 us -> none  [visit(): lax.dynamic_update_slice_in_dim(slope_store, slopes, step * sub, 0)]
  transfers between devices with their start and end apart: 34 -> 24, of which waited for: 24 -> 10; matrix products, arithmetic and copies ran while one was open for 18% -> 3% of each run, Pallas kernels for 0% -> 1%
where the time goes in v2:
time: 188 us; the launch traced here: 187 us
  waiting for transfers between devices  68.9 us (37%)
  starting transfers between devices  54.9 us (29%)
  blocking collectives  26.6 us (14%)
  local copies, waits for them, and re-layouts  16.2 us (9%)
  Pallas kernels  12.3 us (7%)
  other arithmetic  5.86 us (3%)
  between operations  2.35 us (1%)
    ppermute x14, starting transfers between devices, along_z(): lax.ppermute(value, 'dp', [(d, (d + 2 * steps) % 16) for d in range(16)])  33.7 us
    all_to_all x1, blocking collectives, shards(): parts = lax.all_to_all(cut, 'dp', 0, 0, tiled=True)  26.6 us
    ppermute x1, waiting for transfers between devices, swap_y(): return lax.ppermute(value, 'dp', [(d, d ^ 1) for d in range(16)])  17.8 us
    all_to_all x1, waiting for transfers between devices, shards(): lax.all_to_all(spread, 'mp', 0, 0, tiled=True, axis_index_groups=same_core)  17.3 us
    all_to_all x1, waiting for transfers between devices, shards(): weights = lax.all_to_all(summed, 'dp', 0, 0, tiled=True)  16.2 us
    unnamed x57, local copies, waits for them, and re-layouts  14.9 us
    pallas_call x10, Pallas kernels, local(): pl.pallas_call(kernel, out_shape=shapes, in_specs=specs or [VMEM] * len(o...  12.3 us
    ppermute x14, waiting for transfers between devices, along_z(): lax.ppermute(value, 'dp', [(d, (d + 2 * steps) % 16) for d in range(16)])  8.93 us
  transfers between devices with their start and end apart: 24, of which 10 were waited for; matrix products, arithmetic and copies ran while one was open for 3% of the time, Pallas kernels for 1%

profile of v2, /device:TPU:2, one launch (start us, length us, event | category | flops | bytes accessed | tf_op | source)
XLA Modules:
  0.0 187.1 jit_solution(15574998192328369728)
XLA Ops:
  0.7 1.4 copy-done
  2.1 1.7 collective-permute-start.7
  3.8 17.8 %collective-permute-done.7 = bf16[256,1536]{1,0:T(8,128)(2,1)} collective-permute-done((bf16[256,1536]{1,0:T(8,128)(2,1)S(1)}, bf16[256,1536]{1,0:T(8,128)(2,1)}, u32[]{:S(2)}, u32[]{:S(2)}) %collective-permute-start.7) | collective-permute-done | bytes 786464 | tf_op jit(solution)/shard_map/ppermute | solution.py:45
  21.6 2.3 %maximum_select_fusion.raw_ref = bf16[512,1536]{1,0:T(8,128)(2,1)S(1)} fusion(bf16[256,1536]{1,0:T(8,128)(2,1)} %collective-permute-done.7, bf16[256,1536]{1,0:T(8,128)(2,1)} %copy-done.26, pred[]{:T(512)S(6)} %eq.19), kind=kLoop, calls=%fused_computation | loop fusion | flops 7077888 | bytes 3145729 | tf_op jit(solution)/shard_map/jit(_where)/select_n | solution.py:200
  24.0 0.1 shard_map.85.refs_3_
  24.1 2.0 %collective-permute-start = (bf16[32,1536]{1,0:T(8,128)(2,1)S(1)}, bf16[32,1536]{1,0:T(8,128)(2,1)S(1)}, u32[]{:S(2)}, u32[]{:S(2)}) collective-permute-start(bf16[32,1536]{1,0:T(8,128)(2,1)S(1)} %shard_map.85.refs_3_), channel_id=1, source_target_pairs={{0,32},{16,48},{32,64},{48,80},{64,96},{80,112},{96,128},{112,144}... | collective-permute-start | bytes 294920 | tf_op jit(solution)/shard_map/ppermute | solution.py:41
  26.1 4.0 %collective-permute-start.1 = (bf16[32,1536]{1,0:T(8,128)(2,1)S(1)}, bf16[32,1536]{1,0:T(8,128)(2,1)}, u32[]{:S(2)}, u32[]{:S(2)}) collective-permute-start(bf16[32,1536]{1,0:T(8,128)(2,1)S(1)} %shard_map.85.refs_3_), channel_id=1, source_target_pairs={{0,224},{16,240},{32,0},{48,16},{64,32},{80,48},{96,64},{112,80},{... | collective-permute-start | bytes 294920 | tf_op jit(solution)/shard_map/ppermute | solution.py:41
  30.1 4.1 %collective-permute-start.3 = (bf16[32,1536]{1,0:T(8,128)(2,1)S(1)}, bf16[32,1536]{1,0:T(8,128)(2,1)}, u32[]{:S(2)}, u32[]{:S(2)}) collective-permute-start(bf16[32,1536]{1,0:T(8,128)(2,1)S(1)} %shard_map.85.refs_3_), channel_id=1, source_target_pairs={{0,192},{16,208},{32,224},{48,240},{64,0},{80,16},{96,32},{112,48}... | collective-permute-start | bytes 294920 | tf_op jit(solution)/shard_map/ppermute | solution.py:41
  35.9 0.6 collective-permute-start.4
  36.5 4.4 %collective-permute-start.5 = (bf16[32,1536]{1,0:T(8,128)(2,1)S(1)}, bf16[32,1536]{1,0:T(8,128)(2,1)S(1)}, u32[]{:S(2)}, u32[]{:S(2)}) collective-permute-start(bf16[32,1536]{1,0:T(8,128)(2,1)S(1)} %shard_map.85.refs_3_), channel_id=1, source_target_pairs={{0,160},{16,176},{32,192},{48,208},{64,224},{80,240},{96,0},{112,1... | collective-permute-start | bytes 294920 | tf_op jit(solution)/shard_map/ppermute | solution.py:41
  41.0 4.5 %collective-permute-start.6 = (bf16[32,1536]{1,0:T(8,128)(2,1)S(1)}, bf16[32,1536]{1,0:T(8,128)(2,1)S(1)}, u32[]{:S(2)}, u32[]{:S(2)}) collective-permute-start(bf16[32,1536]{1,0:T(8,128)(2,1)S(1)} %shard_map.85.refs_3_), channel_id=1, source_target_pairs={{0,128},{16,144},{32,160},{48,176},{64,192},{80,208},{96,224},{112... | collective-permute-start | bytes 294920 | tf_op jit(solution)/shard_map/ppermute | solution.py:41
  45.5 0.5 shard_map.86.refs_11_
  46.0 1.9 %shard_map.87.refs_12_ = bf16[512,1536]{1,0:T(8,128)(2,1)S(1)} custom-call(bf16[512,1536]{1,0:T(8,128)(2,1)} %collective-permute-done.8.raw_ref), custom_call_target="tpu_custom_call" | custom-call | tf_op jit(solution)/shard_map/pallas_call | solution.py:19
  47.9 3.3 %collective-permute-done.6.refs_10_ = bf16[32,1536]{1,0:T(8,128)(2,1)S(1)} collective-permute-done((bf16[32,1536]{1,0:T(8,128)(2,1)S(1)}, bf16[32,1536]{1,0:T(8,128)(2,1)S(1)}, u32[]{:S(2)}, u32[]{:S(2)}) %collective-permute-start.6) | collective-permute-done | bytes 98336 | tf_op jit(solution)/shard_map/ppermute | solution.py:41
  51.2 4.9 %shard_map.88 = (f32[512,1536]{1,0:T(8,128)S(1)}, f32[512,1]{1,0:T(8,128)S(1)}, bf16[512,1664]{1,0:T(8,128)(2,1)S(1)}, bf16[32,1536]{1,0:T(8,128)(2,1)S(1)}, bf1...) custom-call(f32[2]{0:T(128)S(1)} %pad_maximum_fusion.1.refs_0_, ...), custom_call_target="tpu_custom_call" | custom-call | tf_op jit(solution)/shard_map/pallas_call | solution.py:19
  56.2 0.3 collective-permute-start.9
  56.5 3.6 %collective-permute-done.9.came_ref = bf16[512,1664]{1,0:T(8,128)(2,1)S(1)} collective-permute-done((bf16[512,1664]{1,0:T(8,128)(2,1)S(1)}, bf16[512,1664]{1,0:T(8,128)(2,1)S(1)}, u32[]{:S(2)}, u32[]{:S(2)}) %collective-permute-start.9) | collective-permute-done | bytes 1703968 | tf_op jit(solution)/shard_map/ppermute | solution.py:49
  60.1 0.8 shard_map.89
  60.9 1.2 copy-done.2
  62.1 7.5 %all-to-all-start = ((bf16[16,32,1664]{2,1,0:T(8,128)(2,1)}), bf16[16,32,1664]{2,1,0:T(8,128)(2,1)S(1)}, u32[]{:S(2)}, u32[]{:S(2)}) async-start(bf16[16,32,1664]{2,1,0:T(8,128)(2,1)} %bitcast.15), calls=%async_computation | async-start | bytes 3407872 | tf_op jit(solution)/shard_map/all_to_all | solution.py:233
  69.6 4.6 %collective-permute-start.11 = (bf16[32,1536]{1,0:T(8,128)(2,1)}, bf16[32,1536]{1,0:T(8,128)(2,1)}, u32[]{:S(2)}, u32[]{:S(2)}) collective-permute-start(bf16[32,1536]{1,0:T(8,128)(2,1)} %copy-done.24), channel_id=1, source_target_pairs={{0,32},{16,48},{32,64},{48,80},{64,96},{80,112},{96,128},{112,144}... | collective-permute-start | bytes 294920 | tf_op jit(solution)/shard_map/ppermute | solution.py:41
  74.3 0.6 collective-permute-start.12
  74.9 2.3 %collective-permute-start.13 = (bf16[32,1536]{1,0:T(8,128)(2,1)}, bf16[32,1536]{1,0:T(8,128)(2,1)S(1)}, u32[]{:S(2)}, u32[]{:S(2)}) collective-permute-start(bf16[32,1536]{1,0:T(8,128)(2,1)} %copy-done.22), channel_id=1, source_target_pairs={{0,64},{16,80},{32,96},{48,112},{64,128},{80,144},{96,160},{112,17... | collective-permute-start | bytes 294920 | tf_op jit(solution)/shard_map/ppermute | solution.py:41
  77.2 2.1 %collective-permute-start.14 = (bf16[32,1536]{1,0:T(8,128)(2,1)}, bf16[32,1536]{1,0:T(8,128)(2,1)S(1)}, u32[]{:S(2)}, u32[]{:S(2)}) collective-permute-start(bf16[32,1536]{1,0:T(8,128)(2,1)} %copy-done.21), channel_id=1, source_target_pairs={{0,160},{16,176},{32,192},{48,208},{64,224},{80,240},{96,0},{112,1... | collective-permute-start | bytes 294920 | tf_op jit(solution)/shard_map/ppermute | solution.py:41
  79.3 0.6 copy-done.7
  79.9 1.7 collective-permute-start.15
  81.7 2.6 %collective-permute-start.16 = (bf16[32,1536]{1,0:T(8,128)(2,1)}, bf16[32,1536]{1,0:T(8,128)(2,1)S(1)}, u32[]{:S(2)}, u32[]{:S(2)}) collective-permute-start(bf16[32,1536]{1,0:T(8,128)(2,1)} %copy-done.19), channel_id=1, source_target_pairs={{0,128},{16,144},{32,160},{48,176},{64,192},{80,208},{96,224},{112... | collective-permute-start | bytes 294920 | tf_op jit(solution)/shard_map/ppermute | solution.py:41
  84.3 0.6 copy-done.9
  84.9 0.6 copy-done.11
  85.5 5.6 %collective-permute-done.14.refs_6_ = bf16[32,1536]{1,0:T(8,128)(2,1)S(1)} collective-permute-done((bf16[32,1536]{1,0:T(8,128)(2,1)}, bf16[32,1536]{1,0:T(8,128)(2,1)S(1)}, u32[]{:S(2)}, u32[]{:S(2)}) %collective-permute-start.14) | collective-permute-done | bytes 98336 | tf_op jit(solution)/shard_map/ppermute | solution.py:41
  91.2 0.6 copy-done.13
  91.8 0.7 copy-done.15
  92.5 0.6 copy-done.17
  93.1 0.9 all-to-all-done.refs_0_
  94.0 0.9 copy-done.6
  94.9 0.9 copy-done.8
  95.8 0.9 copy-done.10
  96.7 0.9 copy-done.12
  97.6 0.9 copy-done.14
  98.5 0.9 copy-done.16
  99.4 0.9 copy-done.18
  100.2 1.4 shard_map.90
  101.7 1.2 copy-done.1
  102.9 6.8 %all-to-all-start.1 = ((bf16[8,64,1664]{2,1,0:T(8,128)(2,1)}), bf16[8,64,1664]{2,1,0:T(8,128)(2,1)S(1)}, u32[]{:S(2)}, u32[]{:S(2)}) async-start(bf16[8,64,1664]{2,1,0:T(8,128)(2,1)} %copy-done.1), calls=%async_computation.1 | async-start | bytes 3407872 | tf_op jit(solution)/shard_map/all_to_all | solution.py:242
  109.7 0.1 copy.12
  109.8 0.1 collective-permute-start.19
  109.9 0.5 collective-permute-start.18
  110.4 1.0 collective-permute-done.19
  111.4 1.0 pad_maximum_fusion
  112.5 0.7 slice_select_fusion
  113.1 1.0 copy.13.txt_ref
  114.1 0.8 fusion.1.img_ref
  115.0 17.3 %all-to-all-done.1.grads_ref = bf16[8,64,1664]{2,1,0:T(8,128)(2,1)S(1)} async-done(((bf16[8,64,1664]{2,1,0:T(8,128)(2,1)}), bf16[8,64,1664]{2,1,0:T(8,128)(2,1)S(1)}, u32[]{:S(2)}, u32[]{:S(2)}) %all-to-all-start.1) | async-done | bytes 1703968 | tf_op jit(solution)/shard_map/all_to_all | solution.py:242
  132.3 0.5 shard_map.91
  132.9 2.0 %collective-permute-done.20.came_ref = bf16[192,1536]{1,0:T(8,128)(2,1)S(1)} collective-permute-done((bf16[192,1536]{1,0:T(8,128)(2,1)S(1)}, bf16[192,1536]{1,0:T(8,128)(2,1)S(1)}, u32[]{:S(2)}, u32[]{:S(2)}) %collective-permute-start.20) | collective-permute-done | bytes 589856 | tf_op jit(solution)/shard_map/ppermute | solution.py:49
  134.9 0.1 shard_map.92
  135.0 26.6 %all_to_all.20.parts_ref = bf16[16,48,384]{2,1,0:T(8,128)(2,1)S(1)} all-to-all(bf16[16,48,384]{2,1,0:T(8,128)(2,1)S(1)} %shard_map.92), channel_id=1, replica_groups=mesh['dp'=16,'mp'=16] {'dp'}, dimensions={0} | all-to-all | bytes 1179648 | tf_op jit(solution)/shard_map/all_to_all | solution.py:256
  161.7 0.8 copy-done.3
  162.5 4.3 %all-to-all-start.3 = ((bf16[16,48,384]{2,1,0:T(8,128)(2,1)}), bf16[16,48,384]{2,1,0:T(8,128)(2,1)}, u32[]{:S(2)}, u32[]{:S(2)}) async-start(bf16[16,48,384]{2,1,0:T(8,128)(2,1)} %copy-done.3), calls=%async_computation.3 | async-start | bytes 1179648 | tf_op jit(solution)/shard_map/all_to_all | solution.py:258
  166.8 0.2 fusion
  167.1 1.1 collective-permute-done.17
  168.2 0.6 maximum_select_fusion.1
  168.8 16.2 %all-to-all-done.3.parts_ref = bf16[16,48,384]{2,1,0:T(8,128)(2,1)} async-done(((bf16[16,48,384]{2,1,0:T(8,128)(2,1)}), bf16[16,48,384]{2,1,0:T(8,128)(2,1)}, u32[]{:S(2)}, u32[]{:S(2)}) %all-to-all-start.3) | async-done | bytes 589856 | tf_op jit(solution)/shard_map/all_to_all | solution.py:258
  185.0 2.1 %shard_map.94 = (f32[96,1536]{1,0:T(8,128)}, f32[96,1536]{1,0:T(8,128)}) custom-call(bf16[16,48,384]{2,1,0:T(8,128)(2,1)} %all-to-all-done.3.parts_ref), custom_call_target="tpu_custom_call" | custom-call | tf_op jit(solution)/shard_map/pallas_call | solution.py:19
  (69 shorter events, 1.0 us)
Async XLA Ops:
  0.6 1.4 copy-start
  2.1 1.7 copy-start.26
  2.1 19.5 %collective-permute-start.7 = (bf16[256,1536]{1,0:T(8,128)(2,1)S(1)}, bf16[256,1536]{1,0:T(8,128)(2,1)}, u32[]{:S(2)}, u32[]{:S(2)}) collective-permute-start(bf16[256,1536]{1,0:T(8,128)(2,1)S(1)} %constant_dynamic-slice_fusion.1), channel_id=1, source_target_pairs={{0,16},{16,0},{32,48},{48,32},{64,80},{80,64},{96,112},{112,96},{1... | collective-permute-start | bytes 2359304 | tf_op jit(solution)/shard_map/ppermute | solution.py:45
  3.8 20.2 %copy-start.4 = (bf16[32,1536]{1,0:T(8,128)(2,1)S(1)}, bf16[32,1536]{1,0:T(8,128)(2,1)}, u32[]{:S(2)}) copy-start(bf16[32,1536]{1,0:T(8,128)(2,1)} %refs_10_.1) | copy-start | bytes 294916
  23.9 17.1 %collective-permute-start.8 = (bf16[512,1536]{1,0:T(8,128)(2,1)S(1)}, bf16[512,1536]{1,0:T(8,128)(2,1)}, u32[]{:S(2)}, u32[]{:S(2)}) collective-permute-start(bf16[512,1536]{1,0:T(8,128)(2,1)S(1)} %maximum_select_fusion.raw_ref), channel_id=1, source_target_pairs={{0,1},{1,0},{2,3},{3,2},{4,5},{5,4},{6,7},{7,6},{8,9},{9,8},{10,11... | collective-permute-start | bytes 4718600 | tf_op jit(solution)/shard_map/ppermute | solution.py:49
  24.1 11.8 %collective-permute-start = (bf16[32,1536]{1,0:T(8,128)(2,1)S(1)}, bf16[32,1536]{1,0:T(8,128)(2,1)S(1)}, u32[]{:S(2)}, u32[]{:S(2)}) collective-permute-start(bf16[32,1536]{1,0:T(8,128)(2,1)S(1)} %shard_map.85.refs_3_), channel_id=1, source_target_pairs={{0,32},{16,48},{32,64},{48,80},{64,96},{80,112},{96,128},{112,144}... | collective-permute-start | bytes 294920 | tf_op jit(solution)/shard_map/ppermute | solution.py:41
  26.1 10.4 %collective-permute-start.1 = (bf16[32,1536]{1,0:T(8,128)(2,1)S(1)}, bf16[32,1536]{1,0:T(8,128)(2,1)}, u32[]{:S(2)}, u32[]{:S(2)}) collective-permute-start(bf16[32,1536]{1,0:T(8,128)(2,1)S(1)} %shard_map.85.refs_3_), channel_id=1, source_target_pairs={{0,224},{16,240},{32,0},{48,16},{64,32},{80,48},{96,64},{112,80},{... | collective-permute-start | bytes 294920 | tf_op jit(solution)/shard_map/ppermute | solution.py:41
  30.1 17.8 %collective-permute-start.2 = (bf16[32,1536]{1,0:T(8,128)(2,1)S(1)}, bf16[32,1536]{1,0:T(8,128)(2,1)}, u32[]{:S(2)}, u32[]{:S(2)}) collective-permute-start(bf16[32,1536]{1,0:T(8,128)(2,1)S(1)} %shard_map.85.refs_3_), channel_id=1, source_target_pairs={{0,64},{16,80},{32,96},{48,112},{64,128},{80,144},{96,160},{112,17... | collective-permute-start | bytes 294920 | tf_op jit(solution)/shard_map/ppermute | solution.py:41
  30.1 17.8 %collective-permute-start.3 = (bf16[32,1536]{1,0:T(8,128)(2,1)S(1)}, bf16[32,1536]{1,0:T(8,128)(2,1)}, u32[]{:S(2)}, u32[]{:S(2)}) collective-permute-start(bf16[32,1536]{1,0:T(8,128)(2,1)S(1)} %shard_map.85.refs_3_), channel_id=1, source_target_pairs={{0,192},{16,208},{32,224},{48,240},{64,0},{80,16},{96,32},{112,48}... | collective-permute-start | bytes 294920 | tf_op jit(solution)/shard_map/ppermute | solution.py:41
  35.9 12.0 %collective-permute-start.4 = (bf16[32,1536]{1,0:T(8,128)(2,1)S(1)}, bf16[32,1536]{1,0:T(8,128)(2,1)S(1)}, u32[]{:S(2)}, u32[]{:S(2)}) collective-permute-start(bf16[32,1536]{1,0:T(8,128)(2,1)S(1)} %shard_map.85.refs_3_), channel_id=1, source_target_pairs={{0,96},{16,112},{32,128},{48,144},{64,160},{80,176},{96,192},{112,... | collective-permute-start | bytes 294920 | tf_op jit(solution)/shard_map/ppermute | solution.py:41
  36.5 11.4 %collective-permute-start.5 = (bf16[32,1536]{1,0:T(8,128)(2,1)S(1)}, bf16[32,1536]{1,0:T(8,128)(2,1)S(1)}, u32[]{:S(2)}, u32[]{:S(2)}) collective-permute-start(bf16[32,1536]{1,0:T(8,128)(2,1)S(1)} %shard_map.85.refs_3_), channel_id=1, source_target_pairs={{0,160},{16,176},{32,192},{48,208},{64,224},{80,240},{96,0},{112,1... | collective-permute-start | bytes 294920 | tf_op jit(solution)/shard_map/ppermute | solution.py:41
  41.0 10.3 %collective-permute-start.6 = (bf16[32,1536]{1,0:T(8,128)(2,1)S(1)}, bf16[32,1536]{1,0:T(8,128)(2,1)S(1)}, u32[]{:S(2)}, u32[]{:S(2)}) collective-permute-start(bf16[32,1536]{1,0:T(8,128)(2,1)S(1)} %shard_map.85.refs_3_), channel_id=1, source_target_pairs={{0,128},{16,144},{32,160},{48,176},{64,192},{80,208},{96,224},{112... | collective-permute-start | bytes 294920 | tf_op jit(solution)/shard_map/ppermute | solution.py:41
  56.1 4.7 %copy-start.5 = (bf16[32,1536]{1,0:T(8,128)(2,1)}, bf16[32,1536]{1,0:T(8,128)(2,1)S(1)}, u32[]{:S(2)}) copy-start(bf16[32,1536]{1,0:T(8,128)(2,1)S(1)} %get-tuple-element.21.refs_1_) | copy-start | bytes 294916
  56.1 4.7 %copy-start.19 = (bf16[32,1536]{1,0:T(8,128)(2,1)}, bf16[32,1536]{1,0:T(8,128)(2,1)S(1)}, u32[]{:S(2)}) copy-start(bf16[32,1536]{1,0:T(8,128)(2,1)S(1)} %get-tuple-element.28) | copy-start | bytes 294916
  56.1 4.7 %copy-start.20 = (bf16[32,1536]{1,0:T(8,128)(2,1)}, bf16[32,1536]{1,0:T(8,128)(2,1)S(1)}, u32[]{:S(2)}) copy-start(bf16[32,1536]{1,0:T(8,128)(2,1)S(1)} %get-tuple-element.27) | copy-start | bytes 294916
  56.2 4.7 %copy-start.21 = (bf16[32,1536]{1,0:T(8,128)(2,1)}, bf16[32,1536]{1,0:T(8,128)(2,1)S(1)}, u32[]{:S(2)}) copy-start(bf16[32,1536]{1,0:T(8,128)(2,1)S(1)} %get-tuple-element.26) | copy-start | bytes 294916
  56.2 4.7 %copy-start.22 = (bf16[32,1536]{1,0:T(8,128)(2,1)}, bf16[32,1536]{1,0:T(8,128)(2,1)S(1)}, u32[]{:S(2)}) copy-start(bf16[32,1536]{1,0:T(8,128)(2,1)S(1)} %get-tuple-element.25) | copy-start | bytes 294916
  56.2 4.7 %copy-start.23 = (bf16[32,1536]{1,0:T(8,128)(2,1)}, bf16[32,1536]{1,0:T(8,128)(2,1)S(1)}, u32[]{:S(2)}) copy-start(bf16[32,1536]{1,0:T(8,128)(2,1)S(1)} %get-tuple-element.24) | copy-start | bytes 294916
  56.2 4.7 %copy-start.24 = (bf16[32,1536]{1,0:T(8,128)(2,1)}, bf16[32,1536]{1,0:T(8,128)(2,1)S(1)}, u32[]{:S(2)}) copy-start(bf16[32,1536]{1,0:T(8,128)(2,1)S(1)} %get-tuple-element.23) | copy-start | bytes 294916
  56.2 4.7 %copy-start.25 = (bf16[32,1536]{1,0:T(8,128)(2,1)}, bf16[32,1536]{1,0:T(8,128)(2,1)S(1)}, u32[]{:S(2)}) copy-start(bf16[32,1536]{1,0:T(8,128)(2,1)S(1)} %get-tuple-element.22) | copy-start | bytes 294916
  56.2 3.9 %collective-permute-start.9 = (bf16[512,1664]{1,0:T(8,128)(2,1)S(1)}, bf16[512,1664]{1,0:T(8,128)(2,1)S(1)}, u32[]{:S(2)}, u32[]{:S(2)}) collective-permute-start(bf16[512,1664]{1,0:T(8,128)(2,1)S(1)} %get-tuple-element.20), channel_id=1, source_target_pairs={{0,1},{1,0},{2,3},{3,2},{4,5},{5,4},{6,7},{7,6},{8,9},{9,8},{10,11... | collective-permute-start | bytes 5111816 | tf_op jit(solution)/shard_map/ppermute | solution.py:49
  60.9 1.2 copy-start.2
  62.1 31.8 %all-to-all-start = ((bf16[16,32,1664]{2,1,0:T(8,128)(2,1)}), bf16[16,32,1664]{2,1,0:T(8,128)(2,1)S(1)}, u32[]{:S(2)}, u32[]{:S(2)}) async-start(bf16[16,32,1664]{2,1,0:T(8,128)(2,1)} %bitcast.15), calls=%async_computation | async-start | bytes 3407872 | tf_op jit(solution)/shard_map/all_to_all | solution.py:233
  69.6 9.7 %collective-permute-start.10 = (bf16[32,1536]{1,0:T(8,128)(2,1)}, bf16[32,1536]{1,0:T(8,128)(2,1)S(1)}, u32[]{:S(2)}, u32[]{:S(2)}) collective-permute-start(bf16[32,1536]{1,0:T(8,128)(2,1)} %copy-done.25), channel_id=1, source_target_pairs={{0,224},{16,240},{32,0},{48,16},{64,32},{80,48},{96,64},{112,80},{... | collective-permute-start | bytes 294920 | tf_op jit(solution)/shard_map/ppermute | solution.py:41
  69.6 12.0 %collective-permute-start.11 = (bf16[32,1536]{1,0:T(8,128)(2,1)}, bf16[32,1536]{1,0:T(8,128)(2,1)}, u32[]{:S(2)}, u32[]{:S(2)}) collective-permute-start(bf16[32,1536]{1,0:T(8,128)(2,1)} %copy-done.24), channel_id=1, source_target_pairs={{0,32},{16,48},{32,64},{48,80},{64,96},{80,112},{96,128},{112,144}... | collective-permute-start | bytes 294920 | tf_op jit(solution)/shard_map/ppermute | solution.py:41
  74.3 10.0 %collective-permute-start.12 = (bf16[32,1536]{1,0:T(8,128)(2,1)}, bf16[32,1536]{1,0:T(8,128)(2,1)S(1)}, u32[]{:S(2)}, u32[]{:S(2)}) collective-permute-start(bf16[32,1536]{1,0:T(8,128)(2,1)} %copy-done.23), channel_id=1, source_target_pairs={{0,192},{16,208},{32,224},{48,240},{64,0},{80,16},{96,32},{112,48}... | collective-permute-start | bytes 294920 | tf_op jit(solution)/shard_map/ppermute | solution.py:41
  74.9 10.0 %collective-permute-start.13 = (bf16[32,1536]{1,0:T(8,128)(2,1)}, bf16[32,1536]{1,0:T(8,128)(2,1)S(1)}, u32[]{:S(2)}, u32[]{:S(2)}) collective-permute-start(bf16[32,1536]{1,0:T(8,128)(2,1)} %copy-done.22), channel_id=1, source_target_pairs={{0,64},{16,80},{32,96},{48,112},{64,128},{80,144},{96,160},{112,17... | collective-permute-start | bytes 294920 | tf_op jit(solution)/shard_map/ppermute | solution.py:41
  77.2 14.0 %collective-permute-start.14 = (bf16[32,1536]{1,0:T(8,128)(2,1)}, bf16[32,1536]{1,0:T(8,128)(2,1)S(1)}, u32[]{:S(2)}, u32[]{:S(2)}) collective-permute-start(bf16[32,1536]{1,0:T(8,128)(2,1)} %copy-done.21), channel_id=1, source_target_pairs={{0,160},{16,176},{32,192},{48,208},{64,224},{80,240},{96,0},{112,1... | collective-permute-start | bytes 294920 | tf_op jit(solution)/shard_map/ppermute | solution.py:41
  79.3 0.6 copy-start.7
  79.9 11.9 %collective-permute-start.15 = (bf16[32,1536]{1,0:T(8,128)(2,1)}, bf16[32,1536]{1,0:T(8,128)(2,1)S(1)}, u32[]{:S(2)}, u32[]{:S(2)}) collective-permute-start(bf16[32,1536]{1,0:T(8,128)(2,1)} %copy-done.20), channel_id=1, source_target_pairs={{0,96},{16,112},{32,128},{48,144},{64,160},{80,176},{96,192},{112,... | collective-permute-start | bytes 294920 | tf_op jit(solution)/shard_map/ppermute | solution.py:41
  81.7 10.8 %collective-permute-start.16 = (bf16[32,1536]{1,0:T(8,128)(2,1)}, bf16[32,1536]{1,0:T(8,128)(2,1)S(1)}, u32[]{:S(2)}, u32[]{:S(2)}) collective-permute-start(bf16[32,1536]{1,0:T(8,128)(2,1)} %copy-done.19), channel_id=1, source_target_pairs={{0,128},{16,144},{32,160},{48,176},{64,192},{80,208},{96,224},{112... | collective-permute-start | bytes 294920 | tf_op jit(solution)/shard_map/ppermute | solution.py:41
  84.3 0.6 copy-start.9
  84.9 0.6 copy-start.11
  91.2 0.6 copy-start.13
  91.8 0.7 copy-start.15
  92.4 0.6 copy-start.17
  94.0 0.9 copy-start.6
  94.9 0.9 copy-start.8
  95.8 0.9 copy-start.10
  96.7 0.9 copy-start.12
  97.6 0.9 copy-start.14
  98.5 0.9 copy-start.16
  99.4 0.9 copy-start.18
  101.7 1.2 copy-start.1
  102.9 6.8 %copy-start.27 = (bf16[96,512]{1,0:T(8,128)(2,1)S(1)}, bf16[96,512]{1,0:T(8,128)(2,1)}, u32[]{:S(2)}) copy-start(bf16[96,512]{1,0:T(8,128)(2,1)} %param.9) | copy-start | bytes 294916
  102.9 29.4 %all-to-all-start.1 = ((bf16[8,64,1664]{2,1,0:T(8,128)(2,1)}), bf16[8,64,1664]{2,1,0:T(8,128)(2,1)S(1)}, u32[]{:S(2)}, u32[]{:S(2)}) async-start(bf16[8,64,1664]{2,1,0:T(8,128)(2,1)} %copy-done.1), calls=%async_computation.1 | async-start | bytes 3407872 | tf_op jit(solution)/shard_map/all_to_all | solution.py:242
  109.8 1.6 collective-permute-start.19
  109.9 4.2 %collective-permute-start.18 = (bf16[96,512]{1,0:T(8,128)(2,1)}, bf16[96,512]{1,0:T(8,128)(2,1)}, u32[]{:S(2)}, u32[]{:S(2)}) collective-permute-start(bf16[96,512]{1,0:T(8,128)(2,1)} %param.8), channel_id=1, source_target_pairs={{0,1},{1,0},{2,3},{3,2},{4,5},{5,4},{6,7},{7,6},{8,9},{9,8},{10,11... | collective-permute-start | bytes 294920 | tf_op jit(solution)/shard_map/ppermute | solution.py:49
  132.8 2.1 %collective-permute-start.20 = (bf16[192,1536]{1,0:T(8,128)(2,1)S(1)}, bf16[192,1536]{1,0:T(8,128)(2,1)S(1)}, u32[]{:S(2)}, u32[]{:S(2)}) collective-permute-start(bf16[192,1536]{1,0:T(8,128)(2,1)S(1)} %get-tuple-element.30), channel_id=1, source_target_pairs={{0,1},{1,0},{2,3},{3,2},{4,5},{5,4},{6,7},{7,6},{8,9},{9,8},{10,11... | collective-permute-start | bytes 1769480 | tf_op jit(solution)/shard_map/ppermute | solution.py:49
  161.7 0.8 copy-start.3
  162.5 22.5 %all-to-all-start.3 = ((bf16[16,48,384]{2,1,0:T(8,128)(2,1)}), bf16[16,48,384]{2,1,0:T(8,128)(2,1)}, u32[]{:S(2)}, u32[]{:S(2)}) async-start(bf16[16,48,384]{2,1,0:T(8,128)(2,1)} %copy-done.3), calls=%async_computation.3 | async-start | bytes 1179648 | tf_op jit(solution)/shard_map/all_to_all | solution.py:258
  167.0 1.2 collective-permute-start.17

commit v3 on v2

v3 whole, which is shorter than its diff:
```python
import jax
import jax.numpy as jnp
from jax import lax
from jax.experimental import pallas as pl
from jax.experimental.pallas import tpu as pltpu
from jax.sharding import PartitionSpec as P

F32 = jnp.float32
BF16 = jnp.bfloat16
LANES = 128
ALONG = (0, 1, -1, 2, -2, 3, -3, 4)
VMEM = pl.BlockSpec(memory_space=pltpu.VMEM)
SMEM = pl.BlockSpec(memory_space=pltpu.SMEM)


def local(kernel, outs, operands, mib, specs=None, scratch=()):
    single = not isinstance(outs, list)
    shapes = [jax.ShapeDtypeStruct(*out) for out in ([outs] if single else outs)]
    result = pl.pallas_call(
        kernel,
        out_shape=shapes,
        in_specs=specs or [VMEM] * len(operands),
        out_specs=[VMEM] * len(shapes),
        scratch_shapes=list(scratch),
        compiler_params=pltpu.CompilerParams(vmem_limit_bytes=mib * 2**20),
    )(*operands)
    return result[0] if single else result


def normalize(raw):
    values = raw.astype(F32)
    inverse = lax.rsqrt(jnp.sum(values * values, axis=1, keepdims=True) + 1e-06)
    return (values * inverse, inverse)


def through_norm(upstream, normed, inverse):
    return (upstream - normed * jnp.sum(normed * upstream, axis=1, keepdims=True)) * inverse


def along_z(value, steps):
    return lax.ppermute(value, "dp", [(d, (d + 2 * steps) % 16) for d in range(16)])


def swap_y(value):
    return lax.ppermute(value, "dp", [(d, d ^ 1) for d in range(16)])


def swap_core(value):
    return lax.ppermute(value, "mp", [(m, m ^ 1) for m in range(16)])


def normalize_kernel(raw_ref, out_ref):
    out_ref[...] = normalize(raw_ref[...])[0].astype(BF16)


def loss_columns(losses):
    high = losses.astype(BF16)
    low = (losses - high.astype(F32)).astype(BF16)
    lane = lax.broadcasted_iota(jnp.int32, (losses.shape[0], LANES), 1)
    zero = jnp.zeros((), BF16)
    return jnp.where(lane == 0, high, jnp.where(lane == 1, low, zero))


def column_loss(extra):
    values = extra.astype(F32)
    return values[:, 0:1] + values[:, 1:2]


def tile_kernel(*refs):
    numbers, places, text_ids = refs[0], refs[1], refs[2]
    blocks, own, partner = refs[3:19], refs[19], refs[20]
    image_out, keep_ref, send_ref, texts, images, slopes = refs[21:]
    sub, width = blocks[0].shape
    for i, block in enumerate(blocks):
        texts[pl.ds(i * sub, sub), :] = block[...]
    scale, bias = numbers[0], numbers[1]
    rows = own.shape[0]
    pieces = rows // sub
    for part, source in enumerate((own, partner)):
        place = pl.ds(part * rows, rows)
        images[place, :] = normalize(source[...])[0].astype(BF16)
        logits = scale * lax.dot_general(
            images[place, :], texts[...], (((1,), (1,)), ((), ())), preferred_element_type=F32
        ) + bias
        ids = places[part] + lax.broadcasted_iota(jnp.int32, logits.shape, 0)
        match = ids == text_ids[...]
        u = jnp.where(match, -logits, logits)
        e = jnp.exp(-jnp.abs(u))
        w = 1.0 + e
        grown = jnp.where(w == 1.0, e, jnp.log(w) * (e / jnp.where(w == 1.0, 1.0, w - 1.0)))
        losses = jnp.sum(jnp.maximum(u, 0.0) + grown, axis=1, keepdims=True)
        slope = jnp.where(match, -scale, scale) * (jnp.where(u >= 0.0, 1.0, e) / w)
        slopes[place, :] = slope.astype(BF16)
        grad = jnp.dot(slopes[place, :], texts[...], preferred_element_type=F32).astype(BF16)
        extra = loss_columns(losses)
        first = places[2 + part]
        for i in range(pieces):
            image_out[first + i, :, pl.ds(0, width)] = grad[i * sub : (i + 1) * sub]
            image_out[first + i, :, pl.ds(width, LANES)] = extra[i * sub : (i + 1) * sub]
    text_grad = lax.dot_general(
        slopes[...], images[...], (((0,), (0,)), ((), ())), preferred_element_type=F32
    )
    half = text_grad.shape[0] // 2
    keep_ref[...] = text_grad[:half]
    send_ref[...] = text_grad[half:].astype(BF16)


def join_kernel(keep_ref, came_ref, *outs):
    sub = outs[0].shape[0]
    for i, out in enumerate(outs):
        place = pl.ds(i * sub, sub)
        out[...] = (keep_ref[place, :] + came_ref[place, :].astype(F32)).astype(BF16)


def grad_kernel(*refs):
    pieces, blocks = refs[0], refs[1:9]
    raw_img, raw_txt, out_ref = refs[9], refs[10], refs[11]
    width = raw_img.shape[1]
    image_grad = pieces[0, :, pl.ds(0, width)].astype(F32)
    losses = column_loss(pieces[0, :, pl.ds(width, LANES)])
    for i in range(1, pieces.shape[0]):
        image_grad += pieces[i, :, pl.ds(0, width)].astype(F32)
        losses += column_loss(pieces[i, :, pl.ds(width, LANES)])
    text_grad = blocks[0][...].astype(F32)
    for block in blocks[1:]:
        text_grad += block[...].astype(F32)
    d_img = through_norm(image_grad, *normalize(raw_img[...])).astype(BF16)
    d_txt = through_norm(text_grad, *normalize(raw_txt[...])).astype(BF16)
    extra = loss_columns(losses)
    count = out_ref.shape[0] // 2
    for i in range(2 * count):
        out_ref[i, :, pl.ds(0, width)] = d_img if i < count else d_txt
        out_ref[i, :, pl.ds(width, LANES)] = extra


def weight_kernel(feats_ref, grads_ref, keep_ref, send_ref):
    count, width = keep_ref.shape
    grads = jnp.concatenate(
        [grads_ref[j, :, pl.ds(0, width)] for j in range(grads_ref.shape[0])], axis=0
    )
    both = jnp.dot(feats_ref[...], grads, preferred_element_type=F32)
    keep_ref[...] = both[:count]
    send_ref[...] = both[count:].astype(BF16)


def cut_kernel(keep_ref, came_ref, out_ref):
    rows, cols = out_ref.shape[1:]
    for r in range(2):
        for c in range(4):
            place = (pl.ds(r * rows, rows), pl.ds(c * cols, cols))
            out_ref[4 * r + c] = (keep_ref[place] + came_ref[place].astype(F32)).astype(BF16)


def spread_kernel(parts_ref, out_ref):
    total = parts_ref[0].astype(F32)
    for i in range(1, parts_ref.shape[0]):
        total += parts_ref[i].astype(F32)
    total = total.astype(BF16)
    for i in range(out_ref.shape[0]):
        out_ref[i] = total


def paste_kernel(parts_ref, img_ref, txt_ref):
    rows, cols = parts_ref.shape[1:]
    for s in range(8):
        place = (pl.ds((s // 4) * rows, rows), pl.ds((s % 4) * cols, cols))
        img_ref[place] = parts_ref[2 * s].astype(F32)
        txt_ref[place] = parts_ref[2 * s + 1].astype(F32)


def shards(img_emb, txt_emb, img_feat_t, txt_feat_t, logit_scale, logit_bias):
    rows, width = img_emb.shape
    sub = txt_emb.shape[0]
    half = rows // 2
    feats = img_feat_t.shape[0]
    full = width + LANES
    dp_index = lax.axis_index("dp").astype(jnp.int32)
    mp_index = lax.axis_index("mp").astype(jnp.int32)
    core, chip = mp_index % 2, mp_index // 2
    z, y = dp_index // 2, dp_index % 2

    texts = local(normalize_kernel, ((sub, width), BF16), [txt_emb], 4)
    blocks = [texts] + [along_z(texts, steps) for steps in ALONG[1:]]
    blocks += [swap_core(block) for block in blocks]
    own = lax.dynamic_slice_in_dim(img_emb, core * half, half, 0)
    partner = swap_y(own)

    owners = jnp.stack([2 * ((z - steps) % 8) + y for steps in ALONG])
    cores = jnp.stack([mp_index, mp_index ^ 1])
    text_ids = owners[None, :, None] * rows + cores[:, None, None] * sub
    text_ids = text_ids + jnp.arange(sub, dtype=jnp.int32)[None, None]
    image_start = 2 * z * rows + core * half
    places = jnp.stack([image_start + y * rows, image_start + (1 - y) * rows, 8 * y, 8 * (1 - y)])
    numbers = jnp.concatenate([logit_scale, logit_bias])
    image_part, keep, send = local(
        tile_kernel,
        [((16, sub, full), BF16), ((half, width), F32), ((half, width), BF16)],
        [
            numbers,
            places.astype(jnp.int32),
            text_ids.astype(jnp.int32).reshape(1, rows),
            *blocks,
            own,
            partner,
        ],
        24,
        [SMEM, SMEM] + [VMEM] * 19,
        [pltpu.VMEM((rows, width), BF16)] * 2 + [pltpu.VMEM((rows, rows), BF16)],
    )
    plane = [
        [(2 * s + t) * 16 + 2 * k + c for t in range(2) for k in range(8)]
        for s in range(8)
        for c in range(2)
    ]

    def over_plane(value):
        return lax.all_to_all(
            value, ("dp", "mp"), 0, 0, tiled=True, axis_index_groups=plane
        )

    image_pieces = over_plane(image_part)
    text_parts = local(join_kernel, [((sub, width), BF16)] * 8, [keep, swap_core(send)], 8)
    text_came = [text_parts[0]] + [
        along_z(part, -steps) for part, steps in zip(text_parts[1:], ALONG[1:], strict=True)
    ]
    raw_img = lax.dynamic_slice_in_dim(img_emb, core * half + chip * sub, sub, 0)
    spread = local(
        grad_kernel, ((16, sub, full), BF16), [image_pieces, *text_came, raw_img, txt_emb], 12
    )
    grads = over_plane(spread)

    mine = jnp.where(y == 0, img_feat_t, txt_feat_t)
    came = swap_y(jnp.where(y == 0, txt_feat_t, img_feat_t))
    pair = jnp.where(y == 0, jnp.stack([mine, came], 1), jnp.stack([came, mine], 1))
    pair = jnp.concatenate([pair, swap_core(pair)])
    by_half = pair.reshape(2 * feats, 2, 2, half)
    by_half = jnp.where(core == 0, by_half[:, :, 0], by_half[:, :, 1])
    by_turn = pair.reshape(2 * feats, 2, 8, 2, sub)
    by_turn = jnp.where(core == 0, by_turn[:, :, :, 0], by_turn[:, :, :, 1])
    feat_part = jnp.where(y == 0, by_half.reshape(2 * feats, rows), by_turn.reshape(2 * feats, rows))
    kept, sent = local(
        weight_kernel,
        [((feats, width), F32), ((feats, width), BF16)],
        [feat_part, grads],
        12,
    )
    shape = (feats // 2, width // 4)
    cut = local(cut_kernel, ((8, *shape), BF16), [kept, swap_core(sent)], 6)
    same_y = [[2 * s + t for s in range(8)] for t in range(2)]
    parts = lax.all_to_all(cut, "dp", 0, 0, tiled=True, axis_index_groups=same_y)
    summed = local(spread_kernel, ((16, *shape), BF16), [parts], 6)
    weights = lax.all_to_all(summed, "dp", 0, 0, tiled=True)
    img_weight, txt_weight = local(paste_kernel, [((feats, width), F32)] * 2, [weights], 8)

    extra = grads[:, :, width : width + 2].astype(F32)
    both_loss = (extra[:, :, 0] + extra[:, :, 1]).reshape(2, half)
    own_loss = jnp.where(y == 0, both_loss[0], both_loss[1])
    other_loss = swap_core(own_loss)
    row_loss = jnp.where(
        core == 0,
        jnp.concatenate([own_loss, other_loss]),
        jnp.concatenate([other_loss, own_loss]),
    )
    return (row_loss, img_weight, txt_weight)


def solution(mesh):
    in_specs = (P("dp", None), P(("dp", "mp"), None), P("mp", "dp"), P("mp", "dp"), P(), P())
    out_specs = (P("dp"), P("mp", None), P("mp", None))
    return jax.shard_map(shards, mesh=mesh, in_specs=in_specs, out_specs=out_specs, check_vma=False)
```

time: 188 us -> 174 us (0.926)
  waiting for transfers between devices: 68.9 us -> 54.4 us
  local copies, waits for them, and re-layouts: 16.2 us -> 23.2 us
  blocking collectives: 26.6 us -> 19.9 us
  starting transfers between devices: 54.9 us -> 57.4 us
  Pallas kernels: 12.3 us -> 9.92 us
    all_to_all x2, waiting for transfers between devices: 18.2 us -> 0.01 us  [over_plane(): lax.all_to_all(value, ('dp', 'mp'), 0, 0, tiled=True, axis_index_groups=p...]
    all_to_all x1, blocking collectives: 26.6 us -> 19.9 us  [shards(): lax.all_to_all(cut, 'dp', 0, 0, tiled=True, axis_index_groups=same_y)]
    unnamed x57 -> x47, local copies, waits for them, and re-layouts: 14.9 us -> 21.4 us
    ppermute x1 -> x2, waiting for transfers between devices: 17.8 us -> 20.4 us  [swap_y(): return lax.ppermute(value, 'dp', [(d, d ^ 1) for d in range(16)])]
    pallas_call x10 -> x8, Pallas kernels: 12.3 us -> 9.92 us  [local(): pl.pallas_call(kernel, out_shape=shapes, in_specs=specs or [VMEM] * len(o...]
    ppermute x6 -> x12, waiting for transfers between devices: 7.67 us -> 8.17 us  [swap_core(): return lax.ppermute(value, 'mp', [(m, m ^ 1) for m in range(16)])]
  transfers between devices with their start and end apart: 24 -> 31, of which waited for: 10 -> 15; matrix products, arithmetic and copies ran while one was open for 3% -> 8% of each run, Pallas kernels for 1% -> 0%
where the time goes in v3:
time: 174 us; the launch traced here: 173 us
  starting transfers between devices  57.4 us (33%)
  waiting for transfers between devices  54.4 us (31%)
  local copies, waits for them, and re-layouts  23.2 us (13%)
  blocking collectives  19.9 us (11%)
  Pallas kernels  9.92 us (6%)
  other arithmetic  5.48 us (3%)
  between operations  2.21 us (1%)
    ppermute x14, starting transfers between devices, along_z(): lax.ppermute(value, 'dp', [(d, (d + 2 * steps) % 16) for d in range(16)])  32.8 us
    unnamed x47, local copies, waits for them, and re-layouts  21.4 us
    ppermute x2, waiting for transfers between devices, swap_y(): return lax.ppermute(value, 'dp', [(d, d ^ 1) for d in range(16)])  20.4 us
    all_to_all x1, blocking collectives, shards(): lax.all_to_all(cut, 'dp', 0, 0, tiled=True, axis_index_groups=same_y)  19.9 us
    all_to_all x1, waiting for transfers between devices, shards(): weights = lax.all_to_all(summed, 'dp', 0, 0, tiled=True)  16.7 us
    all_to_all x2, starting transfers between devices, over_plane(): lax.all_to_all(value, ('dp', 'mp'), 0, 0, tiled=True, axis_index_groups=p...  14.8 us
    pallas_call x8, Pallas kernels, local(): pl.pallas_call(kernel, out_shape=shapes, in_specs=specs or [VMEM] * len(o...  9.92 us
    ppermute x14, waiting for transfers between devices, along_z(): lax.ppermute(value, 'dp', [(d, (d + 2 * steps) % 16) for d in range(16)])  9.11 us
  transfers between devices with their start and end apart: 31, of which 15 were waited for; matrix products, arithmetic and copies ran while one was open for 8% of the time, Pallas kernels for 0%

profile of v3, /device:TPU:2, one launch (start us, length us, event | category | flops | bytes accessed | tf_op | source)
XLA Modules:
  0.0 172.6 jit_solution(13102874139724522520)
XLA Ops:
  0.7 1.0 copy-done.6
  1.8 2.0 %collective-permute-start = (bf16[32,1536]{1,0:T(8,128)(2,1)S(1)}, bf16[32,1536]{1,0:T(8,128)(2,1)S(1)}, u32[]{:S(2)}, u32[]{:S(2)}) collective-permute-start(bf16[32,1536]{1,0:T(8,128)(2,1)S(1)} %shard_map.85.refs_3_), channel_id=1, source_target_pairs={{0,32},{16,48},{32,64},{48,80},{64,96},{80,112},{96,128},{112,144}... | collective-permute-start | bytes 294920 | tf_op jit(solution)/shard_map/ppermute | solution.py:41
  3.8 4.0 %collective-permute-start.1 = (bf16[32,1536]{1,0:T(8,128)(2,1)S(1)}, bf16[32,1536]{1,0:T(8,128)(2,1)S(1)}, u32[]{:S(2)}, u32[]{:S(2)}) collective-permute-start(bf16[32,1536]{1,0:T(8,128)(2,1)S(1)} %shard_map.85.refs_3_), channel_id=1, source_target_pairs={{0,224},{16,240},{32,0},{48,16},{64,32},{80,48},{96,64},{112,80},{... | collective-permute-start | bytes 294920 | tf_op jit(solution)/shard_map/ppermute | solution.py:41
  7.8 4.1 %collective-permute-start.3 = (bf16[32,1536]{1,0:T(8,128)(2,1)S(1)}, bf16[32,1536]{1,0:T(8,128)(2,1)}, u32[]{:S(2)}, u32[]{:S(2)}) collective-permute-start(bf16[32,1536]{1,0:T(8,128)(2,1)S(1)} %shard_map.85.refs_3_), channel_id=1, source_target_pairs={{0,192},{16,208},{32,224},{48,240},{64,0},{80,16},{96,32},{112,48}... | collective-permute-start | bytes 294920 | tf_op jit(solution)/shard_map/ppermute | solution.py:41
  12.0 1.7 collective-permute-start.15
  13.9 0.6 collective-permute-start.4
  14.5 4.4 %collective-permute-start.5 = (bf16[32,1536]{1,0:T(8,128)(2,1)S(1)}, bf16[32,1536]{1,0:T(8,128)(2,1)}, u32[]{:S(2)}, u32[]{:S(2)}) collective-permute-start(bf16[32,1536]{1,0:T(8,128)(2,1)S(1)} %shard_map.85.refs_3_), channel_id=1, source_target_pairs={{0,160},{16,176},{32,192},{48,208},{64,224},{80,240},{96,0},{112,1... | collective-permute-start | bytes 294920 | tf_op jit(solution)/shard_map/ppermute | solution.py:41
  18.9 4.5 %collective-permute-start.6 = (bf16[32,1536]{1,0:T(8,128)(2,1)S(1)}, bf16[32,1536]{1,0:T(8,128)(2,1)}, u32[]{:S(2)}, u32[]{:S(2)}) collective-permute-start(bf16[32,1536]{1,0:T(8,128)(2,1)S(1)} %shard_map.85.refs_3_), channel_id=1, source_target_pairs={{0,128},{16,144},{32,160},{48,176},{64,192},{80,208},{96,224},{112... | collective-permute-start | bytes 294920 | tf_op jit(solution)/shard_map/ppermute | solution.py:41
  25.0 0.5 collective-permute-start.8
  25.4 2.7 %collective-permute-done.5.refs_9_ = bf16[32,1536]{1,0:T(8,128)(2,1)} collective-permute-done((bf16[32,1536]{1,0:T(8,128)(2,1)S(1)}, bf16[32,1536]{1,0:T(8,128)(2,1)}, u32[]{:S(2)}, u32[]{:S(2)}) %collective-permute-start.5) | collective-permute-done | bytes 98336 | tf_op jit(solution)/shard_map/ppermute | solution.py:41
  28.1 1.1 collective-permute-done.6.refs_10_
  29.3 0.5 collective-permute-start.11
  31.5 0.5 collective-permute-done.14.refs_18_
  32.1 4.6 %shard_map.86 = (bf16[16,32,1664]{2,1,0:T(8,128)(2,1)S(1)}, f32[256,1536]{1,0:T(8,128)S(1)}, bf16[256,1536]{1,0:T(8,128)(2,1)S(1)}) custom-call(f32[2]{0:T(128)S(1)} %pad_maximum_fusion.1.refs_0_, s32[4]{0:T(128)S(1)} %pad_add_fusion.refs_1_, s32[1,512]{1,0:T(1,128)S(1)} %add.154.refs_2_, bf16[32,1536]{1,0:T(8,128)(2,1)S(1)} %shard_map.85.refs_3_, ...), custom_call_target="tpu_custom_call" | custom-call | tf_op jit(solution)/shard_map/pallas_call | solution.py:19
  36.7 1.2 copy-done.3
  37.9 1.1 copy-done.4
  39.1 0.9 copy-done.12
  40.0 7.5 %all-to-all-start = ((bf16[16,32,1664]{2,1,0:T(8,128)(2,1)}), bf16[16,32,1664]{2,1,0:T(8,128)(2,1)S(1)}, u32[]{:S(2)}, u32[]{:S(2)}) async-start(bf16[16,32,1664]{2,1,0:T(8,128)(2,1)} %copy-done.3), calls=%async_computation | async-start | bytes 3407872 | tf_op jit(solution)/shard_map/all_to_all | solution.py:217
  47.4 2.5 %collective-permute-done.16.came_ref = bf16[256,1536]{1,0:T(8,128)(2,1)S(1)} collective-permute-done((bf16[256,1536]{1,0:T(8,128)(2,1)}, bf16[256,1536]{1,0:T(8,128)(2,1)S(1)}, u32[]{:S(2)}, u32[]{:S(2)}) %collective-permute-start.16) | collective-permute-done | bytes 786464 | tf_op jit(solution)/shard_map/ppermute | solution.py:49
  49.9 1.4 copy-done.5
  51.3 0.8 shard_map.87
  52.1 0.6 copy-done.8
  52.7 0.6 copy-done.13
  53.4 0.6 copy-done.14
  54.0 0.6 copy-done.15
  54.7 0.6 copy-done.16
  55.3 0.6 copy-done.17
  56.2 3.4 %collective-permute-start.18 = (bf16[32,1536]{1,0:T(8,128)(2,1)}, bf16[32,1536]{1,0:T(8,128)(2,1)}, u32[]{:S(2)}, u32[]{:S(2)}) collective-permute-start(bf16[32,1536]{1,0:T(8,128)(2,1)} %get-tuple-element.23), channel_id=1, source_target_pairs={{0,32},{16,48},{32,64},{48,80},{64,96},{80,112},{96,128},{112,144}... | collective-permute-start | bytes 294920 | tf_op jit(solution)/shard_map/ppermute | solution.py:41
  59.7 1.4 collective-permute-start.19
  61.0 1.5 collective-permute-start.20
  62.6 2.8 %collective-permute-start.21 = (bf16[32,1536]{1,0:T(8,128)(2,1)}, bf16[32,1536]{1,0:T(8,128)(2,1)}, u32[]{:S(2)}, u32[]{:S(2)}) collective-permute-start(bf16[32,1536]{1,0:T(8,128)(2,1)} %copy-done.15), channel_id=1, source_target_pairs={{0,160},{16,176},{32,192},{48,208},{64,224},{80,240},{96,0},{112,1... | collective-permute-start | bytes 294920 | tf_op jit(solution)/shard_map/ppermute | solution.py:41
  65.4 0.6 copy-done.10
  66.1 1.0 collective-permute-start.22
  67.1 2.7 %collective-permute-start.23 = (bf16[32,1536]{1,0:T(8,128)(2,1)}, bf16[32,1536]{1,0:T(8,128)(2,1)}, u32[]{:S(2)}, u32[]{:S(2)}) collective-permute-start(bf16[32,1536]{1,0:T(8,128)(2,1)} %copy-done.13), channel_id=1, source_target_pairs={{0,128},{16,144},{32,160},{48,176},{64,192},{80,208},{96,224},{112... | collective-permute-start | bytes 294920 | tf_op jit(solution)/shard_map/ppermute | solution.py:41
  69.7 1.7 copy.13
  71.4 1.7 copy.14
  73.1 3.0 %collective-permute-done.21.refs_6_ = bf16[32,1536]{1,0:T(8,128)(2,1)} collective-permute-done((bf16[32,1536]{1,0:T(8,128)(2,1)}, bf16[32,1536]{1,0:T(8,128)(2,1)}, u32[]{:S(2)}, u32[]{:S(2)}) %collective-permute-start.21) | collective-permute-done | bytes 98336 | tf_op jit(solution)/shard_map/ppermute | solution.py:41
  76.1 2.3 %collective-permute-done.22.refs_7_ = bf16[32,1536]{1,0:T(8,128)(2,1)} collective-permute-done((bf16[32,1536]{1,0:T(8,128)(2,1)}, bf16[32,1536]{1,0:T(8,128)(2,1)}, u32[]{:S(2)}, u32[]{:S(2)}) %collective-permute-start.22) | collective-permute-done | bytes 98336 | tf_op jit(solution)/shard_map/ppermute | solution.py:41
  78.4 0.9 copy-done.9
  79.3 0.9 copy-done.11
  80.2 1.7 shard_map.88
  81.8 1.2 copy-done.1
  83.1 7.4 %all-to-all-start.1 = ((bf16[16,32,1664]{2,1,0:T(8,128)(2,1)}), bf16[16,32,1664]{2,1,0:T(8,128)(2,1)S(1)}, u32[]{:S(2)}, u32[]{:S(2)}) async-start(bf16[16,32,1664]{2,1,0:T(8,128)(2,1)} %copy-done.1), calls=%async_computation.1 | async-start | bytes 3407872 | tf_op jit(solution)/shard_map/all_to_all | solution.py:217
  90.5 1.6 collective-permute-start.25
  92.0 20.4 %collective-permute-done.25 = bf16[96,512]{0,1:T(8,128)(2,1)S(1)} collective-permute-done((bf16[96,512]{0,1:T(8,128)(2,1)S(1)}, bf16[96,512]{0,1:T(8,128)(2,1)S(1)}, u32[]{:S(2)}, u32[]{:S(2)}) %collective-permute-start.25) | collective-permute-done | bytes 98336 | tf_op jit(solution)/shard_map/ppermute | solution.py:45
  112.9 1.6 collective-permute-done.26
  114.5 1.2 pad_maximum_fusion
  115.7 0.8 copy-done.18
  116.5 0.7 fusion.1
  117.2 1.8 %copy.20 = bf16[192,2,1,256]{3,1,0,2:T(2,128)(2,1)} copy(bf16[192,2,1,256]{0,3,2,1:T(8,128)(2,1)} %get-tuple-element.34) | data formatting | bytes 393216
  119.0 0.8 copy.21
  119.9 1.0 broadcast_select_fusion
  120.8 0.7 copy.22
  121.5 1.1 slice_select_fusion
  122.6 0.8 copy.19
  123.4 1.0 broadcast_select_fusion.1.feats_ref
  125.1 1.4 collective-permute-done.27.came_ref
  126.6 19.9 %all_to_all.20.parts_ref = bf16[8,48,384]{2,1,0:T(8,128)(2,1)S(1)} all-to-all(bf16[8,48,384]{2,1,0:T(8,128)(2,1)S(1)} %shard_map.90), channel_id=1, replica_groups={{0,32,64,96,128,160,192,224},{16,48,80,112,144,176,208,240},{1,33,65,97..., dimensions={0} | all-to-all | bytes 589824 | tf_op jit(solution)/shard_map/all_to_all | solution.py:250
  146.6 0.8 copy-done.2
  147.4 4.2 %all-to-all-start.3 = ((bf16[16,48,384]{2,1,0:T(8,128)(2,1)}), bf16[16,48,384]{2,1,0:T(8,128)(2,1)}, u32[]{:S(2)}, u32[]{:S(2)}) async-start(bf16[16,48,384]{2,1,0:T(8,128)(2,1)} %copy-done.2), calls=%async_computation.3 | async-start | bytes 1179648 | tf_op jit(solution)/shard_map/all_to_all | solution.py:252
  152.0 1.1 collective-permute-done.24
  153.2 0.6 maximum_select_fusion.1
  153.8 16.7 %all-to-all-done.3.parts_ref = bf16[16,48,384]{2,1,0:T(8,128)(2,1)} async-done(((bf16[16,48,384]{2,1,0:T(8,128)(2,1)}), bf16[16,48,384]{2,1,0:T(8,128)(2,1)}, u32[]{:S(2)}, u32[]{:S(2)}) %all-to-all-start.3) | async-done | bytes 589856 | tf_op jit(solution)/shard_map/all_to_all | solution.py:252
  170.4 2.1 %shard_map.92 = (f32[96,1536]{1,0:T(8,128)}, f32[96,1536]{1,0:T(8,128)}) custom-call(bf16[16,48,384]{2,1,0:T(8,128)(2,1)} %all-to-all-done.3.parts_ref), custom_call_target="tpu_custom_call" | custom-call | tf_op jit(solution)/shard_map/pallas_call | solution.py:19
  (77 shorter events, 4.3 us)
Async XLA Ops:
  0.6 11.3 %copy-start = (bf16[512,1536]{1,0:T(8,128)(2,1)S(1)}, bf16[512,1536]{1,0:T(8,128)(2,1)}, u32[]{:S(2)}) copy-start(bf16[512,1536]{1,0:T(8,128)(2,1)} %param.6) | copy-start | bytes 4718596
  0.6 1.0 copy-start.6
  1.8 12.1 %collective-permute-start = (bf16[32,1536]{1,0:T(8,128)(2,1)S(1)}, bf16[32,1536]{1,0:T(8,128)(2,1)S(1)}, u32[]{:S(2)}, u32[]{:S(2)}) collective-permute-start(bf16[32,1536]{1,0:T(8,128)(2,1)S(1)} %shard_map.85.refs_3_), channel_id=1, source_target_pairs={{0,32},{16,48},{32,64},{48,80},{64,96},{80,112},{96,128},{112,144}... | collective-permute-start | bytes 294920 | tf_op jit(solution)/shard_map/ppermute | solution.py:41
  3.8 10.7 %collective-permute-start.1 = (bf16[32,1536]{1,0:T(8,128)(2,1)S(1)}, bf16[32,1536]{1,0:T(8,128)(2,1)S(1)}, u32[]{:S(2)}, u32[]{:S(2)}) collective-permute-start(bf16[32,1536]{1,0:T(8,128)(2,1)S(1)} %shard_map.85.refs_3_), channel_id=1, source_target_pairs={{0,224},{16,240},{32,0},{48,16},{64,32},{80,48},{96,64},{112,80},{... | collective-permute-start | bytes 294920 | tf_op jit(solution)/shard_map/ppermute | solution.py:41
  7.8 11.1 %collective-permute-start.2 = (bf16[32,1536]{1,0:T(8,128)(2,1)S(1)}, bf16[32,1536]{1,0:T(8,128)(2,1)S(1)}, u32[]{:S(2)}, u32[]{:S(2)}) collective-permute-start(bf16[32,1536]{1,0:T(8,128)(2,1)S(1)} %shard_map.85.refs_3_), channel_id=1, source_target_pairs={{0,64},{16,80},{32,96},{48,112},{64,128},{80,144},{96,160},{112,17... | collective-permute-start | bytes 294920 | tf_op jit(solution)/shard_map/ppermute | solution.py:41
  7.8 17.1 %collective-permute-start.3 = (bf16[32,1536]{1,0:T(8,128)(2,1)S(1)}, bf16[32,1536]{1,0:T(8,128)(2,1)}, u32[]{:S(2)}, u32[]{:S(2)}) collective-permute-start(bf16[32,1536]{1,0:T(8,128)(2,1)S(1)} %shard_map.85.refs_3_), channel_id=1, source_target_pairs={{0,192},{16,208},{32,224},{48,240},{64,0},{80,16},{96,32},{112,48}... | collective-permute-start | bytes 294920 | tf_op jit(solution)/shard_map/ppermute | solution.py:41
  12.0 20.1 %collective-permute-start.15 = (bf16[256,1536]{1,0:T(8,128)(2,1)S(1)}, bf16[256,1536]{1,0:T(8,128)(2,1)S(1)}, u32[]{:S(2)}, u32[]{:S(2)}) collective-permute-start(bf16[256,1536]{1,0:T(8,128)(2,1)S(1)} %constant_dynamic-slice_fusion.1.refs_19_), channel_id=1, source_target_pairs={{0,16},{16,0},{32,48},{48,32},{64,80},{80,64},{96,112},{112,96},{1... | collective-permute-start | bytes 2359304 | tf_op jit(solution)/shard_map/ppermute | solution.py:45
  13.9 11.1 %collective-permute-start.4 = (bf16[32,1536]{1,0:T(8,128)(2,1)S(1)}, bf16[32,1536]{1,0:T(8,128)(2,1)}, u32[]{:S(2)}, u32[]{:S(2)}) collective-permute-start(bf16[32,1536]{1,0:T(8,128)(2,1)S(1)} %shard_map.85.refs_3_), channel_id=1, source_target_pairs={{0,96},{16,112},{32,128},{48,144},{64,160},{80,176},{96,192},{112,... | collective-permute-start | bytes 294920 | tf_op jit(solution)/shard_map/ppermute | solution.py:41
  14.5 13.6 %collective-permute-start.5 = (bf16[32,1536]{1,0:T(8,128)(2,1)S(1)}, bf16[32,1536]{1,0:T(8,128)(2,1)}, u32[]{:S(2)}, u32[]{:S(2)}) collective-permute-start(bf16[32,1536]{1,0:T(8,128)(2,1)S(1)} %shard_map.85.refs_3_), channel_id=1, source_target_pairs={{0,160},{16,176},{32,192},{48,208},{64,224},{80,240},{96,0},{112,1... | collective-permute-start | bytes 294920 | tf_op jit(solution)/shard_map/ppermute | solution.py:41
  18.9 10.3 %collective-permute-start.6 = (bf16[32,1536]{1,0:T(8,128)(2,1)S(1)}, bf16[32,1536]{1,0:T(8,128)(2,1)}, u32[]{:S(2)}, u32[]{:S(2)}) collective-permute-start(bf16[32,1536]{1,0:T(8,128)(2,1)S(1)} %shard_map.85.refs_3_), channel_id=1, source_target_pairs={{0,128},{16,144},{32,160},{48,176},{64,192},{80,208},{96,224},{112... | collective-permute-start | bytes 294920 | tf_op jit(solution)/shard_map/ppermute | solution.py:41
  24.9 4.4 %collective-permute-start.7 = (bf16[32,1536]{1,0:T(8,128)(2,1)S(1)}, bf16[32,1536]{1,0:T(8,128)(2,1)S(1)}, u32[]{:S(2)}, u32[]{:S(2)}) collective-permute-start(bf16[32,1536]{1,0:T(8,128)(2,1)S(1)} %shard_map.85.refs_3_), channel_id=1, source_target_pairs={{0,1},{1,0},{2,3},{3,2},{4,5},{5,4},{6,7},{7,6},{8,9},{9,8},{10,11... | collective-permute-start | bytes 294920 | tf_op jit(solution)/shard_map/ppermute | solution.py:49
  25.0 4.9 %collective-permute-start.8 = (bf16[32,1536]{1,0:T(8,128)(2,1)S(1)}, bf16[32,1536]{1,0:T(8,128)(2,1)S(1)}, u32[]{:S(2)}, u32[]{:S(2)}) collective-permute-start(bf16[32,1536]{1,0:T(8,128)(2,1)S(1)} %collective-permute-done.refs_4_), channel_id=1, source_target_pairs={{0,1},{1,0},{2,3},{3,2},{4,5},{5,4},{6,7},{7,6},{8,9},{9,8},{10,11... | collective-permute-start | bytes 294920 | tf_op jit(solution)/shard_map/ppermute | solution.py:49
  28.1 1.9 %collective-permute-start.9 = (bf16[32,1536]{1,0:T(8,128)(2,1)S(1)}, bf16[32,1536]{1,0:T(8,128)(2,1)S(1)}, u32[]{:S(2)}, u32[]{:S(2)}) collective-permute-start(bf16[32,1536]{1,0:T(8,128)(2,1)S(1)} %collective-permute-done.1.refs_5_), channel_id=1, source_target_pairs={{0,1},{1,0},{2,3},{3,2},{4,5},{5,4},{6,7},{7,6},{8,9},{9,8},{10,11... | collective-permute-start | bytes 294920 | tf_op jit(solution)/shard_map/ppermute | solution.py:49
  29.2 1.3 collective-permute-start.10
  29.3 1.7 collective-permute-start.11
  29.8 1.5 collective-permute-start.12
  30.0 1.6 collective-permute-start.13
  30.5 1.5 collective-permute-start.14
  36.7 1.2 copy-start.3
  37.9 1.2 copy-start.4
  39.1 0.9 copy-start.12
  40.0 38.4 %copy-start.7 = (bf16[32,1536]{1,0:T(8,128)(2,1)S(1)}, bf16[32,1536]{1,0:T(8,128)(2,1)}, u32[]{:S(2)}) copy-start(bf16[32,1536]{1,0:T(8,128)(2,1)} %refs_10_.1) | copy-start | bytes 294916
  40.0 38.4 %all-to-all-start = ((bf16[16,32,1664]{2,1,0:T(8,128)(2,1)}), bf16[16,32,1664]{2,1,0:T(8,128)(2,1)S(1)}, u32[]{:S(2)}, u32[]{:S(2)}) async-start(bf16[16,32,1664]{2,1,0:T(8,128)(2,1)} %copy-done.3), calls=%async_computation | async-start | bytes 3407872 | tf_op jit(solution)/shard_map/all_to_all | solution.py:217
  47.4 2.5 %collective-permute-start.16 = (bf16[256,1536]{1,0:T(8,128)(2,1)}, bf16[256,1536]{1,0:T(8,128)(2,1)S(1)}, u32[]{:S(2)}, u32[]{:S(2)}) collective-permute-start(bf16[256,1536]{1,0:T(8,128)(2,1)} %copy-done.12), channel_id=1, source_target_pairs={{0,1},{1,0},{2,3},{3,2},{4,5},{5,4},{6,7},{7,6},{8,9},{9,8},{10,11... | collective-permute-start | bytes 2359304 | tf_op jit(solution)/shard_map/ppermute | solution.py:49
  49.9 1.4 copy-start.5
  52.1 0.6 copy-start.8
  52.7 0.6 copy-start.13
  53.4 0.6 copy-start.14
  54.0 0.6 copy-start.15
  54.7 0.6 copy-start.16
  55.3 0.6 copy-start.17
  55.9 9.5 %collective-permute-start.17 = (bf16[32,1536]{1,0:T(8,128)(2,1)}, bf16[32,1536]{1,0:T(8,128)(2,1)S(1)}, u32[]{:S(2)}, u32[]{:S(2)}) collective-permute-start(bf16[32,1536]{1,0:T(8,128)(2,1)} %get-tuple-element.22), channel_id=1, source_target_pairs={{0,224},{16,240},{32,0},{48,16},{64,32},{80,48},{96,64},{112,80},{... | collective-permute-start | bytes 294920 | tf_op jit(solution)/shard_map/ppermute | solution.py:41
  56.2 10.8 %collective-permute-start.18 = (bf16[32,1536]{1,0:T(8,128)(2,1)}, bf16[32,1536]{1,0:T(8,128)(2,1)}, u32[]{:S(2)}, u32[]{:S(2)}) collective-permute-start(bf16[32,1536]{1,0:T(8,128)(2,1)} %get-tuple-element.23), channel_id=1, source_target_pairs={{0,32},{16,48},{32,64},{48,80},{64,96},{80,112},{96,128},{112,144}... | collective-permute-start | bytes 294920 | tf_op jit(solution)/shard_map/ppermute | solution.py:41
  59.7 13.4 %collective-permute-start.19 = (bf16[32,1536]{1,0:T(8,128)(2,1)}, bf16[32,1536]{1,0:T(8,128)(2,1)}, u32[]{:S(2)}, u32[]{:S(2)}) collective-permute-start(bf16[32,1536]{1,0:T(8,128)(2,1)} %copy-done.17), channel_id=1, source_target_pairs={{0,192},{16,208},{32,224},{48,240},{64,0},{80,16},{96,32},{112,48}... | collective-permute-start | bytes 294920 | tf_op jit(solution)/shard_map/ppermute | solution.py:41
  61.0 12.0 %collective-permute-start.20 = (bf16[32,1536]{1,0:T(8,128)(2,1)}, bf16[32,1536]{1,0:T(8,128)(2,1)}, u32[]{:S(2)}, u32[]{:S(2)}) collective-permute-start(bf16[32,1536]{1,0:T(8,128)(2,1)} %copy-done.16), channel_id=1, source_target_pairs={{0,64},{16,80},{32,96},{48,112},{64,128},{80,144},{96,160},{112,17... | collective-permute-start | bytes 294920 | tf_op jit(solution)/shard_map/ppermute | solution.py:41
  62.6 13.5 %collective-permute-start.21 = (bf16[32,1536]{1,0:T(8,128)(2,1)}, bf16[32,1536]{1,0:T(8,128)(2,1)}, u32[]{:S(2)}, u32[]{:S(2)}) collective-permute-start(bf16[32,1536]{1,0:T(8,128)(2,1)} %copy-done.15), channel_id=1, source_target_pairs={{0,160},{16,176},{32,192},{48,208},{64,224},{80,240},{96,0},{112,1... | collective-permute-start | bytes 294920 | tf_op jit(solution)/shard_map/ppermute | solution.py:41
  65.4 0.6 copy-start.10
  66.1 12.3 %collective-permute-start.22 = (bf16[32,1536]{1,0:T(8,128)(2,1)}, bf16[32,1536]{1,0:T(8,128)(2,1)}, u32[]{:S(2)}, u32[]{:S(2)}) collective-permute-start(bf16[32,1536]{1,0:T(8,128)(2,1)} %copy-done.14), channel_id=1, source_target_pairs={{0,96},{16,112},{32,128},{48,144},{64,160},{80,176},{96,192},{112,... | collective-permute-start | bytes 294920 | tf_op jit(solution)/shard_map/ppermute | solution.py:41
  67.1 11.3 %collective-permute-start.23 = (bf16[32,1536]{1,0:T(8,128)(2,1)}, bf16[32,1536]{1,0:T(8,128)(2,1)}, u32[]{:S(2)}, u32[]{:S(2)}) collective-permute-start(bf16[32,1536]{1,0:T(8,128)(2,1)} %copy-done.13), channel_id=1, source_target_pairs={{0,128},{16,144},{32,160},{48,176},{64,192},{80,208},{96,224},{112... | collective-permute-start | bytes 294920 | tf_op jit(solution)/shard_map/ppermute | solution.py:41
  78.4 0.9 copy-start.9
  79.3 0.9 copy-start.11
  81.8 1.2 copy-start.1
  83.1 7.4 %copy-start.19 = (bf16[96,512]{0,1:T(8,128)(2,1)S(1)}, bf16[96,512]{0,1:T(8,128)(2,1)}, u32[]{:S(2)}) copy-start(bf16[96,512]{0,1:T(8,128)(2,1)} %copy.13) | copy-start | bytes 294916
  83.1 7.4 %copy-start.20 = (bf16[96,512]{0,1:T(8,128)(2,1)S(1)}, bf16[96,512]{0,1:T(8,128)(2,1)}, u32[]{:S(2)}) copy-start(bf16[96,512]{0,1:T(8,128)(2,1)} %copy.14) | copy-start | bytes 294916
  83.1 41.3 %all-to-all-start.1 = ((bf16[16,32,1664]{2,1,0:T(8,128)(2,1)}), bf16[16,32,1664]{2,1,0:T(8,128)(2,1)S(1)}, u32[]{:S(2)}, u32[]{:S(2)}) async-start(bf16[16,32,1664]{2,1,0:T(8,128)(2,1)} %copy-done.1), calls=%async_computation.1 | async-start | bytes 3407872 | tf_op jit(solution)/shard_map/all_to_all | solution.py:217
  90.5 22.0 %collective-permute-start.25 = (bf16[96,512]{0,1:T(8,128)(2,1)S(1)}, bf16[96,512]{0,1:T(8,128)(2,1)S(1)}, u32[]{:S(2)}, u32[]{:S(2)}) collective-permute-start(bf16[96,512]{0,1:T(8,128)(2,1)S(1)} %get-tuple-element.36), channel_id=1, source_target_pairs={{0,16},{16,0},{32,48},{48,32},{64,80},{80,64},{96,112},{112,96},{1... | collective-permute-start | bytes 294920 | tf_op jit(solution)/shard_map/ppermute | solution.py:45
  112.6 2.0 %collective-permute-start.26 = (bf16[96,2,512]{0,2,1:T(8,128)(2,1)S(1)}, bf16[96,2,512]{0,2,1:T(8,128)(2,1)}, u32[]{:S(2)}, u32[]{:S(2)}) collective-permute-start(bf16[96,2,512]{0,2,1:T(8,128)(2,1)S(1)} %maximum_select_fusion), channel_id=1, source_target_pairs={{0,1},{1,0},{2,3},{3,2},{4,5},{5,4},{6,7},{7,6},{8,9},{9,8},{10,11... | collective-permute-start | bytes 589832 | tf_op jit(solution)/shard_map/ppermute | solution.py:49
  115.7 0.8 copy-start.18
  124.8 1.7 collective-permute-start.27
  146.6 0.8 copy-start.2
  147.4 23.0 %all-to-all-start.3 = ((bf16[16,48,384]{2,1,0:T(8,128)(2,1)}), bf16[16,48,384]{2,1,0:T(8,128)(2,1)}, u32[]{:S(2)}, u32[]{:S(2)}) async-start(bf16[16,48,384]{2,1,0:T(8,128)(2,1)} %copy-done.2), calls=%async_computation.3 | async-start | bytes 1179648 | tf_op jit(solution)/shard_map/all_to_all | solution.py:252
  152.0 1.2 collective-permute-start.24

commit v4 on v3

v4 whole, which is shorter than its diff:
```python
import jax
import jax.numpy as jnp
from jax import lax
from jax.experimental import pallas as pl
from jax.experimental.pallas import tpu as pltpu
from jax.sharding import PartitionSpec as P

F32 = jnp.float32
BF16 = jnp.bfloat16
LANES = 128
ALONG = (0, 1, -1, 2, -2, 3, -3, 4)
VMEM = pl.BlockSpec(memory_space=pltpu.VMEM)
SMEM = pl.BlockSpec(memory_space=pltpu.SMEM)
HBM = pl.BlockSpec(memory_space=pltpu.HBM)
ANY = pl.BlockSpec(memory_space=pl.ANY)
DMA = pltpu.SemaphoreType.DMA


def local(kernel, outs, operands, mib, specs=None, out_specs=None, scratch=()):
    single = not isinstance(outs, list)
    shapes = [jax.ShapeDtypeStruct(*out) for out in ([outs] if single else outs)]
    result = pl.pallas_call(
        kernel,
        out_shape=shapes,
        in_specs=specs or [VMEM] * len(operands),
        out_specs=out_specs or [VMEM] * len(shapes),
        scratch_shapes=list(scratch),
        compiler_params=pltpu.CompilerParams(vmem_limit_bytes=mib * 2**20),
    )(*operands)
    return result[0] if single else result


def start_all(pairs, sems):
    copies = [
        pltpu.make_async_copy(source, target, sems.at[i]) for i, (source, target) in enumerate(pairs)
    ]
    for copy in copies:
        copy.start()
    return copies


def wait_all(copies):
    for copy in copies:
        copy.wait()


def normalize(raw):
    values = raw.astype(F32)
    inverse = lax.rsqrt(jnp.sum(values * values, axis=1, keepdims=True) + 1e-06)
    return (values * inverse, inverse)


def through_norm(upstream, normed, inverse):
    return (upstream - normed * jnp.sum(normed * upstream, axis=1, keepdims=True)) * inverse


def along_z(value, steps):
    return lax.ppermute(value, "dp", [(d, (d + 2 * steps) % 16) for d in range(16)])


def swap_y(value):
    return lax.ppermute(value, "dp", [(d, d ^ 1) for d in range(16)])


def swap_core(value):
    return lax.ppermute(value, "mp", [(m, m ^ 1) for m in range(16)])


def normalize_kernel(raw_ref, out_ref):
    out_ref[...] = normalize(raw_ref[...])[0].astype(BF16)


def loss_columns(losses):
    high = losses.astype(BF16)
    low = (losses - high.astype(F32)).astype(BF16)
    lane = lax.broadcasted_iota(jnp.int32, (losses.shape[0], LANES), 1)
    zero = jnp.zeros((), BF16)
    return jnp.where(lane == 0, high, jnp.where(lane == 1, low, zero))


def column_loss(extra):
    values = extra.astype(F32)
    return values[:, 0:1] + values[:, 1:2]


def feature_kernel(flags, mine, came, mine_next, came_next, out_ref):
    count, rows = mine.shape
    half = rows // 2
    y, core = flags[0], flags[1]
    source = lax.broadcasted_iota(jnp.int32, (rows, half), 0)
    target = lax.broadcasted_iota(jnp.int32, (rows, half), 1)
    chosen = source == (target // 32) * 64 + core * 32 + target % 32
    pick = jnp.where(chosen, 1.0, 0.0).astype(BF16)
    for i, (here, there) in enumerate(((mine, came), (mine_next, came_next))):
        own = jnp.dot(here[...], pick, preferred_element_type=F32).astype(BF16)
        other = jnp.dot(there[...], pick, preferred_element_type=F32).astype(BF16)
        place = pl.ds(i * count, count)
        out_ref[place, pl.ds(0, half)] = jnp.where(y == 0, own, other)
        out_ref[place, pl.ds(half, half)] = jnp.where(y == 0, other, own)


def tile_kernel(*refs):
    numbers, places, text_ids, image_ids = refs[0], refs[1], refs[2], refs[3]
    blocks, own, partner = refs[4:20], refs[20], refs[21]
    image_out, keep_ref, send_ref, texts, images, slopes, stage, sems = refs[22:]
    sub, width = blocks[0].shape
    for i, block in enumerate(blocks):
        texts[pl.ds(i * sub, sub), :] = block[...]
    scale, bias = numbers[0], numbers[1]
    rows = own.shape[0]
    pieces = rows // sub
    copies = []
    for part, source in enumerate((own, partner)):
        place = pl.ds(part * rows, rows)
        images[place, :] = normalize(source[...])[0].astype(BF16)
        logits = scale * lax.dot_general(
            images[place, :], texts[...], (((1,), (1,)), ((), ())), preferred_element_type=F32
        ) + bias
        match = image_ids[place, :] == text_ids[...]
        u = jnp.where(match, -logits, logits)
        e = jnp.exp(-jnp.abs(u))
        w = 1.0 + e
        grown = jnp.where(w == 1.0, e, jnp.log(w) * (e / jnp.where(w == 1.0, 1.0, w - 1.0)))
        losses = jnp.sum(jnp.maximum(u, 0.0) + grown, axis=1, keepdims=True)
        slope = jnp.where(match, -scale, scale) * (jnp.where(u >= 0.0, 1.0, e) / w)
        slopes[place, :] = slope.astype(BF16)
        grad = jnp.dot(slopes[place, :], texts[...], preferred_element_type=F32).astype(BF16)
        extra = loss_columns(losses)
        for i in range(pieces):
            stage[part * pieces + i, :, pl.ds(0, width)] = grad[i * sub : (i + 1) * sub]
            stage[part * pieces + i, :, pl.ds(width, LANES)] = extra[i * sub : (i + 1) * sub]
        copy = pltpu.make_async_copy(
            stage.at[pl.ds(part * pieces, pieces)],
            image_out.at[pl.ds(places[part], pieces)],
            sems.at[part],
        )
        copy.start()
        copies.append(copy)
    text_grad = lax.dot_general(
        slopes[...], images[...], (((0,), (0,)), ((), ())), preferred_element_type=F32
    )
    half = text_grad.shape[0] // 2
    keep_ref[...] = text_grad[:half]
    send_ref[...] = text_grad[half:].astype(BF16)
    wait_all(copies)


def join_kernel(keep_ref, came_ref, *refs):
    outs, stage, sems = refs[:8], refs[8], refs[9]
    sub = stage.shape[1]
    for i in range(8):
        place = pl.ds(i * sub, sub)
        stage[i] = (keep_ref[place, :] + came_ref[place, :].astype(F32)).astype(BF16)
    wait_all(start_all([(stage.at[i], out) for i, out in enumerate(outs)], sems))


def grad_kernel(*refs):
    pieces, blocks = refs[0], refs[1:9]
    raw_img, raw_txt, out_ref, came, stage, sems = refs[9:]
    width = raw_img.shape[1]
    loads = start_all([(block, came.at[i]) for i, block in enumerate(blocks)], sems)
    image_grad = pieces[0, :, pl.ds(0, width)].astype(F32)
    losses = column_loss(pieces[0, :, pl.ds(width, LANES)])
    for i in range(1, pieces.shape[0]):
        image_grad += pieces[i, :, pl.ds(0, width)].astype(F32)
        losses += column_loss(pieces[i, :, pl.ds(width, LANES)])
    d_img = through_norm(image_grad, *normalize(raw_img[...])).astype(BF16)
    extra = loss_columns(losses)
    wait_all(loads)
    text_grad = came[0].astype(F32)
    for i in range(1, came.shape[0]):
        text_grad += came[i].astype(F32)
    d_txt = through_norm(text_grad, *normalize(raw_txt[...])).astype(BF16)
    for i, value in enumerate((d_img, d_txt)):
        stage[i, :, pl.ds(0, width)] = value
        stage[i, :, pl.ds(width, LANES)] = extra
    count = out_ref.shape[0]
    wait_all(
        start_all([(stage.at[i // (count // 2)], out_ref.at[i]) for i in range(count)], sems)
    )


def weight_kernel(feats_ref, grads_ref, keep_ref, send_ref):
    count, width = keep_ref.shape
    grads = jnp.concatenate(
        [grads_ref[j, :, pl.ds(0, width)] for j in range(grads_ref.shape[0])], axis=0
    )
    both = jnp.dot(feats_ref[...], grads, preferred_element_type=F32)
    keep_ref[...] = both[:count]
    send_ref[...] = both[count:].astype(BF16)


def cut_kernel(keep_ref, came_ref, out_ref, stage, sem):
    rows, cols = out_ref.shape[1:]
    for r in range(2):
        for c in range(4):
            place = (pl.ds(r * rows, rows), pl.ds(c * cols, cols))
            stage[4 * r + c] = (keep_ref[place] + came_ref[place].astype(F32)).astype(BF16)
    wait_all(start_all([(stage, out_ref)], sem))


def spread_kernel(parts_ref, out_ref, stage, sems):
    total = parts_ref[0].astype(F32)
    for i in range(1, parts_ref.shape[0]):
        total += parts_ref[i].astype(F32)
    stage[...] = total.astype(BF16)
    wait_all(start_all([(stage, out_ref.at[i]) for i in range(out_ref.shape[0])], sems))


def paste_kernel(parts_ref, img_ref, txt_ref):
    rows, cols = parts_ref.shape[1:]
    for s in range(8):
        place = (pl.ds((s // 4) * rows, rows), pl.ds((s % 4) * cols, cols))
        img_ref[place] = parts_ref[2 * s].astype(F32)
        txt_ref[place] = parts_ref[2 * s + 1].astype(F32)


def shards(img_emb, txt_emb, img_feat_t, txt_feat_t, logit_scale, logit_bias):
    rows, width = img_emb.shape
    sub = txt_emb.shape[0]
    half = rows // 2
    feats = img_feat_t.shape[0]
    full = width + LANES
    dp_index = lax.axis_index("dp").astype(jnp.int32)
    mp_index = lax.axis_index("mp").astype(jnp.int32)
    core, chip = mp_index % 2, mp_index // 2
    z, y = dp_index // 2, dp_index % 2

    texts = local(normalize_kernel, ((sub, width), BF16), [txt_emb], 4)
    blocks = [texts] + [along_z(texts, steps) for steps in ALONG[1:]]
    blocks += [swap_core(block) for block in blocks]
    by_core = img_emb.reshape(8, 2, sub, width)
    own = lax.dynamic_slice_in_dim(by_core, core, 1, 1).reshape(half, width)
    partner = swap_y(own)

    mine = jnp.where(y == 0, img_feat_t, txt_feat_t)
    came = swap_y(jnp.where(y == 0, txt_feat_t, img_feat_t))
    feat_part = local(
        feature_kernel,
        ((2 * feats, rows), BF16),
        [jnp.stack([y, core]), mine, came, swap_core(mine), swap_core(came)],
        8,
        [SMEM] + [VMEM] * 4,
    )

    owners = jnp.stack([2 * ((z - steps) % 8) + y for steps in ALONG])
    cores = jnp.stack([mp_index, mp_index ^ 1])
    text_ids = owners[None, :, None] * rows + cores[:, None, None] * sub
    text_ids = text_ids + jnp.arange(sub, dtype=jnp.int32)[None, None]
    count = jnp.arange(half, dtype=jnp.int32)
    in_shard = (count // sub) * 2 * sub + core * sub + count % sub
    image_ids = jnp.concatenate(
        [(2 * z + y) * rows + in_shard, (2 * z + 1 - y) * rows + in_shard]
    )
    places = jnp.stack([8 * y, 8 * (1 - y)])
    numbers = jnp.concatenate([logit_scale, logit_bias])
    numbers, feat_part = lax.optimization_barrier((numbers, feat_part))
    image_part, keep, send = local(
        tile_kernel,
        [((16, sub, full), BF16), ((half, width), F32), ((half, width), BF16)],
        [
            numbers,
            places.astype(jnp.int32),
            text_ids.astype(jnp.int32).reshape(1, rows),
            image_ids.astype(jnp.int32).reshape(rows, 1),
            *blocks,
            own,
            partner,
        ],
        24,
        [SMEM, SMEM] + [VMEM] * 20,
        [HBM, VMEM, VMEM],
        [pltpu.VMEM((rows, width), BF16)] * 2
        + [pltpu.VMEM((rows, rows), BF16), pltpu.VMEM((16, sub, full), BF16), DMA((2,))],
    )
    plane = [
        [(2 * s + t) * 16 + 2 * k + c for t in range(2) for k in range(8)]
        for s in range(8)
        for c in range(2)
    ]

    def over_plane(value):
        return lax.all_to_all(
            value, ("dp", "mp"), 0, 0, tiled=True, axis_index_groups=plane
        )

    text_parts = local(
        join_kernel,
        [((sub, width), BF16)] * 8,
        [keep, swap_core(send)],
        10,
        None,
        [HBM] * 8,
        [pltpu.VMEM((8, sub, width), BF16), DMA((8,))],
    )
    image_part, *text_parts = lax.optimization_barrier((image_part, *text_parts))
    image_pieces = over_plane(image_part)
    text_came = [text_parts[0]] + [
        along_z(part, -steps) for part, steps in zip(text_parts[1:], ALONG[1:], strict=True)
    ]
    raw_img = lax.dynamic_slice_in_dim(img_emb, (2 * chip + core) * sub, sub, 0)
    spread = local(
        grad_kernel,
        ((16, sub, full), BF16),
        [image_pieces, *text_came, raw_img, txt_emb],
        12,
        [VMEM] + [ANY] * 8 + [VMEM] * 2,
        [HBM],
        [pltpu.VMEM((8, sub, width), BF16), pltpu.VMEM((2, sub, full), BF16), DMA((16,))],
    )
    grads = over_plane(spread)

    kept, sent = local(
        weight_kernel,
        [((feats, width), F32), ((feats, width), BF16)],
        [feat_part, grads],
        12,
    )
    shape = (feats // 2, width // 4)
    cut = local(
        cut_kernel,
        ((8, *shape), BF16),
        [kept, swap_core(sent)],
        6,
        None,
        [HBM],
        [pltpu.VMEM((8, *shape), BF16), DMA((1,))],
    )
    same_y = [[2 * s + t for s in range(8)] for t in range(2)]
    parts = lax.all_to_all(cut, "dp", 0, 0, tiled=True, axis_index_groups=same_y)
    summed = local(
        spread_kernel,
        ((16, *shape), BF16),
        [parts],
        6,
        None,
        [HBM],
        [pltpu.VMEM(shape, BF16), DMA((16,))],
    )
    weights = lax.all_to_all(summed, "dp", 0, 0, tiled=True)
    img_weight, txt_weight = local(paste_kernel, [((feats, width), F32)] * 2, [weights], 8)

    extra = grads[:, :, width : width + 2].astype(F32)
    both_loss = (extra[:, :, 0] + extra[:, :, 1]).reshape(2, 8, sub)
    own_loss = jnp.where(y == 0, both_loss[0], both_loss[1])
    other_loss = swap_core(own_loss)
    row_loss = jnp.where(
        core == 0, jnp.stack([own_loss, other_loss], 1), jnp.stack([other_loss, own_loss], 1)
    ).reshape(rows)
    return (row_loss, img_weight, txt_weight)


def solution(mesh):
    in_specs = (P("dp", None), P(("dp", "mp"), None), P("mp", "dp"), P("mp", "dp"), P(), P())
    out_specs = (P("dp"), P("mp", None), P("mp", None))
    return jax.shard_map(shards, mesh=mesh, in_specs=in_specs, out_specs=out_specs, check_vma=False)
```

time: 174 us -> 188 us (1.080)
  blocking collectives: 19.9 us -> 47.2 us
  starting transfers between devices: 57.4 us -> 48.7 us
  Pallas kernels: 9.92 us -> 15.5 us
  other arithmetic: 5.48 us -> 0.75 us
  waiting for transfers between devices: 54.4 us -> 51.7 us
    all_to_all x0 -> x1, blocking collectives: none -> 28.9 us  [over_plane(): lax.all_to_all(value, ('dp', 'mp'), 0, 0, tiled=True, axis_index_groups=p...]
    all_to_all x2 -> x1, starting transfers between devices: 14.8 us -> 7.65 us  [over_plane(): lax.all_to_all(value, ('dp', 'mp'), 0, 0, tiled=True, axis_index_groups=p...]
    pallas_call x8 -> x9, Pallas kernels: 9.92 us -> 15.5 us  [local(): pl.pallas_call(kernel, out_shape=shapes, in_specs=specs or [VMEM] * len(o...]
    select_n x5 -> x2, other arithmetic: 3.64 us -> 0.02 us  [the longest x1 0.02 us: shards(): came = swap_y(jnp.where(y == 0, txt_feat_t, img_feat_t))]
    ppermute x14, waiting for transfers between devices: 9.11 us -> 12.4 us  [along_z(): lax.ppermute(value, 'dp', [(d, (d + 2 * steps) % 16) for d in range(16)])]
    ppermute x2, waiting for transfers between devices: 20.4 us -> 17.2 us  [swap_y(): return lax.ppermute(value, 'dp', [(d, d ^ 1) for d in range(16)])]
    ppermute x12 -> x13, waiting for transfers between devices: 8.17 us -> 5.01 us  [swap_core(): return lax.ppermute(value, 'mp', [(m, m ^ 1) for m in range(16)])]
    unnamed x47 -> x62, local copies, waits for them, and re-layouts: 21.4 us -> 19.7 us
  transfers between devices with their start and end apart: 31 -> 31, of which waited for: 15 -> 13; matrix products, arithmetic and copies ran while one was open for 8% -> 1% of each run, Pallas kernels for 0% -> 0%
where the time goes in v4:
time: 188 us; the launch traced here: 187 us
  waiting for transfers between devices  51.7 us (28%)
  starting transfers between devices  48.7 us (26%)
  blocking collectives  47.2 us (25%)
  local copies, waits for them, and re-layouts  21.4 us (11%)
  Pallas kernels  15.5 us (8%)
  between operations  2.26 us (1%)
    ppermute x14, starting transfers between devices, along_z(): lax.ppermute(value, 'dp', [(d, (d + 2 * steps) % 16) for d in range(16)])  32.6 us
    all_to_all x1, blocking collectives, over_plane(): lax.all_to_all(value, ('dp', 'mp'), 0, 0, tiled=True, axis_index_groups=p...  28.9 us
    unnamed x62, local copies, waits for them, and re-layouts  19.7 us
    all_to_all x1, blocking collectives, shards(): lax.all_to_all(cut, 'dp', 0, 0, tiled=True, axis_index_groups=same_y)  18.3 us
    ppermute x2, waiting for transfers between devices, swap_y(): return lax.ppermute(value, 'dp', [(d, d ^ 1) for d in range(16)])  17.2 us
    all_to_all x1, waiting for transfers between devices, shards(): weights = lax.all_to_all(summed, 'dp', 0, 0, tiled=True)  16.6 us
    pallas_call x9, Pallas kernels, local(): pl.pallas_call(kernel, out_shape=shapes, in_specs=specs or [VMEM] * len(o...  15.5 us
    ppermute x14, waiting for transfers between devices, along_z(): lax.ppermute(value, 'dp', [(d, (d + 2 * steps) % 16) for d in range(16)])  12.4 us
  transfers between devices with their start and end apart: 31, of which 13 were waited for; matrix products, arithmetic and copies ran while one was open for 1% of the time, Pallas kernels for 0%

profile of v4, /device:TPU:2, one launch (start us, length us, event | category | flops | bytes accessed | tf_op | source)
XLA Modules:
  0.0 187.4 jit_solution(12552584910593447856)
XLA Ops:
  0.7 1.0 copy-done.3
  1.8 2.0 %collective-permute-start.3 = (bf16[32,1536]{1,0:T(8,128)(2,1)S(1)}, bf16[32,1536]{1,0:T(8,128)(2,1)S(1)}, u32[]{:S(2)}, u32[]{:S(2)}) collective-permute-start(bf16[32,1536]{1,0:T(8,128)(2,1)S(1)} %shard_map.86.refs_4_), channel_id=1, source_target_pairs={{0,32},{16,48},{32,64},{48,80},{64,96},{80,112},{96,128},{112,144}... | collective-permute-start | bytes 294920 | tf_op jit(solution)/shard_map/ppermute | solution.py:58
  3.8 4.0 %collective-permute-start.4 = (bf16[32,1536]{1,0:T(8,128)(2,1)S(1)}, bf16[32,1536]{1,0:T(8,128)(2,1)S(1)}, u32[]{:S(2)}, u32[]{:S(2)}) collective-permute-start(bf16[32,1536]{1,0:T(8,128)(2,1)S(1)} %shard_map.86.refs_4_), channel_id=1, source_target_pairs={{0,224},{16,240},{32,0},{48,16},{64,32},{80,48},{96,64},{112,80},{... | collective-permute-start | bytes 294920 | tf_op jit(solution)/shard_map/ppermute | solution.py:58
  7.9 1.7 collective-permute-start.18
  9.6 0.5 collective-permute-start
  11.8 17.2 %collective-permute-done.came = bf16[96,512]{1,0:T(8,128)(2,1)S(1)} collective-permute-done((bf16[96,512]{1,0:T(8,128)(2,1)S(1)}, bf16[96,512]{1,0:T(8,128)(2,1)S(1)}, u32[]{:S(2)}, u32[]{:S(2)}) %collective-permute-start) | collective-permute-done | bytes 98336 | tf_op jit(solution)/shard_map/ppermute | solution.py:62
  29.1 0.6 copy-done.8
  29.7 4.1 %collective-permute-start.6 = (bf16[32,1536]{1,0:T(8,128)(2,1)S(1)}, bf16[32,1536]{1,0:T(8,128)(2,1)S(1)}, u32[]{:S(2)}, u32[]{:S(2)}) collective-permute-start(bf16[32,1536]{1,0:T(8,128)(2,1)S(1)} %shard_map.86.refs_4_), channel_id=1, source_target_pairs={{0,192},{16,208},{32,224},{48,240},{64,0},{80,16},{96,32},{112,48}... | collective-permute-start | bytes 294920 | tf_op jit(solution)/shard_map/ppermute | solution.py:58
  34.0 0.7 collective-permute-start.7
  34.7 4.4 %collective-permute-start.8 = (bf16[32,1536]{1,0:T(8,128)(2,1)S(1)}, bf16[32,1536]{1,0:T(8,128)(2,1)S(1)}, u32[]{:S(2)}, u32[]{:S(2)}) collective-permute-start(bf16[32,1536]{1,0:T(8,128)(2,1)S(1)} %shard_map.86.refs_4_), channel_id=1, source_target_pairs={{0,160},{16,176},{32,192},{48,208},{64,224},{80,240},{96,0},{112,1... | collective-permute-start | bytes 294920 | tf_op jit(solution)/shard_map/ppermute | solution.py:58
  39.1 4.2 %collective-permute-start.9 = (bf16[32,1536]{1,0:T(8,128)(2,1)S(1)}, bf16[32,1536]{1,0:T(8,128)(2,1)S(1)}, u32[]{:S(2)}, u32[]{:S(2)}) collective-permute-start(bf16[32,1536]{1,0:T(8,128)(2,1)S(1)} %shard_map.86.refs_4_), channel_id=1, source_target_pairs={{0,128},{16,144},{32,160},{48,176},{64,192},{80,208},{96,224},{112... | collective-permute-start | bytes 294920 | tf_op jit(solution)/shard_map/ppermute | solution.py:58
  43.4 2.3 %collective-permute-done.7.refs_9_ = bf16[32,1536]{1,0:T(8,128)(2,1)S(1)} collective-permute-done((bf16[32,1536]{1,0:T(8,128)(2,1)S(1)}, bf16[32,1536]{1,0:T(8,128)(2,1)S(1)}, u32[]{:S(2)}, u32[]{:S(2)}) %collective-permute-start.7) | collective-permute-done | bytes 98336 | tf_op jit(solution)/shard_map/ppermute | solution.py:58
  45.8 2.2 %collective-permute-done.8.refs_10_ = bf16[32,1536]{1,0:T(8,128)(2,1)S(1)} collective-permute-done((bf16[32,1536]{1,0:T(8,128)(2,1)S(1)}, bf16[32,1536]{1,0:T(8,128)(2,1)S(1)}, u32[]{:S(2)}, u32[]{:S(2)}) %collective-permute-start.8) | collective-permute-done | bytes 98336 | tf_op jit(solution)/shard_map/ppermute | solution.py:58
  47.9 0.9 collective-permute-done.9.refs_11_
  50.8 0.9 copy-done.7
  51.7 0.9 copy-done.9
  52.5 0.9 shard_map.85.feats_ref
  53.5 5.8 %shard_map.87 = (bf16[16,32,1664]{2,1,0:T(8,128)(2,1)S(1)}, f32[256,1536]{1,0:T(8,128)S(1)}, bf16[256,1536]{1,0:T(8,128)(2,1)S(1)}) custom-call(f32[2]{0:T(128)S(1)} %pad_maximum_fusion.refs_0_, s32[2]{0:T(128)S(1)} %pad_add_fusion.2.refs_1_, s32[1,512]{1,0:T(1,128)S(1)} %add.176.refs_2_, s32[512,1]{1,0:T(8,128)S(1)} %copy.11.refs_3_, ...), custom_call_target="tpu_custom_call" | custom-call | tf_op jit(solution)/shard_map/pallas_call | solution.py:22
  59.5 2.1 %collective-permute-done.19.came_ref = bf16[256,1536]{1,0:T(8,128)(2,1)S(1)} collective-permute-done((bf16[256,1536]{1,0:T(8,128)(2,1)S(1)}, bf16[256,1536]{1,0:T(8,128)(2,1)S(1)}, u32[]{:S(2)}, u32[]{:S(2)}) %collective-permute-start.19) | collective-permute-done | bytes 786464 | tf_op jit(solution)/shard_map/ppermute | solution.py:66
  61.6 1.3 shard_map.88
  63.0 0.6 copy-done.10
  63.6 0.6 copy-done.22
  64.2 0.6 copy-done.24
  64.9 0.6 copy-done.25
  65.5 0.6 copy-done.26
  66.1 0.6 copy-done.27
  66.8 0.6 copy-done.28
  67.4 0.6 copy-done.23
  68.1 7.6 %all-to-all-start = ((bf16[16,32,1664]{2,1,0:T(8,128)(2,1)}), bf16[16,32,1664]{2,1,0:T(8,128)(2,1)S(1)}, u32[]{:S(2)}, u32[]{:S(2)}) async-start(bf16[16,32,1664]{2,1,0:T(8,128)(2,1)} %copy-done.2), calls=%async_computation | async-start | bytes 3407872 | tf_op jit(solution)/shard_map/all_to_all | solution.py:283
  75.7 3.7 %collective-permute-start.21 = (bf16[32,1536]{1,0:T(8,128)(2,1)}, bf16[32,1536]{1,0:T(8,128)(2,1)}, u32[]{:S(2)}, u32[]{:S(2)}) collective-permute-start(bf16[32,1536]{1,0:T(8,128)(2,1)} %copy-done.27), channel_id=1, source_target_pairs={{0,32},{16,48},{32,64},{48,80},{64,96},{80,112},{96,128},{112,144}... | collective-permute-start | bytes 294920 | tf_op jit(solution)/shard_map/ppermute | solution.py:58
  79.4 1.5 collective-permute-start.22
  80.9 1.5 collective-permute-start.23
  82.3 2.9 %collective-permute-start.24 = (bf16[32,1536]{1,0:T(8,128)(2,1)}, bf16[32,1536]{1,0:T(8,128)(2,1)S(1)}, u32[]{:S(2)}, u32[]{:S(2)}) collective-permute-start(bf16[32,1536]{1,0:T(8,128)(2,1)} %copy-done.24), channel_id=1, source_target_pairs={{0,160},{16,176},{32,192},{48,208},{64,224},{80,240},{96,0},{112,1... | collective-permute-start | bytes 294920 | tf_op jit(solution)/shard_map/ppermute | solution.py:58
  85.3 0.9 collective-permute-start.25
  86.2 2.7 %collective-permute-start.26 = (bf16[32,1536]{1,0:T(8,128)(2,1)}, bf16[32,1536]{1,0:T(8,128)(2,1)S(1)}, u32[]{:S(2)}, u32[]{:S(2)}) collective-permute-start(bf16[32,1536]{1,0:T(8,128)(2,1)} %copy-done.22), channel_id=1, source_target_pairs={{0,128},{16,144},{32,160},{48,176},{64,192},{80,208},{96,224},{112... | collective-permute-start | bytes 294920 | tf_op jit(solution)/shard_map/ppermute | solution.py:58
  88.9 0.6 constant_dynamic-slice_fusion.refs_9_
  89.5 1.2 collective-permute-done.22.refs_4_
  90.7 0.6 copy-done.12
  91.4 0.6 copy-done.14
  92.0 4.3 %collective-permute-done.24.refs_6_ = bf16[32,1536]{1,0:T(8,128)(2,1)S(1)} collective-permute-done((bf16[32,1536]{1,0:T(8,128)(2,1)}, bf16[32,1536]{1,0:T(8,128)(2,1)S(1)}, u32[]{:S(2)}, u32[]{:S(2)}) %collective-permute-start.24) | collective-permute-done | bytes 98336 | tf_op jit(solution)/shard_map/ppermute | solution.py:58
  96.3 0.6 copy-done.16
  96.9 1.4 collective-permute-done.25.refs_7_
  98.3 0.6 copy-done.18
  99.0 0.6 copy-done.20
  99.6 0.5 all-to-all-done.refs_0_
  100.1 0.9 copy-done.4
  101.0 0.9 copy-done.5
  101.9 0.9 copy-done.11
  102.8 0.9 copy-done.13
  103.7 0.9 copy-done.15
  104.6 0.9 copy-done.17
  105.5 0.9 copy-done.19
  106.4 0.9 copy-done.21
  107.3 3.7 %shard_map.89 = bf16[16,32,1664]{2,1,0:T(8,128)(2,1)S(1)} custom-call(bf16[16,32,1664]{2,1,0:T(8,128)(2,1)S(1)} %all-to-all-done.refs_0_, bf16[32,1536]{1,0:T(8,128)(2,1)S(1)} %copy-done.11, bf16[32,1536]{1,0:T(8,128)(2,1)} %collective-permute-done.20.refs_2_, bf16[32,1536]{1,0:T(8,128)(2,1)} %collective-permute-done.21.refs_3_, ...), custom_call_target="tpu_custom_call" | custom-call | tf_op jit(solution)/shard_map/pallas_call | solution.py:22
  111.0 28.9 %all_to_all.20.grads_ref = bf16[16,32,1664]{2,1,0:T(8,128)(2,1)S(1)} all-to-all(bf16[16,32,1664]{2,1,0:T(8,128)(2,1)S(1)} %shard_map.89), channel_id=1, replica_groups={{0,2,4,6,8,10,12,14,16,18,20,22,24,26,28,30},{1,3,5,7,9,11,13,15,17,19,..., dimensions={0} | all-to-all | bytes 3407872 | tf_op jit(solution)/shard_map/all_to_all | solution.py:283
  140.4 1.6 collective-permute-done.28.came_ref
  142.1 18.3 %all_to_all.21.parts_ref = bf16[8,48,384]{2,1,0:T(8,128)(2,1)S(1)} all-to-all(bf16[8,48,384]{2,1,0:T(8,128)(2,1)S(1)} %shard_map.91), channel_id=1, replica_groups={{0,32,64,96,128,160,192,224},{16,48,80,112,144,176,208,240},{1,33,65,97..., dimensions={0} | all-to-all | bytes 589824 | tf_op jit(solution)/shard_map/all_to_all | solution.py:330
  160.4 1.0 shard_map.92
  161.4 0.8 copy-done.1
  162.2 4.2 %all-to-all-start.3 = ((bf16[16,48,384]{2,1,0:T(8,128)(2,1)}), bf16[16,48,384]{2,1,0:T(8,128)(2,1)}, u32[]{:S(2)}, u32[]{:S(2)}) async-start(bf16[16,48,384]{2,1,0:T(8,128)(2,1)} %copy-done.1), calls=%async_computation.3 | async-start | bytes 1179648 | tf_op jit(solution)/shard_map/all_to_all | solution.py:340
  166.9 1.1 collective-permute-done.27
  168.0 0.7 select_n.131
  168.7 16.6 %all-to-all-done.3.parts_ref = bf16[16,48,384]{2,1,0:T(8,128)(2,1)} async-done(((bf16[16,48,384]{2,1,0:T(8,128)(2,1)}), bf16[16,48,384]{2,1,0:T(8,128)(2,1)}, u32[]{:S(2)}, u32[]{:S(2)}) %all-to-all-start.3) | async-done | bytes 589856 | tf_op jit(solution)/shard_map/all_to_all | solution.py:340
  185.3 2.1 %shard_map.93 = (f32[96,1536]{1,0:T(8,128)}, f32[96,1536]{1,0:T(8,128)}) custom-call(bf16[16,48,384]{2,1,0:T(8,128)(2,1)} %all-to-all-done.3.parts_ref), custom_call_target="tpu_custom_call" | custom-call | tf_op jit(solution)/shard_map/pallas_call | solution.py:22
  (92 shorter events, 4.1 us)
Async XLA Ops:
  0.6 7.2 %copy-start = (bf16[512,1536]{1,0:T(8,128)(2,1)S(1)}, bf16[512,1536]{1,0:T(8,128)(2,1)}, u32[]{:S(2)}) copy-start(bf16[512,1536]{1,0:T(8,128)(2,1)} %param.6) | copy-start | bytes 4718596
  0.6 1.0 copy-start.3
  1.7 7.9 %copy-start.29 = (bf16[96,512]{1,0:T(8,128)(2,1)S(1)}, bf16[96,512]{1,0:T(8,128)(2,1)}, u32[]{:S(2)}) copy-start(bf16[96,512]{1,0:T(8,128)(2,1)} %param.9) | copy-start | bytes 294916
  1.7 7.9 %copy-start.30 = (bf16[96,512]{1,0:T(8,128)(2,1)S(1)}, bf16[96,512]{1,0:T(8,128)(2,1)}, u32[]{:S(2)}) copy-start(bf16[96,512]{1,0:T(8,128)(2,1)} %param.8) | copy-start | bytes 294916
  1.8 32.2 %collective-permute-start.3 = (bf16[32,1536]{1,0:T(8,128)(2,1)S(1)}, bf16[32,1536]{1,0:T(8,128)(2,1)S(1)}, u32[]{:S(2)}, u32[]{:S(2)}) collective-permute-start(bf16[32,1536]{1,0:T(8,128)(2,1)S(1)} %shard_map.86.refs_4_), channel_id=1, source_target_pairs={{0,32},{16,48},{32,64},{48,80},{64,96},{80,112},{96,128},{112,144}... | collective-permute-start | bytes 294920 | tf_op jit(solution)/shard_map/ppermute | solution.py:58
  3.8 30.9 %collective-permute-start.4 = (bf16[32,1536]{1,0:T(8,128)(2,1)S(1)}, bf16[32,1536]{1,0:T(8,128)(2,1)S(1)}, u32[]{:S(2)}, u32[]{:S(2)}) collective-permute-start(bf16[32,1536]{1,0:T(8,128)(2,1)S(1)} %shard_map.86.refs_4_), channel_id=1, source_target_pairs={{0,224},{16,240},{32,0},{48,16},{64,32},{80,48},{96,64},{112,80},{... | collective-permute-start | bytes 294920 | tf_op jit(solution)/shard_map/ppermute | solution.py:58
  7.9 45.6 %collective-permute-start.18 = (bf16[256,1536]{1,0:T(8,128)(2,1)S(1)}, bf16[256,1536]{1,0:T(8,128)(2,1)}, u32[]{:S(2)}, u32[]{:S(2)}) collective-permute-start(bf16[256,1536]{1,0:T(8,128)(2,1)S(1)} %bitcast.22), channel_id=1, source_target_pairs={{0,16},{16,0},{32,48},{48,32},{64,80},{80,64},{96,112},{112,96},{1... | collective-permute-start | bytes 2359304 | tf_op jit(solution)/shard_map/ppermute | solution.py:62
  9.6 19.5 %collective-permute-start = (bf16[96,512]{1,0:T(8,128)(2,1)S(1)}, bf16[96,512]{1,0:T(8,128)(2,1)S(1)}, u32[]{:S(2)}, u32[]{:S(2)}) collective-permute-start(bf16[96,512]{1,0:T(8,128)(2,1)S(1)} %get-tuple-element.55), channel_id=1, source_target_pairs={{0,16},{16,0},{32,48},{48,32},{64,80},{80,64},{96,112},{112,96},{1... | collective-permute-start | bytes 294920 | tf_op jit(solution)/shard_map/ppermute | solution.py:62
  10.1 19.0 %collective-permute-start.1 = (bf16[96,512]{1,0:T(8,128)(2,1)S(1)}, bf16[96,512]{1,0:T(8,128)(2,1)S(1)}, u32[]{:S(2)}, u32[]{:S(2)}) collective-permute-start(bf16[96,512]{1,0:T(8,128)(2,1)S(1)} %get-tuple-element.56.mine), channel_id=1, source_target_pairs={{0,1},{1,0},{2,3},{3,2},{4,5},{5,4},{6,7},{7,6},{8,9},{9,8},{10,11... | collective-permute-start | bytes 294920 | tf_op jit(solution)/shard_map/ppermute | solution.py:66
  29.1 21.6 %copy-start.6 = (bf16[96,512]{1,0:T(8,128)(2,1)}, bf16[96,512]{1,0:T(8,128)(2,1)S(1)}, u32[]{:S(2)}) copy-start(bf16[96,512]{1,0:T(8,128)(2,1)S(1)} %collective-permute-done.came) | copy-start | bytes 294916
  29.1 10.1 %collective-permute-start.5 = (bf16[32,1536]{1,0:T(8,128)(2,1)S(1)}, bf16[32,1536]{1,0:T(8,128)(2,1)S(1)}, u32[]{:S(2)}, u32[]{:S(2)}) collective-permute-start(bf16[32,1536]{1,0:T(8,128)(2,1)S(1)} %shard_map.86.refs_4_), channel_id=1, source_target_pairs={{0,64},{16,80},{32,96},{48,112},{64,128},{80,144},{96,160},{112,17... | collective-permute-start | bytes 294920 | tf_op jit(solution)/shard_map/ppermute | solution.py:58
  29.1 0.7 copy-start.8
  29.7 13.6 %collective-permute-start.6 = (bf16[32,1536]{1,0:T(8,128)(2,1)S(1)}, bf16[32,1536]{1,0:T(8,128)(2,1)S(1)}, u32[]{:S(2)}, u32[]{:S(2)}) collective-permute-start(bf16[32,1536]{1,0:T(8,128)(2,1)S(1)} %shard_map.86.refs_4_), channel_id=1, source_target_pairs={{0,192},{16,208},{32,224},{48,240},{64,0},{80,16},{96,32},{112,48}... | collective-permute-start | bytes 294920 | tf_op jit(solution)/shard_map/ppermute | solution.py:58
  34.0 11.7 %collective-permute-start.7 = (bf16[32,1536]{1,0:T(8,128)(2,1)S(1)}, bf16[32,1536]{1,0:T(8,128)(2,1)S(1)}, u32[]{:S(2)}, u32[]{:S(2)}) collective-permute-start(bf16[32,1536]{1,0:T(8,128)(2,1)S(1)} %shard_map.86.refs_4_), channel_id=1, source_target_pairs={{0,96},{16,112},{32,128},{48,144},{64,160},{80,176},{96,192},{112,... | collective-permute-start | bytes 294920 | tf_op jit(solution)/shard_map/ppermute | solution.py:58
  34.7 13.2 %collective-permute-start.8 = (bf16[32,1536]{1,0:T(8,128)(2,1)S(1)}, bf16[32,1536]{1,0:T(8,128)(2,1)S(1)}, u32[]{:S(2)}, u32[]{:S(2)}) collective-permute-start(bf16[32,1536]{1,0:T(8,128)(2,1)S(1)} %shard_map.86.refs_4_), channel_id=1, source_target_pairs={{0,160},{16,176},{32,192},{48,208},{64,224},{80,240},{96,0},{112,1... | collective-permute-start | bytes 294920 | tf_op jit(solution)/shard_map/ppermute | solution.py:58
  39.1 9.7 %collective-permute-start.9 = (bf16[32,1536]{1,0:T(8,128)(2,1)S(1)}, bf16[32,1536]{1,0:T(8,128)(2,1)S(1)}, u32[]{:S(2)}, u32[]{:S(2)}) collective-permute-start(bf16[32,1536]{1,0:T(8,128)(2,1)S(1)} %shard_map.86.refs_4_), channel_id=1, source_target_pairs={{0,128},{16,144},{32,160},{48,176},{64,192},{80,208},{96,224},{112... | collective-permute-start | bytes 294920 | tf_op jit(solution)/shard_map/ppermute | solution.py:58
  43.3 5.5 %collective-permute-start.10 = (bf16[32,1536]{1,0:T(8,128)(2,1)S(1)}, bf16[32,1536]{1,0:T(8,128)(2,1)S(1)}, u32[]{:S(2)}, u32[]{:S(2)}) collective-permute-start(bf16[32,1536]{1,0:T(8,128)(2,1)S(1)} %shard_map.86.refs_4_), channel_id=1, source_target_pairs={{0,1},{1,0},{2,3},{3,2},{4,5},{5,4},{6,7},{7,6},{8,9},{9,8},{10,11... | collective-permute-start | bytes 294920 | tf_op jit(solution)/shard_map/ppermute | solution.py:66
  45.8 3.7 %collective-permute-start.2 = (bf16[96,512]{1,0:T(8,128)(2,1)S(1)}, bf16[96,512]{1,0:T(8,128)(2,1)S(1)}, u32[]{:S(2)}, u32[]{:S(2)}) collective-permute-start(bf16[96,512]{1,0:T(8,128)(2,1)S(1)} %collective-permute-done.came), channel_id=1, source_target_pairs={{0,1},{1,0},{2,3},{3,2},{4,5},{5,4},{6,7},{7,6},{8,9},{9,8},{10,11... | collective-permute-start | bytes 294920 | tf_op jit(solution)/shard_map/ppermute | solution.py:66
  47.9 1.6 collective-permute-start.11
  48.9 1.3 collective-permute-start.12
  48.9 1.5 collective-permute-start.13
  49.5 4.0 %collective-permute-start.14 = (bf16[32,1536]{1,0:T(8,128)(2,1)S(1)}, bf16[32,1536]{1,0:T(8,128)(2,1)S(1)}, u32[]{:S(2)}, u32[]{:S(2)}) collective-permute-start(bf16[32,1536]{1,0:T(8,128)(2,1)S(1)} %collective-permute-done.6.refs_8_), channel_id=1, source_target_pairs={{0,1},{1,0},{2,3},{3,2},{4,5},{5,4},{6,7},{7,6},{8,9},{9,8},{10,11... | collective-permute-start | bytes 294920 | tf_op jit(solution)/shard_map/ppermute | solution.py:66
  49.5 3.9 %collective-permute-start.15 = (bf16[32,1536]{1,0:T(8,128)(2,1)S(1)}, bf16[32,1536]{1,0:T(8,128)(2,1)S(1)}, u32[]{:S(2)}, u32[]{:S(2)}) collective-permute-start(bf16[32,1536]{1,0:T(8,128)(2,1)S(1)} %collective-permute-done.7.refs_9_), channel_id=1, source_target_pairs={{0,1},{1,0},{2,3},{3,2},{4,5},{5,4},{6,7},{7,6},{8,9},{9,8},{10,11... | collective-permute-start | bytes 294920 | tf_op jit(solution)/shard_map/ppermute | solution.py:66
  50.2 3.3 %collective-permute-start.16 = (bf16[32,1536]{1,0:T(8,128)(2,1)S(1)}, bf16[32,1536]{1,0:T(8,128)(2,1)S(1)}, u32[]{:S(2)}, u32[]{:S(2)}) collective-permute-start(bf16[32,1536]{1,0:T(8,128)(2,1)S(1)} %collective-permute-done.8.refs_10_), channel_id=1, source_target_pairs={{0,1},{1,0},{2,3},{3,2},{4,5},{5,4},{6,7},{7,6},{8,9},{9,8},{10,11... | collective-permute-start | bytes 294920 | tf_op jit(solution)/shard_map/ppermute | solution.py:66
  50.3 3.1 %collective-permute-start.17 = (bf16[32,1536]{1,0:T(8,128)(2,1)S(1)}, bf16[32,1536]{1,0:T(8,128)(2,1)S(1)}, u32[]{:S(2)}, u32[]{:S(2)}) collective-permute-start(bf16[32,1536]{1,0:T(8,128)(2,1)S(1)} %collective-permute-done.9.refs_11_), channel_id=1, source_target_pairs={{0,1},{1,0},{2,3},{3,2},{4,5},{5,4},{6,7},{7,6},{8,9},{9,8},{10,11... | collective-permute-start | bytes 294920 | tf_op jit(solution)/shard_map/ppermute | solution.py:66
  50.8 0.9 copy-start.7
  51.7 0.9 copy-start.9
  59.3 8.8 %copy-start.2 = (bf16[16,32,1664]{2,1,0:T(8,128)(2,1)}, bf16[16,32,1664]{2,1,0:T(8,128)(2,1)S(1)}, u32[]{:S(2)}) copy-start(bf16[16,32,1664]{2,1,0:T(8,128)(2,1)S(1)} %get-tuple-element.41) | copy-start | bytes 5111812
  59.3 2.4 %collective-permute-start.19 = (bf16[256,1536]{1,0:T(8,128)(2,1)S(1)}, bf16[256,1536]{1,0:T(8,128)(2,1)S(1)}, u32[]{:S(2)}, u32[]{:S(2)}) collective-permute-start(bf16[256,1536]{1,0:T(8,128)(2,1)S(1)} %get-tuple-element.32), channel_id=1, source_target_pairs={{0,1},{1,0},{2,3},{3,2},{4,5},{5,4},{6,7},{7,6},{8,9},{9,8},{10,11... | collective-permute-start | bytes 2359304 | tf_op jit(solution)/shard_map/ppermute | solution.py:66
  63.0 0.6 copy-start.10
  63.6 0.6 copy-start.22
  64.2 0.6 copy-start.24
  64.9 0.6 copy-start.25
  65.5 0.6 copy-start.26
  66.1 0.6 copy-start.27
  66.8 0.6 copy-start.28
  67.4 0.6 copy-start.23
  68.1 32.1 %all-to-all-start = ((bf16[16,32,1664]{2,1,0:T(8,128)(2,1)}), bf16[16,32,1664]{2,1,0:T(8,128)(2,1)S(1)}, u32[]{:S(2)}, u32[]{:S(2)}) async-start(bf16[16,32,1664]{2,1,0:T(8,128)(2,1)} %copy-done.2), calls=%async_computation | async-start | bytes 3407872 | tf_op jit(solution)/shard_map/all_to_all | solution.py:283
  75.7 9.6 %collective-permute-start.20 = (bf16[32,1536]{1,0:T(8,128)(2,1)}, bf16[32,1536]{1,0:T(8,128)(2,1)}, u32[]{:S(2)}, u32[]{:S(2)}) collective-permute-start(bf16[32,1536]{1,0:T(8,128)(2,1)} %copy-done.28), channel_id=1, source_target_pairs={{0,224},{16,240},{32,0},{48,16},{64,32},{80,48},{96,64},{112,80},{... | collective-permute-start | bytes 294920 | tf_op jit(solution)/shard_map/ppermute | solution.py:58
  75.7 10.5 %collective-permute-start.21 = (bf16[32,1536]{1,0:T(8,128)(2,1)}, bf16[32,1536]{1,0:T(8,128)(2,1)}, u32[]{:S(2)}, u32[]{:S(2)}) collective-permute-start(bf16[32,1536]{1,0:T(8,128)(2,1)} %copy-done.27), channel_id=1, source_target_pairs={{0,32},{16,48},{32,64},{48,80},{64,96},{80,112},{96,128},{112,144}... | collective-permute-start | bytes 294920 | tf_op jit(solution)/shard_map/ppermute | solution.py:58
  79.4 11.3 %collective-permute-start.22 = (bf16[32,1536]{1,0:T(8,128)(2,1)}, bf16[32,1536]{1,0:T(8,128)(2,1)S(1)}, u32[]{:S(2)}, u32[]{:S(2)}) collective-permute-start(bf16[32,1536]{1,0:T(8,128)(2,1)} %copy-done.26), channel_id=1, source_target_pairs={{0,192},{16,208},{32,224},{48,240},{64,0},{80,16},{96,32},{112,48}... | collective-permute-start | bytes 294920 | tf_op jit(solution)/shard_map/ppermute | solution.py:58
  80.9 10.5 %collective-permute-start.23 = (bf16[32,1536]{1,0:T(8,128)(2,1)}, bf16[32,1536]{1,0:T(8,128)(2,1)S(1)}, u32[]{:S(2)}, u32[]{:S(2)}) collective-permute-start(bf16[32,1536]{1,0:T(8,128)(2,1)} %copy-done.25), channel_id=1, source_target_pairs={{0,64},{16,80},{32,96},{48,112},{64,128},{80,144},{96,160},{112,17... | collective-permute-start | bytes 294920 | tf_op jit(solution)/shard_map/ppermute | solution.py:58
  82.3 13.9 %collective-permute-start.24 = (bf16[32,1536]{1,0:T(8,128)(2,1)}, bf16[32,1536]{1,0:T(8,128)(2,1)S(1)}, u32[]{:S(2)}, u32[]{:S(2)}) collective-permute-start(bf16[32,1536]{1,0:T(8,128)(2,1)} %copy-done.24), channel_id=1, source_target_pairs={{0,160},{16,176},{32,192},{48,208},{64,224},{80,240},{96,0},{112,1... | collective-permute-start | bytes 294920 | tf_op jit(solution)/shard_map/ppermute | solution.py:58
  85.3 13.1 %collective-permute-start.25 = (bf16[32,1536]{1,0:T(8,128)(2,1)}, bf16[32,1536]{1,0:T(8,128)(2,1)S(1)}, u32[]{:S(2)}, u32[]{:S(2)}) collective-permute-start(bf16[32,1536]{1,0:T(8,128)(2,1)} %copy-done.23), channel_id=1, source_target_pairs={{0,96},{16,112},{32,128},{48,144},{64,160},{80,176},{96,192},{112,... | collective-permute-start | bytes 294920 | tf_op jit(solution)/shard_map/ppermute | solution.py:58
  86.2 12.8 %collective-permute-start.26 = (bf16[32,1536]{1,0:T(8,128)(2,1)}, bf16[32,1536]{1,0:T(8,128)(2,1)S(1)}, u32[]{:S(2)}, u32[]{:S(2)}) collective-permute-start(bf16[32,1536]{1,0:T(8,128)(2,1)} %copy-done.22), channel_id=1, source_target_pairs={{0,128},{16,144},{32,160},{48,176},{64,192},{80,208},{96,224},{112... | collective-permute-start | bytes 294920 | tf_op jit(solution)/shard_map/ppermute | solution.py:58
  90.7 0.6 copy-start.12
  91.4 0.6 copy-start.14
  96.3 0.6 copy-start.16
  98.3 0.6 copy-start.18
  99.0 0.6 copy-start.20
  100.1 0.9 copy-start.4
  101.0 0.9 copy-start.5
  101.9 0.9 copy-start.11
  102.8 0.9 copy-start.13
  103.7 0.9 copy-start.15
  104.6 0.9 copy-start.17
  105.5 0.9 copy-start.19
  106.4 0.9 copy-start.21
  140.3 1.7 collective-permute-start.28
  161.4 0.8 copy-start.1
  162.2 23.0 %all-to-all-start.3 = ((bf16[16,48,384]{2,1,0:T(8,128)(2,1)}), bf16[16,48,384]{2,1,0:T(8,128)(2,1)}, u32[]{:S(2)}, u32[]{:S(2)}) async-start(bf16[16,48,384]{2,1,0:T(8,128)(2,1)} %copy-done.1), calls=%async_computation.3 | async-start | bytes 1179648 | tf_op jit(solution)/shard_map/all_to_all | solution.py:340
  166.8 1.3 collective-permute-start.27

commit v5 on v4

--- a/solution.py
+++ b/solution.py
@@ -14,6 +14,7 @@
 HBM = pl.BlockSpec(memory_space=pltpu.HBM)
 ANY = pl.BlockSpec(memory_space=pl.ANY)
 DMA = pltpu.SemaphoreType.DMA
+WHOLE = 58
 
 
 def local(kernel, outs, operands, mib, specs=None, out_specs=None, scratch=()):
@@ -234,12 +235,14 @@
     partner = swap_y(own)
 
     mine = jnp.where(y == 0, img_feat_t, txt_feat_t)
-    came = swap_y(jnp.where(y == 0, txt_feat_t, img_feat_t))
+    theirs = jnp.where(y == 0, txt_feat_t, img_feat_t)
+    mine, theirs, *blocks = lax.optimization_barrier((mine, theirs, *blocks))
+    came = swap_y(theirs)
     feat_part = local(
         feature_kernel,
         ((2 * feats, rows), BF16),
         [jnp.stack([y, core]), mine, came, swap_core(mine), swap_core(came)],
-        8,
+        WHOLE,
         [SMEM] + [VMEM] * 4,
     )
 
@@ -254,7 +257,6 @@
     )
     places = jnp.stack([8 * y, 8 * (1 - y)])
     numbers = jnp.concatenate([logit_scale, logit_bias])
-    numbers, feat_part = lax.optimization_barrier((numbers, feat_part))
     image_part, keep, send = local(
         tile_kernel,
         [((16, sub, full), BF16), ((half, width), F32), ((half, width), BF16)],
@@ -288,12 +290,14 @@
         join_kernel,
         [((sub, width), BF16)] * 8,
         [keep, swap_core(send)],
-        10,
+        WHOLE,
         None,
         [HBM] * 8,
         [pltpu.VMEM((8, sub, width), BF16), DMA((8,))],
     )
-    image_part, *text_parts = lax.optimization_barrier((image_part, *text_parts))
+    image_part, feat_part, *text_parts = lax.optimization_barrier(
+        (image_part, feat_part, *text_parts)
+    )
     image_pieces = over_plane(image_part)
     text_came = [text_parts[0]] + [
         along_z(part, -steps) for part, steps in zip(text_parts[1:], ALONG[1:], strict=True)
@@ -303,7 +307,7 @@
         grad_kernel,
         ((16, sub, full), BF16),
         [image_pieces, *text_came, raw_img, txt_emb],
-        12,
+        WHOLE,
         [VMEM] + [ANY] * 8 + [VMEM] * 2,
         [HBM],
         [pltpu.VMEM((8, sub, width), BF16), pltpu.VMEM((2, sub, full), BF16), DMA((16,))],
@@ -332,7 +336,7 @@
         spread_kernel,
         ((16, *shape), BF16),
         [parts],
-        6,
+        WHOLE,
         None,
         [HBM],
         [pltpu.VMEM(shape, BF16), DMA((16,))],

time: 188 us -> 168 us (0.89)
  local copies, waits for them, and re-layouts: 21.4 us -> 7.24 us
  waiting for transfers between devices: 51.7 us -> 37.7 us
  Pallas kernels: 15.5 us -> 18.8 us
    unnamed x62 -> x38, local copies, waits for them, and re-layouts: 19.7 us -> 5.56 us
    ppermute x2, waiting for transfers between devices: 17.2 us -> 4.33 us  [swap_y(): return lax.ppermute(value, 'dp', [(d, d ^ 1) for d in range(16)])]
    ppermute x14, waiting for transfers between devices: 12.4 us -> 8.61 us  [along_z(): lax.ppermute(value, 'dp', [(d, (d + 2 * steps) % 16) for d in range(16)])]
    pallas_call x9, Pallas kernels: 15.5 us -> 18.8 us  [local(): pl.pallas_call(kernel, out_shape=shapes, in_specs=specs or [VMEM] * len(o...]
    all_to_all x1, waiting for transfers between devices: 0.51 us -> 3.2 us  [over_plane(): lax.all_to_all(value, ('dp', 'mp'), 0, 0, tiled=True, axis_index_groups=p...]
  transfers between devices with their start and end apart: 31 -> 31, of which waited for: 13 -> 16; matrix products, arithmetic and copies ran while one was open for 1% -> 2% of each run, Pallas kernels for 0% -> 1%
where the time goes in v5:
time: 168 us; the launch traced here: 167 us
  starting transfers between devices  50.3 us (30%)
  blocking collectives  49 us (29%)
  waiting for transfers between devices  37.7 us (22%)
  Pallas kernels  18.8 us (11%)
  local copies, waits for them, and re-layouts  7.24 us (4%)
  between operations  2.18 us (1%)
  other arithmetic  1.97 us (1%)
    ppermute x14, starting transfers between devices, along_z(): lax.ppermute(value, 'dp', [(d, (d + 2 * steps) % 16) for d in range(16)])  33.2 us
    all_to_all x1, blocking collectives, over_plane(): lax.all_to_all(value, ('dp', 'mp'), 0, 0, tiled=True, axis_index_groups=p...  30.3 us
    pallas_call x9, Pallas kernels, local(): pl.pallas_call(kernel, out_shape=shapes, in_specs=specs or [VMEM] * len(o...  18.8 us
    all_to_all x1, blocking collectives, shards(): lax.all_to_all(cut, 'dp', 0, 0, tiled=True, axis_index_groups=same_y)  18.7 us
    all_to_all x1, waiting for transfers between devices, shards(): weights = lax.all_to_all(summed, 'dp', 0, 0, tiled=True)  16.6 us
    ppermute x14, waiting for transfers between devices, along_z(): lax.ppermute(value, 'dp', [(d, (d + 2 * steps) % 16) for d in range(16)])  8.61 us
    all_to_all x1, starting transfers between devices, over_plane(): lax.all_to_all(value, ('dp', 'mp'), 0, 0, tiled=True, axis_index_groups=p...  7.49 us
    unnamed x38, local copies, waits for them, and re-layouts  5.56 us
  transfers between devices with their start and end apart: 31, of which 16 were waited for; matrix products, arithmetic and copies ran while one was open for 2% of the time, Pallas kernels for 1%

profile of v5, /device:TPU:2, one launch (start us, length us, event | category | flops | bytes accessed | tf_op | source)
XLA Modules:
  0.0 167.1 jit_solution(13386465067788617797)
XLA Ops:
  0.7 1.0 copy-done.3
  1.7 0.1 shard_map.85.refs_4_
  1.8 3.3 %collective-permute-start.2 = (bf16[32,1536]{1,0:T(8,128)(2,1)S(1)}, bf16[32,1536]{1,0:T(8,128)(2,1)}, u32[]{:S(2)}, u32[]{:S(2)}) collective-permute-start(bf16[32,1536]{1,0:T(8,128)(2,1)S(1)} %shard_map.85.refs_4_), channel_id=1, source_target_pairs={{0,64},{16,80},{32,96},{48,112},{64,128},{80,144},{96,160},{112,17... | collective-permute-start | bytes 294920 | tf_op jit(solution)/shard_map/ppermute | solution.py:59
  5.1 3.1 %collective-permute-start.3 = (bf16[32,1536]{1,0:T(8,128)(2,1)S(1)}, bf16[32,1536]{1,0:T(8,128)(2,1)}, u32[]{:S(2)}, u32[]{:S(2)}) collective-permute-start(bf16[32,1536]{1,0:T(8,128)(2,1)S(1)} %shard_map.85.refs_4_), channel_id=1, source_target_pairs={{0,192},{16,208},{32,224},{48,240},{64,0},{80,16},{96,32},{112,48}... | collective-permute-start | bytes 294920 | tf_op jit(solution)/shard_map/ppermute | solution.py:59
  8.2 1.8 %collective-permute-start.4 = (bf16[32,1536]{1,0:T(8,128)(2,1)S(1)}, bf16[32,1536]{1,0:T(8,128)(2,1)}, u32[]{:S(2)}, u32[]{:S(2)}) collective-permute-start(bf16[32,1536]{1,0:T(8,128)(2,1)S(1)} %shard_map.85.refs_4_), channel_id=1, source_target_pairs={{0,96},{16,112},{32,128},{48,144},{64,160},{80,176},{96,192},{112,... | collective-permute-start | bytes 294920 | tf_op jit(solution)/shard_map/ppermute | solution.py:59
  10.1 3.2 %collective-permute-start.5 = (bf16[32,1536]{1,0:T(8,128)(2,1)S(1)}, bf16[32,1536]{1,0:T(8,128)(2,1)}, u32[]{:S(2)}, u32[]{:S(2)}) collective-permute-start(bf16[32,1536]{1,0:T(8,128)(2,1)S(1)} %shard_map.85.refs_4_), channel_id=1, source_target_pairs={{0,160},{16,176},{32,192},{48,208},{64,224},{80,240},{96,0},{112,1... | collective-permute-start | bytes 294920 | tf_op jit(solution)/shard_map/ppermute | solution.py:59
  13.3 1.7 collective-permute-start.15
  15.3 0.7 broadcast_select_fusion
  16.0 5.0 %collective-permute-start.6 = (bf16[32,1536]{1,0:T(8,128)(2,1)S(1)}, bf16[32,1536]{1,0:T(8,128)(2,1)}, u32[]{:S(2)}, u32[]{:S(2)}) collective-permute-start(bf16[32,1536]{1,0:T(8,128)(2,1)S(1)} %shard_map.85.refs_4_), channel_id=1, source_target_pairs={{0,128},{16,144},{32,160},{48,176},{64,192},{80,208},{96,224},{112... | collective-permute-start | bytes 294920 | tf_op jit(solution)/shard_map/ppermute | solution.py:59
  21.1 1.0 collective-permute-start
  22.1 2.2 %collective-permute-start.1 = (bf16[32,1536]{1,0:T(8,128)(2,1)S(1)}, bf16[32,1536]{1,0:T(8,128)(2,1)}, u32[]{:S(2)}, u32[]{:S(2)}) collective-permute-start(bf16[32,1536]{1,0:T(8,128)(2,1)S(1)} %shard_map.85.refs_4_), channel_id=1, source_target_pairs={{0,224},{16,240},{32,0},{48,16},{64,32},{80,48},{96,64},{112,80},{... | collective-permute-start | bytes 294920 | tf_op jit(solution)/shard_map/ppermute | solution.py:59
  24.3 0.1 copy.11.refs_3_
  26.0 1.4 collective-permute-done.6.refs_11_
  27.4 0.2 collective-permute-done.refs_5_
  27.6 0.3 collective-permute-start.11
  27.9 0.2 collective-permute-start.12
  28.2 0.3 collective-permute-start.13
  28.5 0.4 collective-permute-done.10.refs_15_
  28.9 0.2 collective-permute-start.14
  29.1 0.3 collective-permute-start.8
  29.4 0.3 collective-permute-start.9
  29.8 0.6 collective-permute-done.14.refs_19_
  30.4 0.2 collective-permute-done.8.refs_13_
  30.6 0.3 collective-permute-done.9.refs_14_
  30.9 0.9 collective-permute-done.15.refs_21_
  31.9 4.9 %shard_map.86 = (bf16[16,32,1664]{2,1,0:T(8,128)(2,1)}, f32[256,1536]{1,0:T(8,128)S(1)}, bf16[256,1536]{1,0:T(8,128)(2,1)S(1)}) custom-call(f32[2]{0:T(128)S(1)} %pad_maximum_fusion.refs_0_, s32[2]{0:T(128)S(1)} %pad_add_fusion.1.refs_1_, s32[1,512]{1,0:T(1,128)S(1)} %add.176.refs_2_, s32[512,1]{1,0:T(8,128)S(1)} %copy.11.refs_3_, ...), custom_call_target="tpu_custom_call" | custom-call | tf_op jit(solution)/shard_map/pallas_call | solution.py:23
  36.8 1.1 copy-done.1
  37.9 1.6 collective-permute-start.16
  39.5 0.2 collective-permute-start.17
  39.8 3.4 %collective-permute-done.16.came = bf16[96,512]{1,0:T(8,128)(2,1)S(1)} collective-permute-done((bf16[96,512]{1,0:T(8,128)(2,1)S(1)}, bf16[96,512]{1,0:T(8,128)(2,1)S(1)}, u32[]{:S(2)}, u32[]{:S(2)}) %collective-permute-start.16) | collective-permute-done | bytes 98336 | tf_op jit(solution)/shard_map/ppermute | solution.py:63
  43.2 0.6 pad_add_fusion.2.flags
  43.8 0.7 collective-permute-done.18.came_next
  44.5 0.6 copy-done.12
  45.1 2.1 %shard_map.87.feats_ref = bf16[192,512]{1,0:T(8,128)(2,1)} custom-call(s32[2]{0:T(128)} %pad_add_fusion.2.flags, bf16[96,512]{1,0:T(8,128)(2,1)} %get-tuple-element.63.mine, bf16[96,512]{1,0:T(8,128)(2,1)} %copy-done.10, bf16[96,512]{1,0:T(8,128)(2,1)} %copy-done.11, bf16[96,512]{1,0:T(8,128)(2,1)} %copy-done.12), custom_call_target="tpu_custom_call" | custom-call | tf_op jit(solution)/shard_map/pallas_call | solution.py:23
  47.2 0.9 copy-done.5
  48.1 2.7 %shard_map.88 = (bf16[32,1536]{1,0:T(8,128)(2,1)}, bf16[32,1536]{1,0:T(8,128)(2,1)}, bf16[32,1536]{1,0:T(8,128)(2,1)}, bf16[32,1536]{1,0:T(8,128)(2,1)}, bf16[32...) custom-call(f32[256,1536]{1,0:T(8,128)} %copy-done.1, ...), custom_call_target="tpu_custom_call" | custom-call | tf_op jit(solution)/shard_map/pallas_call | solution.py:23
  50.7 7.5 %all-to-all-start = ((bf16[16,32,1664]{2,1,0:T(8,128)(2,1)}), bf16[16,32,1664]{2,1,0:T(8,128)(2,1)S(1)}, u32[]{:S(2)}, u32[]{:S(2)}) async-start(bf16[16,32,1664]{2,1,0:T(8,128)(2,1)} %get-tuple-element.75), calls=%async_computation | async-start | bytes 3407872 | tf_op jit(solution)/shard_map/all_to_all | solution.py:285
  58.2 1.5 collective-permute-start.20
  59.7 0.5 collective-permute-start.21
  60.2 2.7 %collective-permute-start.22 = (bf16[32,1536]{1,0:T(8,128)(2,1)}, bf16[32,1536]{1,0:T(8,128)(2,1)S(1)}, u32[]{:S(2)}, u32[]{:S(2)}) collective-permute-start(bf16[32,1536]{1,0:T(8,128)(2,1)} %get-tuple-element.79), channel_id=1, source_target_pairs={{0,192},{16,208},{32,224},{48,240},{64,0},{80,16},{96,32},{112,48}... | collective-permute-start | bytes 294920 | tf_op jit(solution)/shard_map/ppermute | solution.py:59
  63.0 0.2 collective-permute-start.23
  63.2 4.2 %collective-permute-start.24 = (bf16[32,1536]{1,0:T(8,128)(2,1)}, bf16[32,1536]{1,0:T(8,128)(2,1)S(1)}, u32[]{:S(2)}, u32[]{:S(2)}) collective-permute-start(bf16[32,1536]{1,0:T(8,128)(2,1)} %get-tuple-element.81), channel_id=1, source_target_pairs={{0,160},{16,176},{32,192},{48,208},{64,224},{80,240},{96,0},{112,1... | collective-permute-start | bytes 294920 | tf_op jit(solution)/shard_map/ppermute | solution.py:59
  67.4 0.6 collective-permute-start.25
  68.0 3.6 %collective-permute-start.26 = (bf16[32,1536]{1,0:T(8,128)(2,1)}, bf16[32,1536]{1,0:T(8,128)(2,1)}, u32[]{:S(2)}, u32[]{:S(2)}) collective-permute-start(bf16[32,1536]{1,0:T(8,128)(2,1)} %get-tuple-element.83), channel_id=1, source_target_pairs={{0,128},{16,144},{32,160},{48,176},{64,192},{80,208},{96,224},{112... | collective-permute-start | bytes 294920 | tf_op jit(solution)/shard_map/ppermute | solution.py:59
  71.7 0.6 constant_dynamic-slice_fusion.refs_9_
  72.3 1.3 collective-permute-done.24.refs_6_
  73.6 4.9 %collective-permute-done.25.refs_7_ = bf16[32,1536]{1,0:T(8,128)(2,1)S(1)} collective-permute-done((bf16[32,1536]{1,0:T(8,128)(2,1)}, bf16[32,1536]{1,0:T(8,128)(2,1)S(1)}, u32[]{:S(2)}, u32[]{:S(2)}) %collective-permute-start.25) | collective-permute-done | bytes 98336 | tf_op jit(solution)/shard_map/ppermute | solution.py:59
  78.5 0.6 copy-done.18
  79.2 0.8 collective-permute-done.26.refs_8_
  79.9 3.2 %all-to-all-done.refs_0_ = bf16[16,32,1664]{2,1,0:T(8,128)(2,1)S(1)} async-done(((bf16[16,32,1664]{2,1,0:T(8,128)(2,1)}), bf16[16,32,1664]{2,1,0:T(8,128)(2,1)S(1)}, u32[]{:S(2)}, u32[]{:S(2)}) %all-to-all-start) | async-done | bytes 1703968 | tf_op jit(solution)/shard_map/all_to_all | solution.py:285
  83.1 1.2 copy-done.4
  84.4 4.3 %shard_map.89 = bf16[16,32,1664]{2,1,0:T(8,128)(2,1)} custom-call(bf16[16,32,1664]{2,1,0:T(8,128)(2,1)} %copy-done.4, bf16[32,1536]{1,0:T(8,128)(2,1)} %get-tuple-element.76.refs_1_, bf16[32,1536]{1,0:T(8,128)(2,1)} %copy-done.13, bf16[32,1536]{1,0:T(8,128)(2,1)} %copy-done.14, bf16[32,1536]{1,0:T(8,128)(2,1)} %copy-done.15, bf16[32,1536]{1,0:T(8,128)(2,1)} %copy-done.16, ...), custom_call_target="tpu_custom_call" | custom-call | tf_op jit(solution)/shard_map/pallas_call | solution.py:23
  88.7 30.3 %all_to_all.20.grads_ref = bf16[16,32,1664]{2,1,0:T(8,128)(2,1)S(1)} all-to-all(bf16[16,32,1664]{2,1,0:T(8,128)(2,1)} %shard_map.89), channel_id=1, replica_groups={{0,2,4,6,8,10,12,14,16,18,20,22,24,26,28,30},{1,3,5,7,9,11,13,15,17,19,..., dimensions={0} | all-to-all | bytes 3407872 | tf_op jit(solution)/shard_map/all_to_all | solution.py:285
  119.0 0.5 shard_map.90
  119.5 1.6 collective-permute-done.28.came_ref
  121.1 0.1 shard_map.91
  121.2 18.7 %all_to_all.21.parts_ref = bf16[8,48,384]{2,1,0:T(8,128)(2,1)} all-to-all(bf16[8,48,384]{2,1,0:T(8,128)(2,1)S(1)} %shard_map.91), channel_id=1, replica_groups={{0,32,64,96,128,160,192,224},{16,48,80,112,144,176,208,240},{1,33,65,97..., dimensions={0} | all-to-all | bytes 589824 | tf_op jit(solution)/shard_map/all_to_all | solution.py:334
  140.0 1.9 %shard_map.92 = bf16[16,48,384]{2,1,0:T(8,128)(2,1)} custom-call(bf16[8,48,384]{2,1,0:T(8,128)(2,1)} %all_to_all.21.parts_ref), custom_call_target="tpu_custom_call" | custom-call | tf_op jit(solution)/shard_map/pallas_call | solution.py:23
  141.9 4.3 %all-to-all-start.3 = ((bf16[16,48,384]{2,1,0:T(8,128)(2,1)}), bf16[16,48,384]{2,1,0:T(8,128)(2,1)}, u32[]{:S(2)}, u32[]{:S(2)}) async-start(bf16[16,48,384]{2,1,0:T(8,128)(2,1)} %shard_map.92), calls=%async_computation.3 | async-start | bytes 1179648 | tf_op jit(solution)/shard_map/all_to_all | solution.py:344
  146.2 0.1 slice_add_fusion
  146.6 1.1 collective-permute-done.27
  147.7 0.7 select_n.131
  148.4 16.6 %all-to-all-done.3.parts_ref = bf16[16,48,384]{2,1,0:T(8,128)(2,1)} async-done(((bf16[16,48,384]{2,1,0:T(8,128)(2,1)}), bf16[16,48,384]{2,1,0:T(8,128)(2,1)}, u32[]{:S(2)}, u32[]{:S(2)}) %all-to-all-start.3) | async-done | bytes 589856 | tf_op jit(solution)/shard_map/all_to_all | solution.py:344
  165.0 2.1 %shard_map.93 = (f32[96,1536]{1,0:T(8,128)}, f32[96,1536]{1,0:T(8,128)}) custom-call(bf16[16,48,384]{2,1,0:T(8,128)(2,1)} %all-to-all-done.3.parts_ref), custom_call_target="tpu_custom_call" | custom-call | tf_op jit(solution)/shard_map/pallas_call | solution.py:23
  (68 shorter events, 1.2 us)
Async XLA Ops:
  0.6 12.7 %copy-start = (bf16[512,1536]{1,0:T(8,128)(2,1)S(1)}, bf16[512,1536]{1,0:T(8,128)(2,1)}, u32[]{:S(2)}) copy-start(bf16[512,1536]{1,0:T(8,128)(2,1)} %param.6) | copy-start | bytes 4718596
  0.6 1.0 copy-start.3
  1.7 13.7 %copy-start.7 = (bf16[96,512]{1,0:T(8,128)(2,1)S(1)}, bf16[96,512]{1,0:T(8,128)(2,1)}, u32[]{:S(2)}) copy-start(bf16[96,512]{1,0:T(8,128)(2,1)} %param.9) | copy-start | bytes 294916
  1.7 13.7 %copy-start.8 = (bf16[96,512]{1,0:T(8,128)(2,1)S(1)}, bf16[96,512]{1,0:T(8,128)(2,1)}, u32[]{:S(2)}) copy-start(bf16[96,512]{1,0:T(8,128)(2,1)} %param.8) | copy-start | bytes 294916
  1.8 14.3 %collective-permute-start.2 = (bf16[32,1536]{1,0:T(8,128)(2,1)S(1)}, bf16[32,1536]{1,0:T(8,128)(2,1)}, u32[]{:S(2)}, u32[]{:S(2)}) collective-permute-start(bf16[32,1536]{1,0:T(8,128)(2,1)S(1)} %shard_map.85.refs_4_), channel_id=1, source_target_pairs={{0,64},{16,80},{32,96},{48,112},{64,128},{80,144},{96,160},{112,17... | collective-permute-start | bytes 294920 | tf_op jit(solution)/shard_map/ppermute | solution.py:59
  5.1 15.9 %collective-permute-start.3 = (bf16[32,1536]{1,0:T(8,128)(2,1)S(1)}, bf16[32,1536]{1,0:T(8,128)(2,1)}, u32[]{:S(2)}, u32[]{:S(2)}) collective-permute-start(bf16[32,1536]{1,0:T(8,128)(2,1)S(1)} %shard_map.85.refs_4_), channel_id=1, source_target_pairs={{0,192},{16,208},{32,224},{48,240},{64,0},{80,16},{96,32},{112,48}... | collective-permute-start | bytes 294920 | tf_op jit(solution)/shard_map/ppermute | solution.py:59
  8.2 13.8 %collective-permute-start.4 = (bf16[32,1536]{1,0:T(8,128)(2,1)S(1)}, bf16[32,1536]{1,0:T(8,128)(2,1)}, u32[]{:S(2)}, u32[]{:S(2)}) collective-permute-start(bf16[32,1536]{1,0:T(8,128)(2,1)S(1)} %shard_map.85.refs_4_), channel_id=1, source_target_pairs={{0,96},{16,112},{32,128},{48,144},{64,160},{80,176},{96,192},{112,... | collective-permute-start | bytes 294920 | tf_op jit(solution)/shard_map/ppermute | solution.py:59
  10.1 15.8 %collective-permute-start.5 = (bf16[32,1536]{1,0:T(8,128)(2,1)S(1)}, bf16[32,1536]{1,0:T(8,128)(2,1)}, u32[]{:S(2)}, u32[]{:S(2)}) collective-permute-start(bf16[32,1536]{1,0:T(8,128)(2,1)S(1)} %shard_map.85.refs_4_), channel_id=1, source_target_pairs={{0,160},{16,176},{32,192},{48,208},{64,224},{80,240},{96,0},{112,1... | collective-permute-start | bytes 294920 | tf_op jit(solution)/shard_map/ppermute | solution.py:59
  13.3 18.5 %collective-permute-start.15 = (bf16[256,1536]{1,0:T(8,128)(2,1)S(1)}, bf16[256,1536]{1,0:T(8,128)(2,1)S(1)}, u32[]{:S(2)}, u32[]{:S(2)}) collective-permute-start(bf16[256,1536]{1,0:T(8,128)(2,1)S(1)} %bitcast.22), channel_id=1, source_target_pairs={{0,16},{16,0},{32,48},{48,32},{64,80},{80,64},{96,112},{112,96},{1... | collective-permute-start | bytes 2359304 | tf_op jit(solution)/shard_map/ppermute | solution.py:63
  16.0 11.4 %collective-permute-start.6 = (bf16[32,1536]{1,0:T(8,128)(2,1)S(1)}, bf16[32,1536]{1,0:T(8,128)(2,1)}, u32[]{:S(2)}, u32[]{:S(2)}) collective-permute-start(bf16[32,1536]{1,0:T(8,128)(2,1)S(1)} %shard_map.85.refs_4_), channel_id=1, source_target_pairs={{0,128},{16,144},{32,160},{48,176},{64,192},{80,208},{96,224},{112... | collective-permute-start | bytes 294920 | tf_op jit(solution)/shard_map/ppermute | solution.py:59
  21.1 6.5 %collective-permute-start = (bf16[32,1536]{1,0:T(8,128)(2,1)S(1)}, bf16[32,1536]{1,0:T(8,128)(2,1)}, u32[]{:S(2)}, u32[]{:S(2)}) collective-permute-start(bf16[32,1536]{1,0:T(8,128)(2,1)S(1)} %shard_map.85.refs_4_), channel_id=1, source_target_pairs={{0,32},{16,48},{32,64},{48,80},{64,96},{80,112},{96,128},{112,144}... | collective-permute-start | bytes 294920 | tf_op jit(solution)/shard_map/ppermute | solution.py:59
  22.1 5.8 %collective-permute-start.1 = (bf16[32,1536]{1,0:T(8,128)(2,1)S(1)}, bf16[32,1536]{1,0:T(8,128)(2,1)}, u32[]{:S(2)}, u32[]{:S(2)}) collective-permute-start(bf16[32,1536]{1,0:T(8,128)(2,1)S(1)} %shard_map.85.refs_4_), channel_id=1, source_target_pairs={{0,224},{16,240},{32,0},{48,16},{64,32},{80,48},{96,64},{112,80},{... | collective-permute-start | bytes 294920 | tf_op jit(solution)/shard_map/ppermute | solution.py:59
  25.9 2.3 %collective-permute-start.7 = (bf16[32,1536]{1,0:T(8,128)(2,1)S(1)}, bf16[32,1536]{1,0:T(8,128)(2,1)S(1)}, u32[]{:S(2)}, u32[]{:S(2)}) collective-permute-start(bf16[32,1536]{1,0:T(8,128)(2,1)S(1)} %shard_map.85.refs_4_), channel_id=1, source_target_pairs={{0,1},{1,0},{2,3},{3,2},{4,5},{5,4},{6,7},{7,6},{8,9},{9,8},{10,11... | collective-permute-start | bytes 294920 | tf_op jit(solution)/shard_map/ppermute | solution.py:67
  27.4 1.5 collective-permute-start.10
  27.6 1.5 collective-permute-start.11
  27.9 1.5 collective-permute-start.12
  28.2 1.6 collective-permute-start.13
  28.9 1.5 collective-permute-start.14
  29.1 1.5 collective-permute-start.8
  29.4 1.5 collective-permute-start.9
  30.9 7.0 %copy-start.9 = (bf16[96,512]{1,0:T(8,128)(2,1)S(1)}, bf16[96,512]{1,0:T(8,128)(2,1)}, u32[]{:S(2)}) copy-start(bf16[96,512]{1,0:T(8,128)(2,1)} %get-tuple-element.64) | copy-start | bytes 294916
  30.9 8.6 %copy-start.6 = (bf16[96,512]{1,0:T(8,128)(2,1)S(1)}, bf16[96,512]{1,0:T(8,128)(2,1)}, u32[]{:S(2)}) copy-start(bf16[96,512]{1,0:T(8,128)(2,1)} %get-tuple-element.63.mine) | copy-start | bytes 294916
  36.8 1.1 copy-start.1
  37.9 9.2 %collective-permute-start.19 = (bf16[256,1536]{1,0:T(8,128)(2,1)S(1)}, bf16[256,1536]{1,0:T(8,128)(2,1)S(1)}, u32[]{:S(2)}, u32[]{:S(2)}) collective-permute-start(bf16[256,1536]{1,0:T(8,128)(2,1)S(1)} %get-tuple-element.66), channel_id=1, source_target_pairs={{0,1},{1,0},{2,3},{3,2},{4,5},{5,4},{6,7},{7,6},{8,9},{9,8},{10,11... | collective-permute-start | bytes 2359304 | tf_op jit(solution)/shard_map/ppermute | solution.py:67
  37.9 5.2 %collective-permute-start.16 = (bf16[96,512]{1,0:T(8,128)(2,1)S(1)}, bf16[96,512]{1,0:T(8,128)(2,1)S(1)}, u32[]{:S(2)}, u32[]{:S(2)}) collective-permute-start(bf16[96,512]{1,0:T(8,128)(2,1)S(1)} %copy-done.9), channel_id=1, source_target_pairs={{0,16},{16,0},{32,48},{48,32},{64,80},{80,64},{96,112},{112,96},{1... | collective-permute-start | bytes 294920 | tf_op jit(solution)/shard_map/ppermute | solution.py:63
  39.5 4.3 %collective-permute-start.17 = (bf16[96,512]{1,0:T(8,128)(2,1)S(1)}, bf16[96,512]{1,0:T(8,128)(2,1)S(1)}, u32[]{:S(2)}, u32[]{:S(2)}) collective-permute-start(bf16[96,512]{1,0:T(8,128)(2,1)S(1)} %copy-done.6), channel_id=1, source_target_pairs={{0,1},{1,0},{2,3},{3,2},{4,5},{5,4},{6,7},{7,6},{8,9},{9,8},{10,11... | collective-permute-start | bytes 294920 | tf_op jit(solution)/shard_map/ppermute | solution.py:67
  43.2 1.3 copy-start.10
  43.2 1.3 collective-permute-start.18
  43.8 0.7 copy-start.11
  44.5 0.6 copy-start.12
  47.2 0.9 copy-start.5
  50.7 32.4 %all-to-all-start = ((bf16[16,32,1664]{2,1,0:T(8,128)(2,1)}), bf16[16,32,1664]{2,1,0:T(8,128)(2,1)S(1)}, u32[]{:S(2)}, u32[]{:S(2)}) async-start(bf16[16,32,1664]{2,1,0:T(8,128)(2,1)} %get-tuple-element.75), calls=%async_computation | async-start | bytes 3407872 | tf_op jit(solution)/shard_map/all_to_all | solution.py:285
  58.2 9.2 %collective-permute-start.20 = (bf16[32,1536]{1,0:T(8,128)(2,1)}, bf16[32,1536]{1,0:T(8,128)(2,1)S(1)}, u32[]{:S(2)}, u32[]{:S(2)}) collective-permute-start(bf16[32,1536]{1,0:T(8,128)(2,1)} %get-tuple-element.77), channel_id=1, source_target_pairs={{0,224},{16,240},{32,0},{48,16},{64,32},{80,48},{96,64},{112,80},{... | collective-permute-start | bytes 294920 | tf_op jit(solution)/shard_map/ppermute | solution.py:59
  59.7 8.3 %collective-permute-start.21 = (bf16[32,1536]{1,0:T(8,128)(2,1)}, bf16[32,1536]{1,0:T(8,128)(2,1)S(1)}, u32[]{:S(2)}, u32[]{:S(2)}) collective-permute-start(bf16[32,1536]{1,0:T(8,128)(2,1)} %get-tuple-element.78), channel_id=1, source_target_pairs={{0,32},{16,48},{32,64},{48,80},{64,96},{80,112},{96,128},{112,144}... | collective-permute-start | bytes 294920 | tf_op jit(solution)/shard_map/ppermute | solution.py:59
  60.2 12.1 %collective-permute-start.22 = (bf16[32,1536]{1,0:T(8,128)(2,1)}, bf16[32,1536]{1,0:T(8,128)(2,1)S(1)}, u32[]{:S(2)}, u32[]{:S(2)}) collective-permute-start(bf16[32,1536]{1,0:T(8,128)(2,1)} %get-tuple-element.79), channel_id=1, source_target_pairs={{0,192},{16,208},{32,224},{48,240},{64,0},{80,16},{96,32},{112,48}... | collective-permute-start | bytes 294920 | tf_op jit(solution)/shard_map/ppermute | solution.py:59
  63.0 9.3 %collective-permute-start.23 = (bf16[32,1536]{1,0:T(8,128)(2,1)}, bf16[32,1536]{1,0:T(8,128)(2,1)S(1)}, u32[]{:S(2)}, u32[]{:S(2)}) collective-permute-start(bf16[32,1536]{1,0:T(8,128)(2,1)} %get-tuple-element.80), channel_id=1, source_target_pairs={{0,64},{16,80},{32,96},{48,112},{64,128},{80,144},{96,160},{112,17... | collective-permute-start | bytes 294920 | tf_op jit(solution)/shard_map/ppermute | solution.py:59
  63.2 10.4 %collective-permute-start.24 = (bf16[32,1536]{1,0:T(8,128)(2,1)}, bf16[32,1536]{1,0:T(8,128)(2,1)S(1)}, u32[]{:S(2)}, u32[]{:S(2)}) collective-permute-start(bf16[32,1536]{1,0:T(8,128)(2,1)} %get-tuple-element.81), channel_id=1, source_target_pairs={{0,160},{16,176},{32,192},{48,208},{64,224},{80,240},{96,0},{112,1... | collective-permute-start | bytes 294920 | tf_op jit(solution)/shard_map/ppermute | solution.py:59
  67.4 15.8 %copy-start.13 = (bf16[32,1536]{1,0:T(8,128)(2,1)}, bf16[32,1536]{1,0:T(8,128)(2,1)S(1)}, u32[]{:S(2)}) copy-start(bf16[32,1536]{1,0:T(8,128)(2,1)S(1)} %collective-permute-done.20.refs_2_) | copy-start | bytes 294916
  67.4 11.2 %collective-permute-start.25 = (bf16[32,1536]{1,0:T(8,128)(2,1)}, bf16[32,1536]{1,0:T(8,128)(2,1)S(1)}, u32[]{:S(2)}, u32[]{:S(2)}) collective-permute-start(bf16[32,1536]{1,0:T(8,128)(2,1)} %get-tuple-element.82), channel_id=1, source_target_pairs={{0,96},{16,112},{32,128},{48,144},{64,160},{80,176},{96,192},{112,... | collective-permute-start | bytes 294920 | tf_op jit(solution)/shard_map/ppermute | solution.py:59
  68.0 15.1 %copy-start.14 = (bf16[32,1536]{1,0:T(8,128)(2,1)}, bf16[32,1536]{1,0:T(8,128)(2,1)S(1)}, u32[]{:S(2)}) copy-start(bf16[32,1536]{1,0:T(8,128)(2,1)S(1)} %collective-permute-done.21.refs_3_) | copy-start | bytes 294916
  68.0 11.9 %collective-permute-start.26 = (bf16[32,1536]{1,0:T(8,128)(2,1)}, bf16[32,1536]{1,0:T(8,128)(2,1)}, u32[]{:S(2)}, u32[]{:S(2)}) collective-permute-start(bf16[32,1536]{1,0:T(8,128)(2,1)} %get-tuple-element.83), channel_id=1, source_target_pairs={{0,128},{16,144},{32,160},{48,176},{64,192},{80,208},{96,224},{112... | collective-permute-start | bytes 294920 | tf_op jit(solution)/shard_map/ppermute | solution.py:59
  72.3 6.2 %copy-start.15 = (bf16[32,1536]{1,0:T(8,128)(2,1)}, bf16[32,1536]{1,0:T(8,128)(2,1)S(1)}, u32[]{:S(2)}) copy-start(bf16[32,1536]{1,0:T(8,128)(2,1)S(1)} %collective-permute-done.22.refs_4_) | copy-start | bytes 294916
  72.3 6.2 %copy-start.16 = (bf16[32,1536]{1,0:T(8,128)(2,1)}, bf16[32,1536]{1,0:T(8,128)(2,1)S(1)}, u32[]{:S(2)}) copy-start(bf16[32,1536]{1,0:T(8,128)(2,1)S(1)} %collective-permute-done.23.refs_5_) | copy-start | bytes 294916
  73.6 4.9 %copy-start.17 = (bf16[32,1536]{1,0:T(8,128)(2,1)}, bf16[32,1536]{1,0:T(8,128)(2,1)S(1)}, u32[]{:S(2)}) copy-start(bf16[32,1536]{1,0:T(8,128)(2,1)S(1)} %collective-permute-done.24.refs_6_) | copy-start | bytes 294916
  78.5 0.6 copy-start.18
  83.1 1.2 copy-start.4
  88.7 30.3 %copy-start.2 = (bf16[192,512]{1,0:T(8,128)(2,1)S(1)}, bf16[192,512]{1,0:T(8,128)(2,1)}, u32[]{:S(2)}) copy-start(bf16[192,512]{1,0:T(8,128)(2,1)} %shard_map.87.feats_ref) | copy-start | bytes 589828
  119.4 1.7 collective-permute-start.28
  141.9 23.0 %all-to-all-start.3 = ((bf16[16,48,384]{2,1,0:T(8,128)(2,1)}), bf16[16,48,384]{2,1,0:T(8,128)(2,1)}, u32[]{:S(2)}, u32[]{:S(2)}) async-start(bf16[16,48,384]{2,1,0:T(8,128)(2,1)} %shard_map.92), calls=%async_computation.3 | async-start | bytes 1179648 | tf_op jit(solution)/shard_map/all_to_all | solution.py:344
  146.5 1.3 collective-permute-start.27

commit v6 on v4

--- a/solution.py
+++ b/solution.py
@@ -14,6 +14,7 @@
 HBM = pl.BlockSpec(memory_space=pltpu.HBM)
 ANY = pl.BlockSpec(memory_space=pl.ANY)
 DMA = pltpu.SemaphoreType.DMA
+WHOLE = 58
 
 
 def local(kernel, outs, operands, mib, specs=None, out_specs=None, scratch=()):
@@ -66,6 +67,10 @@
     return lax.ppermute(value, "mp", [(m, m ^ 1) for m in range(16)])
 
 
+def swap_x(value):
+    return lax.ppermute(value, "mp", [(m, m ^ 2) for m in range(16)])
+
+
 def normalize_kernel(raw_ref, out_ref):
     out_ref[...] = normalize(raw_ref[...])[0].astype(BF16)
 
@@ -83,17 +88,18 @@
     return values[:, 0:1] + values[:, 1:2]
 
 
-def feature_kernel(flags, mine, came, mine_next, came_next, out_ref):
-    count, rows = mine.shape
-    half = rows // 2
+def feature_kernel(flags, *refs):
+    sources, out_ref = refs[:4], refs[4]
+    rows = sources[0].shape[1]
+    count, half = sources[0].shape[0] // 2, rows // 2
     y, core = flags[0], flags[1]
     source = lax.broadcasted_iota(jnp.int32, (rows, half), 0)
     target = lax.broadcasted_iota(jnp.int32, (rows, half), 1)
     chosen = source == (target // 32) * 64 + core * 32 + target % 32
     pick = jnp.where(chosen, 1.0, 0.0).astype(BF16)
-    for i, (here, there) in enumerate(((mine, came), (mine_next, came_next))):
-        own = jnp.dot(here[...], pick, preferred_element_type=F32).astype(BF16)
-        other = jnp.dot(there[...], pick, preferred_element_type=F32).astype(BF16)
+    for i, ref in enumerate(sources):
+        both = jnp.dot(ref[...], pick, preferred_element_type=F32)
+        own, other = both[:count].astype(BF16), both[count:].astype(BF16)
         place = pl.ds(i * count, count)
         out_ref[place, pl.ds(0, half)] = jnp.where(y == 0, own, other)
         out_ref[place, pl.ds(half, half)] = jnp.where(y == 0, other, own)
@@ -102,14 +108,13 @@
 def tile_kernel(*refs):
     numbers, places, text_ids, image_ids = refs[0], refs[1], refs[2], refs[3]
     blocks, own, partner = refs[4:20], refs[20], refs[21]
-    image_out, keep_ref, send_ref, texts, images, slopes, stage, sems = refs[22:]
+    image_out, keep_ref, send_ref, texts, images, slopes = refs[22:]
     sub, width = blocks[0].shape
     for i, block in enumerate(blocks):
         texts[pl.ds(i * sub, sub), :] = block[...]
     scale, bias = numbers[0], numbers[1]
     rows = own.shape[0]
     pieces = rows // sub
-    copies = []
     for part, source in enumerate((own, partner)):
         place = pl.ds(part * rows, rows)
         images[place, :] = normalize(source[...])[0].astype(BF16)
@@ -126,23 +131,16 @@
         slopes[place, :] = slope.astype(BF16)
         grad = jnp.dot(slopes[place, :], texts[...], preferred_element_type=F32).astype(BF16)
         extra = loss_columns(losses)
+        first = places[part]
         for i in range(pieces):
-            stage[part * pieces + i, :, pl.ds(0, width)] = grad[i * sub : (i + 1) * sub]
-            stage[part * pieces + i, :, pl.ds(width, LANES)] = extra[i * sub : (i + 1) * sub]
-        copy = pltpu.make_async_copy(
-            stage.at[pl.ds(part * pieces, pieces)],
-            image_out.at[pl.ds(places[part], pieces)],
-            sems.at[part],
-        )
-        copy.start()
-        copies.append(copy)
+            image_out[first + i, :, pl.ds(0, width)] = grad[i * sub : (i + 1) * sub]
+            image_out[first + i, :, pl.ds(width, LANES)] = extra[i * sub : (i + 1) * sub]
     text_grad = lax.dot_general(
         slopes[...], images[...], (((0,), (0,)), ((), ())), preferred_element_type=F32
     )
     half = text_grad.shape[0] // 2
     keep_ref[...] = text_grad[:half]
     send_ref[...] = text_grad[half:].astype(BF16)
-    wait_all(copies)
 
 
 def join_kernel(keep_ref, came_ref, *refs):
@@ -154,11 +152,18 @@
     wait_all(start_all([(stage.at[i], out) for i, out in enumerate(outs)], sems))
 
 
-def grad_kernel(*refs):
-    pieces, blocks = refs[0], refs[1:9]
-    raw_img, raw_txt, out_ref, came, stage, sems = refs[9:]
+def text_kernel(*refs):
+    blocks, raw_txt, out_ref, came, sems = refs[:8], *refs[8:]
+    wait_all(start_all([(block, came.at[i]) for i, block in enumerate(blocks)], sems))
+    text_grad = came[0].astype(F32)
+    for i in range(1, came.shape[0]):
+        text_grad += came[i].astype(F32)
+    out_ref[...] = through_norm(text_grad, *normalize(raw_txt[...])).astype(BF16)
+
+
+def grad_kernel(pieces, d_txt, raw_img, out_ref):
     width = raw_img.shape[1]
-    loads = start_all([(block, came.at[i]) for i, block in enumerate(blocks)], sems)
+    half = width // 2
     image_grad = pieces[0, :, pl.ds(0, width)].astype(F32)
     losses = column_loss(pieces[0, :, pl.ds(width, LANES)])
     for i in range(1, pieces.shape[0]):
@@ -166,18 +171,12 @@
         losses += column_loss(pieces[i, :, pl.ds(width, LANES)])
     d_img = through_norm(image_grad, *normalize(raw_img[...])).astype(BF16)
     extra = loss_columns(losses)
-    wait_all(loads)
-    text_grad = came[0].astype(F32)
-    for i in range(1, came.shape[0]):
-        text_grad += came[i].astype(F32)
-    d_txt = through_norm(text_grad, *normalize(raw_txt[...])).astype(BF16)
-    for i, value in enumerate((d_img, d_txt)):
-        stage[i, :, pl.ds(0, width)] = value
-        stage[i, :, pl.ds(width, LANES)] = extra
-    count = out_ref.shape[0]
-    wait_all(
-        start_all([(stage.at[i // (count // 2)], out_ref.at[i]) for i in range(count)], sems)
-    )
+    for h in range(2):
+        place = pl.ds(h * half, half)
+        out_ref[0, h, :, pl.ds(0, half)] = d_img[:, h * half : (h + 1) * half]
+        out_ref[1, h, :, pl.ds(0, half)] = d_txt[:, place]
+        for kind in range(2):
+            out_ref[kind, h, :, pl.ds(half, LANES)] = extra
 
 
 def weight_kernel(feats_ref, grads_ref, keep_ref, send_ref):
@@ -190,29 +189,34 @@
     send_ref[...] = both[count:].astype(BF16)
 
 
-def cut_kernel(keep_ref, came_ref, out_ref, stage, sem):
-    rows, cols = out_ref.shape[1:]
-    for r in range(2):
-        for c in range(4):
-            place = (pl.ds(r * rows, rows), pl.ds(c * cols, cols))
-            stage[4 * r + c] = (keep_ref[place] + came_ref[place].astype(F32)).astype(BF16)
-    wait_all(start_all([(stage, out_ref)], sem))
-
-
-def spread_kernel(parts_ref, out_ref, stage, sems):
-    total = parts_ref[0].astype(F32)
-    for i in range(1, parts_ref.shape[0]):
-        total += parts_ref[i].astype(F32)
-    stage[...] = total.astype(BF16)
-    wait_all(start_all([(stage, out_ref.at[i]) for i in range(out_ref.shape[0])], sems))
-
-
-def paste_kernel(parts_ref, img_ref, txt_ref):
-    rows, cols = parts_ref.shape[1:]
+def cut_kernel(keep_ref, came_ref, out_ref):
+    rows, cols = out_ref.shape[2:]
+    total = keep_ref[...] + came_ref[...].astype(F32)
+    for part in range(2):
+        for s in range(8):
+            row, col = part * 4 * rows + (s // 2) * rows, (s % 2) * cols
+            out_ref[s, part] = total[row : row + rows, col : col + cols].astype(BF16)
+
+
+def sum_kernel(parts_ref, own_ref, other_ref):
+    for part, out in enumerate((own_ref, other_ref)):
+        total = parts_ref[0, part].astype(F32)
+        for i in range(1, parts_ref.shape[0]):
+            total += parts_ref[i, part].astype(F32)
+        out[...] = total.astype(BF16)
+
+
+def paste_kernel(flags, parts_ref, img_ref, txt_ref):
+    rows, cols = parts_ref.shape[2:]
+    first = flags[0] == 0
     for s in range(8):
-        place = (pl.ds((s // 4) * rows, rows), pl.ds((s % 4) * cols, cols))
-        img_ref[place] = parts_ref[2 * s].astype(F32)
-        txt_ref[place] = parts_ref[2 * s + 1].astype(F32)
+        row, col = (s // 2) * rows, (s % 2) * cols
+        for kind, out in enumerate((img_ref, txt_ref)):
+            own, other = parts_ref[2 * s + kind, 0], parts_ref[2 * s + kind, 1]
+            out[pl.ds(row, rows), pl.ds(col, cols)] = jnp.where(first, own, other).astype(F32)
+            out[pl.ds(row, rows), pl.ds(2 * cols + col, cols)] = jnp.where(
+                first, other, own
+            ).astype(F32)
 
 
 def shards(img_emb, txt_emb, img_feat_t, txt_feat_t, logit_scale, logit_bias):
@@ -229,16 +233,18 @@
     texts = local(normalize_kernel, ((sub, width), BF16), [txt_emb], 4)
     blocks = [texts] + [along_z(texts, steps) for steps in ALONG[1:]]
     blocks += [swap_core(block) for block in blocks]
+    mine = jnp.where(y == 0, img_feat_t, txt_feat_t)
+    came = swap_y(jnp.where(y == 0, txt_feat_t, img_feat_t))
     by_core = img_emb.reshape(8, 2, sub, width)
     own = lax.dynamic_slice_in_dim(by_core, core, 1, 1).reshape(half, width)
+    own, came = lax.optimization_barrier((own, came))
     partner = swap_y(own)
-
-    mine = jnp.where(y == 0, img_feat_t, txt_feat_t)
-    came = swap_y(jnp.where(y == 0, txt_feat_t, img_feat_t))
+    pair = jnp.concatenate([mine, came])
+    pair_x = swap_x(pair)
     feat_part = local(
         feature_kernel,
-        ((2 * feats, rows), BF16),
-        [jnp.stack([y, core]), mine, came, swap_core(mine), swap_core(came)],
+        ((4 * feats, rows), BF16),
+        [jnp.stack([y, core]), pair, pair_x, swap_core(pair), swap_core(pair_x)],
         8,
         [SMEM] + [VMEM] * 4,
     )
@@ -269,9 +275,9 @@
         ],
         24,
         [SMEM, SMEM] + [VMEM] * 20,
-        [HBM, VMEM, VMEM],
+        None,
         [pltpu.VMEM((rows, width), BF16)] * 2
-        + [pltpu.VMEM((rows, rows), BF16), pltpu.VMEM((16, sub, full), BF16), DMA((2,))],
+        + [pltpu.VMEM((rows, rows), BF16)],
     )
     plane = [
         [(2 * s + t) * 16 + 2 * k + c for t in range(2) for k in range(8)]
@@ -288,59 +294,59 @@
         join_kernel,
         [((sub, width), BF16)] * 8,
         [keep, swap_core(send)],
-        10,
+        WHOLE,
         None,
         [HBM] * 8,
         [pltpu.VMEM((8, sub, width), BF16), DMA((8,))],
     )
-    image_part, *text_parts = lax.optimization_barrier((image_part, *text_parts))
     image_pieces = over_plane(image_part)
     text_came = [text_parts[0]] + [
         along_z(part, -steps) for part, steps in zip(text_parts[1:], ALONG[1:], strict=True)
     ]
+    d_txt = local(
+        text_kernel,
+        ((sub, width), BF16),
+        [*text_came, txt_emb],
+        WHOLE,
+        [ANY] * 8 + [VMEM],
+        None,
+        [pltpu.VMEM((8, sub, width), BF16), DMA((8,))],
+    )
     raw_img = lax.dynamic_slice_in_dim(img_emb, (2 * chip + core) * sub, sub, 0)
-    spread = local(
+    narrow = width // 2
+    kinds = local(
         grad_kernel,
-        ((16, sub, full), BF16),
-        [image_pieces, *text_came, raw_img, txt_emb],
+        ((2, 2, sub, narrow + LANES), BF16),
+        [image_pieces, d_txt, raw_img],
         12,
-        [VMEM] + [ANY] * 8 + [VMEM] * 2,
-        [HBM],
-        [pltpu.VMEM((8, sub, width), BF16), pltpu.VMEM((2, sub, full), BF16), DMA((16,))],
-    )
-    grads = over_plane(spread)
+    )
+    spread = jnp.broadcast_to(kinds[:, None], (2, 4, 2, sub, narrow + LANES))
+    grads = over_plane(spread.reshape(16, sub, narrow + LANES))
 
     kept, sent = local(
         weight_kernel,
-        [((feats, width), F32), ((feats, width), BF16)],
+        [((2 * feats, narrow), F32), ((2 * feats, narrow), BF16)],
         [feat_part, grads],
         12,
     )
-    shape = (feats // 2, width // 4)
-    cut = local(
-        cut_kernel,
-        ((8, *shape), BF16),
-        [kept, swap_core(sent)],
-        6,
-        None,
-        [HBM],
-        [pltpu.VMEM((8, *shape), BF16), DMA((1,))],
-    )
+    shape = (feats // 4, narrow // 2)
+    cut = local(cut_kernel, ((8, 2, *shape), BF16), [kept, swap_core(sent)], 6)
     same_y = [[2 * s + t for s in range(8)] for t in range(2)]
     parts = lax.all_to_all(cut, "dp", 0, 0, tiled=True, axis_index_groups=same_y)
-    summed = local(
-        spread_kernel,
-        ((16, *shape), BF16),
-        [parts],
-        6,
-        None,
-        [HBM],
-        [pltpu.VMEM(shape, BF16), DMA((16,))],
-    )
-    weights = lax.all_to_all(summed, "dp", 0, 0, tiled=True)
-    img_weight, txt_weight = local(paste_kernel, [((feats, width), F32)] * 2, [weights], 8)
-
-    extra = grads[:, :, width : width + 2].astype(F32)
+    own_sum, other_sum = local(sum_kernel, [(shape, BF16)] * 2, [parts], 6)
+    summed = jnp.stack([own_sum, swap_x(other_sum)])
+    weights = lax.all_to_all(
+        jnp.broadcast_to(summed[None], (16, 2, *shape)), "dp", 0, 0, tiled=True
+    )
+    img_weight, txt_weight = local(
+        paste_kernel,
+        [((feats, width), F32)] * 2,
+        [(chip % 2).reshape(1), weights],
+        8,
+        [SMEM, VMEM],
+    )
+
+    extra = grads[:, :, narrow : narrow + 2].astype(F32)
     both_loss = (extra[:, :, 0] + extra[:, :, 1]).reshape(2, 8, sub)
     own_loss = jnp.where(y == 0, both_loss[0], both_loss[1])
     other_loss = swap_core(own_loss)

time: 188 us -> 166 us (0.88)
  waiting for transfers between devices: 51.7 us -> 39.7 us
  local copies, waits for them, and re-layouts: 21.4 us -> 12.5 us
  blocking collectives: 47.2 us -> 41.4 us
  other arithmetic: 0.75 us -> 3.96 us
  starting transfers between devices: 48.7 us -> 51.9 us
    ppermute x2, waiting for transfers between devices: 17.2 us -> 2.72 us  [swap_y(): return lax.ppermute(value, 'dp', [(d, d ^ 1) for d in range(16)])]
    unnamed x62 -> x42, local copies, waits for them, and re-layouts: 19.7 us -> 10.5 us
    all_to_all x1, blocking collectives: 28.9 us -> 20.5 us  [over_plane(): lax.all_to_all(value, ('dp', 'mp'), 0, 0, tiled=True, axis_index_groups=p...]
    all_to_all x1, blocking collectives: 18.3 us -> 20.9 us  [shards(): lax.all_to_all(cut, 'dp', 0, 0, tiled=True, axis_index_groups=same_y)]
    ppermute x0 -> x2, waiting for transfers between devices: none -> 2.3 us  [swap_x(): return lax.ppermute(value, 'mp', [(m, m ^ 2) for m in range(16)])]
    ppermute x13, waiting for transfers between devices: 5.01 us -> 7.19 us  [swap_core(): return lax.ppermute(value, 'mp', [(m, m ^ 1) for m in range(16)])]
    ppermute x0 -> x2, starting transfers between devices: none -> 2.08 us  [swap_x(): return lax.ppermute(value, 'mp', [(m, m ^ 2) for m in range(16)])]
    pallas_call x9 -> x10, Pallas kernels: 15.5 us -> 13.9 us  [local(): pl.pallas_call(kernel, out_shape=shapes, in_specs=specs or [VMEM] * len(o...]
  transfers between devices with their start and end apart: 31 -> 33, of which waited for: 13 -> 16; matrix products, arithmetic and copies ran while one was open for 1% -> 3% of each run, Pallas kernels for 0% -> 4%
where the time goes in v6:
time: 166 us
  starting transfers between devices  51.9 us (31%)
  blocking collectives  41.4 us (25%)
  waiting for transfers between devices  39.7 us (24%)
  Pallas kernels  13.9 us (8%)
  local copies, waits for them, and re-layouts  12.5 us (8%)
  other arithmetic  3.96 us (2%)
  between operations  2.28 us (1%)
    ppermute x14, starting transfers between devices, along_z(): lax.ppermute(value, 'dp', [(d, (d + 2 * steps) % 16) for d in range(16)])  33.5 us
    all_to_all x1, blocking collectives, shards(): lax.all_to_all(cut, 'dp', 0, 0, tiled=True, axis_index_groups=same_y)  20.9 us
    all_to_all x1, blocking collectives, over_plane(): lax.all_to_all(value, ('dp', 'mp'), 0, 0, tiled=True, axis_index_groups=p...  20.5 us
    all_to_all x1, waiting for transfers between devices, shards(): lax.all_to_all(jnp.broadcast_to(summed[None], (16, 2, *shape)), 'dp', 0,...  15.1 us
    pallas_call x10, Pallas kernels, local(): pl.pallas_call(kernel, out_shape=shapes, in_specs=specs or [VMEM] * len(o...  13.9 us
    ppermute x14, waiting for transfers between devices, along_z(): lax.ppermute(value, 'dp', [(d, (d + 2 * steps) % 16) for d in range(16)])  12.3 us
    unnamed x42, local copies, waits for them, and re-layouts  10.5 us
    all_to_all x1, starting transfers between devices, over_plane(): lax.all_to_all(value, ('dp', 'mp'), 0, 0, tiled=True, axis_index_groups=p...  7.86 us
  transfers between devices with their start and end apart: 33, of which 16 were waited for; matrix products, arithmetic and copies ran while one was open for 3% of the time, Pallas kernels for 4%

profile of v6, /device:TPU:2, one launch (start us, length us, event | category | flops | bytes accessed | tf_op | source)
XLA Modules:
  0.0 165.6 jit_solution(7593024271297826467)
XLA Ops:
  0.7 1.0 copy-done.6
  1.8 2.0 %collective-permute-start.4 = (bf16[32,1536]{1,0:T(8,128)(2,1)S(1)}, bf16[32,1536]{1,0:T(8,128)(2,1)S(1)}, u32[]{:S(2)}, u32[]{:S(2)}) collective-permute-start(bf16[32,1536]{1,0:T(8,128)(2,1)S(1)} %shard_map.86.refs_4_), channel_id=1, source_target_pairs={{0,32},{16,48},{32,64},{48,80},{64,96},{80,112},{96,128},{112,144}... | collective-permute-start | bytes 294920 | tf_op jit(solution)/shard_map/ppermute | solution.py:59
  3.8 4.0 %collective-permute-start.5 = (bf16[32,1536]{1,0:T(8,128)(2,1)S(1)}, bf16[32,1536]{1,0:T(8,128)(2,1)}, u32[]{:S(2)}, u32[]{:S(2)}) collective-permute-start(bf16[32,1536]{1,0:T(8,128)(2,1)S(1)} %shard_map.86.refs_4_), channel_id=1, source_target_pairs={{0,224},{16,240},{32,0},{48,16},{64,32},{80,48},{96,64},{112,80},{... | collective-permute-start | bytes 294920 | tf_op jit(solution)/shard_map/ppermute | solution.py:59
  7.8 4.1 %collective-permute-start.7 = (bf16[32,1536]{1,0:T(8,128)(2,1)S(1)}, bf16[32,1536]{1,0:T(8,128)(2,1)S(1)}, u32[]{:S(2)}, u32[]{:S(2)}) collective-permute-start(bf16[32,1536]{1,0:T(8,128)(2,1)S(1)} %shard_map.86.refs_4_), channel_id=1, source_target_pairs={{0,192},{16,208},{32,224},{48,240},{64,0},{80,16},{96,32},{112,48}... | collective-permute-start | bytes 294920 | tf_op jit(solution)/shard_map/ppermute | solution.py:59
  11.9 1.6 broadcast_select_fusion.1
  13.5 1.6 collective-permute-start
  15.4 2.7 %collective-permute-done = bf16[96,512]{1,0:T(8,128)(2,1)S(1)} collective-permute-done((bf16[96,512]{1,0:T(8,128)(2,1)S(1)}, bf16[96,512]{1,0:T(8,128)(2,1)S(1)}, u32[]{:S(2)}, u32[]{:S(2)}) %collective-permute-start) | collective-permute-done | bytes 98336 | tf_op jit(solution)/shard_map/ppermute | solution.py:63
  18.1 0.6 copy-done.13
  18.8 1.6 collective-permute-start.19
  21.8 1.6 pad_maximum_fusion.refs_0_
  23.5 0.5 collective-permute-start.1
  24.0 0.7 collective-permute-start.8
  24.7 4.4 %collective-permute-start.9 = (bf16[32,1536]{1,0:T(8,128)(2,1)S(1)}, bf16[32,1536]{1,0:T(8,128)(2,1)}, u32[]{:S(2)}, u32[]{:S(2)}) collective-permute-start(bf16[32,1536]{1,0:T(8,128)(2,1)S(1)} %shard_map.86.refs_4_), channel_id=1, source_target_pairs={{0,160},{16,176},{32,192},{48,208},{64,224},{80,240},{96,0},{112,1... | collective-permute-start | bytes 294920 | tf_op jit(solution)/shard_map/ppermute | solution.py:59
  29.1 4.5 %collective-permute-start.10 = (bf16[32,1536]{1,0:T(8,128)(2,1)S(1)}, bf16[32,1536]{1,0:T(8,128)(2,1)}, u32[]{:S(2)}, u32[]{:S(2)}) collective-permute-start(bf16[32,1536]{1,0:T(8,128)(2,1)S(1)} %shard_map.86.refs_4_), channel_id=1, source_target_pairs={{0,128},{16,144},{32,160},{48,176},{64,192},{80,208},{96,224},{112... | collective-permute-start | bytes 294920 | tf_op jit(solution)/shard_map/ppermute | solution.py:59
  33.8 1.1 collective-permute-done.8.refs_9_
  34.9 1.9 %collective-permute-done.9.refs_10_ = bf16[32,1536]{1,0:T(8,128)(2,1)} collective-permute-done((bf16[32,1536]{1,0:T(8,128)(2,1)S(1)}, bf16[32,1536]{1,0:T(8,128)(2,1)}, u32[]{:S(2)}, u32[]{:S(2)}) %collective-permute-start.9) | collective-permute-done | bytes 98336 | tf_op jit(solution)/shard_map/ppermute | solution.py:59
  36.9 1.1 collective-permute-done.10.refs_11_
  37.9 0.5 collective-permute-start.3
  38.6 0.9 collective-permute-done.12.refs_13_
  39.7 0.4 collective-permute-done.13.refs_14_
  40.1 0.2 collective-permute-start.15
  40.2 0.7 collective-permute-done.14.refs_15_
  41.1 0.4 collective-permute-start.17
  41.5 0.2 collective-permute-start.18
  41.7 1.4 shard_map.85.feats_ref
  43.2 0.7 copy-done.3
  44.0 0.9 copy-done.8
  44.8 0.9 copy-done.10
  45.7 4.6 %shard_map.87 = (bf16[16,32,1664]{2,1,0:T(8,128)(2,1)S(1)}, f32[256,1536]{1,0:T(8,128)S(1)}, bf16[256,1536]{1,0:T(8,128)(2,1)S(1)}) custom-call(f32[2]{0:T(128)S(1)} %pad_maximum_fusion.2.refs_0_, s32[2]{0:T(128)S(1)} %pad_add_fusion.2.refs_1_, s32[1,512]{1,0:T(1,128)S(1)} %add.180.refs_2_, s32[512,1]{1,0:T(8,128)S(1)} %copy.11.refs_3_, ...), custom_call_target="tpu_custom_call" | custom-call | tf_op jit(solution)/shard_map/pallas_call | solution.py:23
  50.3 1.2 copy-done.1
  51.6 1.1 copy-done.2
  52.7 0.9 copy-done.11
  53.6 7.9 %all-to-all-start = ((bf16[16,32,1664]{2,1,0:T(8,128)(2,1)}), bf16[16,32,1664]{2,1,0:T(8,128)(2,1)S(1)}, u32[]{:S(2)}, u32[]{:S(2)}) async-start(bf16[16,32,1664]{2,1,0:T(8,128)(2,1)} %copy-done.1), calls=%async_computation | async-start | bytes 3407872 | tf_op jit(solution)/shard_map/all_to_all | solution.py:289
  61.5 2.5 %collective-permute-done.20.came_ref = bf16[256,1536]{1,0:T(8,128)(2,1)S(1)} collective-permute-done((bf16[256,1536]{1,0:T(8,128)(2,1)}, bf16[256,1536]{1,0:T(8,128)(2,1)S(1)}, u32[]{:S(2)}, u32[]{:S(2)}) %collective-permute-start.20) | collective-permute-done | bytes 786464 | tf_op jit(solution)/shard_map/ppermute | solution.py:67
  63.9 0.9 copy-done.12
  64.8 2.7 %shard_map.88 = (bf16[32,1536]{1,0:T(8,128)(2,1)}, bf16[32,1536]{1,0:T(8,128)(2,1)}, bf16[32,1536]{1,0:T(8,128)(2,1)}, bf16[32,1536]{1,0:T(8,128)(2,1)}, bf16[32...) custom-call(f32[256,1536]{1,0:T(8,128)} %copy-done.2, ...), custom_call_target="tpu_custom_call" | custom-call | tf_op jit(solution)/shard_map/pallas_call | solution.py:23
  67.5 2.3 %collective-permute-start.21 = (bf16[32,1536]{1,0:T(8,128)(2,1)}, bf16[32,1536]{1,0:T(8,128)(2,1)S(1)}, u32[]{:S(2)}, u32[]{:S(2)}) collective-permute-start(bf16[32,1536]{1,0:T(8,128)(2,1)} %get-tuple-element.31), channel_id=1, source_target_pairs={{0,224},{16,240},{32,0},{48,16},{64,32},{80,48},{96,64},{112,80},{... | collective-permute-start | bytes 294920 | tf_op jit(solution)/shard_map/ppermute | solution.py:59
  69.9 2.0 %collective-permute-start.22 = (bf16[32,1536]{1,0:T(8,128)(2,1)}, bf16[32,1536]{1,0:T(8,128)(2,1)S(1)}, u32[]{:S(2)}, u32[]{:S(2)}) collective-permute-start(bf16[32,1536]{1,0:T(8,128)(2,1)} %get-tuple-element.32), channel_id=1, source_target_pairs={{0,32},{16,48},{32,64},{48,80},{64,96},{80,112},{96,128},{112,144}... | collective-permute-start | bytes 294920 | tf_op jit(solution)/shard_map/ppermute | solution.py:59
  71.9 1.1 collective-permute-start.23
  73.0 1.8 %collective-permute-start.24 = (bf16[32,1536]{1,0:T(8,128)(2,1)}, bf16[32,1536]{1,0:T(8,128)(2,1)S(1)}, u32[]{:S(2)}, u32[]{:S(2)}) collective-permute-start(bf16[32,1536]{1,0:T(8,128)(2,1)} %get-tuple-element.34), channel_id=1, source_target_pairs={{0,64},{16,80},{32,96},{48,112},{64,128},{80,144},{96,160},{112,17... | collective-permute-start | bytes 294920 | tf_op jit(solution)/shard_map/ppermute | solution.py:59
  74.8 2.6 %collective-permute-start.25 = (bf16[32,1536]{1,0:T(8,128)(2,1)}, bf16[32,1536]{1,0:T(8,128)(2,1)S(1)}, u32[]{:S(2)}, u32[]{:S(2)}) collective-permute-start(bf16[32,1536]{1,0:T(8,128)(2,1)} %get-tuple-element.35), channel_id=1, source_target_pairs={{0,160},{16,176},{32,192},{48,208},{64,224},{80,240},{96,0},{112,1... | collective-permute-start | bytes 294920 | tf_op jit(solution)/shard_map/ppermute | solution.py:59
  77.4 1.2 collective-permute-start.26
  78.6 0.6 copy-done.15
  79.3 2.6 %collective-permute-start.27 = (bf16[32,1536]{1,0:T(8,128)(2,1)}, bf16[32,1536]{1,0:T(8,128)(2,1)S(1)}, u32[]{:S(2)}, u32[]{:S(2)}) collective-permute-start(bf16[32,1536]{1,0:T(8,128)(2,1)} %get-tuple-element.37), channel_id=1, source_target_pairs={{0,128},{16,144},{32,160},{48,176},{64,192},{80,208},{96,224},{112... | collective-permute-start | bytes 294920 | tf_op jit(solution)/shard_map/ppermute | solution.py:59
  81.9 1.3 collective-permute-done.23.refs_3_
  83.2 1.1 collective-permute-done.24.refs_4_
  84.3 3.5 %collective-permute-done.25.refs_5_ = bf16[32,1536]{1,0:T(8,128)(2,1)S(1)} collective-permute-done((bf16[32,1536]{1,0:T(8,128)(2,1)}, bf16[32,1536]{1,0:T(8,128)(2,1)S(1)}, u32[]{:S(2)}, u32[]{:S(2)}) %collective-permute-start.25) | collective-permute-done | bytes 98336 | tf_op jit(solution)/shard_map/ppermute | solution.py:59
  87.8 2.3 %collective-permute-done.26.refs_6_ = bf16[32,1536]{1,0:T(8,128)(2,1)S(1)} collective-permute-done((bf16[32,1536]{1,0:T(8,128)(2,1)}, bf16[32,1536]{1,0:T(8,128)(2,1)S(1)}, u32[]{:S(2)}, u32[]{:S(2)}) %collective-permute-start.26) | collective-permute-done | bytes 98336 | tf_op jit(solution)/shard_map/ppermute | solution.py:59
  90.1 0.6 copy-done.19
  90.8 3.0 %shard_map.89.d_txt = bf16[32,1536]{1,0:T(8,128)(2,1)} custom-call(bf16[32,1536]{1,0:T(8,128)(2,1)} %get-tuple-element.30.refs_0_, bf16[32,1536]{1,0:T(8,128)(2,1)} %copy-done.14, bf16[32,1536]{1,0:T(8,128)(2,1)} %copy-done.15, bf16[32,1536]{1,0:T(8,128)(2,1)} %copy-done.16, bf16[32,1536]{1,0:T(8,128)(2,1)} %copy-done.17, bf16[32,1536]{1,0:T(8,128)(2,1)} %copy-done.18, ...), custom_call_target="tpu_custom_call" | custom-call | tf_op jit(solution)/shard_map/pallas_call | solution.py:23
  93.8 0.9 copy-done.5
  94.7 0.4 shard_map.90
  95.2 20.5 %all_to_all.20.grads_ref = bf16[16,32,896]{2,1,0:T(8,128)(2,1)S(1)} all-to-all(bf16[16,32,896]{2,1,0:T(8,128)(2,1)S(1)} %bitcast.29), channel_id=1, replica_groups={{0,2,4,6,8,10,12,14,16,18,20,22,24,26,28,30},{1,3,5,7,9,11,13,15,17,19,..., dimensions={0} | all-to-all | bytes 1835008 | tf_op jit(solution)/shard_map/all_to_all | solution.py:289
  115.7 0.5 shard_map.91
  116.3 1.6 collective-permute-done.29.came_ref
  117.9 20.9 %all_to_all.21.parts_ref = bf16[8,2,24,384]{3,2,1,0:T(8,128)(2,1)S(1)} all-to-all(bf16[8,2,24,384]{3,2,1,0:T(8,128)(2,1)S(1)} %shard_map.92), channel_id=1, replica_groups={{0,32,64,96,128,160,192,224},{16,48,80,112,144,176,208,240},{1,33,65,97..., dimensions={0} | all-to-all | bytes 589824 | tf_op jit(solution)/shard_map/all_to_all | solution.py:335
  138.8 1.5 collective-permute-start.30
  140.4 2.3 %collective-permute-done.30 = bf16[24,384]{1,0:T(8,128)(2,1)S(1)} collective-permute-done((bf16[24,384]{1,0:T(8,128)(2,1)S(1)}, bf16[24,384]{1,0:T(8,128)(2,1)S(1)}, u32[]{:S(2)}, u32[]{:S(2)}) %collective-permute-start.30) | collective-permute-done | bytes 18464 | tf_op jit(solution)/shard_map/ppermute | solution.py:71
  142.7 0.9 broadcast_in_dim.5
  143.6 3.6 %all-to-all-start.3 = ((bf16[16,2,24,384]{3,2,1,0:T(8,128)(2,1)}), bf16[16,2,24,384]{3,2,1,0:T(8,128)(2,1)S(1)}, u32[]{:S(2)}, u32[]{:S(2)}) async-start(bf16[16,2,24,384]{3,2,1,0:T(8,128)(2,1)} %broadcast_in_dim.5), calls=%async_computation.3 | async-start | bytes 1179648 | tf_op jit(solution)/shard_map/all_to_all | solution.py:338
  147.5 1.1 collective-permute-done.28
  148.7 0.7 select_n.135
  149.4 15.1 %all-to-all-done.3.parts_ref = bf16[16,2,24,384]{3,2,1,0:T(8,128)(2,1)S(1)} async-done(((bf16[16,2,24,384]{3,2,1,0:T(8,128)(2,1)}), bf16[16,2,24,384]{3,2,1,0:T(8,128)(2,1)S(1)}, u32[]{:S(2)}, u32[]{:S(2)}) %all-to-all-start.3) | async-done | bytes 589856 | tf_op jit(solution)/shard_map/all_to_all | solution.py:338
  164.5 1.1 shard_map.94
  (81 shorter events, 2.1 us)
Async XLA Ops:
  0.6 14.6 %copy-start = (bf16[512,1536]{1,0:T(8,128)(2,1)S(1)}, bf16[512,1536]{1,0:T(8,128)(2,1)}, u32[]{:S(2)}) copy-start(bf16[512,1536]{1,0:T(8,128)(2,1)} %param.6) | copy-start | bytes 4718596
  0.6 1.0 copy-start.6
  1.8 21.7 %collective-permute-start.4 = (bf16[32,1536]{1,0:T(8,128)(2,1)S(1)}, bf16[32,1536]{1,0:T(8,128)(2,1)S(1)}, u32[]{:S(2)}, u32[]{:S(2)}) collective-permute-start(bf16[32,1536]{1,0:T(8,128)(2,1)S(1)} %shard_map.86.refs_4_), channel_id=1, source_target_pairs={{0,32},{16,48},{32,64},{48,80},{64,96},{80,112},{96,128},{112,144}... | collective-permute-start | bytes 294920 | tf_op jit(solution)/shard_map/ppermute | solution.py:59
  3.8 20.2 %collective-permute-start.5 = (bf16[32,1536]{1,0:T(8,128)(2,1)S(1)}, bf16[32,1536]{1,0:T(8,128)(2,1)}, u32[]{:S(2)}, u32[]{:S(2)}) collective-permute-start(bf16[32,1536]{1,0:T(8,128)(2,1)S(1)} %shard_map.86.refs_4_), channel_id=1, source_target_pairs={{0,224},{16,240},{32,0},{48,16},{64,32},{80,48},{96,64},{112,80},{... | collective-permute-start | bytes 294920 | tf_op jit(solution)/shard_map/ppermute | solution.py:59
  7.8 16.9 %collective-permute-start.6 = (bf16[32,1536]{1,0:T(8,128)(2,1)S(1)}, bf16[32,1536]{1,0:T(8,128)(2,1)}, u32[]{:S(2)}, u32[]{:S(2)}) collective-permute-start(bf16[32,1536]{1,0:T(8,128)(2,1)S(1)} %shard_map.86.refs_4_), channel_id=1, source_target_pairs={{0,64},{16,80},{32,96},{48,112},{64,128},{80,144},{96,160},{112,17... | collective-permute-start | bytes 294920 | tf_op jit(solution)/shard_map/ppermute | solution.py:59
  7.8 21.3 %collective-permute-start.7 = (bf16[32,1536]{1,0:T(8,128)(2,1)S(1)}, bf16[32,1536]{1,0:T(8,128)(2,1)S(1)}, u32[]{:S(2)}, u32[]{:S(2)}) collective-permute-start(bf16[32,1536]{1,0:T(8,128)(2,1)S(1)} %shard_map.86.refs_4_), channel_id=1, source_target_pairs={{0,192},{16,208},{32,224},{48,240},{64,0},{80,16},{96,32},{112,48}... | collective-permute-start | bytes 294920 | tf_op jit(solution)/shard_map/ppermute | solution.py:59
  13.5 4.6 %collective-permute-start = (bf16[96,512]{1,0:T(8,128)(2,1)S(1)}, bf16[96,512]{1,0:T(8,128)(2,1)S(1)}, u32[]{:S(2)}, u32[]{:S(2)}) collective-permute-start(bf16[96,512]{1,0:T(8,128)(2,1)S(1)} %get-tuple-element.46), channel_id=1, source_target_pairs={{0,16},{16,0},{32,48},{48,32},{64,80},{80,64},{96,112},{112,96},{1... | collective-permute-start | bytes 294920 | tf_op jit(solution)/shard_map/ppermute | solution.py:63
  18.1 0.6 copy-start.13
  18.8 25.2 %collective-permute-start.19 = (bf16[256,1536]{1,0:T(8,128)(2,1)S(1)}, bf16[256,1536]{1,0:T(8,128)(2,1)S(1)}, u32[]{:S(2)}, u32[]{:S(2)}) collective-permute-start(bf16[256,1536]{1,0:T(8,128)(2,1)S(1)} %bitcast.26), channel_id=1, source_target_pairs={{0,16},{16,0},{32,48},{48,32},{64,80},{80,64},{96,112},{112,96},{1... | collective-permute-start | bytes 2359304 | tf_op jit(solution)/shard_map/ppermute | solution.py:63
  23.5 10.2 %copy-start.7 = (bf16[32,1536]{1,0:T(8,128)(2,1)}, bf16[32,1536]{1,0:T(8,128)(2,1)S(1)}, u32[]{:S(2)}) copy-start(bf16[32,1536]{1,0:T(8,128)(2,1)S(1)} %collective-permute-done.4.refs_5_) | copy-start | bytes 294916
  23.5 14.5 %collective-permute-start.1 = (bf16[192,512]{1,0:T(8,128)(2,1)}, bf16[192,512]{1,0:T(8,128)(2,1)}, u32[]{:S(2)}, u32[]{:S(2)}) collective-permute-start(bf16[192,512]{1,0:T(8,128)(2,1)} %pad_maximum_fusion.refs_0_), channel_id=1, source_target_pairs={{0,2},{1,3},{2,0},{3,1},{4,6},{5,7},{6,4},{7,5},{8,10},{9,11},{10,... | collective-permute-start | bytes 589832 | tf_op jit(solution)/shard_map/ppermute | solution.py:71
  24.0 10.9 %collective-permute-start.8 = (bf16[32,1536]{1,0:T(8,128)(2,1)S(1)}, bf16[32,1536]{1,0:T(8,128)(2,1)}, u32[]{:S(2)}, u32[]{:S(2)}) collective-permute-start(bf16[32,1536]{1,0:T(8,128)(2,1)S(1)} %shard_map.86.refs_4_), channel_id=1, source_target_pairs={{0,96},{16,112},{32,128},{48,144},{64,160},{80,176},{96,192},{112,... | collective-permute-start | bytes 294920 | tf_op jit(solution)/shard_map/ppermute | solution.py:59
  24.7 12.2 %collective-permute-start.9 = (bf16[32,1536]{1,0:T(8,128)(2,1)S(1)}, bf16[32,1536]{1,0:T(8,128)(2,1)}, u32[]{:S(2)}, u32[]{:S(2)}) collective-permute-start(bf16[32,1536]{1,0:T(8,128)(2,1)S(1)} %shard_map.86.refs_4_), channel_id=1, source_target_pairs={{0,160},{16,176},{32,192},{48,208},{64,224},{80,240},{96,0},{112,1... | collective-permute-start | bytes 294920 | tf_op jit(solution)/shard_map/ppermute | solution.py:59
  29.1 4.5 %copy-start.9 = (bf16[32,1536]{1,0:T(8,128)(2,1)}, bf16[32,1536]{1,0:T(8,128)(2,1)S(1)}, u32[]{:S(2)}) copy-start(bf16[32,1536]{1,0:T(8,128)(2,1)S(1)} %collective-permute-done.7.refs_8_) | copy-start | bytes 294916
  29.1 8.8 %collective-permute-start.10 = (bf16[32,1536]{1,0:T(8,128)(2,1)S(1)}, bf16[32,1536]{1,0:T(8,128)(2,1)}, u32[]{:S(2)}, u32[]{:S(2)}) collective-permute-start(bf16[32,1536]{1,0:T(8,128)(2,1)S(1)} %shard_map.86.refs_4_), channel_id=1, source_target_pairs={{0,128},{16,144},{32,160},{48,176},{64,192},{80,208},{96,224},{112... | collective-permute-start | bytes 294920 | tf_op jit(solution)/shard_map/ppermute | solution.py:59
  34.9 3.6 %collective-permute-start.11 = (bf16[32,1536]{1,0:T(8,128)(2,1)S(1)}, bf16[32,1536]{1,0:T(8,128)(2,1)S(1)}, u32[]{:S(2)}, u32[]{:S(2)}) collective-permute-start(bf16[32,1536]{1,0:T(8,128)(2,1)S(1)} %shard_map.86.refs_4_), channel_id=1, source_target_pairs={{0,1},{1,0},{2,3},{3,2},{4,5},{5,4},{6,7},{7,6},{8,9},{9,8},{10,11... | collective-permute-start | bytes 294920 | tf_op jit(solution)/shard_map/ppermute | solution.py:67
  36.9 4.3 %collective-permute-start.2 = (bf16[192,512]{1,0:T(8,128)(2,1)}, bf16[192,512]{1,0:T(8,128)(2,1)S(1)}, u32[]{:S(2)}, u32[]{:S(2)}) collective-permute-start(bf16[192,512]{1,0:T(8,128)(2,1)} %pad_maximum_fusion.refs_0_), channel_id=1, source_target_pairs={{0,1},{1,0},{2,3},{3,2},{4,5},{5,4},{6,7},{7,6},{8,9},{9,8},{10,11... | collective-permute-start | bytes 589832 | tf_op jit(solution)/shard_map/ppermute | solution.py:67
  37.9 1.5 collective-permute-start.12
  37.9 3.5 %collective-permute-start.3 = (bf16[192,512]{1,0:T(8,128)(2,1)}, bf16[192,512]{1,0:T(8,128)(2,1)S(1)}, u32[]{:S(2)}, u32[]{:S(2)}) collective-permute-start(bf16[192,512]{1,0:T(8,128)(2,1)} %collective-permute-done.1.refs_1_), channel_id=1, source_target_pairs={{0,1},{1,0},{2,3},{3,2},{4,5},{5,4},{6,7},{7,6},{8,9},{9,8},{10,11... | collective-permute-start | bytes 589832 | tf_op jit(solution)/shard_map/ppermute | solution.py:67
  38.5 1.5 collective-permute-start.13
  39.4 1.5 collective-permute-start.14
  40.1 3.8 %collective-permute-start.15 = (bf16[32,1536]{1,0:T(8,128)(2,1)}, bf16[32,1536]{1,0:T(8,128)(2,1)S(1)}, u32[]{:S(2)}, u32[]{:S(2)}) collective-permute-start(bf16[32,1536]{1,0:T(8,128)(2,1)} %copy-done.9), channel_id=1, source_target_pairs={{0,1},{1,0},{2,3},{3,2},{4,5},{5,4},{6,7},{7,6},{8,9},{9,8},{10,11... | collective-permute-start | bytes 294920 | tf_op jit(solution)/shard_map/ppermute | solution.py:67
  41.0 3.0 %collective-permute-start.16 = (bf16[32,1536]{1,0:T(8,128)(2,1)}, bf16[32,1536]{1,0:T(8,128)(2,1)S(1)}, u32[]{:S(2)}, u32[]{:S(2)}) collective-permute-start(bf16[32,1536]{1,0:T(8,128)(2,1)} %collective-permute-done.8.refs_9_), channel_id=1, source_target_pairs={{0,1},{1,0},{2,3},{3,2},{4,5},{5,4},{6,7},{7,6},{8,9},{9,8},{10,11... | collective-permute-start | bytes 294920 | tf_op jit(solution)/shard_map/ppermute | solution.py:67
  41.1 2.8 %collective-permute-start.17 = (bf16[32,1536]{1,0:T(8,128)(2,1)}, bf16[32,1536]{1,0:T(8,128)(2,1)S(1)}, u32[]{:S(2)}, u32[]{:S(2)}) collective-permute-start(bf16[32,1536]{1,0:T(8,128)(2,1)} %collective-permute-done.9.refs_10_), channel_id=1, source_target_pairs={{0,1},{1,0},{2,3},{3,2},{4,5},{5,4},{6,7},{7,6},{8,9},{9,8},{10,11... | collective-permute-start | bytes 294920 | tf_op jit(solution)/shard_map/ppermute | solution.py:67
  41.5 2.4 %collective-permute-start.18 = (bf16[32,1536]{1,0:T(8,128)(2,1)}, bf16[32,1536]{1,0:T(8,128)(2,1)S(1)}, u32[]{:S(2)}, u32[]{:S(2)}) collective-permute-start(bf16[32,1536]{1,0:T(8,128)(2,1)} %collective-permute-done.10.refs_11_), channel_id=1, source_target_pairs={{0,1},{1,0},{2,3},{3,2},{4,5},{5,4},{6,7},{7,6},{8,9},{9,8},{10,11... | collective-permute-start | bytes 294920 | tf_op jit(solution)/shard_map/ppermute | solution.py:67
  43.2 0.7 copy-start.3
  43.9 0.9 copy-start.8
  44.8 0.9 copy-start.10
  50.3 1.2 copy-start.1
  51.6 1.1 copy-start.2
  52.7 0.9 copy-start.11
  53.6 40.2 %all-to-all-start = ((bf16[16,32,1664]{2,1,0:T(8,128)(2,1)}), bf16[16,32,1664]{2,1,0:T(8,128)(2,1)S(1)}, u32[]{:S(2)}, u32[]{:S(2)}) async-start(bf16[16,32,1664]{2,1,0:T(8,128)(2,1)} %copy-done.1), calls=%async_computation | async-start | bytes 3407872 | tf_op jit(solution)/shard_map/all_to_all | solution.py:289
  61.4 2.5 %collective-permute-start.20 = (bf16[256,1536]{1,0:T(8,128)(2,1)}, bf16[256,1536]{1,0:T(8,128)(2,1)S(1)}, u32[]{:S(2)}, u32[]{:S(2)}) collective-permute-start(bf16[256,1536]{1,0:T(8,128)(2,1)} %copy-done.11), channel_id=1, source_target_pairs={{0,1},{1,0},{2,3},{3,2},{4,5},{5,4},{6,7},{7,6},{8,9},{9,8},{10,11... | collective-permute-start | bytes 2359304 | tf_op jit(solution)/shard_map/ppermute | solution.py:67
  63.9 0.9 copy-start.12
  67.5 9.9 %collective-permute-start.21 = (bf16[32,1536]{1,0:T(8,128)(2,1)}, bf16[32,1536]{1,0:T(8,128)(2,1)S(1)}, u32[]{:S(2)}, u32[]{:S(2)}) collective-permute-start(bf16[32,1536]{1,0:T(8,128)(2,1)} %get-tuple-element.31), channel_id=1, source_target_pairs={{0,224},{16,240},{32,0},{48,16},{64,32},{80,48},{96,64},{112,80},{... | collective-permute-start | bytes 294920 | tf_op jit(solution)/shard_map/ppermute | solution.py:59
  69.9 8.7 %collective-permute-start.22 = (bf16[32,1536]{1,0:T(8,128)(2,1)}, bf16[32,1536]{1,0:T(8,128)(2,1)S(1)}, u32[]{:S(2)}, u32[]{:S(2)}) collective-permute-start(bf16[32,1536]{1,0:T(8,128)(2,1)} %get-tuple-element.32), channel_id=1, source_target_pairs={{0,32},{16,48},{32,64},{48,80},{64,96},{80,112},{96,128},{112,144}... | collective-permute-start | bytes 294920 | tf_op jit(solution)/shard_map/ppermute | solution.py:59
  71.9 11.3 %collective-permute-start.23 = (bf16[32,1536]{1,0:T(8,128)(2,1)}, bf16[32,1536]{1,0:T(8,128)(2,1)S(1)}, u32[]{:S(2)}, u32[]{:S(2)}) collective-permute-start(bf16[32,1536]{1,0:T(8,128)(2,1)} %get-tuple-element.33), channel_id=1, source_target_pairs={{0,192},{16,208},{32,224},{48,240},{64,0},{80,16},{96,32},{112,48}... | collective-permute-start | bytes 294920 | tf_op jit(solution)/shard_map/ppermute | solution.py:59
  73.0 11.3 %collective-permute-start.24 = (bf16[32,1536]{1,0:T(8,128)(2,1)}, bf16[32,1536]{1,0:T(8,128)(2,1)S(1)}, u32[]{:S(2)}, u32[]{:S(2)}) collective-permute-start(bf16[32,1536]{1,0:T(8,128)(2,1)} %get-tuple-element.34), channel_id=1, source_target_pairs={{0,64},{16,80},{32,96},{48,112},{64,128},{80,144},{96,160},{112,17... | collective-permute-start | bytes 294920 | tf_op jit(solution)/shard_map/ppermute | solution.py:59
  74.8 13.0 %collective-permute-start.25 = (bf16[32,1536]{1,0:T(8,128)(2,1)}, bf16[32,1536]{1,0:T(8,128)(2,1)S(1)}, u32[]{:S(2)}, u32[]{:S(2)}) collective-permute-start(bf16[32,1536]{1,0:T(8,128)(2,1)} %get-tuple-element.35), channel_id=1, source_target_pairs={{0,160},{16,176},{32,192},{48,208},{64,224},{80,240},{96,0},{112,1... | collective-permute-start | bytes 294920 | tf_op jit(solution)/shard_map/ppermute | solution.py:59
  77.4 12.7 %copy-start.14 = (bf16[32,1536]{1,0:T(8,128)(2,1)}, bf16[32,1536]{1,0:T(8,128)(2,1)S(1)}, u32[]{:S(2)}) copy-start(bf16[32,1536]{1,0:T(8,128)(2,1)S(1)} %collective-permute-done.21.refs_1_) | copy-start | bytes 294916
  77.4 12.7 %collective-permute-start.26 = (bf16[32,1536]{1,0:T(8,128)(2,1)}, bf16[32,1536]{1,0:T(8,128)(2,1)S(1)}, u32[]{:S(2)}, u32[]{:S(2)}) collective-permute-start(bf16[32,1536]{1,0:T(8,128)(2,1)} %get-tuple-element.36), channel_id=1, source_target_pairs={{0,96},{16,112},{32,128},{48,144},{64,160},{80,176},{96,192},{112,... | collective-permute-start | bytes 294920 | tf_op jit(solution)/shard_map/ppermute | solution.py:59
  78.6 0.6 copy-start.15
  79.3 10.8 %collective-permute-start.27 = (bf16[32,1536]{1,0:T(8,128)(2,1)}, bf16[32,1536]{1,0:T(8,128)(2,1)S(1)}, u32[]{:S(2)}, u32[]{:S(2)}) collective-permute-start(bf16[32,1536]{1,0:T(8,128)(2,1)} %get-tuple-element.37), channel_id=1, source_target_pairs={{0,128},{16,144},{32,160},{48,176},{64,192},{80,208},{96,224},{112... | collective-permute-start | bytes 294920 | tf_op jit(solution)/shard_map/ppermute | solution.py:59
  83.2 6.9 %copy-start.16 = (bf16[32,1536]{1,0:T(8,128)(2,1)}, bf16[32,1536]{1,0:T(8,128)(2,1)S(1)}, u32[]{:S(2)}) copy-start(bf16[32,1536]{1,0:T(8,128)(2,1)S(1)} %collective-permute-done.23.refs_3_) | copy-start | bytes 294916
  84.3 5.8 %copy-start.17 = (bf16[32,1536]{1,0:T(8,128)(2,1)}, bf16[32,1536]{1,0:T(8,128)(2,1)S(1)}, u32[]{:S(2)}) copy-start(bf16[32,1536]{1,0:T(8,128)(2,1)S(1)} %collective-permute-done.24.refs_4_) | copy-start | bytes 294916
  87.8 2.4 %copy-start.18 = (bf16[32,1536]{1,0:T(8,128)(2,1)}, bf16[32,1536]{1,0:T(8,128)(2,1)S(1)}, u32[]{:S(2)}) copy-start(bf16[32,1536]{1,0:T(8,128)(2,1)S(1)} %collective-permute-done.25.refs_5_) | copy-start | bytes 294916
  90.1 0.6 copy-start.19
  90.1 0.7 copy-start.20
  93.8 0.9 copy-start.5
  95.1 20.6 %copy-start.4 = (bf16[384,512]{1,0:T(8,128)(2,1)S(1)}, bf16[384,512]{1,0:T(8,128)(2,1)}, u32[]{:S(2)}) copy-start(bf16[384,512]{1,0:T(8,128)(2,1)} %copy-done.3) | copy-start | bytes 1179652
  116.2 1.7 %collective-permute-start.29 = (bf16[192,768]{1,0:T(8,128)(2,1)S(1)}, bf16[192,768]{1,0:T(8,128)(2,1)S(1)}, u32[]{:S(2)}, u32[]{:S(2)}) collective-permute-start(bf16[192,768]{1,0:T(8,128)(2,1)S(1)} %get-tuple-element.40), channel_id=1, source_target_pairs={{0,1},{1,0},{2,3},{3,2},{4,5},{5,4},{6,7},{7,6},{8,9},{9,8},{10,11... | collective-permute-start | bytes 884744 | tf_op jit(solution)/shard_map/ppermute | solution.py:67
  138.8 3.8 %collective-permute-start.30 = (bf16[24,384]{1,0:T(8,128)(2,1)S(1)}, bf16[24,384]{1,0:T(8,128)(2,1)S(1)}, u32[]{:S(2)}, u32[]{:S(2)}) collective-permute-start(bf16[24,384]{1,0:T(8,128)(2,1)S(1)} %get-tuple-element.42), channel_id=1, source_target_pairs={{0,2},{1,3},{2,0},{3,1},{4,6},{5,7},{6,4},{7,5},{8,10},{9,11},{10,... | collective-permute-start | bytes 55304 | tf_op jit(solution)/shard_map/ppermute | solution.py:71
  143.6 20.9 %all-to-all-start.3 = ((bf16[16,2,24,384]{3,2,1,0:T(8,128)(2,1)}), bf16[16,2,24,384]{3,2,1,0:T(8,128)(2,1)S(1)}, u32[]{:S(2)}, u32[]{:S(2)}) async-start(bf16[16,2,24,384]{3,2,1,0:T(8,128)(2,1)} %broadcast_in_dim.5), calls=%async_computation.3 | async-start | bytes 1179648 | tf_op jit(solution)/shard_map/all_to_all | solution.py:338
  147.4 1.3 collective-permute-start.28

commit v7 on v6

--- a/solution.py
+++ b/solution.py
@@ -69,10 +69,6 @@
 
 def swap_x(value):
     return lax.ppermute(value, "mp", [(m, m ^ 2) for m in range(16)])
-
-
-def normalize_kernel(raw_ref, out_ref):
-    out_ref[...] = normalize(raw_ref[...])[0].astype(BF16)
 
 
 def loss_columns(losses):
@@ -107,14 +103,14 @@
 
 def tile_kernel(*refs):
     numbers, places, text_ids, image_ids = refs[0], refs[1], refs[2], refs[3]
-    blocks, own, partner = refs[4:20], refs[20], refs[21]
-    image_out, keep_ref, send_ref, texts, images, slopes = refs[22:]
-    sub, width = blocks[0].shape
-    for i, block in enumerate(blocks):
-        texts[pl.ds(i * sub, sub), :] = block[...]
+    blocks, own, partner = refs[4:6], refs[6], refs[7]
+    image_out, keep_ref, send_ref, texts, images, slopes = refs[8:]
+    sub, width = image_out.shape[1], own.shape[1]
     scale, bias = numbers[0], numbers[1]
     rows = own.shape[0]
     pieces = rows // sub
+    for i, block in enumerate(blocks):
+        texts[pl.ds(i * rows, rows), :] = normalize(block[...])[0].astype(BF16)
     for part, source in enumerate((own, partner)):
         place = pl.ds(part * rows, rows)
         images[place, :] = normalize(source[...])[0].astype(BF16)
@@ -143,11 +139,12 @@
     send_ref[...] = text_grad[half:].astype(BF16)
 
 
-def join_kernel(keep_ref, came_ref, *refs):
+def join_kernel(flags, keep_ref, came_ref, *refs):
     outs, stage, sems = refs[:8], refs[8], refs[9]
     sub = stage.shape[1]
-    for i in range(8):
-        place = pl.ds(i * sub, sub)
+    for i, steps in enumerate(ALONG):
+        owner = lax.rem(flags[0] + (8 - steps), 8)
+        place = pl.ds(pl.multiple_of(owner * sub, sub), sub)
         stage[i] = (keep_ref[place, :] + came_ref[place, :].astype(F32)).astype(BF16)
     wait_all(start_all([(stage.at[i], out) for i, out in enumerate(outs)], sems))
 
@@ -230,14 +227,16 @@
     core, chip = mp_index % 2, mp_index // 2
     z, y = dp_index // 2, dp_index % 2
 
-    texts = local(normalize_kernel, ((sub, width), BF16), [txt_emb], 4)
-    blocks = [texts] + [along_z(texts, steps) for steps in ALONG[1:]]
-    blocks += [swap_core(block) for block in blocks]
+    same_y = [[2 * s + t for s in range(8)] for t in range(2)]
+
+    def over_z(value):
+        return lax.all_to_all(value, "dp", 0, 0, tiled=True, axis_index_groups=same_y)
+
+    texts = over_z(jnp.broadcast_to(txt_emb[None], (8, sub, width))).reshape(half, width)
     mine = jnp.where(y == 0, img_feat_t, txt_feat_t)
     came = swap_y(jnp.where(y == 0, txt_feat_t, img_feat_t))
     by_core = img_emb.reshape(8, 2, sub, width)
     own = lax.dynamic_slice_in_dim(by_core, core, 1, 1).reshape(half, width)
-    own, came = lax.optimization_barrier((own, came))
     partner = swap_y(own)
     pair = jnp.concatenate([mine, came])
     pair_x = swap_x(pair)
@@ -249,7 +248,7 @@
         [SMEM] + [VMEM] * 4,
     )
 
-    owners = jnp.stack([2 * ((z - steps) % 8) + y for steps in ALONG])
+    owners = 2 * jnp.arange(8, dtype=jnp.int32) + y
     cores = jnp.stack([mp_index, mp_index ^ 1])
     text_ids = owners[None, :, None] * rows + cores[:, None, None] * sub
     text_ids = text_ids + jnp.arange(sub, dtype=jnp.int32)[None, None]
@@ -269,12 +268,13 @@
             places.astype(jnp.int32),
             text_ids.astype(jnp.int32).reshape(1, rows),
             image_ids.astype(jnp.int32).reshape(rows, 1),
-            *blocks,
+            texts,
+            swap_core(texts),
             own,
             partner,
         ],
         24,
-        [SMEM, SMEM] + [VMEM] * 20,
+        [SMEM, SMEM] + [VMEM] * 6,
         None,
         [pltpu.VMEM((rows, width), BF16)] * 2
         + [pltpu.VMEM((rows, rows), BF16)],
@@ -290,12 +290,14 @@
             value, ("dp", "mp"), 0, 0, tiled=True, axis_index_groups=plane
         )
 
+    came_grad = swap_core(send)
+    image_part, came_grad = lax.optimization_barrier((image_part, came_grad))
     text_parts = local(
         join_kernel,
         [((sub, width), BF16)] * 8,
-        [keep, swap_core(send)],
+        [z.reshape(1), keep, came_grad],
         WHOLE,
-        None,
+        [SMEM, VMEM, VMEM],
         [HBM] * 8,
         [pltpu.VMEM((8, sub, width), BF16), DMA((8,))],
     )
@@ -331,8 +333,7 @@
     )
     shape = (feats // 4, narrow // 2)
     cut = local(cut_kernel, ((8, 2, *shape), BF16), [kept, swap_core(sent)], 6)
-    same_y = [[2 * s + t for s in range(8)] for t in range(2)]
-    parts = lax.all_to_all(cut, "dp", 0, 0, tiled=True, axis_index_groups=same_y)
+    parts = over_z(cut)
     own_sum, other_sum = local(sum_kernel, [(shape, BF16)] * 2, [parts], 6)
     summed = jnp.stack([own_sum, swap_x(other_sum)])
     weights = lax.all_to_all(

time: 166 us -> 162 us (0.976)
  waiting for transfers between devices: 39.7 us -> 57.3 us
  starting transfers between devices: 51.9 us -> 39.1 us
  blocking collectives: 41.4 us -> 37.1 us
  other arithmetic: 3.96 us -> 1.44 us
  local copies, waits for them, and re-layouts: 12.5 us -> 10.1 us
    all_to_all x0 -> x1, waiting for transfers between devices: none -> 20.6 us  [over_z(): lax.all_to_all(value, 'dp', 0, 0, tiled=True, axis_index_groups=same_y)]
    ppermute x14 -> x7, starting transfers between devices: 33.5 us -> 14.5 us  [along_z(): lax.ppermute(value, 'dp', [(d, (d + 2 * steps) % 16) for d in range(16)])]
    all_to_all x0 -> x1, starting transfers between devices: none -> 8.6 us  [over_z(): lax.all_to_all(value, 'dp', 0, 0, tiled=True, axis_index_groups=same_y)]
    ppermute x2, waiting for transfers between devices: 2.3 us -> 8.75 us  [swap_x(): return lax.ppermute(value, 'mp', [(m, m ^ 2) for m in range(16)])]
    ppermute x14 -> x7, waiting for transfers between devices: 12.3 us -> 6.38 us  [along_z(): lax.ppermute(value, 'dp', [(d, (d + 2 * steps) % 16) for d in range(16)])]
    all_to_all x1, blocking collectives: 20.9 us -> 16.2 us  [over_z(): lax.all_to_all(value, 'dp', 0, 0, tiled=True, axis_index_groups=same_y)]
    unnamed x42 -> x32, local copies, waits for them, and re-layouts: 10.5 us -> 6.17 us
    ppermute x2, waiting for transfers between devices: 2.72 us -> 0.01 us  [swap_y(): return lax.ppermute(value, 'dp', [(d, d ^ 1) for d in range(16)])]
  transfers between devices with their start and end apart: 33 -> 20, of which waited for: 16 -> 12; matrix products, arithmetic and copies ran while one was open for 3% -> 1% of each run, Pallas kernels for 4% -> 4%
where the time goes in v7:
time: 162 us
  waiting for transfers between devices  57.3 us (35%)
  starting transfers between devices  39.1 us (24%)
  blocking collectives  37.1 us (23%)
  Pallas kernels  14.5 us (9%)
  local copies, waits for them, and re-layouts  10.1 us (6%)
  between operations  2.25 us (1%)
    all_to_all x1, blocking collectives, over_plane(): lax.all_to_all(value, ('dp', 'mp'), 0, 0, tiled=True, axis_index_groups=p...  20.8 us
    all_to_all x1, waiting for transfers between devices, over_z(): lax.all_to_all(value, 'dp', 0, 0, tiled=True, axis_index_groups=same_y)  20.6 us
    all_to_all x1, blocking collectives, over_z(): lax.all_to_all(value, 'dp', 0, 0, tiled=True, axis_index_groups=same_y)  16.2 us
    all_to_all x1, waiting for transfers between devices, shards(): lax.all_to_all(jnp.broadcast_to(summed[None], (16, 2, *shape)), 'dp', 0,...  15.1 us
    ppermute x7, starting transfers between devices, along_z(): lax.ppermute(value, 'dp', [(d, (d + 2 * steps) % 16) for d in range(16)])  14.5 us
    pallas_call x9, Pallas kernels, local(): pl.pallas_call(kernel, out_shape=shapes, in_specs=specs or [VMEM] * len(o...  14.5 us
    ppermute x2, waiting for transfers between devices, swap_x(): return lax.ppermute(value, 'mp', [(m, m ^ 2) for m in range(16)])  8.75 us
    all_to_all x1, starting transfers between devices, over_z(): lax.all_to_all(value, 'dp', 0, 0, tiled=True, axis_index_groups=same_y)  8.6 us
  transfers between devices with their start and end apart: 20, of which 12 were waited for; matrix products, arithmetic and copies ran while one was open for 1% of the time, Pallas kernels for 4%

profile of v7, /device:TPU:2, one launch (start us, length us, event | category | flops | bytes accessed | tf_op | source)
XLA Modules:
  0.0 161.7 jit_solution(10704598652921457805)
XLA Ops:
  0.6 0.0 copy-start
  0.6 2.0 %broadcast_in_dim.6 = bf16[8,32,1536]{2,1,0:T(8,128)(2,1)} broadcast(bf16[32,1536]{1,0:T(8,128)(2,1)} %refs_8_.1), dimensions={1,2} | broadcast | bytes 884736 | tf_op jit(solution)/shard_map/broadcast_in_dim | solution.py:235
  2.6 8.6 %all-to-all-start = ((bf16[8,32,1536]{2,1,0:T(8,128)(2,1)}), bf16[8,32,1536]{2,1,0:T(8,128)(2,1)S(1)}, u32[]{:S(2)}, u32[]{:S(2)}) async-start(bf16[8,32,1536]{2,1,0:T(8,128)(2,1)} %broadcast_in_dim.6), calls=%async_computation | async-start | bytes 1572864 | tf_op jit(solution)/shard_map/all_to_all | solution.py:233
  11.2 0.1 constant_dynamic-slice_fusion.1
  11.3 1.7 %collective-permute-start.5 = (bf16[256,1536]{1,0:T(8,128)(2,1)S(1)}, bf16[256,1536]{1,0:T(8,128)(2,1)}, u32[]{:S(2)}, u32[]{:S(2)}) collective-permute-start(bf16[256,1536]{1,0:T(8,128)(2,1)S(1)} %bitcast.22), channel_id=1, source_target_pairs={{0,16},{16,0},{32,48},{48,32},{64,80},{80,64},{96,112},{112,96},{1... | collective-permute-start | bytes 2359304 | tf_op jit(solution)/shard_map/ppermute | solution.py:63
  13.0 0.5 collective-permute-start
  13.5 0.1 add_multiply_fusion
  13.6 0.1 broadcast_add_fusion.1
  13.7 20.6 %all-to-all-done = bf16[8,32,1536]{2,1,0:T(8,128)(2,1)S(1)} async-done(((bf16[8,32,1536]{2,1,0:T(8,128)(2,1)}), bf16[8,32,1536]{2,1,0:T(8,128)(2,1)S(1)}, u32[]{:S(2)}, u32[]{:S(2)}) %all-to-all-start) | async-done | bytes 786464 | tf_op jit(solution)/shard_map/all_to_all | solution.py:233
  34.3 0.0 collective-permute-start.4
  34.3 0.1 iota_add_fusion
  35.7 0.7 pad_maximum_fusion.refs_0_
  36.4 0.5 collective-permute-start.1
  37.0 0.1 copy.11.refs_3_
  37.1 0.1 add.120.refs_2_
  37.2 0.1 pad_add_fusion.1.flags
  37.3 0.2 collective-permute-start.2
  37.5 6.5 %collective-permute-done.1.refs_1_ = bf16[192,512]{1,0:T(8,128)(2,1)} collective-permute-done((bf16[192,512]{1,0:T(8,128)(2,1)}, bf16[192,512]{1,0:T(8,128)(2,1)}, u32[]{:S(2)}, u32[]{:S(2)}) %collective-permute-start.1) | collective-permute-done | bytes 196640 | tf_op jit(solution)/shard_map/ppermute | solution.py:71
  44.0 0.1 pad_maximum_fusion.2.refs_0_
  44.1 0.1 pad_add_fusion.2.refs_1_
  44.2 1.5 collective-permute-done.3.refs_3_
  45.7 1.4 shard_map.85.feats_ref
  47.2 0.7 copy-done.3
  47.9 5.3 %shard_map.86 = (bf16[16,32,1664]{2,1,0:T(8,128)(2,1)S(1)}, f32[256,1536]{1,0:T(8,128)S(1)}, bf16[256,1536]{1,0:T(8,128)(2,1)S(1)}) custom-call(f32[2]{0:T(128)S(1)} %pad_maximum_fusion.2.refs_0_, s32[2]{0:T(128)S(1)} %pad_add_fusion.2.refs_1_, s32[1,512]{1,0:T(1,128)S(1)} %add.120.refs_2_, s32[512,1]{1,0:T(8,128)S(1)} %copy.11.refs_3_, ...), custom_call_target="tpu_custom_call" | custom-call | tf_op jit(solution)/shard_map/pallas_call | solution.py:23
  53.2 1.2 copy-done.1
  54.4 1.1 copy-done.2
  55.6 0.1 collective-permute-start.6
  55.7 2.2 %collective-permute-done.6.came_ref = bf16[256,1536]{1,0:T(8,128)(2,1)S(1)} collective-permute-done((bf16[256,1536]{1,0:T(8,128)(2,1)S(1)}, bf16[256,1536]{1,0:T(8,128)(2,1)S(1)}, u32[]{:S(2)}, u32[]{:S(2)}) %collective-permute-start.6) | collective-permute-done | bytes 786464 | tf_op jit(solution)/shard_map/ppermute | solution.py:67
  57.9 0.9 copy-done.6
  58.7 7.5 %all-to-all-start.1 = ((bf16[16,32,1664]{2,1,0:T(8,128)(2,1)}), bf16[16,32,1664]{2,1,0:T(8,128)(2,1)S(1)}, u32[]{:S(2)}, u32[]{:S(2)}) async-start(bf16[16,32,1664]{2,1,0:T(8,128)(2,1)} %copy-done.1), calls=%async_computation.1 | async-start | bytes 3407872 | tf_op jit(solution)/shard_map/all_to_all | solution.py:289
  66.2 2.7 %shard_map.87 = (bf16[32,1536]{1,0:T(8,128)(2,1)}, bf16[32,1536]{1,0:T(8,128)(2,1)}, bf16[32,1536]{1,0:T(8,128)(2,1)}, bf16[32,1536]{1,0:T(8,128)(2,1)}, bf16[32...) custom-call(s32[1]{0:T(128)} %bitcast.10.flags, ...), custom_call_target="tpu_custom_call" | custom-call | tf_op jit(solution)/shard_map/pallas_call | solution.py:23
  68.9 0.5 collective-permute-start.10
  69.4 0.7 collective-permute-start.11
  70.1 3.1 %collective-permute-start.12 = (bf16[32,1536]{1,0:T(8,128)(2,1)}, bf16[32,1536]{1,0:T(8,128)(2,1)S(1)}, u32[]{:S(2)}, u32[]{:S(2)}) collective-permute-start(bf16[32,1536]{1,0:T(8,128)(2,1)} %get-tuple-element.36), channel_id=1, source_target_pairs={{0,96},{16,112},{32,128},{48,144},{64,160},{80,176},{96,192},{112,... | collective-permute-start | bytes 294920 | tf_op jit(solution)/shard_map/ppermute | solution.py:59
  73.2 2.3 %collective-permute-start.13 = (bf16[32,1536]{1,0:T(8,128)(2,1)}, bf16[32,1536]{1,0:T(8,128)(2,1)S(1)}, u32[]{:S(2)}, u32[]{:S(2)}) collective-permute-start(bf16[32,1536]{1,0:T(8,128)(2,1)} %get-tuple-element.37), channel_id=1, source_target_pairs={{0,128},{16,144},{32,160},{48,176},{64,192},{80,208},{96,224},{112... | collective-permute-start | bytes 294920 | tf_op jit(solution)/shard_map/ppermute | solution.py:59
  75.5 3.1 %collective-permute-start.7 = (bf16[32,1536]{1,0:T(8,128)(2,1)}, bf16[32,1536]{1,0:T(8,128)(2,1)S(1)}, u32[]{:S(2)}, u32[]{:S(2)}) collective-permute-start(bf16[32,1536]{1,0:T(8,128)(2,1)} %get-tuple-element.31), channel_id=1, source_target_pairs={{0,224},{16,240},{32,0},{48,16},{64,32},{80,48},{96,64},{112,80},{... | collective-permute-start | bytes 294920 | tf_op jit(solution)/shard_map/ppermute | solution.py:59
  78.6 1.8 %collective-permute-done.10.refs_4_ = bf16[32,1536]{1,0:T(8,128)(2,1)S(1)} collective-permute-done((bf16[32,1536]{1,0:T(8,128)(2,1)}, bf16[32,1536]{1,0:T(8,128)(2,1)S(1)}, u32[]{:S(2)}, u32[]{:S(2)}) %collective-permute-start.10) | collective-permute-done | bytes 98336 | tf_op jit(solution)/shard_map/ppermute | solution.py:59
  80.5 0.7 copy-done.10
  81.1 4.8 %collective-permute-start.9 = (bf16[32,1536]{1,0:T(8,128)(2,1)}, bf16[32,1536]{1,0:T(8,128)(2,1)S(1)}, u32[]{:S(2)}, u32[]{:S(2)}) collective-permute-start(bf16[32,1536]{1,0:T(8,128)(2,1)} %get-tuple-element.33), channel_id=1, source_target_pairs={{0,192},{16,208},{32,224},{48,240},{64,0},{80,16},{96,32},{112,48}... | collective-permute-start | bytes 294920 | tf_op jit(solution)/shard_map/ppermute | solution.py:59
  86.0 1.6 collective-permute-done.7.refs_1_
  87.5 2.2 %collective-permute-done.8.refs_2_ = bf16[32,1536]{1,0:T(8,128)(2,1)S(1)} collective-permute-done((bf16[32,1536]{1,0:T(8,128)(2,1)}, bf16[32,1536]{1,0:T(8,128)(2,1)S(1)}, u32[]{:S(2)}, u32[]{:S(2)}) %collective-permute-start.8) | collective-permute-done | bytes 98336 | tf_op jit(solution)/shard_map/ppermute | solution.py:59
  89.7 0.8 collective-permute-done.9.refs_3_
  90.6 0.6 copy-done.15
  91.2 3.0 %shard_map.88.d_txt = bf16[32,1536]{1,0:T(8,128)(2,1)} custom-call(bf16[32,1536]{1,0:T(8,128)(2,1)} %get-tuple-element.30.refs_0_, bf16[32,1536]{1,0:T(8,128)(2,1)} %copy-done.13, bf16[32,1536]{1,0:T(8,128)(2,1)} %copy-done.14, bf16[32,1536]{1,0:T(8,128)(2,1)} %copy-done.15, bf16[32,1536]{1,0:T(8,128)(2,1)} %copy-done.9, bf16[32,1536]{1,0:T(8,128)(2,1)} %copy-done.10, ...), custom_call_target="tpu_custom_call" | custom-call | tf_op jit(solution)/shard_map/pallas_call | solution.py:23
  94.2 0.9 copy-done.5
  95.1 0.4 shard_map.89
  95.5 0.1 broadcast_in_dim.7
  95.6 20.8 %all_to_all.25.grads_ref = bf16[16,32,896]{2,1,0:T(8,128)(2,1)S(1)} all-to-all(bf16[16,32,896]{2,1,0:T(8,128)(2,1)S(1)} %bitcast.25), channel_id=1, replica_groups={{0,2,4,6,8,10,12,14,16,18,20,22,24,26,28,30},{1,3,5,7,9,11,13,15,17,19,..., dimensions={0} | all-to-all | bytes 1835008 | tf_op jit(solution)/shard_map/all_to_all | solution.py:289
  116.4 0.5 shard_map.90
  116.9 0.1 collective-permute-start.15
  117.0 1.6 collective-permute-done.15.came_ref
  118.6 0.1 shard_map.91
  118.7 16.2 %all_to_all.26.parts_ref = bf16[8,2,24,384]{3,2,1,0:T(8,128)(2,1)S(1)} all-to-all(bf16[8,2,24,384]{3,2,1,0:T(8,128)(2,1)S(1)} %shard_map.91), channel_id=1, replica_groups={{0,32,64,96,128,160,192,224},{16,48,80,112,144,176,208,240},{1,33,65,97..., dimensions={0} | all-to-all | bytes 589824 | tf_op jit(solution)/shard_map/all_to_all | solution.py:233
  134.9 1.6 %collective-permute-start.16 = (bf16[24,384]{1,0:T(8,128)(2,1)S(1)}, bf16[24,384]{1,0:T(8,128)(2,1)S(1)}, u32[]{:S(2)}, u32[]{:S(2)}) collective-permute-start(bf16[24,384]{1,0:T(8,128)(2,1)S(1)} %get-tuple-element.42), channel_id=1, source_target_pairs={{0,2},{1,3},{2,0},{3,1},{4,6},{5,7},{6,4},{7,5},{8,10},{9,11},{10,... | collective-permute-start | bytes 55304 | tf_op jit(solution)/shard_map/ppermute | solution.py:71
  136.5 2.2 %collective-permute-done.16 = bf16[24,384]{1,0:T(8,128)(2,1)S(1)} collective-permute-done((bf16[24,384]{1,0:T(8,128)(2,1)S(1)}, bf16[24,384]{1,0:T(8,128)(2,1)S(1)}, u32[]{:S(2)}, u32[]{:S(2)}) %collective-permute-start.16) | collective-permute-done | bytes 18464 | tf_op jit(solution)/shard_map/ppermute | solution.py:71
  138.8 0.9 broadcast_in_dim.8
  139.7 3.6 %all-to-all-start.4 = ((bf16[16,2,24,384]{3,2,1,0:T(8,128)(2,1)}), bf16[16,2,24,384]{3,2,1,0:T(8,128)(2,1)S(1)}, u32[]{:S(2)}, u32[]{:S(2)}) async-start(bf16[16,2,24,384]{3,2,1,0:T(8,128)(2,1)} %broadcast_in_dim.8), calls=%async_computation.4 | async-start | bytes 1179648 | tf_op jit(solution)/shard_map/all_to_all | solution.py:339
  143.3 0.1 slice_add_fusion
  143.4 0.1 fusion
  143.5 0.1 collective-permute-start.14
  143.6 1.1 collective-permute-done.14
  144.8 0.7 select_n.95
  145.5 15.1 %all-to-all-done.4.parts_ref = bf16[16,2,24,384]{3,2,1,0:T(8,128)(2,1)S(1)} async-done(((bf16[16,2,24,384]{3,2,1,0:T(8,128)(2,1)}), bf16[16,2,24,384]{3,2,1,0:T(8,128)(2,1)S(1)}, u32[]{:S(2)}, u32[]{:S(2)}) %all-to-all-start.4) | async-done | bytes 589856 | tf_op jit(solution)/shard_map/all_to_all | solution.py:339
  160.6 1.1 shard_map.93
  (44 shorter events, 0.2 us)
Async XLA Ops:
  0.6 10.6 %copy-start = (bf16[512,1536]{1,0:T(8,128)(2,1)S(1)}, bf16[512,1536]{1,0:T(8,128)(2,1)}, u32[]{:S(2)}) copy-start(bf16[512,1536]{1,0:T(8,128)(2,1)} %param.6) | copy-start | bytes 4718596
  2.6 10.4 %copy-start.7 = (bf16[96,512]{1,0:T(8,128)(2,1)S(1)}, bf16[96,512]{1,0:T(8,128)(2,1)}, u32[]{:S(2)}) copy-start(bf16[96,512]{1,0:T(8,128)(2,1)} %param.8) | copy-start | bytes 294916
  2.6 10.4 %copy-start.8 = (bf16[96,512]{1,0:T(8,128)(2,1)S(1)}, bf16[96,512]{1,0:T(8,128)(2,1)}, u32[]{:S(2)}) copy-start(bf16[96,512]{1,0:T(8,128)(2,1)} %param.9) | copy-start | bytes 294916
  2.6 31.7 %all-to-all-start = ((bf16[8,32,1536]{2,1,0:T(8,128)(2,1)}), bf16[8,32,1536]{2,1,0:T(8,128)(2,1)S(1)}, u32[]{:S(2)}, u32[]{:S(2)}) async-start(bf16[8,32,1536]{2,1,0:T(8,128)(2,1)} %broadcast_in_dim.6), calls=%async_computation | async-start | bytes 1572864 | tf_op jit(solution)/shard_map/all_to_all | solution.py:233
  11.3 36.6 %collective-permute-start.5 = (bf16[256,1536]{1,0:T(8,128)(2,1)S(1)}, bf16[256,1536]{1,0:T(8,128)(2,1)}, u32[]{:S(2)}, u32[]{:S(2)}) collective-permute-start(bf16[256,1536]{1,0:T(8,128)(2,1)S(1)} %bitcast.22), channel_id=1, source_target_pairs={{0,16},{16,0},{32,48},{48,32},{64,80},{80,64},{96,112},{112,96},{1... | collective-permute-start | bytes 2359304 | tf_op jit(solution)/shard_map/ppermute | solution.py:63
  13.0 22.7 %collective-permute-start = (bf16[96,512]{1,0:T(8,128)(2,1)S(1)}, bf16[96,512]{1,0:T(8,128)(2,1)S(1)}, u32[]{:S(2)}, u32[]{:S(2)}) collective-permute-start(bf16[96,512]{1,0:T(8,128)(2,1)S(1)} %get-tuple-element.46), channel_id=1, source_target_pairs={{0,16},{16,0},{32,48},{48,32},{64,80},{80,64},{96,112},{112,96},{1... | collective-permute-start | bytes 294920 | tf_op jit(solution)/shard_map/ppermute | solution.py:63
  34.3 13.6 %collective-permute-start.4 = (bf16[256,1536]{1,0:T(8,128)(2,1)S(1)}, bf16[256,1536]{1,0:T(8,128)(2,1)}, u32[]{:S(2)}, u32[]{:S(2)}) collective-permute-start(bf16[256,1536]{1,0:T(8,128)(2,1)S(1)} %bitcast.20), channel_id=1, source_target_pairs={{0,1},{1,0},{2,3},{3,2},{4,5},{5,4},{6,7},{7,6},{8,9},{9,8},{10,11... | collective-permute-start | bytes 2359304 | tf_op jit(solution)/shard_map/ppermute | solution.py:67
  36.4 7.6 %collective-permute-start.1 = (bf16[192,512]{1,0:T(8,128)(2,1)}, bf16[192,512]{1,0:T(8,128)(2,1)}, u32[]{:S(2)}, u32[]{:S(2)}) collective-permute-start(bf16[192,512]{1,0:T(8,128)(2,1)} %pad_maximum_fusion.refs_0_), channel_id=1, source_target_pairs={{0,2},{1,3},{2,0},{3,1},{4,6},{5,7},{6,4},{7,5},{8,10},{9,11},{10,... | collective-permute-start | bytes 589832 | tf_op jit(solution)/shard_map/ppermute | solution.py:71
  37.3 6.9 %collective-permute-start.2 = (bf16[192,512]{1,0:T(8,128)(2,1)}, bf16[192,512]{1,0:T(8,128)(2,1)S(1)}, u32[]{:S(2)}, u32[]{:S(2)}) collective-permute-start(bf16[192,512]{1,0:T(8,128)(2,1)} %pad_maximum_fusion.refs_0_), channel_id=1, source_target_pairs={{0,1},{1,0},{2,3},{3,2},{4,5},{5,4},{6,7},{7,6},{8,9},{9,8},{10,11... | collective-permute-start | bytes 589832 | tf_op jit(solution)/shard_map/ppermute | solution.py:67
  44.0 1.7 %collective-permute-start.3 = (bf16[192,512]{1,0:T(8,128)(2,1)}, bf16[192,512]{1,0:T(8,128)(2,1)S(1)}, u32[]{:S(2)}, u32[]{:S(2)}) collective-permute-start(bf16[192,512]{1,0:T(8,128)(2,1)} %collective-permute-done.1.refs_1_), channel_id=1, source_target_pairs={{0,1},{1,0},{2,3},{3,2},{4,5},{5,4},{6,7},{7,6},{8,9},{9,8},{10,11... | collective-permute-start | bytes 589832 | tf_op jit(solution)/shard_map/ppermute | solution.py:67
  47.1 0.7 copy-start.3
  53.2 1.2 copy-start.1
  54.4 1.1 copy-start.2
  55.6 2.3 %collective-permute-start.6 = (bf16[256,1536]{1,0:T(8,128)(2,1)S(1)}, bf16[256,1536]{1,0:T(8,128)(2,1)S(1)}, u32[]{:S(2)}, u32[]{:S(2)}) collective-permute-start(bf16[256,1536]{1,0:T(8,128)(2,1)S(1)} %get-tuple-element.26), channel_id=1, source_target_pairs={{0,1},{1,0},{2,3},{3,2},{4,5},{5,4},{6,7},{7,6},{8,9},{9,8},{10,11... | collective-permute-start | bytes 2359304 | tf_op jit(solution)/shard_map/ppermute | solution.py:67
  57.9 0.9 copy-start.6
  58.7 35.5 %all-to-all-start.1 = ((bf16[16,32,1664]{2,1,0:T(8,128)(2,1)}), bf16[16,32,1664]{2,1,0:T(8,128)(2,1)S(1)}, u32[]{:S(2)}, u32[]{:S(2)}) async-start(bf16[16,32,1664]{2,1,0:T(8,128)(2,1)} %copy-done.1), calls=%async_computation.1 | async-start | bytes 3407872 | tf_op jit(solution)/shard_map/all_to_all | solution.py:289
  68.9 11.6 %collective-permute-start.10 = (bf16[32,1536]{1,0:T(8,128)(2,1)}, bf16[32,1536]{1,0:T(8,128)(2,1)S(1)}, u32[]{:S(2)}, u32[]{:S(2)}) collective-permute-start(bf16[32,1536]{1,0:T(8,128)(2,1)} %get-tuple-element.34), channel_id=1, source_target_pairs={{0,64},{16,80},{32,96},{48,112},{64,128},{80,144},{96,160},{112,17... | collective-permute-start | bytes 294920 | tf_op jit(solution)/shard_map/ppermute | solution.py:59
  69.4 11.1 %collective-permute-start.11 = (bf16[32,1536]{1,0:T(8,128)(2,1)}, bf16[32,1536]{1,0:T(8,128)(2,1)S(1)}, u32[]{:S(2)}, u32[]{:S(2)}) collective-permute-start(bf16[32,1536]{1,0:T(8,128)(2,1)} %get-tuple-element.35), channel_id=1, source_target_pairs={{0,160},{16,176},{32,192},{48,208},{64,224},{80,240},{96,0},{112,1... | collective-permute-start | bytes 294920 | tf_op jit(solution)/shard_map/ppermute | solution.py:59
  70.1 15.8 %collective-permute-start.12 = (bf16[32,1536]{1,0:T(8,128)(2,1)}, bf16[32,1536]{1,0:T(8,128)(2,1)S(1)}, u32[]{:S(2)}, u32[]{:S(2)}) collective-permute-start(bf16[32,1536]{1,0:T(8,128)(2,1)} %get-tuple-element.36), channel_id=1, source_target_pairs={{0,96},{16,112},{32,128},{48,144},{64,160},{80,176},{96,192},{112,... | collective-permute-start | bytes 294920 | tf_op jit(solution)/shard_map/ppermute | solution.py:59
  73.2 12.7 %collective-permute-start.13 = (bf16[32,1536]{1,0:T(8,128)(2,1)}, bf16[32,1536]{1,0:T(8,128)(2,1)S(1)}, u32[]{:S(2)}, u32[]{:S(2)}) collective-permute-start(bf16[32,1536]{1,0:T(8,128)(2,1)} %get-tuple-element.37), channel_id=1, source_target_pairs={{0,128},{16,144},{32,160},{48,176},{64,192},{80,208},{96,224},{112... | collective-permute-start | bytes 294920 | tf_op jit(solution)/shard_map/ppermute | solution.py:59
  75.5 12.0 %collective-permute-start.7 = (bf16[32,1536]{1,0:T(8,128)(2,1)}, bf16[32,1536]{1,0:T(8,128)(2,1)S(1)}, u32[]{:S(2)}, u32[]{:S(2)}) collective-permute-start(bf16[32,1536]{1,0:T(8,128)(2,1)} %get-tuple-element.31), channel_id=1, source_target_pairs={{0,224},{16,240},{32,0},{48,16},{64,32},{80,48},{96,64},{112,80},{... | collective-permute-start | bytes 294920 | tf_op jit(solution)/shard_map/ppermute | solution.py:59
  80.5 10.1 %copy-start.9 = (bf16[32,1536]{1,0:T(8,128)(2,1)}, bf16[32,1536]{1,0:T(8,128)(2,1)S(1)}, u32[]{:S(2)}) copy-start(bf16[32,1536]{1,0:T(8,128)(2,1)S(1)} %collective-permute-done.10.refs_4_) | copy-start | bytes 294916
  80.5 9.3 %collective-permute-start.8 = (bf16[32,1536]{1,0:T(8,128)(2,1)}, bf16[32,1536]{1,0:T(8,128)(2,1)S(1)}, u32[]{:S(2)}, u32[]{:S(2)}) collective-permute-start(bf16[32,1536]{1,0:T(8,128)(2,1)} %get-tuple-element.32), channel_id=1, source_target_pairs={{0,32},{16,48},{32,64},{48,80},{64,96},{80,112},{96,128},{112,144}... | collective-permute-start | bytes 294920 | tf_op jit(solution)/shard_map/ppermute | solution.py:59
  80.5 0.7 copy-start.10
  81.1 9.4 %collective-permute-start.9 = (bf16[32,1536]{1,0:T(8,128)(2,1)}, bf16[32,1536]{1,0:T(8,128)(2,1)S(1)}, u32[]{:S(2)}, u32[]{:S(2)}) collective-permute-start(bf16[32,1536]{1,0:T(8,128)(2,1)} %get-tuple-element.33), channel_id=1, source_target_pairs={{0,192},{16,208},{32,224},{48,240},{64,0},{80,16},{96,32},{112,48}... | collective-permute-start | bytes 294920 | tf_op jit(solution)/shard_map/ppermute | solution.py:59
  85.9 4.6 %copy-start.11 = (bf16[32,1536]{1,0:T(8,128)(2,1)}, bf16[32,1536]{1,0:T(8,128)(2,1)S(1)}, u32[]{:S(2)}) copy-start(bf16[32,1536]{1,0:T(8,128)(2,1)S(1)} %collective-permute-done.12.refs_6_) | copy-start | bytes 294916
  86.0 4.6 %copy-start.12 = (bf16[32,1536]{1,0:T(8,128)(2,1)}, bf16[32,1536]{1,0:T(8,128)(2,1)S(1)}, u32[]{:S(2)}) copy-start(bf16[32,1536]{1,0:T(8,128)(2,1)S(1)} %collective-permute-done.13.refs_7_) | copy-start | bytes 294916
  87.5 3.0 %copy-start.13 = (bf16[32,1536]{1,0:T(8,128)(2,1)}, bf16[32,1536]{1,0:T(8,128)(2,1)S(1)}, u32[]{:S(2)}) copy-start(bf16[32,1536]{1,0:T(8,128)(2,1)S(1)} %collective-permute-done.7.refs_1_) | copy-start | bytes 294916
  89.7 0.8 copy-start.14
  90.5 0.6 copy-start.15
  94.2 0.9 copy-start.5
  95.5 21.0 %copy-start.4 = (bf16[384,512]{1,0:T(8,128)(2,1)S(1)}, bf16[384,512]{1,0:T(8,128)(2,1)}, u32[]{:S(2)}) copy-start(bf16[384,512]{1,0:T(8,128)(2,1)} %copy-done.3) | copy-start | bytes 1179652
  116.9 1.7 %collective-permute-start.15 = (bf16[192,768]{1,0:T(8,128)(2,1)S(1)}, bf16[192,768]{1,0:T(8,128)(2,1)S(1)}, u32[]{:S(2)}, u32[]{:S(2)}) collective-permute-start(bf16[192,768]{1,0:T(8,128)(2,1)S(1)} %get-tuple-element.40), channel_id=1, source_target_pairs={{0,1},{1,0},{2,3},{3,2},{4,5},{5,4},{6,7},{7,6},{8,9},{9,8},{10,11... | collective-permute-start | bytes 884744 | tf_op jit(solution)/shard_map/ppermute | solution.py:67
  134.9 3.8 %collective-permute-start.16 = (bf16[24,384]{1,0:T(8,128)(2,1)S(1)}, bf16[24,384]{1,0:T(8,128)(2,1)S(1)}, u32[]{:S(2)}, u32[]{:S(2)}) collective-permute-start(bf16[24,384]{1,0:T(8,128)(2,1)S(1)} %get-tuple-element.42), channel_id=1, source_target_pairs={{0,2},{1,3},{2,0},{3,1},{4,6},{5,7},{6,4},{7,5},{8,10},{9,11},{10,... | collective-permute-start | bytes 55304 | tf_op jit(solution)/shard_map/ppermute | solution.py:71
  139.7 20.9 %all-to-all-start.4 = ((bf16[16,2,24,384]{3,2,1,0:T(8,128)(2,1)}), bf16[16,2,24,384]{3,2,1,0:T(8,128)(2,1)S(1)}, u32[]{:S(2)}, u32[]{:S(2)}) async-start(bf16[16,2,24,384]{3,2,1,0:T(8,128)(2,1)} %broadcast_in_dim.8), calls=%async_computation.4 | async-start | bytes 1179648 | tf_op jit(solution)/shard_map/all_to_all | solution.py:339
  143.5 1.3 collective-permute-start.14

commit v8 on v7

--- a/solution.py
+++ b/solution.py
@@ -17,7 +17,7 @@
 WHOLE = 58
 
 
-def local(kernel, outs, operands, mib, specs=None, out_specs=None, scratch=()):
+def local(kernel, outs, operands, mib, specs=None, out_specs=None, scratch=(), cost=None):
     single = not isinstance(outs, list)
     shapes = [jax.ShapeDtypeStruct(*out) for out in ([outs] if single else outs)]
     result = pl.pallas_call(
@@ -26,6 +26,7 @@
         in_specs=specs or [VMEM] * len(operands),
         out_specs=out_specs or [VMEM] * len(shapes),
         scratch_shapes=list(scratch),
+        cost_estimate=cost and pl.CostEstimate(flops=cost, bytes_accessed=0, transcendentals=0),
         compiler_params=pltpu.CompilerParams(vmem_limit_bytes=mib * 2**20),
     )(*operands)
     return result[0] if single else result
@@ -101,15 +102,13 @@
         out_ref[place, pl.ds(half, half)] = jnp.where(y == 0, other, own)
 
 
-def tile_kernel(*refs):
-    numbers, places, text_ids, image_ids = refs[0], refs[1], refs[2], refs[3]
-    blocks, own, partner = refs[4:6], refs[6], refs[7]
-    image_out, keep_ref, send_ref, texts, images, slopes = refs[8:]
-    sub, width = image_out.shape[1], own.shape[1]
+def tile_kernel(
+    numbers, text_ids, image_ids, near, far, own, partner,
+    texts, slopes, loss_ref, keep_ref, send_ref, images,
+):
     scale, bias = numbers[0], numbers[1]
     rows = own.shape[0]
-    pieces = rows // sub
-    for i, block in enumerate(blocks):
+    for i, block in enumerate((near, far)):
         texts[pl.ds(i * rows, rows), :] = normalize(block[...])[0].astype(BF16)
     for part, source in enumerate((own, partner)):
         place = pl.ds(part * rows, rows)
@@ -122,21 +121,28 @@
         e = jnp.exp(-jnp.abs(u))
         w = 1.0 + e
         grown = jnp.where(w == 1.0, e, jnp.log(w) * (e / jnp.where(w == 1.0, 1.0, w - 1.0)))
-        losses = jnp.sum(jnp.maximum(u, 0.0) + grown, axis=1, keepdims=True)
+        loss_ref[place, :] = jnp.sum(jnp.maximum(u, 0.0) + grown, axis=1, keepdims=True)
         slope = jnp.where(match, -scale, scale) * (jnp.where(u >= 0.0, 1.0, e) / w)
         slopes[place, :] = slope.astype(BF16)
-        grad = jnp.dot(slopes[place, :], texts[...], preferred_element_type=F32).astype(BF16)
-        extra = loss_columns(losses)
-        first = places[part]
-        for i in range(pieces):
-            image_out[first + i, :, pl.ds(0, width)] = grad[i * sub : (i + 1) * sub]
-            image_out[first + i, :, pl.ds(width, LANES)] = extra[i * sub : (i + 1) * sub]
     text_grad = lax.dot_general(
         slopes[...], images[...], (((0,), (0,)), ((), ())), preferred_element_type=F32
     )
     half = text_grad.shape[0] // 2
     keep_ref[...] = text_grad[:half]
     send_ref[...] = text_grad[half:].astype(BF16)
+
+
+def image_kernel(places, texts, slopes, loss_ref, image_out):
+    sub, width = image_out.shape[1], texts.shape[1]
+    rows = slopes.shape[0] // 2
+    for part in range(2):
+        place = pl.ds(part * rows, rows)
+        grad = jnp.dot(slopes[place, :], texts[...], preferred_element_type=F32).astype(BF16)
+        extra = loss_columns(loss_ref[place, :])
+        first = places[part]
+        for i in range(rows // sub):
+            image_out[first + i, :, pl.ds(0, width)] = grad[i * sub : (i + 1) * sub]
+            image_out[first + i, :, pl.ds(width, LANES)] = extra[i * sub : (i + 1) * sub]
 
 
 def join_kernel(flags, keep_ref, came_ref, *refs):
@@ -240,14 +246,6 @@
     partner = swap_y(own)
     pair = jnp.concatenate([mine, came])
     pair_x = swap_x(pair)
-    feat_part = local(
-        feature_kernel,
-        ((4 * feats, rows), BF16),
-        [jnp.stack([y, core]), pair, pair_x, swap_core(pair), swap_core(pair_x)],
-        8,
-        [SMEM] + [VMEM] * 4,
-    )
-
     owners = 2 * jnp.arange(8, dtype=jnp.int32) + y
     cores = jnp.stack([mp_index, mp_index ^ 1])
     text_ids = owners[None, :, None] * rows + cores[:, None, None] * sub
@@ -259,13 +257,17 @@
     )
     places = jnp.stack([8 * y, 8 * (1 - y)])
     numbers = jnp.concatenate([logit_scale, logit_bias])
-    numbers, feat_part = lax.optimization_barrier((numbers, feat_part))
-    image_part, keep, send = local(
+    unit, slope, losses, keep, send = local(
         tile_kernel,
-        [((16, sub, full), BF16), ((half, width), F32), ((half, width), BF16)],
+        [
+            ((rows, width), BF16),
+            ((rows, rows), BF16),
+            ((rows, 1), F32),
+            ((half, width), F32),
+            ((half, width), BF16),
+        ],
         [
             numbers,
-            places.astype(jnp.int32),
             text_ids.astype(jnp.int32).reshape(1, rows),
             image_ids.astype(jnp.int32).reshape(rows, 1),
             texts,
@@ -274,10 +276,19 @@
             partner,
         ],
         24,
-        [SMEM, SMEM] + [VMEM] * 6,
+        [SMEM] + [VMEM] * 6,
         None,
-        [pltpu.VMEM((rows, width), BF16)] * 2
-        + [pltpu.VMEM((rows, rows), BF16)],
+        [pltpu.VMEM((rows, width), BF16)],
+        4 * 10**9,
+    )
+    came_grad = swap_core(send)
+    image_part = local(
+        image_kernel,
+        ((16, sub, full), BF16),
+        [places.astype(jnp.int32), unit, slope, losses],
+        16,
+        [SMEM] + [VMEM] * 3,
+        cost=2 * 10**9,
     )
     plane = [
         [(2 * s + t) * 16 + 2 * k + c for t in range(2) for k in range(8)]
@@ -290,8 +301,6 @@
             value, ("dp", "mp"), 0, 0, tiled=True, axis_index_groups=plane
         )
 
-    came_grad = swap_core(send)
-    image_part, came_grad = lax.optimization_barrier((image_part, came_grad))
     text_parts = local(
         join_kernel,
         [((sub, width), BF16)] * 8,
@@ -301,6 +310,7 @@
         [HBM] * 8,
         [pltpu.VMEM((8, sub, width), BF16), DMA((8,))],
     )
+    image_part, pair_x, *text_parts = lax.optimization_barrier((image_part, pair_x, *text_parts))
     image_pieces = over_plane(image_part)
     text_came = [text_parts[0]] + [
         along_z(part, -steps) for part, steps in zip(text_parts[1:], ALONG[1:], strict=True)
@@ -314,7 +324,15 @@
         None,
         [pltpu.VMEM((8, sub, width), BF16), DMA((8,))],
     )
+    feat_part = local(
+        feature_kernel,
+        ((4 * feats, rows), BF16),
+        [jnp.stack([y, core]), pair, pair_x, swap_core(pair), swap_core(pair_x)],
+        8,
+        [SMEM] + [VMEM] * 4,
+    )
     raw_img = lax.dynamic_slice_in_dim(img_emb, (2 * chip + core) * sub, sub, 0)
+    raw_img, feat_part = lax.optimization_barrier((raw_img, feat_part))
     narrow = width // 2
     kinds = local(
         grad_kernel,

time: 162 us -> 174 us (1.074)
  local copies, waits for them, and re-layouts: 10.1 us -> 18.6 us
  starting transfers between devices: 39.1 us -> 42.7 us
  waiting for transfers between devices: 57.3 us -> 54.9 us
    unnamed x32 -> x46, local copies, waits for them, and re-layouts: 6.17 us -> 14.1 us
    ppermute x2, waiting for transfers between devices: 8.75 us -> 2.3 us  [swap_x(): return lax.ppermute(value, 'mp', [(m, m ^ 2) for m in range(16)])]
    ppermute x2, waiting for transfers between devices: 0.01 us -> 3.48 us  [swap_y(): return lax.ppermute(value, 'dp', [(d, d ^ 1) for d in range(16)])]
    ppermute x6, waiting for transfers between devices: 6.36 us -> 3.24 us  [swap_core(): return lax.ppermute(value, 'mp', [(m, m ^ 1) for m in range(16)])]
    ppermute x7, waiting for transfers between devices: 6.38 us -> 9.43 us  [along_z(): lax.ppermute(value, 'dp', [(d, (d + 2 * steps) % 16) for d in range(16)])]
    all_to_all x1, blocking collectives: 16.2 us -> 19.1 us  [over_z(): lax.all_to_all(value, 'dp', 0, 0, tiled=True, axis_index_groups=same_y)]
    all_to_all x1, blocking collectives: 20.8 us -> 18.1 us  [over_plane(): lax.all_to_all(value, ('dp', 'mp'), 0, 0, tiled=True, axis_index_groups=p...]
    pallas_call x9 -> x10, Pallas kernels: 14.5 us -> 15.7 us  [local(): pl.pallas_call(kernel, out_shape=shapes, in_specs=specs or [VMEM] * len(o...]
  transfers between devices with their start and end apart: 20 -> 20, of which waited for: 12 -> 11; matrix products, arithmetic and copies ran while one was open for 1% -> 2% of each run, Pallas kernels for 4% -> 5%
where the time goes in v8:
time: 174 us; the launch traced here: 173 us
  waiting for transfers between devices  54.9 us (32%)
  starting transfers between devices  42.7 us (25%)
  blocking collectives  37.1 us (21%)
  local copies, waits for them, and re-layouts  18.6 us (11%)
  Pallas kernels  15.7 us (9%)
  between operations  2.28 us (1%)
    all_to_all x1, waiting for transfers between devices, over_z(): lax.all_to_all(value, 'dp', 0, 0, tiled=True, axis_index_groups=same_y)  21.4 us
    all_to_all x1, blocking collectives, over_z(): lax.all_to_all(value, 'dp', 0, 0, tiled=True, axis_index_groups=same_y)  19.1 us
    all_to_all x1, blocking collectives, over_plane(): lax.all_to_all(value, ('dp', 'mp'), 0, 0, tiled=True, axis_index_groups=p...  18.1 us
    ppermute x7, starting transfers between devices, along_z(): lax.ppermute(value, 'dp', [(d, (d + 2 * steps) % 16) for d in range(16)])  16.1 us
    pallas_call x10, Pallas kernels, local(): pl.pallas_call(kernel, out_shape=shapes, in_specs=specs or [VMEM] * len(o...  15.7 us
    all_to_all x1, waiting for transfers between devices, shards(): lax.all_to_all(jnp.broadcast_to(summed[None], (16, 2, *shape)), 'dp', 0,...  15.1 us
    unnamed x46, local copies, waits for them, and re-layouts  14.1 us
    ppermute x7, waiting for transfers between devices, along_z(): lax.ppermute(value, 'dp', [(d, (d + 2 * steps) % 16) for d in range(16)])  9.43 us
  transfers between devices with their start and end apart: 20, of which 11 were waited for; matrix products, arithmetic and copies ran while one was open for 2% of the time, Pallas kernels for 5%

profile of v8, /device:TPU:2, one launch (start us, length us, event | category | flops | bytes accessed | tf_op | source)
XLA Modules:
  0.0 173.1 jit_solution(15352868799955348854)
XLA Ops:
  0.6 2.0 %broadcast_in_dim.6 = bf16[8,32,1536]{2,1,0:T(8,128)(2,1)} broadcast(bf16[32,1536]{1,0:T(8,128)(2,1)} %refs_8_.1), dimensions={1,2} | broadcast | bytes 884736 | tf_op jit(solution)/shard_map/broadcast_in_dim | solution.py:241
  2.6 8.5 %all-to-all-start = ((bf16[8,32,1536]{2,1,0:T(8,128)(2,1)}), bf16[8,32,1536]{2,1,0:T(8,128)(2,1)S(1)}, u32[]{:S(2)}, u32[]{:S(2)}) async-start(bf16[8,32,1536]{2,1,0:T(8,128)(2,1)} %broadcast_in_dim.6), calls=%async_computation | async-start | bytes 1572864 | tf_op jit(solution)/shard_map/all_to_all | solution.py:239
  11.2 1.7 collective-permute-start.1
  12.8 21.4 %all-to-all-done = bf16[8,32,1536]{2,1,0:T(8,128)(2,1)S(1)} async-done(((bf16[8,32,1536]{2,1,0:T(8,128)(2,1)}), bf16[8,32,1536]{2,1,0:T(8,128)(2,1)S(1)}, u32[]{:S(2)}, u32[]{:S(2)}) %all-to-all-start) | async-done | bytes 786464 | tf_op jit(solution)/shard_map/all_to_all | solution.py:239
  34.2 0.1 copy.11.image_ids
  34.6 0.1 add.120.text_ids
  36.1 0.5 collective-permute-done.far
  36.6 5.4 %shard_map.85 = (bf16[512,1536]{1,0:T(8,128)(2,1)S(1)}, bf16[512,512]{1,0:T(8,128)(2,1)S(1)}, f32[512,1]{1,0:T(8,128)S(1)}, f32[256,1536]{1,0:T(8,128)S(1)}, bf16[256,1536]{1,0:T(8,128)(2,1)}) custom-call(f32[2]{0:T(128)S(1)} %pad_maximum_fusion.2.numbers, s32[1,512]{1,0:T(1,128)S(1)} %add.120.text_ids, s32[512,1]{1,0:T(8,128)S(1)} %copy.11.image_ids, ...), custom_call_target="tpu_custom_call" | custom-call | flops 4000000000 | tf_op jit(solution)/shard_map/pallas_call | solution.py:23
  42.1 1.1 copy-done.2
  43.2 1.2 copy-done.9
  44.4 0.8 copy-done.11
  45.2 0.7 copy-done.13
  45.9 0.1 collective-permute-start.4
  46.0 0.9 broadcast_select_fusion.1
  46.9 1.7 collective-permute-start.2
  48.6 3.5 %collective-permute-done.2 = bf16[96,512]{1,0:T(8,128)(2,1)S(1)} collective-permute-done((bf16[96,512]{1,0:T(8,128)(2,1)S(1)}, bf16[96,512]{1,0:T(8,128)(2,1)S(1)}, u32[]{:S(2)}, u32[]{:S(2)}) %collective-permute-start.2) | collective-permute-done | bytes 98336 | tf_op jit(solution)/shard_map/ppermute | solution.py:64
  52.1 0.6 collective-permute-start.3
  52.8 1.4 copy-done.10
  54.2 1.0 copy-done.12
  55.2 0.9 copy-done.14
  56.2 1.5 shard_map.86
  57.7 1.2 copy-done.1
  58.9 0.9 copy-done.15
  59.8 2.7 %shard_map.87 = (bf16[32,1536]{1,0:T(8,128)(2,1)}, bf16[32,1536]{1,0:T(8,128)(2,1)}, bf16[32,1536]{1,0:T(8,128)(2,1)}, bf16[32,1536]{1,0:T(8,128)(2,1)}, bf16[32...) custom-call(s32[1]{0:T(128)} %bitcast.8.flags, ...), custom_call_target="tpu_custom_call" | custom-call | tf_op jit(solution)/shard_map/pallas_call | solution.py:23
  62.5 0.7 copy-done.7
  63.2 8.1 %all-to-all-start.1 = ((bf16[16,32,1664]{2,1,0:T(8,128)(2,1)}), bf16[16,32,1664]{2,1,0:T(8,128)(2,1)S(1)}, u32[]{:S(2)}, u32[]{:S(2)}) async-start(bf16[16,32,1664]{2,1,0:T(8,128)(2,1)} %copy-done.1), calls=%async_computation.1 | async-start | bytes 3407872 | tf_op jit(solution)/shard_map/all_to_all | solution.py:300
  71.4 0.1 collective-permute-start.12
  71.5 0.5 collective-permute-start.13
  72.0 2.0 %collective-permute-start.11 = (bf16[32,1536]{1,0:T(8,128)(2,1)}, bf16[32,1536]{1,0:T(8,128)(2,1)S(1)}, u32[]{:S(2)}, u32[]{:S(2)}) collective-permute-start(bf16[32,1536]{1,0:T(8,128)(2,1)} %get-tuple-element.55), channel_id=1, source_target_pairs={{0,128},{16,144},{32,160},{48,176},{64,192},{80,208},{96,224},{112... | collective-permute-start | bytes 294920 | tf_op jit(solution)/shard_map/ppermute | solution.py:60
  73.9 3.3 %collective-permute-start.5 = (bf16[32,1536]{1,0:T(8,128)(2,1)}, bf16[32,1536]{1,0:T(8,128)(2,1)S(1)}, u32[]{:S(2)}, u32[]{:S(2)}) collective-permute-start(bf16[32,1536]{1,0:T(8,128)(2,1)} %get-tuple-element.49), channel_id=1, source_target_pairs={{0,224},{16,240},{32,0},{48,16},{64,32},{80,48},{96,64},{112,80},{... | collective-permute-start | bytes 294920 | tf_op jit(solution)/shard_map/ppermute | solution.py:60
  77.3 2.7 %collective-permute-done.10.refs_6_ = bf16[32,1536]{1,0:T(8,128)(2,1)} collective-permute-done((bf16[32,1536]{1,0:T(8,128)(2,1)}, bf16[32,1536]{1,0:T(8,128)(2,1)}, u32[]{:S(2)}, u32[]{:S(2)}) %collective-permute-start.10) | collective-permute-done | bytes 98336 | tf_op jit(solution)/shard_map/ppermute | solution.py:60
  80.0 3.6 %collective-permute-start.6 = (bf16[32,1536]{1,0:T(8,128)(2,1)}, bf16[32,1536]{1,0:T(8,128)(2,1)S(1)}, u32[]{:S(2)}, u32[]{:S(2)}) collective-permute-start(bf16[32,1536]{1,0:T(8,128)(2,1)} %get-tuple-element.50), channel_id=1, source_target_pairs={{0,32},{16,48},{32,64},{48,80},{64,96},{80,112},{96,128},{112,144}... | collective-permute-start | bytes 294920 | tf_op jit(solution)/shard_map/ppermute | solution.py:60
  83.6 0.7 constant_dynamic-slice_fusion.raw_img
  84.2 3.1 %collective-permute-start.7 = (bf16[32,1536]{1,0:T(8,128)(2,1)}, bf16[32,1536]{1,0:T(8,128)(2,1)S(1)}, u32[]{:S(2)}, u32[]{:S(2)}) collective-permute-start(bf16[32,1536]{1,0:T(8,128)(2,1)} %get-tuple-element.51), channel_id=1, source_target_pairs={{0,192},{16,208},{32,224},{48,240},{64,0},{80,16},{96,32},{112,48}... | collective-permute-start | bytes 294920 | tf_op jit(solution)/shard_map/ppermute | solution.py:60
  87.3 1.6 collective-permute-start.8
  88.9 2.6 %collective-permute-start.9 = (bf16[32,1536]{1,0:T(8,128)(2,1)}, bf16[32,1536]{1,0:T(8,128)(2,1)S(1)}, u32[]{:S(2)}, u32[]{:S(2)}) collective-permute-start(bf16[32,1536]{1,0:T(8,128)(2,1)} %get-tuple-element.53), channel_id=1, source_target_pairs={{0,160},{16,176},{32,192},{48,208},{64,224},{80,240},{96,0},{112,1... | collective-permute-start | bytes 294920 | tf_op jit(solution)/shard_map/ppermute | solution.py:60
  91.6 3.3 %collective-permute-done.7.refs_3_ = bf16[32,1536]{1,0:T(8,128)(2,1)S(1)} collective-permute-done((bf16[32,1536]{1,0:T(8,128)(2,1)}, bf16[32,1536]{1,0:T(8,128)(2,1)S(1)}, u32[]{:S(2)}, u32[]{:S(2)}) %collective-permute-start.7) | collective-permute-done | bytes 98336 | tf_op jit(solution)/shard_map/ppermute | solution.py:60
  94.8 0.5 collective-permute-done.8.refs_4_
  95.3 2.9 %collective-permute-done.9.refs_5_ = bf16[32,1536]{1,0:T(8,128)(2,1)S(1)} collective-permute-done((bf16[32,1536]{1,0:T(8,128)(2,1)}, bf16[32,1536]{1,0:T(8,128)(2,1)S(1)}, u32[]{:S(2)}, u32[]{:S(2)}) %collective-permute-start.9) | collective-permute-done | bytes 98336 | tf_op jit(solution)/shard_map/ppermute | solution.py:60
  98.3 0.6 copy-done.22
  99.0 3.1 %shard_map.88.d_txt = bf16[32,1536]{1,0:T(8,128)(2,1)} custom-call(bf16[32,1536]{1,0:T(8,128)(2,1)} %get-tuple-element.48.refs_0_, bf16[32,1536]{1,0:T(8,128)(2,1)} %copy-done.18, bf16[32,1536]{1,0:T(8,128)(2,1)} %copy-done.19, bf16[32,1536]{1,0:T(8,128)(2,1)} %copy-done.20, bf16[32,1536]{1,0:T(8,128)(2,1)} %copy-done.21, bf16[32,1536]{1,0:T(8,128)(2,1)} %copy-done.22, ...), custom_call_target="tpu_custom_call" | custom-call | tf_op jit(solution)/shard_map/pallas_call | solution.py:23
  102.0 0.9 copy-done.8
  103.0 1.0 shard_map.89.feats_ref
  103.9 0.7 copy-done.3
  104.7 0.9 copy-done.5
  105.6 0.9 copy-done.6
  106.5 0.4 shard_map.90
  106.9 0.1 broadcast_in_dim.7
  107.0 18.1 %all_to_all.25.grads_ref = bf16[16,32,896]{2,1,0:T(8,128)(2,1)S(1)} all-to-all(bf16[16,32,896]{2,1,0:T(8,128)(2,1)S(1)} %bitcast.25), channel_id=1, replica_groups={{0,2,4,6,8,10,12,14,16,18,20,22,24,26,28,30},{1,3,5,7,9,11,13,15,17,19,..., dimensions={0} | all-to-all | bytes 1835008 | tf_op jit(solution)/shard_map/all_to_all | solution.py:300
  125.0 0.5 shard_map.91
  125.5 0.1 collective-permute-start.15
  125.6 1.6 collective-permute-done.15.came_ref
  127.2 19.1 %all_to_all.26.parts_ref = bf16[8,2,24,384]{3,2,1,0:T(8,128)(2,1)S(1)} all-to-all(bf16[8,2,24,384]{3,2,1,0:T(8,128)(2,1)S(1)} %shard_map.92), channel_id=1, replica_groups={{0,32,64,96,128,160,192,224},{16,48,80,112,144,176,208,240},{1,33,65,97..., dimensions={0} | all-to-all | bytes 589824 | tf_op jit(solution)/shard_map/all_to_all | solution.py:239
  146.3 1.5 collective-permute-start.16
  147.9 2.3 %collective-permute-done.16 = bf16[24,384]{1,0:T(8,128)(2,1)S(1)} collective-permute-done((bf16[24,384]{1,0:T(8,128)(2,1)S(1)}, bf16[24,384]{1,0:T(8,128)(2,1)S(1)}, u32[]{:S(2)}, u32[]{:S(2)}) %collective-permute-start.16) | collective-permute-done | bytes 18464 | tf_op jit(solution)/shard_map/ppermute | solution.py:72
  150.2 0.9 broadcast_in_dim.8
  151.1 3.6 %all-to-all-start.4 = ((bf16[16,2,24,384]{3,2,1,0:T(8,128)(2,1)}), bf16[16,2,24,384]{3,2,1,0:T(8,128)(2,1)S(1)}, u32[]{:S(2)}, u32[]{:S(2)}) async-start(bf16[16,2,24,384]{3,2,1,0:T(8,128)(2,1)} %broadcast_in_dim.8), calls=%async_computation.4 | async-start | bytes 1179648 | tf_op jit(solution)/shard_map/all_to_all | solution.py:357
  154.7 0.1 slice_add_fusion
  154.8 0.1 fusion
  154.9 0.1 collective-permute-start.14
  155.1 1.1 collective-permute-done.14
  156.2 0.7 select_n.95
  156.9 15.1 %all-to-all-done.4.parts_ref = bf16[16,2,24,384]{3,2,1,0:T(8,128)(2,1)S(1)} async-done(((bf16[16,2,24,384]{3,2,1,0:T(8,128)(2,1)}), bf16[16,2,24,384]{3,2,1,0:T(8,128)(2,1)S(1)}, u32[]{:S(2)}, u32[]{:S(2)}) %all-to-all-start.4) | async-done | bytes 589856 | tf_op jit(solution)/shard_map/all_to_all | solution.py:357
  172.0 1.1 shard_map.94
  (59 shorter events, 0.8 us)
Async XLA Ops:
  0.6 10.5 %copy-start = (bf16[512,1536]{1,0:T(8,128)(2,1)S(1)}, bf16[512,1536]{1,0:T(8,128)(2,1)}, u32[]{:S(2)}) copy-start(bf16[512,1536]{1,0:T(8,128)(2,1)} %param.6) | copy-start | bytes 4718596
  2.6 31.6 %all-to-all-start = ((bf16[8,32,1536]{2,1,0:T(8,128)(2,1)}), bf16[8,32,1536]{2,1,0:T(8,128)(2,1)S(1)}, u32[]{:S(2)}, u32[]{:S(2)}) async-start(bf16[8,32,1536]{2,1,0:T(8,128)(2,1)} %broadcast_in_dim.6), calls=%async_computation | async-start | bytes 1572864 | tf_op jit(solution)/shard_map/all_to_all | solution.py:239
  11.2 24.9 %collective-permute-start.1 = (bf16[256,1536]{1,0:T(8,128)(2,1)S(1)}, bf16[256,1536]{1,0:T(8,128)(2,1)}, u32[]{:S(2)}, u32[]{:S(2)}) collective-permute-start(bf16[256,1536]{1,0:T(8,128)(2,1)S(1)} %bitcast.22), channel_id=1, source_target_pairs={{0,16},{16,0},{32,48},{48,32},{64,80},{80,64},{96,112},{112,96},{1... | collective-permute-start | bytes 2359304 | tf_op jit(solution)/shard_map/ppermute | solution.py:64
  34.2 2.4 %collective-permute-start = (bf16[256,1536]{1,0:T(8,128)(2,1)S(1)}, bf16[256,1536]{1,0:T(8,128)(2,1)}, u32[]{:S(2)}, u32[]{:S(2)}) collective-permute-start(bf16[256,1536]{1,0:T(8,128)(2,1)S(1)} %bitcast.20), channel_id=1, source_target_pairs={{0,1},{1,0},{2,3},{3,2},{4,5},{5,4},{6,7},{7,6},{8,9},{9,8},{10,11... | collective-permute-start | bytes 2359304 | tf_op jit(solution)/shard_map/ppermute | solution.py:68
  36.1 9.9 %copy-start.16 = (bf16[96,512]{1,0:T(8,128)(2,1)S(1)}, bf16[96,512]{1,0:T(8,128)(2,1)}, u32[]{:S(2)}) copy-start(bf16[96,512]{1,0:T(8,128)(2,1)} %param.8) | copy-start | bytes 294916
  42.1 1.1 copy-start.2
  43.2 1.2 copy-start.9
  44.4 0.8 copy-start.11
  45.2 0.7 copy-start.13
  45.9 13.1 %collective-permute-start.4 = (bf16[256,1536]{1,0:T(8,128)(2,1)}, bf16[256,1536]{1,0:T(8,128)(2,1)S(1)}, u32[]{:S(2)}, u32[]{:S(2)}) collective-permute-start(bf16[256,1536]{1,0:T(8,128)(2,1)} %get-tuple-element.38), channel_id=1, source_target_pairs={{0,1},{1,0},{2,3},{3,2},{4,5},{5,4},{6,7},{7,6},{8,9},{9,8},{10,11... | collective-permute-start | bytes 2359304 | tf_op jit(solution)/shard_map/ppermute | solution.py:68
  46.9 5.2 %collective-permute-start.2 = (bf16[96,512]{1,0:T(8,128)(2,1)S(1)}, bf16[96,512]{1,0:T(8,128)(2,1)S(1)}, u32[]{:S(2)}, u32[]{:S(2)}) collective-permute-start(bf16[96,512]{1,0:T(8,128)(2,1)S(1)} %get-tuple-element.66), channel_id=1, source_target_pairs={{0,16},{16,0},{32,48},{48,32},{64,80},{80,64},{96,112},{112,96},{1... | collective-permute-start | bytes 294920 | tf_op jit(solution)/shard_map/ppermute | solution.py:64
  52.1 10.4 %collective-permute-start.3 = (bf16[192,512]{1,0:T(8,128)(2,1)S(1)}, bf16[192,512]{1,0:T(8,128)(2,1)S(1)}, u32[]{:S(2)}, u32[]{:S(2)}) collective-permute-start(bf16[192,512]{1,0:T(8,128)(2,1)S(1)} %pad_maximum_fusion.refs_0_), channel_id=1, source_target_pairs={{0,2},{1,3},{2,0},{3,1},{4,6},{5,7},{6,4},{7,5},{8,10},{9,11},{10,... | collective-permute-start | bytes 589832 | tf_op jit(solution)/shard_map/ppermute | solution.py:72
  52.8 1.4 copy-start.10
  54.2 1.0 copy-start.12
  55.2 0.9 copy-start.14
  57.7 1.2 copy-start.1
  58.9 0.9 copy-start.15
  62.5 0.7 copy-start.7
  63.2 41.5 %all-to-all-start.1 = ((bf16[16,32,1664]{2,1,0:T(8,128)(2,1)}), bf16[16,32,1664]{2,1,0:T(8,128)(2,1)S(1)}, u32[]{:S(2)}, u32[]{:S(2)}) async-start(bf16[16,32,1664]{2,1,0:T(8,128)(2,1)} %copy-done.1), calls=%async_computation.1 | async-start | bytes 3407872 | tf_op jit(solution)/shard_map/all_to_all | solution.py:300
  71.3 8.6 %collective-permute-start.10 = (bf16[32,1536]{1,0:T(8,128)(2,1)}, bf16[32,1536]{1,0:T(8,128)(2,1)}, u32[]{:S(2)}, u32[]{:S(2)}) collective-permute-start(bf16[32,1536]{1,0:T(8,128)(2,1)} %get-tuple-element.54), channel_id=1, source_target_pairs={{0,96},{16,112},{32,128},{48,144},{64,160},{80,176},{96,192},{112,... | collective-permute-start | bytes 294920 | tf_op jit(solution)/shard_map/ppermute | solution.py:60
  71.4 30.6 %collective-permute-start.12 = (bf16[192,512]{1,0:T(8,128)(2,1)S(1)}, bf16[192,512]{1,0:T(8,128)(2,1)S(1)}, u32[]{:S(2)}, u32[]{:S(2)}) collective-permute-start(bf16[192,512]{1,0:T(8,128)(2,1)S(1)} %pad_maximum_fusion.refs_0_), channel_id=1, source_target_pairs={{0,1},{1,0},{2,3},{3,2},{4,5},{5,4},{6,7},{7,6},{8,9},{9,8},{10,11... | collective-permute-start | bytes 589832 | tf_op jit(solution)/shard_map/ppermute | solution.py:68
  71.5 30.5 %collective-permute-start.13 = (bf16[192,512]{1,0:T(8,128)(2,1)}, bf16[192,512]{1,0:T(8,128)(2,1)S(1)}, u32[]{:S(2)}, u32[]{:S(2)}) collective-permute-start(bf16[192,512]{1,0:T(8,128)(2,1)} %copy-done.7), channel_id=1, source_target_pairs={{0,1},{1,0},{2,3},{3,2},{4,5},{5,4},{6,7},{7,6},{8,9},{9,8},{10,11... | collective-permute-start | bytes 589832 | tf_op jit(solution)/shard_map/ppermute | solution.py:68
  72.0 12.3 %collective-permute-start.11 = (bf16[32,1536]{1,0:T(8,128)(2,1)}, bf16[32,1536]{1,0:T(8,128)(2,1)S(1)}, u32[]{:S(2)}, u32[]{:S(2)}) collective-permute-start(bf16[32,1536]{1,0:T(8,128)(2,1)} %get-tuple-element.55), channel_id=1, source_target_pairs={{0,128},{16,144},{32,160},{48,176},{64,192},{80,208},{96,224},{112... | collective-permute-start | bytes 294920 | tf_op jit(solution)/shard_map/ppermute | solution.py:60
  73.9 13.4 %collective-permute-start.5 = (bf16[32,1536]{1,0:T(8,128)(2,1)}, bf16[32,1536]{1,0:T(8,128)(2,1)S(1)}, u32[]{:S(2)}, u32[]{:S(2)}) collective-permute-start(bf16[32,1536]{1,0:T(8,128)(2,1)} %get-tuple-element.49), channel_id=1, source_target_pairs={{0,224},{16,240},{32,0},{48,16},{64,32},{80,48},{96,64},{112,80},{... | collective-permute-start | bytes 294920 | tf_op jit(solution)/shard_map/ppermute | solution.py:60
  80.0 8.9 %collective-permute-start.6 = (bf16[32,1536]{1,0:T(8,128)(2,1)}, bf16[32,1536]{1,0:T(8,128)(2,1)S(1)}, u32[]{:S(2)}, u32[]{:S(2)}) collective-permute-start(bf16[32,1536]{1,0:T(8,128)(2,1)} %get-tuple-element.50), channel_id=1, source_target_pairs={{0,32},{16,48},{32,64},{48,80},{64,96},{80,112},{96,128},{112,144}... | collective-permute-start | bytes 294920 | tf_op jit(solution)/shard_map/ppermute | solution.py:60
  84.2 14.0 %copy-start.17 = (bf16[32,1536]{1,0:T(8,128)(2,1)}, bf16[32,1536]{1,0:T(8,128)(2,1)S(1)}, u32[]{:S(2)}) copy-start(bf16[32,1536]{1,0:T(8,128)(2,1)S(1)} %collective-permute-done.11.refs_7_) | copy-start | bytes 294916
  84.2 10.6 %collective-permute-start.7 = (bf16[32,1536]{1,0:T(8,128)(2,1)}, bf16[32,1536]{1,0:T(8,128)(2,1)S(1)}, u32[]{:S(2)}, u32[]{:S(2)}) collective-permute-start(bf16[32,1536]{1,0:T(8,128)(2,1)} %get-tuple-element.51), channel_id=1, source_target_pairs={{0,192},{16,208},{32,224},{48,240},{64,0},{80,16},{96,32},{112,48}... | collective-permute-start | bytes 294920 | tf_op jit(solution)/shard_map/ppermute | solution.py:60
  87.3 11.0 %copy-start.18 = (bf16[32,1536]{1,0:T(8,128)(2,1)}, bf16[32,1536]{1,0:T(8,128)(2,1)S(1)}, u32[]{:S(2)}) copy-start(bf16[32,1536]{1,0:T(8,128)(2,1)S(1)} %collective-permute-done.5.refs_1_) | copy-start | bytes 294916
  87.3 8.0 %collective-permute-start.8 = (bf16[32,1536]{1,0:T(8,128)(2,1)}, bf16[32,1536]{1,0:T(8,128)(2,1)S(1)}, u32[]{:S(2)}, u32[]{:S(2)}) collective-permute-start(bf16[32,1536]{1,0:T(8,128)(2,1)} %get-tuple-element.52), channel_id=1, source_target_pairs={{0,64},{16,80},{32,96},{48,112},{64,128},{80,144},{96,160},{112,17... | collective-permute-start | bytes 294920 | tf_op jit(solution)/shard_map/ppermute | solution.py:60
  88.9 9.4 %copy-start.19 = (bf16[32,1536]{1,0:T(8,128)(2,1)}, bf16[32,1536]{1,0:T(8,128)(2,1)S(1)}, u32[]{:S(2)}) copy-start(bf16[32,1536]{1,0:T(8,128)(2,1)S(1)} %collective-permute-done.6.refs_2_) | copy-start | bytes 294916
  88.9 9.4 %collective-permute-start.9 = (bf16[32,1536]{1,0:T(8,128)(2,1)}, bf16[32,1536]{1,0:T(8,128)(2,1)S(1)}, u32[]{:S(2)}, u32[]{:S(2)}) collective-permute-start(bf16[32,1536]{1,0:T(8,128)(2,1)} %get-tuple-element.53), channel_id=1, source_target_pairs={{0,160},{16,176},{32,192},{48,208},{64,224},{80,240},{96,0},{112,1... | collective-permute-start | bytes 294920 | tf_op jit(solution)/shard_map/ppermute | solution.py:60
  94.8 3.5 %copy-start.20 = (bf16[32,1536]{1,0:T(8,128)(2,1)}, bf16[32,1536]{1,0:T(8,128)(2,1)S(1)}, u32[]{:S(2)}) copy-start(bf16[32,1536]{1,0:T(8,128)(2,1)S(1)} %collective-permute-done.7.refs_3_) | copy-start | bytes 294916
  95.3 3.0 %copy-start.21 = (bf16[32,1536]{1,0:T(8,128)(2,1)}, bf16[32,1536]{1,0:T(8,128)(2,1)S(1)}, u32[]{:S(2)}) copy-start(bf16[32,1536]{1,0:T(8,128)(2,1)S(1)} %collective-permute-done.8.refs_4_) | copy-start | bytes 294916
  98.3 0.6 copy-start.22
  102.0 0.9 copy-start.8
  103.9 0.7 copy-start.3
  104.7 0.9 copy-start.5
  105.6 0.9 copy-start.6
  106.8 18.2 %copy-start.4 = (bf16[384,512]{1,0:T(8,128)(2,1)S(1)}, bf16[384,512]{1,0:T(8,128)(2,1)}, u32[]{:S(2)}) copy-start(bf16[384,512]{1,0:T(8,128)(2,1)} %copy-done.3) | copy-start | bytes 1179652
  125.5 1.7 collective-permute-start.15
  146.3 3.8 %collective-permute-start.16 = (bf16[24,384]{1,0:T(8,128)(2,1)S(1)}, bf16[24,384]{1,0:T(8,128)(2,1)S(1)}, u32[]{:S(2)}, u32[]{:S(2)}) collective-permute-start(bf16[24,384]{1,0:T(8,128)(2,1)S(1)} %get-tuple-element.62), channel_id=1, source_target_pairs={{0,2},{1,3},{2,0},{3,1},{4,6},{5,7},{6,4},{7,5},{8,10},{9,11},{10,... | collective-permute-start | bytes 55304 | tf_op jit(solution)/shard_map/ppermute | solution.py:72
  151.1 20.9 %all-to-all-start.4 = ((bf16[16,2,24,384]{3,2,1,0:T(8,128)(2,1)}), bf16[16,2,24,384]{3,2,1,0:T(8,128)(2,1)S(1)}, u32[]{:S(2)}, u32[]{:S(2)}) async-start(bf16[16,2,24,384]{3,2,1,0:T(8,128)(2,1)} %broadcast_in_dim.8), calls=%async_computation.4 | async-start | bytes 1179648 | tf_op jit(solution)/shard_map/all_to_all | solution.py:357
  154.9 1.3 collective-permute-start.14

commit v9 on v6

--- a/solution.py
+++ b/solution.py
@@ -110,11 +110,11 @@
     blocks, own, partner = refs[4:20], refs[20], refs[21]
     image_out, keep_ref, send_ref, texts, images, slopes = refs[22:]
     sub, width = blocks[0].shape
-    for i, block in enumerate(blocks):
-        texts[pl.ds(i * sub, sub), :] = block[...]
     scale, bias = numbers[0], numbers[1]
     rows = own.shape[0]
     pieces = rows // sub
+    for i, block in enumerate(blocks):
+        texts[pl.ds(i * sub, sub), :] = block[...]
     for part, source in enumerate((own, partner)):
         place = pl.ds(part * rows, rows)
         images[place, :] = normalize(source[...])[0].astype(BF16)
@@ -230,24 +230,17 @@
     core, chip = mp_index % 2, mp_index // 2
     z, y = dp_index // 2, dp_index % 2
 
+    same_y = [[2 * s + t for s in range(8)] for t in range(2)]
+
+    def over_z(value):
+        return lax.all_to_all(value, "dp", 0, 0, tiled=True, axis_index_groups=same_y)
+
     texts = local(normalize_kernel, ((sub, width), BF16), [txt_emb], 4)
     blocks = [texts] + [along_z(texts, steps) for steps in ALONG[1:]]
     blocks += [swap_core(block) for block in blocks]
-    mine = jnp.where(y == 0, img_feat_t, txt_feat_t)
-    came = swap_y(jnp.where(y == 0, txt_feat_t, img_feat_t))
     by_core = img_emb.reshape(8, 2, sub, width)
     own = lax.dynamic_slice_in_dim(by_core, core, 1, 1).reshape(half, width)
-    own, came = lax.optimization_barrier((own, came))
     partner = swap_y(own)
-    pair = jnp.concatenate([mine, came])
-    pair_x = swap_x(pair)
-    feat_part = local(
-        feature_kernel,
-        ((4 * feats, rows), BF16),
-        [jnp.stack([y, core]), pair, pair_x, swap_core(pair), swap_core(pair_x)],
-        8,
-        [SMEM] + [VMEM] * 4,
-    )
 
     owners = jnp.stack([2 * ((z - steps) % 8) + y for steps in ALONG])
     cores = jnp.stack([mp_index, mp_index ^ 1])
@@ -260,7 +253,6 @@
     )
     places = jnp.stack([8 * y, 8 * (1 - y)])
     numbers = jnp.concatenate([logit_scale, logit_bias])
-    numbers, feat_part = lax.optimization_barrier((numbers, feat_part))
     image_part, keep, send = local(
         tile_kernel,
         [((16, sub, full), BF16), ((half, width), F32), ((half, width), BF16)],
@@ -290,10 +282,24 @@
             value, ("dp", "mp"), 0, 0, tiled=True, axis_index_groups=plane
         )
 
+    came_grad = swap_core(send)
+    mine = jnp.where(y == 0, img_feat_t, txt_feat_t)
+    theirs = jnp.where(y == 0, txt_feat_t, img_feat_t)
+    mine, theirs, partner = lax.optimization_barrier((mine, theirs, partner))
+    pair = jnp.concatenate([mine, swap_y(theirs)])
+    pair_x = swap_x(pair)
+    image_part, came_grad, pair_x = lax.optimization_barrier((image_part, came_grad, pair_x))
+    feat_part = local(
+        feature_kernel,
+        ((4 * feats, rows), BF16),
+        [jnp.stack([y, core]), pair, pair_x, swap_core(pair), swap_core(pair_x)],
+        8,
+        [SMEM] + [VMEM] * 4,
+    )
     text_parts = local(
         join_kernel,
         [((sub, width), BF16)] * 8,
-        [keep, swap_core(send)],
+        [keep, came_grad],
         WHOLE,
         None,
         [HBM] * 8,
@@ -303,10 +309,11 @@
     text_came = [text_parts[0]] + [
         along_z(part, -steps) for part, steps in zip(text_parts[1:], ALONG[1:], strict=True)
     ]
+    raw_txt, feat_part = lax.optimization_barrier((txt_emb, feat_part))
     d_txt = local(
         text_kernel,
         ((sub, width), BF16),
-        [*text_came, txt_emb],
+        [*text_came, raw_txt],
         WHOLE,
         [ANY] * 8 + [VMEM],
         None,
@@ -331,8 +338,7 @@
     )
     shape = (feats // 4, narrow // 2)
     cut = local(cut_kernel, ((8, 2, *shape), BF16), [kept, swap_core(sent)], 6)
-    same_y = [[2 * s + t for s in range(8)] for t in range(2)]
-    parts = lax.all_to_all(cut, "dp", 0, 0, tiled=True, axis_index_groups=same_y)
+    parts = over_z(cut)
     own_sum, other_sum = local(sum_kernel, [(shape, BF16)] * 2, [parts], 6)
     summed = jnp.stack([own_sum, swap_x(other_sum)])
     weights = lax.all_to_all(

time: 166 us -> 166 us (level)
  waiting for transfers between devices: 39.7 us -> 42.2 us
  other arithmetic: 3.96 us -> 1.7 us
  blocking collectives: 41.4 us -> 39.6 us
    ppermute x2, waiting for transfers between devices: 2.3 us -> 8.28 us  [swap_x(): return lax.ppermute(value, 'mp', [(m, m ^ 2) for m in range(16)])]
    ppermute x14, waiting for transfers between devices: 12.3 us -> 9.31 us  [along_z(): lax.ppermute(value, 'dp', [(d, (d + 2 * steps) % 16) for d in range(16)])]
    ppermute x13, waiting for transfers between devices: 7.19 us -> 4.63 us  [swap_core(): return lax.ppermute(value, 'mp', [(m, m ^ 1) for m in range(16)])]
    all_to_all x1, blocking collectives: 20.9 us -> 18.4 us  [over_z(): lax.all_to_all(value, 'dp', 0, 0, tiled=True, axis_index_groups=same_y)]
    ppermute x2, waiting for transfers between devices: 2.72 us -> 4.9 us  [swap_y(): return lax.ppermute(value, 'dp', [(d, d ^ 1) for d in range(16)])]
    unnamed x42 -> x49, local copies, waits for them, and re-layouts: 10.5 us -> 10.8 us
  transfers between devices with their start and end apart: 33 -> 33, of which waited for: 16 -> 17; matrix products, arithmetic and copies ran while one was open for 3% -> 2% of each run, Pallas kernels for 4% -> 4%
where the time goes in v9:
time: 166 us; the launch traced here: 165 us
  starting transfers between devices  51.7 us (31%)
  waiting for transfers between devices  42.2 us (25%)
  blocking collectives  39.6 us (24%)
  Pallas kernels  14.3 us (9%)
  local copies, waits for them, and re-layouts  13.5 us (8%)
  between operations  2.31 us (1%)
  other arithmetic  1.7 us (1%)
    ppermute x14, starting transfers between devices, along_z(): lax.ppermute(value, 'dp', [(d, (d + 2 * steps) % 16) for d in range(16)])  33.3 us
    all_to_all x1, blocking collectives, over_plane(): lax.all_to_all(value, ('dp', 'mp'), 0, 0, tiled=True, axis_index_groups=p...  21.2 us
    all_to_all x1, blocking collectives, over_z(): lax.all_to_all(value, 'dp', 0, 0, tiled=True, axis_index_groups=same_y)  18.4 us
    all_to_all x1, waiting for transfers between devices, shards(): lax.all_to_all(jnp.broadcast_to(summed[None], (16, 2, *shape)), 'dp', 0,...  15.1 us
    pallas_call x10, Pallas kernels, local(): pl.pallas_call(kernel, out_shape=shapes, in_specs=specs or [VMEM] * len(o...  14.3 us
    unnamed x49, local copies, waits for them, and re-layouts  10.8 us
    ppermute x14, waiting for transfers between devices, along_z(): lax.ppermute(value, 'dp', [(d, (d + 2 * steps) % 16) for d in range(16)])  9.31 us
    ppermute x2, waiting for transfers between devices, swap_x(): return lax.ppermute(value, 'mp', [(m, m ^ 2) for m in range(16)])  8.28 us
  transfers between devices with their start and end apart: 33, of which 17 were waited for; matrix products, arithmetic and copies ran while one was open for 2% of the time, Pallas kernels for 4%

profile of v9, /device:TPU:2, one launch (start us, length us, event | category | flops | bytes accessed | tf_op | source)
XLA Modules:
  0.0 165.3 jit_solution(16336844285761420825)
XLA Ops:
  0.7 1.0 copy-done.7
  1.8 3.3 %collective-permute-start.2 = (bf16[32,1536]{1,0:T(8,128)(2,1)S(1)}, bf16[32,1536]{1,0:T(8,128)(2,1)S(1)}, u32[]{:S(2)}, u32[]{:S(2)}) collective-permute-start(bf16[32,1536]{1,0:T(8,128)(2,1)S(1)} %shard_map.85.refs_4_), channel_id=1, source_target_pairs={{0,64},{16,80},{32,96},{48,112},{64,128},{80,144},{96,160},{112,17... | collective-permute-start | bytes 294920 | tf_op jit(solution)/shard_map/ppermute | solution.py:59
  5.1 3.1 %collective-permute-start.3 = (bf16[32,1536]{1,0:T(8,128)(2,1)S(1)}, bf16[32,1536]{1,0:T(8,128)(2,1)S(1)}, u32[]{:S(2)}, u32[]{:S(2)}) collective-permute-start(bf16[32,1536]{1,0:T(8,128)(2,1)S(1)} %shard_map.85.refs_4_), channel_id=1, source_target_pairs={{0,192},{16,208},{32,224},{48,240},{64,0},{80,16},{96,32},{112,48}... | collective-permute-start | bytes 294920 | tf_op jit(solution)/shard_map/ppermute | solution.py:59
  8.2 1.8 %collective-permute-start.4 = (bf16[32,1536]{1,0:T(8,128)(2,1)S(1)}, bf16[32,1536]{1,0:T(8,128)(2,1)S(1)}, u32[]{:S(2)}, u32[]{:S(2)}) collective-permute-start(bf16[32,1536]{1,0:T(8,128)(2,1)S(1)} %shard_map.85.refs_4_), channel_id=1, source_target_pairs={{0,96},{16,112},{32,128},{48,144},{64,160},{80,176},{96,192},{112,... | collective-permute-start | bytes 294920 | tf_op jit(solution)/shard_map/ppermute | solution.py:59
  10.1 3.2 %collective-permute-start.5 = (bf16[32,1536]{1,0:T(8,128)(2,1)S(1)}, bf16[32,1536]{1,0:T(8,128)(2,1)}, u32[]{:S(2)}, u32[]{:S(2)}) collective-permute-start(bf16[32,1536]{1,0:T(8,128)(2,1)S(1)} %shard_map.85.refs_4_), channel_id=1, source_target_pairs={{0,160},{16,176},{32,192},{48,208},{64,224},{80,240},{96,0},{112,1... | collective-permute-start | bytes 294920 | tf_op jit(solution)/shard_map/ppermute | solution.py:59
  13.4 1.7 %collective-permute-start.15 = (bf16[256,1536]{1,0:T(8,128)(2,1)S(1)}, bf16[256,1536]{1,0:T(8,128)(2,1)S(1)}, u32[]{:S(2)}, u32[]{:S(2)}) collective-permute-start(bf16[256,1536]{1,0:T(8,128)(2,1)S(1)} %bitcast.26), channel_id=1, source_target_pairs={{0,16},{16,0},{32,48},{48,32},{64,80},{80,64},{96,112},{112,96},{1... | collective-permute-start | bytes 2359304 | tf_op jit(solution)/shard_map/ppermute | solution.py:63
  15.4 5.0 %collective-permute-start.6 = (bf16[32,1536]{1,0:T(8,128)(2,1)S(1)}, bf16[32,1536]{1,0:T(8,128)(2,1)}, u32[]{:S(2)}, u32[]{:S(2)}) collective-permute-start(bf16[32,1536]{1,0:T(8,128)(2,1)S(1)} %shard_map.85.refs_4_), channel_id=1, source_target_pairs={{0,128},{16,144},{32,160},{48,176},{64,192},{80,208},{96,224},{112... | collective-permute-start | bytes 294920 | tf_op jit(solution)/shard_map/ppermute | solution.py:59
  20.4 1.0 collective-permute-start
  21.4 2.2 %collective-permute-start.1 = (bf16[32,1536]{1,0:T(8,128)(2,1)S(1)}, bf16[32,1536]{1,0:T(8,128)(2,1)}, u32[]{:S(2)}, u32[]{:S(2)}) collective-permute-start(bf16[32,1536]{1,0:T(8,128)(2,1)S(1)} %shard_map.85.refs_4_), channel_id=1, source_target_pairs={{0,224},{16,240},{32,0},{48,16},{64,32},{80,48},{96,64},{112,80},{... | collective-permute-start | bytes 294920 | tf_op jit(solution)/shard_map/ppermute | solution.py:59
  25.3 1.3 collective-permute-done.6.refs_11_
  26.6 0.5 collective-permute-done.refs_5_
  27.1 0.4 collective-permute-done.1.refs_6_
  27.7 0.5 collective-permute-start.13
  28.3 0.3 collective-permute-done.11.refs_16_
  28.8 0.3 collective-permute-done.12.refs_17_
  29.3 0.4 collective-permute-done.14.refs_19_
  29.7 0.4 collective-permute-done.8.refs_13_
  30.1 0.5 collective-permute-done.9.refs_14_
  30.6 1.3 collective-permute-done.15.refs_21_
  31.9 0.9 copy-done.11
  32.8 0.9 copy-done.13
  33.7 0.9 copy-done.15
  34.6 5.5 %shard_map.86 = (bf16[16,32,1664]{2,1,0:T(8,128)(2,1)S(1)}, f32[256,1536]{1,0:T(8,128)S(1)}, bf16[256,1536]{1,0:T(8,128)(2,1)}) custom-call(f32[2]{0:T(128)S(1)} %pad_maximum_fusion.1.refs_0_, s32[2]{0:T(128)S(1)} %pad_add_fusion.1.refs_1_, s32[1,512]{1,0:T(1,128)S(1)} %add.179.refs_2_, s32[512,1]{1,0:T(8,128)S(1)} %copy.11.refs_3_, ...), custom_call_target="tpu_custom_call" | custom-call | tf_op jit(solution)/shard_map/pallas_call | solution.py:23
  40.0 1.2 copy-done.1
  41.3 1.1 copy-done.2
  42.4 1.0 broadcast_select_fusion
  43.4 1.7 %collective-permute-start.17 = (bf16[96,512]{1,0:T(8,128)(2,1)S(1)}, bf16[96,512]{1,0:T(8,128)(2,1)S(1)}, u32[]{:S(2)}, u32[]{:S(2)}) collective-permute-start(bf16[96,512]{1,0:T(8,128)(2,1)S(1)} %get-tuple-element.30), channel_id=1, source_target_pairs={{0,16},{16,0},{32,48},{48,32},{64,80},{80,64},{96,112},{112,96},{1... | collective-permute-start | bytes 294920 | tf_op jit(solution)/shard_map/ppermute | solution.py:63
  45.0 3.6 %collective-permute-done.17 = bf16[96,512]{1,0:T(8,128)(2,1)S(1)} collective-permute-done((bf16[96,512]{1,0:T(8,128)(2,1)S(1)}, bf16[96,512]{1,0:T(8,128)(2,1)S(1)}, u32[]{:S(2)}, u32[]{:S(2)}) %collective-permute-start.17) | collective-permute-done | bytes 98336 | tf_op jit(solution)/shard_map/ppermute | solution.py:63
  48.7 0.6 collective-permute-start.18
  49.3 6.0 %collective-permute-done.18.refs_1_ = bf16[192,512]{1,0:T(8,128)(2,1)S(1)} collective-permute-done((bf16[192,512]{1,0:T(8,128)(2,1)S(1)}, bf16[192,512]{1,0:T(8,128)(2,1)S(1)}, u32[]{:S(2)}, u32[]{:S(2)}) %collective-permute-start.18) | collective-permute-done | bytes 196640 | tf_op jit(solution)/shard_map/ppermute | solution.py:71
  55.3 0.7 copy-done.8
  56.0 0.9 copy-done.16
  56.9 7.5 %all-to-all-start = ((bf16[16,32,1664]{2,1,0:T(8,128)(2,1)}), bf16[16,32,1664]{2,1,0:T(8,128)(2,1)S(1)}, u32[]{:S(2)}, u32[]{:S(2)}) async-start(bf16[16,32,1664]{2,1,0:T(8,128)(2,1)} %copy-done.1), calls=%async_computation | async-start | bytes 3407872 | tf_op jit(solution)/shard_map/all_to_all | solution.py:281
  64.5 0.5 collective-permute-start.27
  64.9 2.7 %shard_map.87 = (bf16[32,1536]{1,0:T(8,128)(2,1)}, bf16[32,1536]{1,0:T(8,128)(2,1)}, bf16[32,1536]{1,0:T(8,128)(2,1)}, bf16[32,1536]{1,0:T(8,128)(2,1)}, bf16[32...) custom-call(f32[256,1536]{1,0:T(8,128)} %copy-done.2, ...), custom_call_target="tpu_custom_call" | custom-call | tf_op jit(solution)/shard_map/pallas_call | solution.py:23
  67.6 0.9 collective-permute-start.19
  68.5 1.2 collective-permute-start.20
  69.7 0.6 constant_dynamic-slice_fusion.raw_img
  70.4 2.7 %collective-permute-start.21 = (bf16[32,1536]{1,0:T(8,128)(2,1)}, bf16[32,1536]{1,0:T(8,128)(2,1)S(1)}, u32[]{:S(2)}, u32[]{:S(2)}) collective-permute-start(bf16[32,1536]{1,0:T(8,128)(2,1)} %get-tuple-element.37), channel_id=1, source_target_pairs={{0,192},{16,208},{32,224},{48,240},{64,0},{80,16},{96,32},{112,48}... | collective-permute-start | bytes 294920 | tf_op jit(solution)/shard_map/ppermute | solution.py:59
  73.1 0.2 collective-permute-start.22
  73.3 4.2 %collective-permute-start.23 = (bf16[32,1536]{1,0:T(8,128)(2,1)}, bf16[32,1536]{1,0:T(8,128)(2,1)S(1)}, u32[]{:S(2)}, u32[]{:S(2)}) collective-permute-start(bf16[32,1536]{1,0:T(8,128)(2,1)} %get-tuple-element.39), channel_id=1, source_target_pairs={{0,160},{16,176},{32,192},{48,208},{64,224},{80,240},{96,0},{112,1... | collective-permute-start | bytes 294920 | tf_op jit(solution)/shard_map/ppermute | solution.py:59
  77.5 0.4 collective-permute-start.24
  77.9 3.9 %collective-permute-start.25 = (bf16[32,1536]{1,0:T(8,128)(2,1)}, bf16[32,1536]{1,0:T(8,128)(2,1)S(1)}, u32[]{:S(2)}, u32[]{:S(2)}) collective-permute-start(bf16[32,1536]{1,0:T(8,128)(2,1)} %get-tuple-element.41), channel_id=1, source_target_pairs={{0,128},{16,144},{32,160},{48,176},{64,192},{80,208},{96,224},{112... | collective-permute-start | bytes 294920 | tf_op jit(solution)/shard_map/ppermute | solution.py:59
  81.9 1.0 shard_map.88.feats_ref
  82.9 0.7 copy-done.3
  83.6 4.6 %collective-permute-done.24.refs_6_ = bf16[32,1536]{1,0:T(8,128)(2,1)S(1)} collective-permute-done((bf16[32,1536]{1,0:T(8,128)(2,1)}, bf16[32,1536]{1,0:T(8,128)(2,1)S(1)}, u32[]{:S(2)}, u32[]{:S(2)}) %collective-permute-start.24) | collective-permute-done | bytes 98336 | tf_op jit(solution)/shard_map/ppermute | solution.py:59
  88.2 2.5 %collective-permute-done.25.refs_7_ = bf16[32,1536]{1,0:T(8,128)(2,1)S(1)} collective-permute-done((bf16[32,1536]{1,0:T(8,128)(2,1)}, bf16[32,1536]{1,0:T(8,128)(2,1)S(1)}, u32[]{:S(2)}, u32[]{:S(2)}) %collective-permute-start.25) | collective-permute-done | bytes 98336 | tf_op jit(solution)/shard_map/ppermute | solution.py:59
  90.7 0.6 copy-done.23
  91.3 3.0 %shard_map.89.d_txt = bf16[32,1536]{1,0:T(8,128)(2,1)} custom-call(bf16[32,1536]{1,0:T(8,128)(2,1)} %get-tuple-element.34.refs_0_, bf16[32,1536]{1,0:T(8,128)(2,1)} %copy-done.17, bf16[32,1536]{1,0:T(8,128)(2,1)} %copy-done.18, bf16[32,1536]{1,0:T(8,128)(2,1)} %copy-done.19, bf16[32,1536]{1,0:T(8,128)(2,1)} %copy-done.20, bf16[32,1536]{1,0:T(8,128)(2,1)} %copy-done.21, ...), custom_call_target="tpu_custom_call" | custom-call | tf_op jit(solution)/shard_map/pallas_call | solution.py:23
  94.4 0.9 copy-done.5
  95.3 0.9 copy-done.6
  96.2 0.4 shard_map.90
  96.6 21.2 %all_to_all.20.grads_ref = bf16[16,32,896]{2,1,0:T(8,128)(2,1)S(1)} all-to-all(bf16[16,32,896]{2,1,0:T(8,128)(2,1)S(1)} %bitcast.29), channel_id=1, replica_groups={{0,2,4,6,8,10,12,14,16,18,20,22,24,26,28,30},{1,3,5,7,9,11,13,15,17,19,..., dimensions={0} | all-to-all | bytes 1835008 | tf_op jit(solution)/shard_map/all_to_all | solution.py:281
  117.8 0.5 shard_map.91
  118.4 1.6 collective-permute-done.29.came_ref
  120.0 18.4 %all_to_all.21.parts_ref = bf16[8,2,24,384]{3,2,1,0:T(8,128)(2,1)S(1)} all-to-all(bf16[8,2,24,384]{3,2,1,0:T(8,128)(2,1)S(1)} %shard_map.92), channel_id=1, replica_groups={{0,32,64,96,128,160,192,224},{16,48,80,112,144,176,208,240},{1,33,65,97..., dimensions={0} | all-to-all | bytes 589824 | tf_op jit(solution)/shard_map/all_to_all | solution.py:236
  138.5 1.5 collective-permute-start.30
  140.1 2.3 %collective-permute-done.30 = bf16[24,384]{1,0:T(8,128)(2,1)S(1)} collective-permute-done((bf16[24,384]{1,0:T(8,128)(2,1)S(1)}, bf16[24,384]{1,0:T(8,128)(2,1)S(1)}, u32[]{:S(2)}, u32[]{:S(2)}) %collective-permute-start.30) | collective-permute-done | bytes 18464 | tf_op jit(solution)/shard_map/ppermute | solution.py:71
  142.4 0.9 broadcast_in_dim.5
  143.2 3.6 %all-to-all-start.3 = ((bf16[16,2,24,384]{3,2,1,0:T(8,128)(2,1)}), bf16[16,2,24,384]{3,2,1,0:T(8,128)(2,1)S(1)}, u32[]{:S(2)}, u32[]{:S(2)}) async-start(bf16[16,2,24,384]{3,2,1,0:T(8,128)(2,1)} %broadcast_in_dim.5), calls=%async_computation.3 | async-start | bytes 1179648 | tf_op jit(solution)/shard_map/all_to_all | solution.py:344
  147.2 1.1 collective-permute-done.28
  148.4 0.7 select_n.135
  149.1 15.1 %all-to-all-done.3.parts_ref = bf16[16,2,24,384]{3,2,1,0:T(8,128)(2,1)S(1)} async-done(((bf16[16,2,24,384]{3,2,1,0:T(8,128)(2,1)}), bf16[16,2,24,384]{3,2,1,0:T(8,128)(2,1)S(1)}, u32[]{:S(2)}, u32[]{:S(2)}) %all-to-all-start.3) | async-done | bytes 589856 | tf_op jit(solution)/shard_map/all_to_all | solution.py:344
  164.2 1.1 shard_map.94
  (88 shorter events, 2.4 us)
Async XLA Ops:
  0.6 12.6 %copy-start = (bf16[512,1536]{1,0:T(8,128)(2,1)S(1)}, bf16[512,1536]{1,0:T(8,128)(2,1)}, u32[]{:S(2)}) copy-start(bf16[512,1536]{1,0:T(8,128)(2,1)} %param.6) | copy-start | bytes 4718596
  0.6 1.0 copy-start.7
  1.8 13.6 %collective-permute-start.2 = (bf16[32,1536]{1,0:T(8,128)(2,1)S(1)}, bf16[32,1536]{1,0:T(8,128)(2,1)S(1)}, u32[]{:S(2)}, u32[]{:S(2)}) collective-permute-start(bf16[32,1536]{1,0:T(8,128)(2,1)S(1)} %shard_map.85.refs_4_), channel_id=1, source_target_pairs={{0,64},{16,80},{32,96},{48,112},{64,128},{80,144},{96,160},{112,17... | collective-permute-start | bytes 294920 | tf_op jit(solution)/shard_map/ppermute | solution.py:59
  5.1 15.3 %collective-permute-start.3 = (bf16[32,1536]{1,0:T(8,128)(2,1)S(1)}, bf16[32,1536]{1,0:T(8,128)(2,1)S(1)}, u32[]{:S(2)}, u32[]{:S(2)}) collective-permute-start(bf16[32,1536]{1,0:T(8,128)(2,1)S(1)} %shard_map.85.refs_4_), channel_id=1, source_target_pairs={{0,192},{16,208},{32,224},{48,240},{64,0},{80,16},{96,32},{112,48}... | collective-permute-start | bytes 294920 | tf_op jit(solution)/shard_map/ppermute | solution.py:59
  8.2 13.2 %collective-permute-start.4 = (bf16[32,1536]{1,0:T(8,128)(2,1)S(1)}, bf16[32,1536]{1,0:T(8,128)(2,1)S(1)}, u32[]{:S(2)}, u32[]{:S(2)}) collective-permute-start(bf16[32,1536]{1,0:T(8,128)(2,1)S(1)} %shard_map.85.refs_4_), channel_id=1, source_target_pairs={{0,96},{16,112},{32,128},{48,144},{64,160},{80,176},{96,192},{112,... | collective-permute-start | bytes 294920 | tf_op jit(solution)/shard_map/ppermute | solution.py:59
  10.1 15.1 %collective-permute-start.5 = (bf16[32,1536]{1,0:T(8,128)(2,1)S(1)}, bf16[32,1536]{1,0:T(8,128)(2,1)}, u32[]{:S(2)}, u32[]{:S(2)}) collective-permute-start(bf16[32,1536]{1,0:T(8,128)(2,1)S(1)} %shard_map.85.refs_4_), channel_id=1, source_target_pairs={{0,160},{16,176},{32,192},{48,208},{64,224},{80,240},{96,0},{112,1... | collective-permute-start | bytes 294920 | tf_op jit(solution)/shard_map/ppermute | solution.py:59
  13.4 18.5 %collective-permute-start.15 = (bf16[256,1536]{1,0:T(8,128)(2,1)S(1)}, bf16[256,1536]{1,0:T(8,128)(2,1)S(1)}, u32[]{:S(2)}, u32[]{:S(2)}) collective-permute-start(bf16[256,1536]{1,0:T(8,128)(2,1)S(1)} %bitcast.26), channel_id=1, source_target_pairs={{0,16},{16,0},{32,48},{48,32},{64,80},{80,64},{96,112},{112,96},{1... | collective-permute-start | bytes 2359304 | tf_op jit(solution)/shard_map/ppermute | solution.py:63
  15.3 8.3 %copy-start.10 = (bf16[32,1536]{1,0:T(8,128)(2,1)}, bf16[32,1536]{1,0:T(8,128)(2,1)S(1)}, u32[]{:S(2)}) copy-start(bf16[32,1536]{1,0:T(8,128)(2,1)S(1)} %collective-permute-done.2.refs_7_) | copy-start | bytes 294916
  15.4 11.3 %collective-permute-start.6 = (bf16[32,1536]{1,0:T(8,128)(2,1)S(1)}, bf16[32,1536]{1,0:T(8,128)(2,1)}, u32[]{:S(2)}, u32[]{:S(2)}) collective-permute-start(bf16[32,1536]{1,0:T(8,128)(2,1)S(1)} %shard_map.85.refs_4_), channel_id=1, source_target_pairs={{0,128},{16,144},{32,160},{48,176},{64,192},{80,208},{96,224},{112... | collective-permute-start | bytes 294920 | tf_op jit(solution)/shard_map/ppermute | solution.py:59
  20.4 3.3 %copy-start.12 = (bf16[32,1536]{1,0:T(8,128)(2,1)}, bf16[32,1536]{1,0:T(8,128)(2,1)S(1)}, u32[]{:S(2)}) copy-start(bf16[32,1536]{1,0:T(8,128)(2,1)S(1)} %collective-permute-done.3.refs_8_) | copy-start | bytes 294916
  20.4 6.7 %collective-permute-start = (bf16[32,1536]{1,0:T(8,128)(2,1)S(1)}, bf16[32,1536]{1,0:T(8,128)(2,1)}, u32[]{:S(2)}, u32[]{:S(2)}) collective-permute-start(bf16[32,1536]{1,0:T(8,128)(2,1)S(1)} %shard_map.85.refs_4_), channel_id=1, source_target_pairs={{0,32},{16,48},{32,64},{48,80},{64,96},{80,112},{96,128},{112,144}... | collective-permute-start | bytes 294920 | tf_op jit(solution)/shard_map/ppermute | solution.py:59
  21.4 2.2 %copy-start.14 = (bf16[32,1536]{1,0:T(8,128)(2,1)}, bf16[32,1536]{1,0:T(8,128)(2,1)S(1)}, u32[]{:S(2)}) copy-start(bf16[32,1536]{1,0:T(8,128)(2,1)S(1)} %collective-permute-done.4.refs_9_) | copy-start | bytes 294916
  21.4 6.2 %collective-permute-start.1 = (bf16[32,1536]{1,0:T(8,128)(2,1)S(1)}, bf16[32,1536]{1,0:T(8,128)(2,1)}, u32[]{:S(2)}, u32[]{:S(2)}) collective-permute-start(bf16[32,1536]{1,0:T(8,128)(2,1)S(1)} %shard_map.85.refs_4_), channel_id=1, source_target_pairs={{0,224},{16,240},{32,0},{48,16},{64,32},{80,48},{96,64},{112,80},{... | collective-permute-start | bytes 294920 | tf_op jit(solution)/shard_map/ppermute | solution.py:59
  25.2 2.5 %collective-permute-start.7 = (bf16[32,1536]{1,0:T(8,128)(2,1)S(1)}, bf16[32,1536]{1,0:T(8,128)(2,1)S(1)}, u32[]{:S(2)}, u32[]{:S(2)}) collective-permute-start(bf16[32,1536]{1,0:T(8,128)(2,1)S(1)} %shard_map.85.refs_4_), channel_id=1, source_target_pairs={{0,1},{1,0},{2,3},{3,2},{4,5},{5,4},{6,7},{7,6},{8,9},{9,8},{10,11... | collective-permute-start | bytes 294920 | tf_op jit(solution)/shard_map/ppermute | solution.py:67
  26.6 1.6 collective-permute-start.10
  27.1 1.5 collective-permute-start.11
  27.6 1.5 collective-permute-start.12
  27.7 1.6 collective-permute-start.13
  28.2 1.5 collective-permute-start.14
  28.6 1.5 collective-permute-start.8
  29.1 1.5 collective-permute-start.9
  31.9 0.9 copy-start.11
  32.8 0.9 copy-start.13
  33.7 0.9 copy-start.15
  40.0 1.2 copy-start.1
  41.3 1.1 copy-start.2
  42.4 13.6 %collective-permute-start.16 = (bf16[256,1536]{1,0:T(8,128)(2,1)}, bf16[256,1536]{1,0:T(8,128)(2,1)S(1)}, u32[]{:S(2)}, u32[]{:S(2)}) collective-permute-start(bf16[256,1536]{1,0:T(8,128)(2,1)} %get-tuple-element.28), channel_id=1, source_target_pairs={{0,1},{1,0},{2,3},{3,2},{4,5},{5,4},{6,7},{7,6},{8,9},{9,8},{10,11... | collective-permute-start | bytes 2359304 | tf_op jit(solution)/shard_map/ppermute | solution.py:67
  43.4 5.3 %collective-permute-start.17 = (bf16[96,512]{1,0:T(8,128)(2,1)S(1)}, bf16[96,512]{1,0:T(8,128)(2,1)S(1)}, u32[]{:S(2)}, u32[]{:S(2)}) collective-permute-start(bf16[96,512]{1,0:T(8,128)(2,1)S(1)} %get-tuple-element.30), channel_id=1, source_target_pairs={{0,16},{16,0},{32,48},{48,32},{64,80},{80,64},{96,112},{112,96},{1... | collective-permute-start | bytes 294920 | tf_op jit(solution)/shard_map/ppermute | solution.py:63
  48.7 6.6 %collective-permute-start.18 = (bf16[192,512]{1,0:T(8,128)(2,1)S(1)}, bf16[192,512]{1,0:T(8,128)(2,1)S(1)}, u32[]{:S(2)}, u32[]{:S(2)}) collective-permute-start(bf16[192,512]{1,0:T(8,128)(2,1)S(1)} %constant_dynamic-update-slice_fusion.refs_0_), channel_id=1, source_target_pairs={{0,2},{1,3},{2,0},{3,1},{4,6},{5,7},{6,4},{7,5},{8,10},{9,11},{10,... | collective-permute-start | bytes 589832 | tf_op jit(solution)/shard_map/ppermute | solution.py:71
  55.3 0.7 copy-start.8
  56.0 0.9 copy-start.16
  56.9 37.5 %all-to-all-start = ((bf16[16,32,1664]{2,1,0:T(8,128)(2,1)}), bf16[16,32,1664]{2,1,0:T(8,128)(2,1)S(1)}, u32[]{:S(2)}, u32[]{:S(2)}) async-start(bf16[16,32,1664]{2,1,0:T(8,128)(2,1)} %copy-done.1), calls=%async_computation | async-start | bytes 3407872 | tf_op jit(solution)/shard_map/all_to_all | solution.py:281
  64.3 17.5 %copy-start.9 = (bf16[192,512]{1,0:T(8,128)(2,1)S(1)}, bf16[192,512]{1,0:T(8,128)(2,1)}, u32[]{:S(2)}) copy-start(bf16[192,512]{1,0:T(8,128)(2,1)} %copy-done.8) | copy-start | bytes 589828
  64.3 8.8 %collective-permute-start.26 = (bf16[192,512]{1,0:T(8,128)(2,1)S(1)}, bf16[192,512]{1,0:T(8,128)(2,1)S(1)}, u32[]{:S(2)}, u32[]{:S(2)}) collective-permute-start(bf16[192,512]{1,0:T(8,128)(2,1)S(1)} %constant_dynamic-update-slice_fusion.refs_0_), channel_id=1, source_target_pairs={{0,1},{1,0},{2,3},{3,2},{4,5},{5,4},{6,7},{7,6},{8,9},{9,8},{10,11... | collective-permute-start | bytes 589832 | tf_op jit(solution)/shard_map/ppermute | solution.py:67
  64.5 13.5 %collective-permute-start.27 = (bf16[192,512]{1,0:T(8,128)(2,1)}, bf16[192,512]{1,0:T(8,128)(2,1)S(1)}, u32[]{:S(2)}, u32[]{:S(2)}) collective-permute-start(bf16[192,512]{1,0:T(8,128)(2,1)} %copy-done.8), channel_id=1, source_target_pairs={{0,1},{1,0},{2,3},{3,2},{4,5},{5,4},{6,7},{7,6},{8,9},{9,8},{10,11... | collective-permute-start | bytes 589832 | tf_op jit(solution)/shard_map/ppermute | solution.py:67
  67.6 5.7 %collective-permute-start.19 = (bf16[32,1536]{1,0:T(8,128)(2,1)}, bf16[32,1536]{1,0:T(8,128)(2,1)S(1)}, u32[]{:S(2)}, u32[]{:S(2)}) collective-permute-start(bf16[32,1536]{1,0:T(8,128)(2,1)} %get-tuple-element.35), channel_id=1, source_target_pairs={{0,224},{16,240},{32,0},{48,16},{64,32},{80,48},{96,64},{112,80},{... | collective-permute-start | bytes 294920 | tf_op jit(solution)/shard_map/ppermute | solution.py:59
  68.5 9.0 %collective-permute-start.20 = (bf16[32,1536]{1,0:T(8,128)(2,1)}, bf16[32,1536]{1,0:T(8,128)(2,1)S(1)}, u32[]{:S(2)}, u32[]{:S(2)}) collective-permute-start(bf16[32,1536]{1,0:T(8,128)(2,1)} %get-tuple-element.36), channel_id=1, source_target_pairs={{0,32},{16,48},{32,64},{48,80},{64,96},{80,112},{96,128},{112,144}... | collective-permute-start | bytes 294920 | tf_op jit(solution)/shard_map/ppermute | solution.py:59
  70.4 13.2 %collective-permute-start.21 = (bf16[32,1536]{1,0:T(8,128)(2,1)}, bf16[32,1536]{1,0:T(8,128)(2,1)S(1)}, u32[]{:S(2)}, u32[]{:S(2)}) collective-permute-start(bf16[32,1536]{1,0:T(8,128)(2,1)} %get-tuple-element.37), channel_id=1, source_target_pairs={{0,192},{16,208},{32,224},{48,240},{64,0},{80,16},{96,32},{112,48}... | collective-permute-start | bytes 294920 | tf_op jit(solution)/shard_map/ppermute | solution.py:59
  73.1 10.5 %collective-permute-start.22 = (bf16[32,1536]{1,0:T(8,128)(2,1)}, bf16[32,1536]{1,0:T(8,128)(2,1)S(1)}, u32[]{:S(2)}, u32[]{:S(2)}) collective-permute-start(bf16[32,1536]{1,0:T(8,128)(2,1)} %get-tuple-element.38), channel_id=1, source_target_pairs={{0,64},{16,80},{32,96},{48,112},{64,128},{80,144},{96,160},{112,17... | collective-permute-start | bytes 294920 | tf_op jit(solution)/shard_map/ppermute | solution.py:59
  73.3 17.4 %copy-start.17 = (bf16[32,1536]{1,0:T(8,128)(2,1)}, bf16[32,1536]{1,0:T(8,128)(2,1)S(1)}, u32[]{:S(2)}) copy-start(bf16[32,1536]{1,0:T(8,128)(2,1)S(1)} %collective-permute-done.19.refs_1_) | copy-start | bytes 294916
  73.3 10.3 %collective-permute-start.23 = (bf16[32,1536]{1,0:T(8,128)(2,1)}, bf16[32,1536]{1,0:T(8,128)(2,1)S(1)}, u32[]{:S(2)}, u32[]{:S(2)}) collective-permute-start(bf16[32,1536]{1,0:T(8,128)(2,1)} %get-tuple-element.39), channel_id=1, source_target_pairs={{0,160},{16,176},{32,192},{48,208},{64,224},{80,240},{96,0},{112,1... | collective-permute-start | bytes 294920 | tf_op jit(solution)/shard_map/ppermute | solution.py:59
  77.5 13.2 %copy-start.18 = (bf16[32,1536]{1,0:T(8,128)(2,1)}, bf16[32,1536]{1,0:T(8,128)(2,1)S(1)}, u32[]{:S(2)}) copy-start(bf16[32,1536]{1,0:T(8,128)(2,1)S(1)} %collective-permute-done.20.refs_2_) | copy-start | bytes 294916
  77.5 10.7 %collective-permute-start.24 = (bf16[32,1536]{1,0:T(8,128)(2,1)}, bf16[32,1536]{1,0:T(8,128)(2,1)S(1)}, u32[]{:S(2)}, u32[]{:S(2)}) collective-permute-start(bf16[32,1536]{1,0:T(8,128)(2,1)} %get-tuple-element.40), channel_id=1, source_target_pairs={{0,96},{16,112},{32,128},{48,144},{64,160},{80,176},{96,192},{112,... | collective-permute-start | bytes 294920 | tf_op jit(solution)/shard_map/ppermute | solution.py:59
  77.9 12.8 %collective-permute-start.25 = (bf16[32,1536]{1,0:T(8,128)(2,1)}, bf16[32,1536]{1,0:T(8,128)(2,1)S(1)}, u32[]{:S(2)}, u32[]{:S(2)}) collective-permute-start(bf16[32,1536]{1,0:T(8,128)(2,1)} %get-tuple-element.41), channel_id=1, source_target_pairs={{0,128},{16,144},{32,160},{48,176},{64,192},{80,208},{96,224},{112... | collective-permute-start | bytes 294920 | tf_op jit(solution)/shard_map/ppermute | solution.py:59
  82.8 0.7 copy-start.3
  83.6 7.1 %copy-start.19 = (bf16[32,1536]{1,0:T(8,128)(2,1)}, bf16[32,1536]{1,0:T(8,128)(2,1)S(1)}, u32[]{:S(2)}) copy-start(bf16[32,1536]{1,0:T(8,128)(2,1)S(1)} %collective-permute-done.21.refs_3_) | copy-start | bytes 294916
  83.6 7.1 %copy-start.20 = (bf16[32,1536]{1,0:T(8,128)(2,1)}, bf16[32,1536]{1,0:T(8,128)(2,1)S(1)}, u32[]{:S(2)}) copy-start(bf16[32,1536]{1,0:T(8,128)(2,1)S(1)} %collective-permute-done.22.refs_4_) | copy-start | bytes 294916
  83.6 7.1 %copy-start.21 = (bf16[32,1536]{1,0:T(8,128)(2,1)}, bf16[32,1536]{1,0:T(8,128)(2,1)S(1)}, u32[]{:S(2)}) copy-start(bf16[32,1536]{1,0:T(8,128)(2,1)S(1)} %collective-permute-done.23.refs_5_) | copy-start | bytes 294916
  88.2 2.5 %copy-start.22 = (bf16[32,1536]{1,0:T(8,128)(2,1)}, bf16[32,1536]{1,0:T(8,128)(2,1)S(1)}, u32[]{:S(2)}) copy-start(bf16[32,1536]{1,0:T(8,128)(2,1)S(1)} %collective-permute-done.24.refs_6_) | copy-start | bytes 294916
  90.7 0.6 copy-start.23
  94.4 0.9 copy-start.5
  95.3 0.9 copy-start.6
  96.5 21.3 %copy-start.4 = (bf16[384,512]{1,0:T(8,128)(2,1)S(1)}, bf16[384,512]{1,0:T(8,128)(2,1)}, u32[]{:S(2)}) copy-start(bf16[384,512]{1,0:T(8,128)(2,1)} %copy-done.3) | copy-start | bytes 1179652
  118.3 1.7 %collective-permute-start.29 = (bf16[192,768]{1,0:T(8,128)(2,1)S(1)}, bf16[192,768]{1,0:T(8,128)(2,1)S(1)}, u32[]{:S(2)}, u32[]{:S(2)}) collective-permute-start(bf16[192,768]{1,0:T(8,128)(2,1)S(1)} %get-tuple-element.46), channel_id=1, source_target_pairs={{0,1},{1,0},{2,3},{3,2},{4,5},{5,4},{6,7},{7,6},{8,9},{9,8},{10,11... | collective-permute-start | bytes 884744 | tf_op jit(solution)/shard_map/ppermute | solution.py:67
  138.5 3.8 %collective-permute-start.30 = (bf16[24,384]{1,0:T(8,128)(2,1)S(1)}, bf16[24,384]{1,0:T(8,128)(2,1)S(1)}, u32[]{:S(2)}, u32[]{:S(2)}) collective-permute-start(bf16[24,384]{1,0:T(8,128)(2,1)S(1)} %get-tuple-element.48), channel_id=1, source_target_pairs={{0,2},{1,3},{2,0},{3,1},{4,6},{5,7},{6,4},{7,5},{8,10},{9,11},{10,... | collective-permute-start | bytes 55304 | tf_op jit(solution)/shard_map/ppermute | solution.py:71
  143.2 20.9 %all-to-all-start.3 = ((bf16[16,2,24,384]{3,2,1,0:T(8,128)(2,1)}), bf16[16,2,24,384]{3,2,1,0:T(8,128)(2,1)S(1)}, u32[]{:S(2)}, u32[]{:S(2)}) async-start(bf16[16,2,24,384]{3,2,1,0:T(8,128)(2,1)} %broadcast_in_dim.5), calls=%async_computation.3 | async-start | bytes 1179648 | tf_op jit(solution)/shard_map/all_to_all | solution.py:344
  147.1 1.3 collective-permute-start.28

commit v10 on v7

--- a/solution.py
+++ b/solution.py
@@ -69,6 +69,11 @@
 
 def swap_x(value):
     return lax.ppermute(value, "mp", [(m, m ^ 2) for m in range(16)])
+
+
+def swap_both(value):
+    pairs = [(16 * d + m, 16 * (d ^ 1) + (m ^ 2)) for d in range(16) for m in range(16)]
+    return lax.ppermute(value, ("dp", "mp"), pairs)
 
 
 def loss_columns(losses):
@@ -234,20 +239,11 @@
 
     texts = over_z(jnp.broadcast_to(txt_emb[None], (8, sub, width))).reshape(half, width)
     mine = jnp.where(y == 0, img_feat_t, txt_feat_t)
-    came = swap_y(jnp.where(y == 0, txt_feat_t, img_feat_t))
+    theirs = jnp.where(y == 0, txt_feat_t, img_feat_t)
+    came, mine_x, came_x = swap_y(theirs), swap_x(mine), swap_both(theirs)
     by_core = img_emb.reshape(8, 2, sub, width)
     own = lax.dynamic_slice_in_dim(by_core, core, 1, 1).reshape(half, width)
     partner = swap_y(own)
-    pair = jnp.concatenate([mine, came])
-    pair_x = swap_x(pair)
-    feat_part = local(
-        feature_kernel,
-        ((4 * feats, rows), BF16),
-        [jnp.stack([y, core]), pair, pair_x, swap_core(pair), swap_core(pair_x)],
-        8,
-        [SMEM] + [VMEM] * 4,
-    )
-
     owners = 2 * jnp.arange(8, dtype=jnp.int32) + y
     cores = jnp.stack([mp_index, mp_index ^ 1])
     text_ids = owners[None, :, None] * rows + cores[:, None, None] * sub
@@ -259,7 +255,7 @@
     )
     places = jnp.stack([8 * y, 8 * (1 - y)])
     numbers = jnp.concatenate([logit_scale, logit_bias])
-    numbers, feat_part = lax.optimization_barrier((numbers, feat_part))
+    numbers, came, mine_x, came_x = lax.optimization_barrier((numbers, came, mine_x, came_x))
     image_part, keep, send = local(
         tile_kernel,
         [((16, sub, full), BF16), ((half, width), F32), ((half, width), BF16)],
@@ -305,10 +301,20 @@
     text_came = [text_parts[0]] + [
         along_z(part, -steps) for part, steps in zip(text_parts[1:], ALONG[1:], strict=True)
     ]
+    pair = jnp.concatenate([mine, came])
+    pair_x = jnp.concatenate([mine_x, came_x])
+    feat_part = local(
+        feature_kernel,
+        ((4 * feats, rows), BF16),
+        [jnp.stack([y, core]), pair, pair_x, swap_core(pair), swap_core(pair_x)],
+        8,
+        [SMEM] + [VMEM] * 4,
+    )
+    raw_txt, feat_part = lax.optimization_barrier((txt_emb, feat_part))
     d_txt = local(
         text_kernel,
         ((sub, width), BF16),
-        [*text_came, txt_emb],
+        [*text_came, raw_txt],
         WHOLE,
         [ANY] * 8 + [VMEM],
         None,

time: 162 us -> 159 us (0.981)
  waiting for transfers between devices: 57.3 us -> 51 us
    ppermute x2, waiting for transfers between devices: 8.75 us -> 2.3 us  [swap_x(): return lax.ppermute(value, 'mp', [(m, m ^ 2) for m in range(16)])]
    ppermute x7, waiting for transfers between devices: 6.38 us -> 11 us  [along_z(): lax.ppermute(value, 'dp', [(d, (d + 2 * steps) % 16) for d in range(16)])]
    all_to_all x1, waiting for transfers between devices: 20.6 us -> 17.2 us  [over_z(): lax.all_to_all(value, 'dp', 0, 0, tiled=True, axis_index_groups=same_y)]
    all_to_all x1, blocking collectives: 16.2 us -> 19.1 us  [over_z(): lax.all_to_all(value, 'dp', 0, 0, tiled=True, axis_index_groups=same_y)]
    all_to_all x1, blocking collectives: 20.8 us -> 18.7 us  [over_plane(): lax.all_to_all(value, ('dp', 'mp'), 0, 0, tiled=True, axis_index_groups=p...]
    ppermute x7, starting transfers between devices: 14.5 us -> 12.5 us  [along_z(): lax.ppermute(value, 'dp', [(d, (d + 2 * steps) % 16) for d in range(16)])]
    unnamed x32 -> x33, local copies, waits for them, and re-layouts: 6.17 us -> 6.41 us
  transfers between devices with their start and end apart: 20 -> 21, of which waited for: 12 -> 12; matrix products, arithmetic and copies ran while one was open for 1% -> 3% of each run, Pallas kernels for 4% -> 4%
where the time goes in v10:
time: 159 us; the launch traced here: 158 us
  waiting for transfers between devices  51 us (32%)
  starting transfers between devices  39.7 us (25%)
  blocking collectives  37.9 us (24%)
  Pallas kernels  14 us (9%)
  local copies, waits for them, and re-layouts  11.2 us (7%)
  other arithmetic  2.31 us (1%)
  between operations  2.27 us (1%)
    all_to_all x1, blocking collectives, over_z(): lax.all_to_all(value, 'dp', 0, 0, tiled=True, axis_index_groups=same_y)  19.1 us
    all_to_all x1, blocking collectives, over_plane(): lax.all_to_all(value, ('dp', 'mp'), 0, 0, tiled=True, axis_index_groups=p...  18.7 us
    all_to_all x1, waiting for transfers between devices, over_z(): lax.all_to_all(value, 'dp', 0, 0, tiled=True, axis_index_groups=same_y)  17.2 us
    all_to_all x1, waiting for transfers between devices, shards(): lax.all_to_all(jnp.broadcast_to(summed[None], (16, 2, *shape)), 'dp', 0,...  15.1 us
    pallas_call x9, Pallas kernels, local(): pl.pallas_call(kernel, out_shape=shapes, in_specs=specs or [VMEM] * len(o...  14 us
    ppermute x7, starting transfers between devices, along_z(): lax.ppermute(value, 'dp', [(d, (d + 2 * steps) % 16) for d in range(16)])  12.5 us
    ppermute x7, waiting for transfers between devices, along_z(): lax.ppermute(value, 'dp', [(d, (d + 2 * steps) % 16) for d in range(16)])  11 us
    all_to_all x1, starting transfers between devices, over_z(): lax.all_to_all(value, 'dp', 0, 0, tiled=True, axis_index_groups=same_y)  8.47 us
  transfers between devices with their start and end apart: 21, of which 12 were waited for; matrix products, arithmetic and copies ran while one was open for 3% of the time, Pallas kernels for 4%

profile of v10, /device:TPU:2, one launch (start us, length us, event | category | flops | bytes accessed | tf_op | source)
XLA Modules:
  0.0 158.2 jit_solution(348897919850173883)
XLA Ops:
  0.7 2.0 %broadcast_in_dim.6 = bf16[8,32,1536]{2,1,0:T(8,128)(2,1)} broadcast(bf16[32,1536]{1,0:T(8,128)(2,1)} %refs_8_), dimensions={1,2} | broadcast | bytes 884736 | tf_op jit(solution)/shard_map/broadcast_in_dim | solution.py:240
  2.6 8.5 %all-to-all-start = ((bf16[8,32,1536]{2,1,0:T(8,128)(2,1)}), bf16[8,32,1536]{2,1,0:T(8,128)(2,1)S(1)}, u32[]{:S(2)}, u32[]{:S(2)}) async-start(bf16[8,32,1536]{2,1,0:T(8,128)(2,1)} %broadcast_in_dim.6), calls=%async_computation | async-start | bytes 1572864 | tf_op jit(solution)/shard_map/all_to_all | solution.py:238
  11.1 0.7 broadcast_select_fusion
  11.8 1.6 collective-permute-start
  13.4 0.4 collective-permute-start.2
  13.8 0.1 constant_dynamic-slice_fusion.1
  13.9 1.7 %collective-permute-start.4 = (bf16[256,1536]{1,0:T(8,128)(2,1)S(1)}, bf16[256,1536]{1,0:T(8,128)(2,1)}, u32[]{:S(2)}, u32[]{:S(2)}) collective-permute-start(bf16[256,1536]{1,0:T(8,128)(2,1)S(1)} %bitcast.22), channel_id=1, source_target_pairs={{0,16},{16,0},{32,48},{48,32},{64,80},{80,64},{96,112},{112,96},{1... | collective-permute-start | bytes 2359304 | tf_op jit(solution)/shard_map/ppermute | solution.py:63
  15.5 1.5 collective-permute-start.1
  17.0 17.2 %all-to-all-done = bf16[8,32,1536]{2,1,0:T(8,128)(2,1)S(1)} async-done(((bf16[8,32,1536]{2,1,0:T(8,128)(2,1)}), bf16[8,32,1536]{2,1,0:T(8,128)(2,1)S(1)}, u32[]{:S(2)}, u32[]{:S(2)}) %all-to-all-start) | async-done | bytes 786464 | tf_op jit(solution)/shard_map/all_to_all | solution.py:238
  34.2 0.1 copy.11.refs_3_
  35.7 0.1 add_multiply_fusion
  35.8 0.1 broadcast_add_fusion.1
  35.9 0.1 iota_add_fusion
  35.9 0.1 add.120.refs_2_
  36.0 0.1 pad_maximum_fusion.2.refs_0_
  36.1 0.1 pad_add_fusion.1.refs_1_
  36.2 0.4 collective-permute-done.3.refs_5_
  36.6 5.3 %shard_map.85 = (bf16[16,32,1664]{2,1,0:T(8,128)(2,1)S(1)}, f32[256,1536]{1,0:T(8,128)S(1)}, bf16[256,1536]{1,0:T(8,128)(2,1)S(1)}) custom-call(f32[2]{0:T(128)S(1)} %pad_maximum_fusion.2.refs_0_, s32[2]{0:T(128)S(1)} %pad_add_fusion.1.refs_1_, s32[1,512]{1,0:T(1,128)S(1)} %add.120.refs_2_, s32[512,1]{1,0:T(8,128)S(1)} %copy.11.refs_3_, ...), custom_call_target="tpu_custom_call" | custom-call | tf_op jit(solution)/shard_map/pallas_call | solution.py:23
  41.9 1.2 copy-done.1
  43.1 1.1 copy-done.2
  44.3 0.1 collective-permute-start.5
  44.4 2.1 %collective-permute-done.5.came_ref = bf16[256,1536]{1,0:T(8,128)(2,1)S(1)} collective-permute-done((bf16[256,1536]{1,0:T(8,128)(2,1)S(1)}, bf16[256,1536]{1,0:T(8,128)(2,1)S(1)}, u32[]{:S(2)}, u32[]{:S(2)}) %collective-permute-start.5) | collective-permute-done | bytes 786464 | tf_op jit(solution)/shard_map/ppermute | solution.py:67
  46.5 0.9 copy-done.6
  47.4 7.5 %all-to-all-start.1 = ((bf16[16,32,1664]{2,1,0:T(8,128)(2,1)}), bf16[16,32,1664]{2,1,0:T(8,128)(2,1)S(1)}, u32[]{:S(2)}, u32[]{:S(2)}) async-start(bf16[16,32,1664]{2,1,0:T(8,128)(2,1)} %copy-done.1), calls=%async_computation.1 | async-start | bytes 3407872 | tf_op jit(solution)/shard_map/all_to_all | solution.py:285
  54.9 0.9 constant_dynamic-update-slice_fusion.1
  55.8 0.9 constant_dynamic-update-slice_fusion.refs_1_
  56.7 0.9 pad_maximum_fusion.refs_0_
  57.6 0.6 collective-permute-start.13
  58.2 2.7 %shard_map.86 = (bf16[32,1536]{1,0:T(8,128)(2,1)}, bf16[32,1536]{1,0:T(8,128)(2,1)}, bf16[32,1536]{1,0:T(8,128)(2,1)}, bf16[32,1536]{1,0:T(8,128)(2,1)}, bf16[32...) custom-call(s32[1]{0:T(128)} %bitcast.8.flags, ...), custom_call_target="tpu_custom_call" | custom-call | tf_op jit(solution)/shard_map/pallas_call | solution.py:23
  60.9 4.2 %collective-permute-start.10 = (bf16[32,1536]{1,0:T(8,128)(2,1)}, bf16[32,1536]{1,0:T(8,128)(2,1)S(1)}, u32[]{:S(2)}, u32[]{:S(2)}) collective-permute-start(bf16[32,1536]{1,0:T(8,128)(2,1)} %get-tuple-element.39), channel_id=1, source_target_pairs={{0,160},{16,176},{32,192},{48,208},{64,224},{80,240},{96,0},{112,1... | collective-permute-start | bytes 294920 | tf_op jit(solution)/shard_map/ppermute | solution.py:59
  65.1 4.8 %collective-permute-start.12 = (bf16[32,1536]{1,0:T(8,128)(2,1)}, bf16[32,1536]{1,0:T(8,128)(2,1)S(1)}, u32[]{:S(2)}, u32[]{:S(2)}) collective-permute-start(bf16[32,1536]{1,0:T(8,128)(2,1)} %get-tuple-element.41), channel_id=1, source_target_pairs={{0,128},{16,144},{32,160},{48,176},{64,192},{80,208},{96,224},{112... | collective-permute-start | bytes 294920 | tf_op jit(solution)/shard_map/ppermute | solution.py:59
  69.9 1.8 %collective-permute-start.6 = (bf16[32,1536]{1,0:T(8,128)(2,1)}, bf16[32,1536]{1,0:T(8,128)(2,1)S(1)}, u32[]{:S(2)}, u32[]{:S(2)}) collective-permute-start(bf16[32,1536]{1,0:T(8,128)(2,1)} %get-tuple-element.35), channel_id=1, source_target_pairs={{0,224},{16,240},{32,0},{48,16},{64,32},{80,48},{96,64},{112,80},{... | collective-permute-start | bytes 294920 | tf_op jit(solution)/shard_map/ppermute | solution.py:59
  71.6 0.3 collective-permute-start.7
  71.9 4.7 %collective-permute-done.10.refs_5_ = bf16[32,1536]{1,0:T(8,128)(2,1)S(1)} collective-permute-done((bf16[32,1536]{1,0:T(8,128)(2,1)}, bf16[32,1536]{1,0:T(8,128)(2,1)S(1)}, u32[]{:S(2)}, u32[]{:S(2)}) %collective-permute-start.10) | collective-permute-done | bytes 98336 | tf_op jit(solution)/shard_map/ppermute | solution.py:59
  76.7 1.4 collective-permute-done.11.refs_6_
  78.1 1.5 collective-permute-start.9
  79.6 0.1 pad_add_fusion.2.flags
  79.7 1.0 shard_map.87.feats_ref
  80.6 0.7 copy-done.3
  81.4 0.1 collective-permute-done.7.refs_2_
  81.5 1.4 collective-permute-done.8.refs_3_
  82.9 3.4 %collective-permute-done.9.refs_4_ = bf16[32,1536]{1,0:T(8,128)(2,1)S(1)} collective-permute-done((bf16[32,1536]{1,0:T(8,128)(2,1)}, bf16[32,1536]{1,0:T(8,128)(2,1)S(1)}, u32[]{:S(2)}, u32[]{:S(2)}) %collective-permute-start.9) | collective-permute-done | bytes 98336 | tf_op jit(solution)/shard_map/ppermute | solution.py:59
  86.3 0.6 copy-done.15
  86.9 3.0 %shard_map.88.d_txt = bf16[32,1536]{1,0:T(8,128)(2,1)} custom-call(bf16[32,1536]{1,0:T(8,128)(2,1)} %get-tuple-element.34.refs_0_, bf16[32,1536]{1,0:T(8,128)(2,1)} %copy-done.12, bf16[32,1536]{1,0:T(8,128)(2,1)} %copy-done.13, bf16[32,1536]{1,0:T(8,128)(2,1)} %copy-done.14, bf16[32,1536]{1,0:T(8,128)(2,1)} %copy-done.15, bf16[32,1536]{1,0:T(8,128)(2,1)} %copy-done.9, ...), custom_call_target="tpu_custom_call" | custom-call | tf_op jit(solution)/shard_map/pallas_call | solution.py:23
  90.0 0.9 copy-done.5
  90.9 0.4 shard_map.89
  91.3 0.1 broadcast_in_dim.7
  91.4 18.7 %all_to_all.25.grads_ref = bf16[16,32,896]{2,1,0:T(8,128)(2,1)S(1)} all-to-all(bf16[16,32,896]{2,1,0:T(8,128)(2,1)S(1)} %bitcast.25), channel_id=1, replica_groups={{0,2,4,6,8,10,12,14,16,18,20,22,24,26,28,30},{1,3,5,7,9,11,13,15,17,19,..., dimensions={0} | all-to-all | bytes 1835008 | tf_op jit(solution)/shard_map/all_to_all | solution.py:285
  110.1 0.5 shard_map.90
  110.6 0.1 collective-permute-start.16
  110.7 1.6 collective-permute-done.16.came_ref
  112.2 0.1 shard_map.91
  112.3 19.1 %all_to_all.26.parts_ref = bf16[8,2,24,384]{3,2,1,0:T(8,128)(2,1)S(1)} all-to-all(bf16[8,2,24,384]{3,2,1,0:T(8,128)(2,1)S(1)} %shard_map.91), channel_id=1, replica_groups={{0,32,64,96,128,160,192,224},{16,48,80,112,144,176,208,240},{1,33,65,97..., dimensions={0} | all-to-all | bytes 589824 | tf_op jit(solution)/shard_map/all_to_all | solution.py:238
  131.5 1.5 collective-permute-start.17
  133.0 2.3 %collective-permute-done.17 = bf16[24,384]{1,0:T(8,128)(2,1)S(1)} collective-permute-done((bf16[24,384]{1,0:T(8,128)(2,1)S(1)}, bf16[24,384]{1,0:T(8,128)(2,1)S(1)}, u32[]{:S(2)}, u32[]{:S(2)}) %collective-permute-start.17) | collective-permute-done | bytes 18464 | tf_op jit(solution)/shard_map/ppermute | solution.py:71
  135.3 0.9 broadcast_in_dim.8
  136.2 3.6 %all-to-all-start.4 = ((bf16[16,2,24,384]{3,2,1,0:T(8,128)(2,1)}), bf16[16,2,24,384]{3,2,1,0:T(8,128)(2,1)S(1)}, u32[]{:S(2)}, u32[]{:S(2)}) async-start(bf16[16,2,24,384]{3,2,1,0:T(8,128)(2,1)} %broadcast_in_dim.8), calls=%async_computation.4 | async-start | bytes 1179648 | tf_op jit(solution)/shard_map/all_to_all | solution.py:345
  139.8 0.1 slice_add_fusion
  140.0 0.1 fusion
  140.1 0.1 collective-permute-start.15
  140.2 1.1 collective-permute-done.15
  141.3 0.7 select_n.95
  142.0 15.1 %all-to-all-done.4.parts_ref = bf16[16,2,24,384]{3,2,1,0:T(8,128)(2,1)S(1)} async-done(((bf16[16,2,24,384]{3,2,1,0:T(8,128)(2,1)}), bf16[16,2,24,384]{3,2,1,0:T(8,128)(2,1)S(1)}, u32[]{:S(2)}, u32[]{:S(2)}) %all-to-all-start.4) | async-done | bytes 589856 | tf_op jit(solution)/shard_map/all_to_all | solution.py:345
  157.1 1.1 shard_map.93
  (48 shorter events, 0.2 us)
Async XLA Ops:
  0.6 13.1 %copy-start = (bf16[512,1536]{1,0:T(8,128)(2,1)S(1)}, bf16[512,1536]{1,0:T(8,128)(2,1)}, u32[]{:S(2)}) copy-start(bf16[512,1536]{1,0:T(8,128)(2,1)} %param.6) | copy-start | bytes 4718596
  0.6 10.5 %copy-start.7 = (bf16[96,512]{1,0:T(8,128)(2,1)S(1)}, bf16[96,512]{1,0:T(8,128)(2,1)}, u32[]{:S(2)}) copy-start(bf16[96,512]{1,0:T(8,128)(2,1)} %param.8) | copy-start | bytes 294916
  0.7 10.5 %copy-start.8 = (bf16[96,512]{1,0:T(8,128)(2,1)S(1)}, bf16[96,512]{1,0:T(8,128)(2,1)}, u32[]{:S(2)}) copy-start(bf16[96,512]{1,0:T(8,128)(2,1)} %param.9) | copy-start | bytes 294916
  2.6 31.6 %all-to-all-start = ((bf16[8,32,1536]{2,1,0:T(8,128)(2,1)}), bf16[8,32,1536]{2,1,0:T(8,128)(2,1)S(1)}, u32[]{:S(2)}, u32[]{:S(2)}) async-start(bf16[8,32,1536]{2,1,0:T(8,128)(2,1)} %broadcast_in_dim.6), calls=%async_computation | async-start | bytes 1572864 | tf_op jit(solution)/shard_map/all_to_all | solution.py:238
  11.8 24.4 %collective-permute-start = (bf16[96,512]{1,0:T(8,128)(2,1)}, bf16[96,512]{1,0:T(8,128)(2,1)}, u32[]{:S(2)}, u32[]{:S(2)}) collective-permute-start(bf16[96,512]{1,0:T(8,128)(2,1)} %get-tuple-element.54), channel_id=1, source_target_pairs={{0,16},{16,0},{32,48},{48,32},{64,80},{80,64},{96,112},{112,96},{1... | collective-permute-start | bytes 294920 | tf_op jit(solution)/shard_map/ppermute | solution.py:63
  13.4 22.8 %collective-permute-start.2 = (bf16[96,512]{1,0:T(8,128)(2,1)}, bf16[96,512]{1,0:T(8,128)(2,1)}, u32[]{:S(2)}, u32[]{:S(2)}) collective-permute-start(bf16[96,512]{1,0:T(8,128)(2,1)} %get-tuple-element.54), channel_id=1, source_target_pairs={{0,18},{1,19},{2,16},{3,17},{4,22},{5,23},{6,20},{7,21},{8,26},{9,... | collective-permute-start | bytes 294920 | tf_op jit(solution)/shard_map/ppermute | solution.py:76
  13.9 22.3 %collective-permute-start.4 = (bf16[256,1536]{1,0:T(8,128)(2,1)S(1)}, bf16[256,1536]{1,0:T(8,128)(2,1)}, u32[]{:S(2)}, u32[]{:S(2)}) collective-permute-start(bf16[256,1536]{1,0:T(8,128)(2,1)S(1)} %bitcast.22), channel_id=1, source_target_pairs={{0,16},{16,0},{32,48},{48,32},{64,80},{80,64},{96,112},{112,96},{1... | collective-permute-start | bytes 2359304 | tf_op jit(solution)/shard_map/ppermute | solution.py:63
  15.5 20.7 %collective-permute-start.1 = (bf16[96,512]{1,0:T(8,128)(2,1)S(1)}, bf16[96,512]{1,0:T(8,128)(2,1)}, u32[]{:S(2)}, u32[]{:S(2)}) collective-permute-start(bf16[96,512]{1,0:T(8,128)(2,1)S(1)} %get-tuple-element.53), channel_id=1, source_target_pairs={{0,2},{1,3},{2,0},{3,1},{4,6},{5,7},{6,4},{7,5},{8,10},{9,11},{10,... | collective-permute-start | bytes 294920 | tf_op jit(solution)/shard_map/ppermute | solution.py:71
  34.2 2.4 %collective-permute-start.3 = (bf16[256,1536]{1,0:T(8,128)(2,1)S(1)}, bf16[256,1536]{1,0:T(8,128)(2,1)}, u32[]{:S(2)}, u32[]{:S(2)}) collective-permute-start(bf16[256,1536]{1,0:T(8,128)(2,1)S(1)} %bitcast.20), channel_id=1, source_target_pairs={{0,1},{1,0},{2,3},{3,2},{4,5},{5,4},{6,7},{7,6},{8,9},{9,8},{10,11... | collective-permute-start | bytes 2359304 | tf_op jit(solution)/shard_map/ppermute | solution.py:67
  41.9 1.2 copy-start.1
  43.1 1.1 copy-start.2
  44.3 2.3 %collective-permute-start.5 = (bf16[256,1536]{1,0:T(8,128)(2,1)S(1)}, bf16[256,1536]{1,0:T(8,128)(2,1)S(1)}, u32[]{:S(2)}, u32[]{:S(2)}) collective-permute-start(bf16[256,1536]{1,0:T(8,128)(2,1)S(1)} %get-tuple-element.30), channel_id=1, source_target_pairs={{0,1},{1,0},{2,3},{3,2},{4,5},{5,4},{6,7},{7,6},{8,9},{9,8},{10,11... | collective-permute-start | bytes 2359304 | tf_op jit(solution)/shard_map/ppermute | solution.py:67
  46.5 0.9 copy-start.6
  47.4 42.5 %all-to-all-start.1 = ((bf16[16,32,1664]{2,1,0:T(8,128)(2,1)}), bf16[16,32,1664]{2,1,0:T(8,128)(2,1)S(1)}, u32[]{:S(2)}, u32[]{:S(2)}) async-start(bf16[16,32,1664]{2,1,0:T(8,128)(2,1)} %copy-done.1), calls=%async_computation.1 | async-start | bytes 3407872 | tf_op jit(solution)/shard_map/all_to_all | solution.py:285
  56.7 13.1 %collective-permute-start.14 = (bf16[192,512]{1,0:T(8,128)(2,1)S(1)}, bf16[192,512]{1,0:T(8,128)(2,1)S(1)}, u32[]{:S(2)}, u32[]{:S(2)}) collective-permute-start(bf16[192,512]{1,0:T(8,128)(2,1)S(1)} %constant_dynamic-update-slice_fusion.refs_1_), channel_id=1, source_target_pairs={{0,1},{1,0},{2,3},{3,2},{4,5},{5,4},{6,7},{7,6},{8,9},{9,8},{10,11... | collective-permute-start | bytes 589832 | tf_op jit(solution)/shard_map/ppermute | solution.py:67
  57.6 14.0 %collective-permute-start.13 = (bf16[192,512]{1,0:T(8,128)(2,1)S(1)}, bf16[192,512]{1,0:T(8,128)(2,1)S(1)}, u32[]{:S(2)}, u32[]{:S(2)}) collective-permute-start(bf16[192,512]{1,0:T(8,128)(2,1)S(1)} %pad_maximum_fusion.refs_0_), channel_id=1, source_target_pairs={{0,1},{1,0},{2,3},{3,2},{4,5},{5,4},{6,7},{7,6},{8,9},{9,8},{10,11... | collective-permute-start | bytes 589832 | tf_op jit(solution)/shard_map/ppermute | solution.py:67
  60.9 15.8 %collective-permute-start.10 = (bf16[32,1536]{1,0:T(8,128)(2,1)}, bf16[32,1536]{1,0:T(8,128)(2,1)S(1)}, u32[]{:S(2)}, u32[]{:S(2)}) collective-permute-start(bf16[32,1536]{1,0:T(8,128)(2,1)} %get-tuple-element.39), channel_id=1, source_target_pairs={{0,160},{16,176},{32,192},{48,208},{64,224},{80,240},{96,0},{112,1... | collective-permute-start | bytes 294920 | tf_op jit(solution)/shard_map/ppermute | solution.py:59
  65.1 13.0 %collective-permute-start.11 = (bf16[32,1536]{1,0:T(8,128)(2,1)}, bf16[32,1536]{1,0:T(8,128)(2,1)S(1)}, u32[]{:S(2)}, u32[]{:S(2)}) collective-permute-start(bf16[32,1536]{1,0:T(8,128)(2,1)} %get-tuple-element.40), channel_id=1, source_target_pairs={{0,96},{16,112},{32,128},{48,144},{64,160},{80,176},{96,192},{112,... | collective-permute-start | bytes 294920 | tf_op jit(solution)/shard_map/ppermute | solution.py:59
  65.1 16.3 %collective-permute-start.12 = (bf16[32,1536]{1,0:T(8,128)(2,1)}, bf16[32,1536]{1,0:T(8,128)(2,1)S(1)}, u32[]{:S(2)}, u32[]{:S(2)}) collective-permute-start(bf16[32,1536]{1,0:T(8,128)(2,1)} %get-tuple-element.41), channel_id=1, source_target_pairs={{0,128},{16,144},{32,160},{48,176},{64,192},{80,208},{96,224},{112... | collective-permute-start | bytes 294920 | tf_op jit(solution)/shard_map/ppermute | solution.py:59
  69.9 11.5 %collective-permute-start.6 = (bf16[32,1536]{1,0:T(8,128)(2,1)}, bf16[32,1536]{1,0:T(8,128)(2,1)S(1)}, u32[]{:S(2)}, u32[]{:S(2)}) collective-permute-start(bf16[32,1536]{1,0:T(8,128)(2,1)} %get-tuple-element.35), channel_id=1, source_target_pairs={{0,224},{16,240},{32,0},{48,16},{64,32},{80,48},{96,64},{112,80},{... | collective-permute-start | bytes 294920 | tf_op jit(solution)/shard_map/ppermute | solution.py:59
  71.6 9.9 %collective-permute-start.7 = (bf16[32,1536]{1,0:T(8,128)(2,1)}, bf16[32,1536]{1,0:T(8,128)(2,1)S(1)}, u32[]{:S(2)}, u32[]{:S(2)}) collective-permute-start(bf16[32,1536]{1,0:T(8,128)(2,1)} %get-tuple-element.36), channel_id=1, source_target_pairs={{0,32},{16,48},{32,64},{48,80},{64,96},{80,112},{96,128},{112,144}... | collective-permute-start | bytes 294920 | tf_op jit(solution)/shard_map/ppermute | solution.py:59
  76.7 9.6 %copy-start.9 = (bf16[32,1536]{1,0:T(8,128)(2,1)}, bf16[32,1536]{1,0:T(8,128)(2,1)S(1)}, u32[]{:S(2)}) copy-start(bf16[32,1536]{1,0:T(8,128)(2,1)S(1)} %collective-permute-done.10.refs_5_) | copy-start | bytes 294916
  76.7 6.2 %collective-permute-start.8 = (bf16[32,1536]{1,0:T(8,128)(2,1)}, bf16[32,1536]{1,0:T(8,128)(2,1)S(1)}, u32[]{:S(2)}, u32[]{:S(2)}) collective-permute-start(bf16[32,1536]{1,0:T(8,128)(2,1)} %get-tuple-element.37), channel_id=1, source_target_pairs={{0,192},{16,208},{32,224},{48,240},{64,0},{80,16},{96,32},{112,48}... | collective-permute-start | bytes 294920 | tf_op jit(solution)/shard_map/ppermute | solution.py:59
  78.1 8.2 %copy-start.10 = (bf16[32,1536]{1,0:T(8,128)(2,1)}, bf16[32,1536]{1,0:T(8,128)(2,1)S(1)}, u32[]{:S(2)}) copy-start(bf16[32,1536]{1,0:T(8,128)(2,1)S(1)} %collective-permute-done.11.refs_6_) | copy-start | bytes 294916
  78.1 8.2 %collective-permute-start.9 = (bf16[32,1536]{1,0:T(8,128)(2,1)}, bf16[32,1536]{1,0:T(8,128)(2,1)S(1)}, u32[]{:S(2)}, u32[]{:S(2)}) collective-permute-start(bf16[32,1536]{1,0:T(8,128)(2,1)} %get-tuple-element.38), channel_id=1, source_target_pairs={{0,64},{16,80},{32,96},{48,112},{64,128},{80,144},{96,160},{112,17... | collective-permute-start | bytes 294920 | tf_op jit(solution)/shard_map/ppermute | solution.py:59
  80.6 0.7 copy-start.3
  81.4 4.9 %copy-start.11 = (bf16[32,1536]{1,0:T(8,128)(2,1)}, bf16[32,1536]{1,0:T(8,128)(2,1)S(1)}, u32[]{:S(2)}) copy-start(bf16[32,1536]{1,0:T(8,128)(2,1)S(1)} %collective-permute-done.12.refs_7_) | copy-start | bytes 294916
  81.4 4.9 %copy-start.12 = (bf16[32,1536]{1,0:T(8,128)(2,1)}, bf16[32,1536]{1,0:T(8,128)(2,1)S(1)}, u32[]{:S(2)}) copy-start(bf16[32,1536]{1,0:T(8,128)(2,1)S(1)} %collective-permute-done.6.refs_1_) | copy-start | bytes 294916
  81.5 4.8 %copy-start.13 = (bf16[32,1536]{1,0:T(8,128)(2,1)}, bf16[32,1536]{1,0:T(8,128)(2,1)S(1)}, u32[]{:S(2)}) copy-start(bf16[32,1536]{1,0:T(8,128)(2,1)S(1)} %collective-permute-done.7.refs_2_) | copy-start | bytes 294916
  82.9 3.4 %copy-start.14 = (bf16[32,1536]{1,0:T(8,128)(2,1)}, bf16[32,1536]{1,0:T(8,128)(2,1)S(1)}, u32[]{:S(2)}) copy-start(bf16[32,1536]{1,0:T(8,128)(2,1)S(1)} %collective-permute-done.8.refs_3_) | copy-start | bytes 294916
  86.3 0.6 copy-start.15
  90.0 0.9 copy-start.5
  91.3 18.8 %copy-start.4 = (bf16[384,512]{1,0:T(8,128)(2,1)S(1)}, bf16[384,512]{1,0:T(8,128)(2,1)}, u32[]{:S(2)}) copy-start(bf16[384,512]{1,0:T(8,128)(2,1)} %copy-done.3) | copy-start | bytes 1179652
  110.6 1.7 %collective-permute-start.16 = (bf16[192,768]{1,0:T(8,128)(2,1)S(1)}, bf16[192,768]{1,0:T(8,128)(2,1)S(1)}, u32[]{:S(2)}, u32[]{:S(2)}) collective-permute-start(bf16[192,768]{1,0:T(8,128)(2,1)S(1)} %get-tuple-element.48), channel_id=1, source_target_pairs={{0,1},{1,0},{2,3},{3,2},{4,5},{5,4},{6,7},{7,6},{8,9},{9,8},{10,11... | collective-permute-start | bytes 884744 | tf_op jit(solution)/shard_map/ppermute | solution.py:67
  131.5 3.8 %collective-permute-start.17 = (bf16[24,384]{1,0:T(8,128)(2,1)S(1)}, bf16[24,384]{1,0:T(8,128)(2,1)S(1)}, u32[]{:S(2)}, u32[]{:S(2)}) collective-permute-start(bf16[24,384]{1,0:T(8,128)(2,1)S(1)} %get-tuple-element.50), channel_id=1, source_target_pairs={{0,2},{1,3},{2,0},{3,1},{4,6},{5,7},{6,4},{7,5},{8,10},{9,11},{10,... | collective-permute-start | bytes 55304 | tf_op jit(solution)/shard_map/ppermute | solution.py:71
  136.2 20.9 %all-to-all-start.4 = ((bf16[16,2,24,384]{3,2,1,0:T(8,128)(2,1)}), bf16[16,2,24,384]{3,2,1,0:T(8,128)(2,1)S(1)}, u32[]{:S(2)}, u32[]{:S(2)}) async-start(bf16[16,2,24,384]{3,2,1,0:T(8,128)(2,1)} %broadcast_in_dim.8), calls=%async_computation.4 | async-start | bytes 1179648 | tf_op jit(solution)/shard_map/all_to_all | solution.py:345
  140.1 1.3 collective-permute-start.15

commit v11 on v10

--- a/solution.py
+++ b/solution.py
@@ -90,17 +90,17 @@
 
 
 def feature_kernel(flags, *refs):
-    sources, out_ref = refs[:4], refs[4]
-    rows = sources[0].shape[1]
-    count, half = sources[0].shape[0] // 2, rows // 2
+    sources, out_ref = refs[:8], refs[8]
+    count, rows = sources[0].shape
+    half = rows // 2
     y, core = flags[0], flags[1]
     source = lax.broadcasted_iota(jnp.int32, (rows, half), 0)
     target = lax.broadcasted_iota(jnp.int32, (rows, half), 1)
     chosen = source == (target // 32) * 64 + core * 32 + target % 32
     pick = jnp.where(chosen, 1.0, 0.0).astype(BF16)
-    for i, ref in enumerate(sources):
-        both = jnp.dot(ref[...], pick, preferred_element_type=F32)
-        own, other = both[:count].astype(BF16), both[count:].astype(BF16)
+    for i in range(4):
+        own = jnp.dot(sources[2 * i][...], pick, preferred_element_type=F32).astype(BF16)
+        other = jnp.dot(sources[2 * i + 1][...], pick, preferred_element_type=F32).astype(BF16)
         place = pl.ds(i * count, count)
         out_ref[place, pl.ds(0, half)] = jnp.where(y == 0, own, other)
         out_ref[place, pl.ds(half, half)] = jnp.where(y == 0, other, own)
@@ -126,9 +126,10 @@
         u = jnp.where(match, -logits, logits)
         e = jnp.exp(-jnp.abs(u))
         w = 1.0 + e
-        grown = jnp.where(w == 1.0, e, jnp.log(w) * (e / jnp.where(w == 1.0, 1.0, w - 1.0)))
+        inverse = 1.0 / w
+        grown = jnp.log(w) + (e - (w - 1.0)) * inverse
         losses = jnp.sum(jnp.maximum(u, 0.0) + grown, axis=1, keepdims=True)
-        slope = jnp.where(match, -scale, scale) * (jnp.where(u >= 0.0, 1.0, e) / w)
+        slope = jnp.where(match, -scale, scale) * (jnp.where(u >= 0.0, 1.0, e) * inverse)
         slopes[place, :] = slope.astype(BF16)
         grad = jnp.dot(slopes[place, :], texts[...], preferred_element_type=F32).astype(BF16)
         extra = loss_columns(losses)
@@ -241,6 +242,15 @@
     mine = jnp.where(y == 0, img_feat_t, txt_feat_t)
     theirs = jnp.where(y == 0, txt_feat_t, img_feat_t)
     came, mine_x, came_x = swap_y(theirs), swap_x(mine), swap_both(theirs)
+    sources = (mine, came, mine_x, came_x)
+    feat_part = local(
+        feature_kernel,
+        ((4 * feats, rows), BF16),
+        [jnp.stack([y, core]), *sources, *map(swap_core, sources)],
+        8,
+        [SMEM] + [VMEM] * 8,
+    )
+    texts, feat_part = lax.optimization_barrier((texts, feat_part))
     by_core = img_emb.reshape(8, 2, sub, width)
     own = lax.dynamic_slice_in_dim(by_core, core, 1, 1).reshape(half, width)
     partner = swap_y(own)
@@ -255,7 +265,6 @@
     )
     places = jnp.stack([8 * y, 8 * (1 - y)])
     numbers = jnp.concatenate([logit_scale, logit_bias])
-    numbers, came, mine_x, came_x = lax.optimization_barrier((numbers, came, mine_x, came_x))
     image_part, keep, send = local(
         tile_kernel,
         [((16, sub, full), BF16), ((half, width), F32), ((half, width), BF16)],
@@ -301,20 +310,10 @@
     text_came = [text_parts[0]] + [
         along_z(part, -steps) for part, steps in zip(text_parts[1:], ALONG[1:], strict=True)
     ]
-    pair = jnp.concatenate([mine, came])
-    pair_x = jnp.concatenate([mine_x, came_x])
-    feat_part = local(
-        feature_kernel,
-        ((4 * feats, rows), BF16),
-        [jnp.stack([y, core]), pair, pair_x, swap_core(pair), swap_core(pair_x)],
-        8,
-        [SMEM] + [VMEM] * 4,
-    )
-    raw_txt, feat_part = lax.optimization_barrier((txt_emb, feat_part))
     d_txt = local(
         text_kernel,
         ((sub, width), BF16),
-        [*text_came, raw_txt],
+        [*text_came, txt_emb],
         WHOLE,
         [ANY] * 8 + [VMEM],
         None,

time: 159 us -> 155 us (0.975)
  waiting for transfers between devices: 51 us -> 44.7 us
  blocking collectives: 37.9 us -> 39.7 us
  starting transfers between devices: 39.7 us -> 41.4 us
    all_to_all x1, waiting for transfers between devices: 17.2 us -> 10.7 us  [over_z(): lax.all_to_all(value, 'dp', 0, 0, tiled=True, axis_index_groups=same_y)]
    ppermute x7, waiting for transfers between devices: 11 us -> 7.73 us  [along_z(): lax.ppermute(value, 'dp', [(d, (d + 2 * steps) % 16) for d in range(16)])]
    ppermute x2, waiting for transfers between devices: 2.3 us -> 4.65 us  [swap_x(): return lax.ppermute(value, 'mp', [(m, m ^ 2) for m in range(16)])]
    ppermute x6 -> x8, waiting for transfers between devices: 5.3 us -> 6.29 us  [swap_core(): return lax.ppermute(value, 'mp', [(m, m ^ 1) for m in range(16)])]
    unnamed x33 -> x32, local copies, waits for them, and re-layouts: 6.41 us -> 6.13 us
  transfers between devices with their start and end apart: 21 -> 23, of which waited for: 12 -> 15; matrix products, arithmetic and copies ran while one was open for 3% -> 2% of each run, Pallas kernels for 4% -> 5%
where the time goes in v11:
time: 155 us; the launch traced here: 154 us
  waiting for transfers between devices  44.7 us (29%)
  starting transfers between devices  41.4 us (27%)
  blocking collectives  39.7 us (26%)
  Pallas kernels  14.4 us (9%)
  local copies, waits for them, and re-layouts  10 us (6%)
  between operations  2.25 us (1%)
    all_to_all x1, blocking collectives, over_z(): lax.all_to_all(value, 'dp', 0, 0, tiled=True, axis_index_groups=same_y)  19.9 us
    all_to_all x1, blocking collectives, over_plane(): lax.all_to_all(value, ('dp', 'mp'), 0, 0, tiled=True, axis_index_groups=p...  19.8 us
    all_to_all x1, waiting for transfers between devices, shards(): lax.all_to_all(jnp.broadcast_to(summed[None], (16, 2, *shape)), 'dp', 0,...  15.1 us
    pallas_call x9, Pallas kernels, local(): pl.pallas_call(kernel, out_shape=shapes, in_specs=specs or [VMEM] * len(o...  14.4 us
    ppermute x7, starting transfers between devices, along_z(): lax.ppermute(value, 'dp', [(d, (d + 2 * steps) % 16) for d in range(16)])  14.1 us
    all_to_all x1, waiting for transfers between devices, over_z(): lax.all_to_all(value, 'dp', 0, 0, tiled=True, axis_index_groups=same_y)  10.7 us
    all_to_all x1, starting transfers between devices, over_z(): lax.all_to_all(value, 'dp', 0, 0, tiled=True, axis_index_groups=same_y)  8.47 us
    ppermute x7, waiting for transfers between devices, along_z(): lax.ppermute(value, 'dp', [(d, (d + 2 * steps) % 16) for d in range(16)])  7.73 us
  transfers between devices with their start and end apart: 23, of which 15 were waited for; matrix products, arithmetic and copies ran while one was open for 2% of the time, Pallas kernels for 5%

profile of v11, /device:TPU:2, one launch (start us, length us, event | category | flops | bytes accessed | tf_op | source)
XLA Modules:
  0.0 153.9 jit_solution(592522874910887695)
XLA Ops:
  0.7 2.0 %broadcast_in_dim.6 = bf16[8,32,1536]{2,1,0:T(8,128)(2,1)} broadcast(bf16[32,1536]{1,0:T(8,128)(2,1)} %refs_8_.1), dimensions={1,2} | broadcast | bytes 884736 | tf_op jit(solution)/shard_map/broadcast_in_dim | solution.py:241
  2.6 8.5 %all-to-all-start = ((bf16[8,32,1536]{2,1,0:T(8,128)(2,1)}), bf16[8,32,1536]{2,1,0:T(8,128)(2,1)S(1)}, u32[]{:S(2)}, u32[]{:S(2)}) async-start(bf16[8,32,1536]{2,1,0:T(8,128)(2,1)} %broadcast_in_dim.6), calls=%async_computation | async-start | bytes 1572864 | tf_op jit(solution)/shard_map/all_to_all | solution.py:239
  11.1 0.7 broadcast_select_fusion
  11.8 1.6 %collective-permute-start = (bf16[96,512]{1,0:T(8,128)(2,1)}, bf16[96,512]{1,0:T(8,128)(2,1)S(1)}, u32[]{:S(2)}, u32[]{:S(2)}) collective-permute-start(bf16[96,512]{1,0:T(8,128)(2,1)} %get-tuple-element.45), channel_id=1, source_target_pairs={{0,16},{16,0},{32,48},{48,32},{64,80},{80,64},{96,112},{112,96},{1... | collective-permute-start | bytes 294920 | tf_op jit(solution)/shard_map/ppermute | solution.py:63
  13.4 0.4 collective-permute-start.2
  13.8 1.5 collective-permute-start.1
  15.3 1.7 %collective-permute-start.8 = (bf16[256,1536]{1,0:T(8,128)(2,1)S(1)}, bf16[256,1536]{1,0:T(8,128)(2,1)}, u32[]{:S(2)}, u32[]{:S(2)}) collective-permute-start(bf16[256,1536]{1,0:T(8,128)(2,1)S(1)} %bitcast.22), channel_id=1, source_target_pairs={{0,16},{16,0},{32,48},{48,32},{64,80},{80,64},{96,112},{112,96},{1... | collective-permute-start | bytes 2359304 | tf_op jit(solution)/shard_map/ppermute | solution.py:63
  17.0 2.5 %collective-permute-done.1.refs_2_ = bf16[96,512]{1,0:T(8,128)(2,1)S(1)} collective-permute-done((bf16[96,512]{1,0:T(8,128)(2,1)S(1)}, bf16[96,512]{1,0:T(8,128)(2,1)S(1)}, u32[]{:S(2)}, u32[]{:S(2)}) %collective-permute-start.1) | collective-permute-done | bytes 98336 | tf_op jit(solution)/shard_map/ppermute | solution.py:71
  19.5 0.5 collective-permute-start.4
  20.1 0.1 collective-permute-start.6
  20.1 0.1 pad_add_fusion.2.flags
  20.2 0.6 collective-permute-done.5.refs_6_
  20.8 0.2 collective-permute-done.4.refs_5_
  21.0 0.4 collective-permute-done.6.refs_7_
  21.4 1.4 shard_map.85.feats_ref
  22.8 0.7 copy-done.3
  23.5 10.7 %all-to-all-done = bf16[8,32,1536]{2,1,0:T(8,128)(2,1)S(1)} async-done(((bf16[8,32,1536]{2,1,0:T(8,128)(2,1)}), bf16[8,32,1536]{2,1,0:T(8,128)(2,1)S(1)}, u32[]{:S(2)}, u32[]{:S(2)}) %all-to-all-start) | async-done | bytes 786464 | tf_op jit(solution)/shard_map/all_to_all | solution.py:239
  34.2 0.1 copy.11.refs_3_
  34.4 0.1 add_multiply_fusion
  34.5 0.1 broadcast_add_fusion.1
  34.6 0.1 iota_add_fusion
  34.6 0.1 add.120.refs_2_
  36.0 0.1 pad_add_fusion.1.refs_1_
  36.1 0.1 pad_maximum_fusion.1.refs_0_
  36.2 0.2 collective-permute-done.8.refs_7_
  36.3 0.3 collective-permute-done.7.refs_5_
  36.6 5.2 %shard_map.86 = (bf16[16,32,1664]{2,1,0:T(8,128)(2,1)S(1)}, f32[256,1536]{1,0:T(8,128)S(1)}, bf16[256,1536]{1,0:T(8,128)(2,1)S(1)}) custom-call(f32[2]{0:T(128)S(1)} %pad_maximum_fusion.1.refs_0_, s32[2]{0:T(128)S(1)} %pad_add_fusion.1.refs_1_, s32[1,512]{1,0:T(1,128)S(1)} %add.120.refs_2_, s32[512,1]{1,0:T(8,128)S(1)} %copy.11.refs_3_, ...), custom_call_target="tpu_custom_call" | custom-call | tf_op jit(solution)/shard_map/pallas_call | solution.py:23
  41.9 1.2 copy-done.1
  43.1 1.1 copy-done.2
  44.2 0.1 collective-permute-start.9
  44.4 2.2 %collective-permute-done.9.came_ref = bf16[256,1536]{1,0:T(8,128)(2,1)S(1)} collective-permute-done((bf16[256,1536]{1,0:T(8,128)(2,1)S(1)}, bf16[256,1536]{1,0:T(8,128)(2,1)S(1)}, u32[]{:S(2)}, u32[]{:S(2)}) %collective-permute-start.9) | collective-permute-done | bytes 786464 | tf_op jit(solution)/shard_map/ppermute | solution.py:67
  46.5 0.9 copy-done.6
  47.4 7.5 %all-to-all-start.1 = ((bf16[16,32,1664]{2,1,0:T(8,128)(2,1)}), bf16[16,32,1664]{2,1,0:T(8,128)(2,1)S(1)}, u32[]{:S(2)}, u32[]{:S(2)}) async-start(bf16[16,32,1664]{2,1,0:T(8,128)(2,1)} %copy-done.1), calls=%async_computation.1 | async-start | bytes 3407872 | tf_op jit(solution)/shard_map/all_to_all | solution.py:294
  54.9 2.7 %shard_map.87 = (bf16[32,1536]{1,0:T(8,128)(2,1)}, bf16[32,1536]{1,0:T(8,128)(2,1)}, bf16[32,1536]{1,0:T(8,128)(2,1)}, bf16[32,1536]{1,0:T(8,128)(2,1)}, bf16[32...) custom-call(s32[1]{0:T(128)} %bitcast.10.flags, ...), custom_call_target="tpu_custom_call" | custom-call | tf_op jit(solution)/shard_map/pallas_call | solution.py:23
  57.6 2.6 %collective-permute-start.10 = (bf16[32,1536]{1,0:T(8,128)(2,1)}, bf16[32,1536]{1,0:T(8,128)(2,1)S(1)}, u32[]{:S(2)}, u32[]{:S(2)}) collective-permute-start(bf16[32,1536]{1,0:T(8,128)(2,1)} %get-tuple-element.31), channel_id=1, source_target_pairs={{0,224},{16,240},{32,0},{48,16},{64,32},{80,48},{96,64},{112,80},{... | collective-permute-start | bytes 294920 | tf_op jit(solution)/shard_map/ppermute | solution.py:59
  60.2 2.9 %collective-permute-start.12 = (bf16[32,1536]{1,0:T(8,128)(2,1)}, bf16[32,1536]{1,0:T(8,128)(2,1)S(1)}, u32[]{:S(2)}, u32[]{:S(2)}) collective-permute-start(bf16[32,1536]{1,0:T(8,128)(2,1)} %get-tuple-element.33), channel_id=1, source_target_pairs={{0,192},{16,208},{32,224},{48,240},{64,0},{80,16},{96,32},{112,48}... | collective-permute-start | bytes 294920 | tf_op jit(solution)/shard_map/ppermute | solution.py:59
  63.1 3.8 %collective-permute-start.14 = (bf16[32,1536]{1,0:T(8,128)(2,1)}, bf16[32,1536]{1,0:T(8,128)(2,1)S(1)}, u32[]{:S(2)}, u32[]{:S(2)}) collective-permute-start(bf16[32,1536]{1,0:T(8,128)(2,1)} %get-tuple-element.35), channel_id=1, source_target_pairs={{0,160},{16,176},{32,192},{48,208},{64,224},{80,240},{96,0},{112,1... | collective-permute-start | bytes 294920 | tf_op jit(solution)/shard_map/ppermute | solution.py:59
  66.9 1.3 collective-permute-start.15
  68.2 0.6 copy-done.10
  68.8 3.4 %collective-permute-start.16 = (bf16[32,1536]{1,0:T(8,128)(2,1)}, bf16[32,1536]{1,0:T(8,128)(2,1)S(1)}, u32[]{:S(2)}, u32[]{:S(2)}) collective-permute-start(bf16[32,1536]{1,0:T(8,128)(2,1)} %get-tuple-element.37), channel_id=1, source_target_pairs={{0,128},{16,144},{32,160},{48,176},{64,192},{80,208},{96,224},{112... | collective-permute-start | bytes 294920 | tf_op jit(solution)/shard_map/ppermute | solution.py:59
  72.3 1.5 collective-permute-done.14.refs_5_
  73.8 4.9 %collective-permute-done.15.refs_6_ = bf16[32,1536]{1,0:T(8,128)(2,1)S(1)} collective-permute-done((bf16[32,1536]{1,0:T(8,128)(2,1)}, bf16[32,1536]{1,0:T(8,128)(2,1)S(1)}, u32[]{:S(2)}, u32[]{:S(2)}) %collective-permute-start.15) | collective-permute-done | bytes 98336 | tf_op jit(solution)/shard_map/ppermute | solution.py:59
  78.7 1.3 collective-permute-done.16.refs_7_
  80.1 0.6 copy-done.15
  80.7 3.1 %shard_map.88.d_txt = bf16[32,1536]{1,0:T(8,128)(2,1)} custom-call(bf16[32,1536]{1,0:T(8,128)(2,1)} %get-tuple-element.30.refs_0_, bf16[32,1536]{1,0:T(8,128)(2,1)} %copy-done.9, bf16[32,1536]{1,0:T(8,128)(2,1)} %copy-done.10, bf16[32,1536]{1,0:T(8,128)(2,1)} %copy-done.11, bf16[32,1536]{1,0:T(8,128)(2,1)} %copy-done.12, bf16[32,1536]{1,0:T(8,128)(2,1)} %copy-done.13, ...), custom_call_target="tpu_custom_call" | custom-call | tf_op jit(solution)/shard_map/pallas_call | solution.py:23
  83.8 0.9 copy-done.5
  84.6 0.4 shard_map.89
  85.0 0.1 broadcast_in_dim.7
  85.1 19.8 %all_to_all.25.grads_ref = bf16[16,32,896]{2,1,0:T(8,128)(2,1)S(1)} all-to-all(bf16[16,32,896]{2,1,0:T(8,128)(2,1)S(1)} %bitcast.25), channel_id=1, replica_groups={{0,2,4,6,8,10,12,14,16,18,20,22,24,26,28,30},{1,3,5,7,9,11,13,15,17,19,..., dimensions={0} | all-to-all | bytes 1835008 | tf_op jit(solution)/shard_map/all_to_all | solution.py:294
  104.9 0.5 shard_map.90
  105.4 0.1 collective-permute-start.18
  105.5 1.6 %collective-permute-done.18.came_ref = bf16[192,768]{1,0:T(8,128)(2,1)S(1)} collective-permute-done((bf16[192,768]{1,0:T(8,128)(2,1)S(1)}, bf16[192,768]{1,0:T(8,128)(2,1)S(1)}, u32[]{:S(2)}, u32[]{:S(2)}) %collective-permute-start.18) | collective-permute-done | bytes 294944 | tf_op jit(solution)/shard_map/ppermute | solution.py:67
  107.2 19.9 %all_to_all.26.parts_ref = bf16[8,2,24,384]{3,2,1,0:T(8,128)(2,1)S(1)} all-to-all(bf16[8,2,24,384]{3,2,1,0:T(8,128)(2,1)S(1)} %shard_map.91), channel_id=1, replica_groups={{0,32,64,96,128,160,192,224},{16,48,80,112,144,176,208,240},{1,33,65,97..., dimensions={0} | all-to-all | bytes 589824 | tf_op jit(solution)/shard_map/all_to_all | solution.py:239
  127.1 1.7 %collective-permute-start.19 = (bf16[24,384]{1,0:T(8,128)(2,1)S(1)}, bf16[24,384]{1,0:T(8,128)(2,1)S(1)}, u32[]{:S(2)}, u32[]{:S(2)}) collective-permute-start(bf16[24,384]{1,0:T(8,128)(2,1)S(1)} %get-tuple-element.42), channel_id=1, source_target_pairs={{0,2},{1,3},{2,0},{3,1},{4,6},{5,7},{6,4},{7,5},{8,10},{9,11},{10,... | collective-permute-start | bytes 55304 | tf_op jit(solution)/shard_map/ppermute | solution.py:71
  128.8 2.2 %collective-permute-done.19 = bf16[24,384]{1,0:T(8,128)(2,1)S(1)} collective-permute-done((bf16[24,384]{1,0:T(8,128)(2,1)S(1)}, bf16[24,384]{1,0:T(8,128)(2,1)S(1)}, u32[]{:S(2)}, u32[]{:S(2)}) %collective-permute-start.19) | collective-permute-done | bytes 18464 | tf_op jit(solution)/shard_map/ppermute | solution.py:71
  131.0 0.9 broadcast_in_dim.8
  131.9 3.6 %all-to-all-start.4 = ((bf16[16,2,24,384]{3,2,1,0:T(8,128)(2,1)}), bf16[16,2,24,384]{3,2,1,0:T(8,128)(2,1)S(1)}, u32[]{:S(2)}, u32[]{:S(2)}) async-start(bf16[16,2,24,384]{3,2,1,0:T(8,128)(2,1)} %broadcast_in_dim.8), calls=%async_computation.4 | async-start | bytes 1179648 | tf_op jit(solution)/shard_map/all_to_all | solution.py:344
  135.5 0.1 slice_add_fusion
  135.6 0.1 fusion
  135.7 0.1 collective-permute-start.17
  135.9 1.1 collective-permute-done.17
  137.0 0.7 select_n.95
  137.7 15.1 %all-to-all-done.4.parts_ref = bf16[16,2,24,384]{3,2,1,0:T(8,128)(2,1)S(1)} async-done(((bf16[16,2,24,384]{3,2,1,0:T(8,128)(2,1)}), bf16[16,2,24,384]{3,2,1,0:T(8,128)(2,1)S(1)}, u32[]{:S(2)}, u32[]{:S(2)}) %all-to-all-start.4) | async-done | bytes 589856 | tf_op jit(solution)/shard_map/all_to_all | solution.py:344
  152.8 1.1 shard_map.93
  (49 shorter events, 0.3 us)
Async XLA Ops:
  0.6 14.6 %copy-start = (bf16[512,1536]{1,0:T(8,128)(2,1)S(1)}, bf16[512,1536]{1,0:T(8,128)(2,1)}, u32[]{:S(2)}) copy-start(bf16[512,1536]{1,0:T(8,128)(2,1)} %param.6) | copy-start | bytes 4718596
  0.6 10.5 %copy-start.8 = (bf16[96,512]{1,0:T(8,128)(2,1)S(1)}, bf16[96,512]{1,0:T(8,128)(2,1)}, u32[]{:S(2)}) copy-start(bf16[96,512]{1,0:T(8,128)(2,1)} %param.8) | copy-start | bytes 294916
  0.7 10.5 %copy-start.7 = (bf16[96,512]{1,0:T(8,128)(2,1)S(1)}, bf16[96,512]{1,0:T(8,128)(2,1)}, u32[]{:S(2)}) copy-start(bf16[96,512]{1,0:T(8,128)(2,1)} %param.9) | copy-start | bytes 294916
  2.6 31.6 %all-to-all-start = ((bf16[8,32,1536]{2,1,0:T(8,128)(2,1)}), bf16[8,32,1536]{2,1,0:T(8,128)(2,1)S(1)}, u32[]{:S(2)}, u32[]{:S(2)}) async-start(bf16[8,32,1536]{2,1,0:T(8,128)(2,1)} %broadcast_in_dim.6), calls=%async_computation | async-start | bytes 1572864 | tf_op jit(solution)/shard_map/all_to_all | solution.py:239
  11.8 7.8 %collective-permute-start = (bf16[96,512]{1,0:T(8,128)(2,1)}, bf16[96,512]{1,0:T(8,128)(2,1)S(1)}, u32[]{:S(2)}, u32[]{:S(2)}) collective-permute-start(bf16[96,512]{1,0:T(8,128)(2,1)} %get-tuple-element.45), channel_id=1, source_target_pairs={{0,16},{16,0},{32,48},{48,32},{64,80},{80,64},{96,112},{112,96},{1... | collective-permute-start | bytes 294920 | tf_op jit(solution)/shard_map/ppermute | solution.py:63
  13.4 6.7 %collective-permute-start.2 = (bf16[96,512]{1,0:T(8,128)(2,1)}, bf16[96,512]{1,0:T(8,128)(2,1)S(1)}, u32[]{:S(2)}, u32[]{:S(2)}) collective-permute-start(bf16[96,512]{1,0:T(8,128)(2,1)} %get-tuple-element.45), channel_id=1, source_target_pairs={{0,18},{1,19},{2,16},{3,17},{4,22},{5,23},{6,20},{7,21},{8,26},{9,... | collective-permute-start | bytes 294920 | tf_op jit(solution)/shard_map/ppermute | solution.py:76
  13.8 5.8 %collective-permute-start.1 = (bf16[96,512]{1,0:T(8,128)(2,1)S(1)}, bf16[96,512]{1,0:T(8,128)(2,1)S(1)}, u32[]{:S(2)}, u32[]{:S(2)}) collective-permute-start(bf16[96,512]{1,0:T(8,128)(2,1)S(1)} %get-tuple-element.46.refs_0_), channel_id=1, source_target_pairs={{0,2},{1,3},{2,0},{3,1},{4,6},{5,7},{6,4},{7,5},{8,10},{9,11},{10,... | collective-permute-start | bytes 294920 | tf_op jit(solution)/shard_map/ppermute | solution.py:71
  15.3 5.0 %collective-permute-start.3 = (bf16[96,512]{1,0:T(8,128)(2,1)S(1)}, bf16[96,512]{1,0:T(8,128)(2,1)}, u32[]{:S(2)}, u32[]{:S(2)}) collective-permute-start(bf16[96,512]{1,0:T(8,128)(2,1)S(1)} %get-tuple-element.46.refs_0_), channel_id=1, source_target_pairs={{0,1},{1,0},{2,3},{3,2},{4,5},{5,4},{6,7},{7,6},{8,9},{9,8},{10,11... | collective-permute-start | bytes 294920 | tf_op jit(solution)/shard_map/ppermute | solution.py:67
  15.3 21.0 %collective-permute-start.8 = (bf16[256,1536]{1,0:T(8,128)(2,1)S(1)}, bf16[256,1536]{1,0:T(8,128)(2,1)}, u32[]{:S(2)}, u32[]{:S(2)}) collective-permute-start(bf16[256,1536]{1,0:T(8,128)(2,1)S(1)} %bitcast.22), channel_id=1, source_target_pairs={{0,16},{16,0},{32,48},{48,32},{64,80},{80,64},{96,112},{112,96},{1... | collective-permute-start | bytes 2359304 | tf_op jit(solution)/shard_map/ppermute | solution.py:63
  19.5 1.3 collective-permute-start.5
  19.5 1.5 collective-permute-start.4
  20.1 1.3 collective-permute-start.6
  22.8 0.7 copy-start.3
  34.2 2.4 %collective-permute-start.7 = (bf16[256,1536]{1,0:T(8,128)(2,1)S(1)}, bf16[256,1536]{1,0:T(8,128)(2,1)}, u32[]{:S(2)}, u32[]{:S(2)}) collective-permute-start(bf16[256,1536]{1,0:T(8,128)(2,1)S(1)} %bitcast.20), channel_id=1, source_target_pairs={{0,1},{1,0},{2,3},{3,2},{4,5},{5,4},{6,7},{7,6},{8,9},{9,8},{10,11... | collective-permute-start | bytes 2359304 | tf_op jit(solution)/shard_map/ppermute | solution.py:67
  41.9 1.2 copy-start.1
  43.1 1.1 copy-start.2
  44.2 2.3 %collective-permute-start.9 = (bf16[256,1536]{1,0:T(8,128)(2,1)S(1)}, bf16[256,1536]{1,0:T(8,128)(2,1)S(1)}, u32[]{:S(2)}, u32[]{:S(2)}) collective-permute-start(bf16[256,1536]{1,0:T(8,128)(2,1)S(1)} %get-tuple-element.26), channel_id=1, source_target_pairs={{0,1},{1,0},{2,3},{3,2},{4,5},{5,4},{6,7},{7,6},{8,9},{9,8},{10,11... | collective-permute-start | bytes 2359304 | tf_op jit(solution)/shard_map/ppermute | solution.py:67
  46.5 0.9 copy-start.6
  47.4 36.3 %all-to-all-start.1 = ((bf16[16,32,1664]{2,1,0:T(8,128)(2,1)}), bf16[16,32,1664]{2,1,0:T(8,128)(2,1)S(1)}, u32[]{:S(2)}, u32[]{:S(2)}) async-start(bf16[16,32,1664]{2,1,0:T(8,128)(2,1)} %copy-done.1), calls=%async_computation.1 | async-start | bytes 3407872 | tf_op jit(solution)/shard_map/all_to_all | solution.py:294
  57.6 9.4 %collective-permute-start.10 = (bf16[32,1536]{1,0:T(8,128)(2,1)}, bf16[32,1536]{1,0:T(8,128)(2,1)S(1)}, u32[]{:S(2)}, u32[]{:S(2)}) collective-permute-start(bf16[32,1536]{1,0:T(8,128)(2,1)} %get-tuple-element.31), channel_id=1, source_target_pairs={{0,224},{16,240},{32,0},{48,16},{64,32},{80,48},{96,64},{112,80},{... | collective-permute-start | bytes 294920 | tf_op jit(solution)/shard_map/ppermute | solution.py:59
  60.1 8.1 %collective-permute-start.11 = (bf16[32,1536]{1,0:T(8,128)(2,1)}, bf16[32,1536]{1,0:T(8,128)(2,1)S(1)}, u32[]{:S(2)}, u32[]{:S(2)}) collective-permute-start(bf16[32,1536]{1,0:T(8,128)(2,1)} %get-tuple-element.32), channel_id=1, source_target_pairs={{0,32},{16,48},{32,64},{48,80},{64,96},{80,112},{96,128},{112,144}... | collective-permute-start | bytes 294920 | tf_op jit(solution)/shard_map/ppermute | solution.py:59
  60.2 12.1 %collective-permute-start.12 = (bf16[32,1536]{1,0:T(8,128)(2,1)}, bf16[32,1536]{1,0:T(8,128)(2,1)S(1)}, u32[]{:S(2)}, u32[]{:S(2)}) collective-permute-start(bf16[32,1536]{1,0:T(8,128)(2,1)} %get-tuple-element.33), channel_id=1, source_target_pairs={{0,192},{16,208},{32,224},{48,240},{64,0},{80,16},{96,32},{112,48}... | collective-permute-start | bytes 294920 | tf_op jit(solution)/shard_map/ppermute | solution.py:59
  63.1 9.2 %collective-permute-start.13 = (bf16[32,1536]{1,0:T(8,128)(2,1)}, bf16[32,1536]{1,0:T(8,128)(2,1)S(1)}, u32[]{:S(2)}, u32[]{:S(2)}) collective-permute-start(bf16[32,1536]{1,0:T(8,128)(2,1)} %get-tuple-element.34), channel_id=1, source_target_pairs={{0,64},{16,80},{32,96},{48,112},{64,128},{80,144},{96,160},{112,17... | collective-permute-start | bytes 294920 | tf_op jit(solution)/shard_map/ppermute | solution.py:59
  63.1 10.7 %collective-permute-start.14 = (bf16[32,1536]{1,0:T(8,128)(2,1)}, bf16[32,1536]{1,0:T(8,128)(2,1)S(1)}, u32[]{:S(2)}, u32[]{:S(2)}) collective-permute-start(bf16[32,1536]{1,0:T(8,128)(2,1)} %get-tuple-element.35), channel_id=1, source_target_pairs={{0,160},{16,176},{32,192},{48,208},{64,224},{80,240},{96,0},{112,1... | collective-permute-start | bytes 294920 | tf_op jit(solution)/shard_map/ppermute | solution.py:59
  66.9 13.1 %copy-start.9 = (bf16[32,1536]{1,0:T(8,128)(2,1)}, bf16[32,1536]{1,0:T(8,128)(2,1)S(1)}, u32[]{:S(2)}) copy-start(bf16[32,1536]{1,0:T(8,128)(2,1)S(1)} %collective-permute-done.10.refs_1_) | copy-start | bytes 294916
  66.9 11.8 %collective-permute-start.15 = (bf16[32,1536]{1,0:T(8,128)(2,1)}, bf16[32,1536]{1,0:T(8,128)(2,1)S(1)}, u32[]{:S(2)}, u32[]{:S(2)}) collective-permute-start(bf16[32,1536]{1,0:T(8,128)(2,1)} %get-tuple-element.36), channel_id=1, source_target_pairs={{0,96},{16,112},{32,128},{48,144},{64,160},{80,176},{96,192},{112,... | collective-permute-start | bytes 294920 | tf_op jit(solution)/shard_map/ppermute | solution.py:59
  68.2 0.6 copy-start.10
  68.8 11.2 %collective-permute-start.16 = (bf16[32,1536]{1,0:T(8,128)(2,1)}, bf16[32,1536]{1,0:T(8,128)(2,1)S(1)}, u32[]{:S(2)}, u32[]{:S(2)}) collective-permute-start(bf16[32,1536]{1,0:T(8,128)(2,1)} %get-tuple-element.37), channel_id=1, source_target_pairs={{0,128},{16,144},{32,160},{48,176},{64,192},{80,208},{96,224},{112... | collective-permute-start | bytes 294920 | tf_op jit(solution)/shard_map/ppermute | solution.py:59
  72.3 7.8 %copy-start.11 = (bf16[32,1536]{1,0:T(8,128)(2,1)}, bf16[32,1536]{1,0:T(8,128)(2,1)S(1)}, u32[]{:S(2)}) copy-start(bf16[32,1536]{1,0:T(8,128)(2,1)S(1)} %collective-permute-done.12.refs_3_) | copy-start | bytes 294916
  72.3 7.7 %copy-start.12 = (bf16[32,1536]{1,0:T(8,128)(2,1)}, bf16[32,1536]{1,0:T(8,128)(2,1)S(1)}, u32[]{:S(2)}) copy-start(bf16[32,1536]{1,0:T(8,128)(2,1)S(1)} %collective-permute-done.13.refs_4_) | copy-start | bytes 294916
  73.8 6.3 %copy-start.13 = (bf16[32,1536]{1,0:T(8,128)(2,1)}, bf16[32,1536]{1,0:T(8,128)(2,1)S(1)}, u32[]{:S(2)}) copy-start(bf16[32,1536]{1,0:T(8,128)(2,1)S(1)} %collective-permute-done.14.refs_5_) | copy-start | bytes 294916
  78.7 1.3 copy-start.14
  80.0 0.6 copy-start.15
  83.7 0.9 copy-start.5
  85.0 19.9 %copy-start.4 = (bf16[384,512]{1,0:T(8,128)(2,1)S(1)}, bf16[384,512]{1,0:T(8,128)(2,1)}, u32[]{:S(2)}) copy-start(bf16[384,512]{1,0:T(8,128)(2,1)} %copy-done.3) | copy-start | bytes 1179652
  105.4 1.7 %collective-permute-start.18 = (bf16[192,768]{1,0:T(8,128)(2,1)S(1)}, bf16[192,768]{1,0:T(8,128)(2,1)S(1)}, u32[]{:S(2)}, u32[]{:S(2)}) collective-permute-start(bf16[192,768]{1,0:T(8,128)(2,1)S(1)} %get-tuple-element.40), channel_id=1, source_target_pairs={{0,1},{1,0},{2,3},{3,2},{4,5},{5,4},{6,7},{7,6},{8,9},{9,8},{10,11... | collective-permute-start | bytes 884744 | tf_op jit(solution)/shard_map/ppermute | solution.py:67
  127.1 3.8 %collective-permute-start.19 = (bf16[24,384]{1,0:T(8,128)(2,1)S(1)}, bf16[24,384]{1,0:T(8,128)(2,1)S(1)}, u32[]{:S(2)}, u32[]{:S(2)}) collective-permute-start(bf16[24,384]{1,0:T(8,128)(2,1)S(1)} %get-tuple-element.42), channel_id=1, source_target_pairs={{0,2},{1,3},{2,0},{3,1},{4,6},{5,7},{6,4},{7,5},{8,10},{9,11},{10,... | collective-permute-start | bytes 55304 | tf_op jit(solution)/shard_map/ppermute | solution.py:71
  131.9 20.9 %all-to-all-start.4 = ((bf16[16,2,24,384]{3,2,1,0:T(8,128)(2,1)}), bf16[16,2,24,384]{3,2,1,0:T(8,128)(2,1)S(1)}, u32[]{:S(2)}, u32[]{:S(2)}) async-start(bf16[16,2,24,384]{3,2,1,0:T(8,128)(2,1)} %broadcast_in_dim.8), calls=%async_computation.4 | async-start | bytes 1179648 | tf_op jit(solution)/shard_map/all_to_all | solution.py:344
  135.7 1.3 collective-permute-start.17

commit v12 on v8

--- a/solution.py
+++ b/solution.py
@@ -72,6 +72,11 @@
     return lax.ppermute(value, "mp", [(m, m ^ 2) for m in range(16)])
 
 
+def swap_both(value):
+    pairs = [(16 * d + m, 16 * (d ^ 1) + (m ^ 2)) for d in range(16) for m in range(16)]
+    return lax.ppermute(value, ("dp", "mp"), pairs)
+
+
 def loss_columns(losses):
     high = losses.astype(BF16)
     low = (losses - high.astype(F32)).astype(BF16)
@@ -86,17 +91,17 @@
 
 
 def feature_kernel(flags, *refs):
-    sources, out_ref = refs[:4], refs[4]
-    rows = sources[0].shape[1]
-    count, half = sources[0].shape[0] // 2, rows // 2
+    sources, out_ref = refs[:8], refs[8]
+    count, rows = sources[0].shape
+    half = rows // 2
     y, core = flags[0], flags[1]
     source = lax.broadcasted_iota(jnp.int32, (rows, half), 0)
     target = lax.broadcasted_iota(jnp.int32, (rows, half), 1)
     chosen = source == (target // 32) * 64 + core * 32 + target % 32
     pick = jnp.where(chosen, 1.0, 0.0).astype(BF16)
-    for i, ref in enumerate(sources):
-        both = jnp.dot(ref[...], pick, preferred_element_type=F32)
-        own, other = both[:count].astype(BF16), both[count:].astype(BF16)
+    for i in range(4):
+        own = jnp.dot(sources[2 * i][...], pick, preferred_element_type=F32).astype(BF16)
+        other = jnp.dot(sources[2 * i + 1][...], pick, preferred_element_type=F32).astype(BF16)
         place = pl.ds(i * count, count)
         out_ref[place, pl.ds(0, half)] = jnp.where(y == 0, own, other)
         out_ref[place, pl.ds(half, half)] = jnp.where(y == 0, other, own)
@@ -120,9 +125,10 @@
         u = jnp.where(match, -logits, logits)
         e = jnp.exp(-jnp.abs(u))
         w = 1.0 + e
-        grown = jnp.where(w == 1.0, e, jnp.log(w) * (e / jnp.where(w == 1.0, 1.0, w - 1.0)))
+        inverse = 1.0 / w
+        grown = jnp.log(w) + (e - (w - 1.0)) * inverse
         loss_ref[place, :] = jnp.sum(jnp.maximum(u, 0.0) + grown, axis=1, keepdims=True)
-        slope = jnp.where(match, -scale, scale) * (jnp.where(u >= 0.0, 1.0, e) / w)
+        slope = jnp.where(match, -scale, scale) * (jnp.where(u >= 0.0, 1.0, e) * inverse)
         slopes[place, :] = slope.astype(BF16)
     text_grad = lax.dot_general(
         slopes[...], images[...], (((0,), (0,)), ((), ())), preferred_element_type=F32
@@ -240,12 +246,20 @@
 
     texts = over_z(jnp.broadcast_to(txt_emb[None], (8, sub, width))).reshape(half, width)
     mine = jnp.where(y == 0, img_feat_t, txt_feat_t)
-    came = swap_y(jnp.where(y == 0, txt_feat_t, img_feat_t))
+    theirs = jnp.where(y == 0, txt_feat_t, img_feat_t)
+    came, mine_x, came_x = swap_y(theirs), swap_x(mine), swap_both(theirs)
+    sources = (mine, came, mine_x, came_x)
+    feat_part = local(
+        feature_kernel,
+        ((4 * feats, rows), BF16),
+        [jnp.stack([y, core]), *sources, *map(swap_core, sources)],
+        8,
+        [SMEM] + [VMEM] * 8,
+    )
+    texts, feat_part = lax.optimization_barrier((texts, feat_part))
     by_core = img_emb.reshape(8, 2, sub, width)
     own = lax.dynamic_slice_in_dim(by_core, core, 1, 1).reshape(half, width)
     partner = swap_y(own)
-    pair = jnp.concatenate([mine, came])
-    pair_x = swap_x(pair)
     owners = 2 * jnp.arange(8, dtype=jnp.int32) + y
     cores = jnp.stack([mp_index, mp_index ^ 1])
     text_ids = owners[None, :, None] * rows + cores[:, None, None] * sub
@@ -301,6 +315,7 @@
             value, ("dp", "mp"), 0, 0, tiled=True, axis_index_groups=plane
         )
 
+    image_part, came_grad = lax.optimization_barrier((image_part, came_grad))
     text_parts = local(
         join_kernel,
         [((sub, width), BF16)] * 8,
@@ -310,7 +325,6 @@
         [HBM] * 8,
         [pltpu.VMEM((8, sub, width), BF16), DMA((8,))],
     )
-    image_part, pair_x, *text_parts = lax.optimization_barrier((image_part, pair_x, *text_parts))
     image_pieces = over_plane(image_part)
     text_came = [text_parts[0]] + [
         along_z(part, -steps) for part, steps in zip(text_parts[1:], ALONG[1:], strict=True)
@@ -324,15 +338,7 @@
         None,
         [pltpu.VMEM((8, sub, width), BF16), DMA((8,))],
     )
-    feat_part = local(
-        feature_kernel,
-        ((4 * feats, rows), BF16),
-        [jnp.stack([y, core]), pair, pair_x, swap_core(pair), swap_core(pair_x)],
-        8,
-        [SMEM] + [VMEM] * 4,
-    )
     raw_img = lax.dynamic_slice_in_dim(img_emb, (2 * chip + core) * sub, sub, 0)
-    raw_img, feat_part = lax.optimization_barrier((raw_img, feat_part))
     narrow = width // 2
     kinds = local(
         grad_kernel,

time: 174 us -> 161 us (0.925)
  waiting for transfers between devices: 54.9 us -> 42 us
  blocking collectives: 37.1 us -> 40.8 us
  local copies, waits for them, and re-layouts: 18.6 us -> 16.2 us
    all_to_all x1, waiting for transfers between devices: 21.4 us -> 10.7 us  [over_z(): lax.all_to_all(value, 'dp', 0, 0, tiled=True, axis_index_groups=same_y)]
    ppermute x2, waiting for transfers between devices: 3.48 us -> 0.23 us  [swap_y(): return lax.ppermute(value, 'dp', [(d, d ^ 1) for d in range(16)])]
    ppermute x2, waiting for transfers between devices: 2.3 us -> 4.8 us  [swap_x(): return lax.ppermute(value, 'mp', [(m, m ^ 2) for m in range(16)])]
    ppermute x7, waiting for transfers between devices: 9.43 us -> 7.05 us  [along_z(): lax.ppermute(value, 'dp', [(d, (d + 2 * steps) % 16) for d in range(16)])]
    ppermute x7, starting transfers between devices: 16.1 us -> 14 us  [along_z(): lax.ppermute(value, 'dp', [(d, (d + 2 * steps) % 16) for d in range(16)])]
    all_to_all x1, blocking collectives: 18.1 us -> 20 us  [over_plane(): lax.all_to_all(value, ('dp', 'mp'), 0, 0, tiled=True, axis_index_groups=p...]
    unnamed x46 -> x44, local copies, waits for them, and re-layouts: 14.1 us -> 12.2 us
    ppermute x6 -> x8, waiting for transfers between devices: 3.24 us -> 4.14 us  [swap_core(): return lax.ppermute(value, 'mp', [(m, m ^ 1) for m in range(16)])]
  transfers between devices with their start and end apart: 20 -> 23, of which waited for: 11 -> 14; matrix products, arithmetic and copies ran while one was open for 2% -> 1% of each run, Pallas kernels for 5% -> 5%
where the time goes in v12:
time: 161 us; the launch traced here: 160 us
  waiting for transfers between devices  42 us (26%)
  starting transfers between devices  41.2 us (26%)
  blocking collectives  40.8 us (25%)
  local copies, waits for them, and re-layouts  16.2 us (10%)
  Pallas kernels  16 us (10%)
  between operations  2.24 us (1%)
    all_to_all x1, blocking collectives, over_z(): lax.all_to_all(value, 'dp', 0, 0, tiled=True, axis_index_groups=same_y)  20.8 us
    all_to_all x1, blocking collectives, over_plane(): lax.all_to_all(value, ('dp', 'mp'), 0, 0, tiled=True, axis_index_groups=p...  20 us
    pallas_call x10, Pallas kernels, local(): pl.pallas_call(kernel, out_shape=shapes, in_specs=specs or [VMEM] * len(o...  16 us
    all_to_all x1, waiting for transfers between devices, shards(): lax.all_to_all(jnp.broadcast_to(summed[None], (16, 2, *shape)), 'dp', 0,...  15.1 us
    ppermute x7, starting transfers between devices, along_z(): lax.ppermute(value, 'dp', [(d, (d + 2 * steps) % 16) for d in range(16)])  14 us
    unnamed x44, local copies, waits for them, and re-layouts  12.2 us
    all_to_all x1, waiting for transfers between devices, over_z(): lax.all_to_all(value, 'dp', 0, 0, tiled=True, axis_index_groups=same_y)  10.7 us
    all_to_all x1, starting transfers between devices, over_z(): lax.all_to_all(value, 'dp', 0, 0, tiled=True, axis_index_groups=same_y)  8.47 us
  transfers between devices with their start and end apart: 23, of which 14 were waited for; matrix products, arithmetic and copies ran while one was open for 1% of the time, Pallas kernels for 5%

profile of v12, /device:TPU:2, one launch (start us, length us, event | category | flops | bytes accessed | tf_op | source)
XLA Modules:
  0.0 159.8 jit_solution(3077731027328774905)
XLA Ops:
  0.7 2.0 %broadcast_in_dim.6 = bf16[8,32,1536]{2,1,0:T(8,128)(2,1)} broadcast(bf16[32,1536]{1,0:T(8,128)(2,1)} %refs_8_.1), dimensions={1,2} | broadcast | bytes 884736 | tf_op jit(solution)/shard_map/broadcast_in_dim | solution.py:247
  2.6 8.5 %all-to-all-start = ((bf16[8,32,1536]{2,1,0:T(8,128)(2,1)}), bf16[8,32,1536]{2,1,0:T(8,128)(2,1)S(1)}, u32[]{:S(2)}, u32[]{:S(2)}) async-start(bf16[8,32,1536]{2,1,0:T(8,128)(2,1)} %broadcast_in_dim.6), calls=%async_computation | async-start | bytes 1572864 | tf_op jit(solution)/shard_map/all_to_all | solution.py:245
  11.1 0.7 broadcast_select_fusion
  11.8 1.6 collective-permute-start
  13.4 0.4 collective-permute-start.2
  13.8 1.5 collective-permute-start.1
  15.4 1.7 %collective-permute-start.8 = (bf16[256,1536]{1,0:T(8,128)(2,1)S(1)}, bf16[256,1536]{1,0:T(8,128)(2,1)}, u32[]{:S(2)}, u32[]{:S(2)}) collective-permute-start(bf16[256,1536]{1,0:T(8,128)(2,1)S(1)} %bitcast.22), channel_id=1, source_target_pairs={{0,16},{16,0},{32,48},{48,32},{64,80},{80,64},{96,112},{112,96},{1... | collective-permute-start | bytes 2359304 | tf_op jit(solution)/shard_map/ppermute | solution.py:64
  17.0 2.5 %collective-permute-done.1.refs_2_ = bf16[96,512]{1,0:T(8,128)(2,1)S(1)} collective-permute-done((bf16[96,512]{1,0:T(8,128)(2,1)S(1)}, bf16[96,512]{1,0:T(8,128)(2,1)S(1)}, u32[]{:S(2)}, u32[]{:S(2)}) %collective-permute-start.1) | collective-permute-done | bytes 98336 | tf_op jit(solution)/shard_map/ppermute | solution.py:72
  19.5 0.5 collective-permute-start.4
  20.1 0.1 collective-permute-start.6
  20.2 0.6 collective-permute-done.5.refs_6_
  20.8 0.2 collective-permute-done.4.refs_5_
  21.0 0.4 collective-permute-done.6.refs_7_
  21.4 1.4 shard_map.85.feats_ref
  22.8 0.7 copy-done.3
  23.5 10.7 %all-to-all-done = bf16[8,32,1536]{2,1,0:T(8,128)(2,1)S(1)} async-done(((bf16[8,32,1536]{2,1,0:T(8,128)(2,1)}), bf16[8,32,1536]{2,1,0:T(8,128)(2,1)S(1)}, u32[]{:S(2)}, u32[]{:S(2)}) %all-to-all-start) | async-done | bytes 786464 | tf_op jit(solution)/shard_map/all_to_all | solution.py:245
  34.2 0.1 copy.11.image_ids
  36.1 0.2 collective-permute-done.8.partner
  36.3 0.3 collective-permute-done.7.far
  36.6 5.3 %shard_map.86 = (bf16[512,1536]{1,0:T(8,128)(2,1)S(1)}, bf16[512,512]{1,0:T(8,128)(2,1)S(1)}, f32[512,1]{1,0:T(8,128)S(1)}, f32[256,1536]{1,0:T(8,128)S(1)}, bf16[256,1536]{1,0:T(8,128)(2,1)}) custom-call(f32[2]{0:T(128)S(1)} %pad_maximum_fusion.1.numbers, s32[1,512]{1,0:T(1,128)S(1)} %add.120.text_ids, s32[512,1]{1,0:T(8,128)S(1)} %copy.11.image_ids, ...), custom_call_target="tpu_custom_call" | custom-call | flops 4000000000 | tf_op jit(solution)/shard_map/pallas_call | solution.py:23
  42.0 1.1 copy-done.2
  43.1 1.2 copy-done.6
  44.3 0.8 copy-done.8
  45.1 0.7 copy-done.10
  45.8 0.1 collective-permute-start.9
  46.0 1.4 copy-done.7
  47.4 1.0 copy-done.9
  48.4 0.9 copy-done.11
  49.4 1.5 shard_map.87
  50.9 1.2 copy-done.1
  52.2 0.9 copy-done.12
  53.0 7.5 %all-to-all-start.1 = ((bf16[16,32,1664]{2,1,0:T(8,128)(2,1)}), bf16[16,32,1664]{2,1,0:T(8,128)(2,1)S(1)}, u32[]{:S(2)}, u32[]{:S(2)}) async-start(bf16[16,32,1664]{2,1,0:T(8,128)(2,1)} %copy-done.1), calls=%async_computation.1 | async-start | bytes 3407872 | tf_op jit(solution)/shard_map/all_to_all | solution.py:314
  60.5 2.7 %shard_map.88 = (bf16[32,1536]{1,0:T(8,128)(2,1)}, bf16[32,1536]{1,0:T(8,128)(2,1)}, bf16[32,1536]{1,0:T(8,128)(2,1)}, bf16[32,1536]{1,0:T(8,128)(2,1)}, bf16[32...) custom-call(s32[1]{0:T(128)} %bitcast.10.flags, ...), custom_call_target="tpu_custom_call" | custom-call | tf_op jit(solution)/shard_map/pallas_call | solution.py:23
  63.2 2.5 %collective-permute-start.10 = (bf16[32,1536]{1,0:T(8,128)(2,1)}, bf16[32,1536]{1,0:T(8,128)(2,1)S(1)}, u32[]{:S(2)}, u32[]{:S(2)}) collective-permute-start(bf16[32,1536]{1,0:T(8,128)(2,1)} %get-tuple-element.35), channel_id=1, source_target_pairs={{0,224},{16,240},{32,0},{48,16},{64,32},{80,48},{96,64},{112,80},{... | collective-permute-start | bytes 294920 | tf_op jit(solution)/shard_map/ppermute | solution.py:60
  65.7 2.9 %collective-permute-start.12 = (bf16[32,1536]{1,0:T(8,128)(2,1)}, bf16[32,1536]{1,0:T(8,128)(2,1)S(1)}, u32[]{:S(2)}, u32[]{:S(2)}) collective-permute-start(bf16[32,1536]{1,0:T(8,128)(2,1)} %get-tuple-element.37), channel_id=1, source_target_pairs={{0,192},{16,208},{32,224},{48,240},{64,0},{80,16},{96,32},{112,48}... | collective-permute-start | bytes 294920 | tf_op jit(solution)/shard_map/ppermute | solution.py:60
  68.6 3.8 %collective-permute-start.14 = (bf16[32,1536]{1,0:T(8,128)(2,1)}, bf16[32,1536]{1,0:T(8,128)(2,1)S(1)}, u32[]{:S(2)}, u32[]{:S(2)}) collective-permute-start(bf16[32,1536]{1,0:T(8,128)(2,1)} %get-tuple-element.39), channel_id=1, source_target_pairs={{0,160},{16,176},{32,192},{48,208},{64,224},{80,240},{96,0},{112,1... | collective-permute-start | bytes 294920 | tf_op jit(solution)/shard_map/ppermute | solution.py:60
  72.5 1.3 collective-permute-start.15
  73.8 0.6 copy-done.16
  74.4 3.4 %collective-permute-start.16 = (bf16[32,1536]{1,0:T(8,128)(2,1)}, bf16[32,1536]{1,0:T(8,128)(2,1)S(1)}, u32[]{:S(2)}, u32[]{:S(2)}) collective-permute-start(bf16[32,1536]{1,0:T(8,128)(2,1)} %get-tuple-element.41), channel_id=1, source_target_pairs={{0,128},{16,144},{32,160},{48,176},{64,192},{80,208},{96,224},{112... | collective-permute-start | bytes 294920 | tf_op jit(solution)/shard_map/ppermute | solution.py:60
  77.9 1.4 collective-permute-done.14.refs_5_
  79.2 5.3 %collective-permute-done.15.refs_6_ = bf16[32,1536]{1,0:T(8,128)(2,1)S(1)} collective-permute-done((bf16[32,1536]{1,0:T(8,128)(2,1)}, bf16[32,1536]{1,0:T(8,128)(2,1)S(1)}, u32[]{:S(2)}, u32[]{:S(2)}) %collective-permute-start.15) | collective-permute-done | bytes 98336 | tf_op jit(solution)/shard_map/ppermute | solution.py:60
  84.5 0.4 collective-permute-done.16.refs_7_
  84.9 0.2 copy-done.20
  85.2 0.4 copy-done.21
  85.6 3.0 %shard_map.89.d_txt = bf16[32,1536]{1,0:T(8,128)(2,1)} custom-call(bf16[32,1536]{1,0:T(8,128)(2,1)} %get-tuple-element.34.refs_0_, bf16[32,1536]{1,0:T(8,128)(2,1)} %copy-done.15, bf16[32,1536]{1,0:T(8,128)(2,1)} %copy-done.16, bf16[32,1536]{1,0:T(8,128)(2,1)} %copy-done.17, bf16[32,1536]{1,0:T(8,128)(2,1)} %copy-done.18, bf16[32,1536]{1,0:T(8,128)(2,1)} %copy-done.19, ...), custom_call_target="tpu_custom_call" | custom-call | tf_op jit(solution)/shard_map/pallas_call | solution.py:23
  88.6 0.9 copy-done.5
  89.5 0.4 shard_map.90
  89.9 0.1 broadcast_in_dim.7
  90.0 20.0 %all_to_all.25.grads_ref = bf16[16,32,896]{2,1,0:T(8,128)(2,1)S(1)} all-to-all(bf16[16,32,896]{2,1,0:T(8,128)(2,1)S(1)} %bitcast.25), channel_id=1, replica_groups={{0,2,4,6,8,10,12,14,16,18,20,22,24,26,28,30},{1,3,5,7,9,11,13,15,17,19,..., dimensions={0} | all-to-all | bytes 1835008 | tf_op jit(solution)/shard_map/all_to_all | solution.py:314
  110.0 0.5 shard_map.91
  110.5 0.1 collective-permute-start.18
  110.6 1.6 collective-permute-done.18.came_ref
  112.2 20.8 %all_to_all.26.parts_ref = bf16[8,2,24,384]{3,2,1,0:T(8,128)(2,1)S(1)} all-to-all(bf16[8,2,24,384]{3,2,1,0:T(8,128)(2,1)S(1)} %shard_map.92), channel_id=1, replica_groups={{0,32,64,96,128,160,192,224},{16,48,80,112,144,176,208,240},{1,33,65,97..., dimensions={0} | all-to-all | bytes 589824 | tf_op jit(solution)/shard_map/all_to_all | solution.py:245
  133.1 1.6 collective-permute-start.19
  134.6 2.3 %collective-permute-done.19 = bf16[24,384]{1,0:T(8,128)(2,1)S(1)} collective-permute-done((bf16[24,384]{1,0:T(8,128)(2,1)S(1)}, bf16[24,384]{1,0:T(8,128)(2,1)S(1)}, u32[]{:S(2)}, u32[]{:S(2)}) %collective-permute-start.19) | collective-permute-done | bytes 18464 | tf_op jit(solution)/shard_map/ppermute | solution.py:72
  136.9 0.9 broadcast_in_dim.8
  137.8 3.6 %all-to-all-start.4 = ((bf16[16,2,24,384]{3,2,1,0:T(8,128)(2,1)}), bf16[16,2,24,384]{3,2,1,0:T(8,128)(2,1)S(1)}, u32[]{:S(2)}, u32[]{:S(2)}) async-start(bf16[16,2,24,384]{3,2,1,0:T(8,128)(2,1)} %broadcast_in_dim.8), calls=%async_computation.4 | async-start | bytes 1179648 | tf_op jit(solution)/shard_map/all_to_all | solution.py:363
  141.4 0.1 slice_add_fusion
  141.6 0.1 fusion
  141.7 0.1 collective-permute-start.17
  141.8 1.1 collective-permute-done.17
  142.9 0.7 select_n.95
  143.6 15.1 %all-to-all-done.4.parts_ref = bf16[16,2,24,384]{3,2,1,0:T(8,128)(2,1)S(1)} async-done(((bf16[16,2,24,384]{3,2,1,0:T(8,128)(2,1)}), bf16[16,2,24,384]{3,2,1,0:T(8,128)(2,1)S(1)}, u32[]{:S(2)}, u32[]{:S(2)}) %all-to-all-start.4) | async-done | bytes 589856 | tf_op jit(solution)/shard_map/all_to_all | solution.py:363
  158.7 1.1 shard_map.94
  (62 shorter events, 0.9 us)
Async XLA Ops:
  0.6 14.7 %copy-start = (bf16[512,1536]{1,0:T(8,128)(2,1)S(1)}, bf16[512,1536]{1,0:T(8,128)(2,1)}, u32[]{:S(2)}) copy-start(bf16[512,1536]{1,0:T(8,128)(2,1)} %param.6) | copy-start | bytes 4718596
  0.6 10.5 %copy-start.14 = (bf16[96,512]{1,0:T(8,128)(2,1)S(1)}, bf16[96,512]{1,0:T(8,128)(2,1)}, u32[]{:S(2)}) copy-start(bf16[96,512]{1,0:T(8,128)(2,1)} %param.8) | copy-start | bytes 294916
  0.7 10.5 %copy-start.13 = (bf16[96,512]{1,0:T(8,128)(2,1)S(1)}, bf16[96,512]{1,0:T(8,128)(2,1)}, u32[]{:S(2)}) copy-start(bf16[96,512]{1,0:T(8,128)(2,1)} %param.9) | copy-start | bytes 294916
  2.6 31.6 %all-to-all-start = ((bf16[8,32,1536]{2,1,0:T(8,128)(2,1)}), bf16[8,32,1536]{2,1,0:T(8,128)(2,1)S(1)}, u32[]{:S(2)}, u32[]{:S(2)}) async-start(bf16[8,32,1536]{2,1,0:T(8,128)(2,1)} %broadcast_in_dim.6), calls=%async_computation | async-start | bytes 1572864 | tf_op jit(solution)/shard_map/all_to_all | solution.py:245
  11.8 7.8 %collective-permute-start = (bf16[96,512]{1,0:T(8,128)(2,1)}, bf16[96,512]{1,0:T(8,128)(2,1)S(1)}, u32[]{:S(2)}, u32[]{:S(2)}) collective-permute-start(bf16[96,512]{1,0:T(8,128)(2,1)} %get-tuple-element.49), channel_id=1, source_target_pairs={{0,16},{16,0},{32,48},{48,32},{64,80},{80,64},{96,112},{112,96},{1... | collective-permute-start | bytes 294920 | tf_op jit(solution)/shard_map/ppermute | solution.py:64
  13.4 6.7 %collective-permute-start.2 = (bf16[96,512]{1,0:T(8,128)(2,1)}, bf16[96,512]{1,0:T(8,128)(2,1)S(1)}, u32[]{:S(2)}, u32[]{:S(2)}) collective-permute-start(bf16[96,512]{1,0:T(8,128)(2,1)} %get-tuple-element.49), channel_id=1, source_target_pairs={{0,18},{1,19},{2,16},{3,17},{4,22},{5,23},{6,20},{7,21},{8,26},{9,... | collective-permute-start | bytes 294920 | tf_op jit(solution)/shard_map/ppermute | solution.py:77
  13.8 5.8 %collective-permute-start.1 = (bf16[96,512]{1,0:T(8,128)(2,1)S(1)}, bf16[96,512]{1,0:T(8,128)(2,1)S(1)}, u32[]{:S(2)}, u32[]{:S(2)}) collective-permute-start(bf16[96,512]{1,0:T(8,128)(2,1)S(1)} %get-tuple-element.50.refs_0_), channel_id=1, source_target_pairs={{0,2},{1,3},{2,0},{3,1},{4,6},{5,7},{6,4},{7,5},{8,10},{9,11},{10,... | collective-permute-start | bytes 294920 | tf_op jit(solution)/shard_map/ppermute | solution.py:72
  15.3 5.0 %collective-permute-start.3 = (bf16[96,512]{1,0:T(8,128)(2,1)S(1)}, bf16[96,512]{1,0:T(8,128)(2,1)}, u32[]{:S(2)}, u32[]{:S(2)}) collective-permute-start(bf16[96,512]{1,0:T(8,128)(2,1)S(1)} %get-tuple-element.50.refs_0_), channel_id=1, source_target_pairs={{0,1},{1,0},{2,3},{3,2},{4,5},{5,4},{6,7},{7,6},{8,9},{9,8},{10,11... | collective-permute-start | bytes 294920 | tf_op jit(solution)/shard_map/ppermute | solution.py:68
  15.4 21.0 %collective-permute-start.8 = (bf16[256,1536]{1,0:T(8,128)(2,1)S(1)}, bf16[256,1536]{1,0:T(8,128)(2,1)}, u32[]{:S(2)}, u32[]{:S(2)}) collective-permute-start(bf16[256,1536]{1,0:T(8,128)(2,1)S(1)} %bitcast.22), channel_id=1, source_target_pairs={{0,16},{16,0},{32,48},{48,32},{64,80},{80,64},{96,112},{112,96},{1... | collective-permute-start | bytes 2359304 | tf_op jit(solution)/shard_map/ppermute | solution.py:64
  19.5 1.3 collective-permute-start.5
  19.5 1.5 collective-permute-start.4
  20.1 1.3 collective-permute-start.6
  22.8 0.8 copy-start.3
  34.2 2.4 %collective-permute-start.7 = (bf16[256,1536]{1,0:T(8,128)(2,1)S(1)}, bf16[256,1536]{1,0:T(8,128)(2,1)}, u32[]{:S(2)}, u32[]{:S(2)}) collective-permute-start(bf16[256,1536]{1,0:T(8,128)(2,1)S(1)} %bitcast.20), channel_id=1, source_target_pairs={{0,1},{1,0},{2,3},{3,2},{4,5},{5,4},{6,7},{7,6},{8,9},{9,8},{10,11... | collective-permute-start | bytes 2359304 | tf_op jit(solution)/shard_map/ppermute | solution.py:68
  42.0 1.1 copy-start.2
  43.1 1.2 copy-start.6
  44.3 0.8 copy-start.8
  45.1 0.7 copy-start.10
  45.8 6.4 %collective-permute-start.9 = (bf16[256,1536]{1,0:T(8,128)(2,1)}, bf16[256,1536]{1,0:T(8,128)(2,1)S(1)}, u32[]{:S(2)}, u32[]{:S(2)}) collective-permute-start(bf16[256,1536]{1,0:T(8,128)(2,1)} %get-tuple-element.30), channel_id=1, source_target_pairs={{0,1},{1,0},{2,3},{3,2},{4,5},{5,4},{6,7},{7,6},{8,9},{9,8},{10,11... | collective-permute-start | bytes 2359304 | tf_op jit(solution)/shard_map/ppermute | solution.py:68
  46.0 1.4 copy-start.7
  47.4 1.0 copy-start.9
  48.4 0.9 copy-start.11
  50.9 1.2 copy-start.1
  52.2 0.9 copy-start.12
  53.0 35.6 %all-to-all-start.1 = ((bf16[16,32,1664]{2,1,0:T(8,128)(2,1)}), bf16[16,32,1664]{2,1,0:T(8,128)(2,1)S(1)}, u32[]{:S(2)}, u32[]{:S(2)}) async-start(bf16[16,32,1664]{2,1,0:T(8,128)(2,1)} %copy-done.1), calls=%async_computation.1 | async-start | bytes 3407872 | tf_op jit(solution)/shard_map/all_to_all | solution.py:314
  63.2 9.3 %collective-permute-start.10 = (bf16[32,1536]{1,0:T(8,128)(2,1)}, bf16[32,1536]{1,0:T(8,128)(2,1)S(1)}, u32[]{:S(2)}, u32[]{:S(2)}) collective-permute-start(bf16[32,1536]{1,0:T(8,128)(2,1)} %get-tuple-element.35), channel_id=1, source_target_pairs={{0,224},{16,240},{32,0},{48,16},{64,32},{80,48},{96,64},{112,80},{... | collective-permute-start | bytes 294920 | tf_op jit(solution)/shard_map/ppermute | solution.py:60
  65.7 8.1 %collective-permute-start.11 = (bf16[32,1536]{1,0:T(8,128)(2,1)}, bf16[32,1536]{1,0:T(8,128)(2,1)S(1)}, u32[]{:S(2)}, u32[]{:S(2)}) collective-permute-start(bf16[32,1536]{1,0:T(8,128)(2,1)} %get-tuple-element.36), channel_id=1, source_target_pairs={{0,32},{16,48},{32,64},{48,80},{64,96},{80,112},{96,128},{112,144}... | collective-permute-start | bytes 294920 | tf_op jit(solution)/shard_map/ppermute | solution.py:60
  65.7 12.1 %collective-permute-start.12 = (bf16[32,1536]{1,0:T(8,128)(2,1)}, bf16[32,1536]{1,0:T(8,128)(2,1)S(1)}, u32[]{:S(2)}, u32[]{:S(2)}) collective-permute-start(bf16[32,1536]{1,0:T(8,128)(2,1)} %get-tuple-element.37), channel_id=1, source_target_pairs={{0,192},{16,208},{32,224},{48,240},{64,0},{80,16},{96,32},{112,48}... | collective-permute-start | bytes 294920 | tf_op jit(solution)/shard_map/ppermute | solution.py:60
  68.6 9.2 %collective-permute-start.13 = (bf16[32,1536]{1,0:T(8,128)(2,1)}, bf16[32,1536]{1,0:T(8,128)(2,1)S(1)}, u32[]{:S(2)}, u32[]{:S(2)}) collective-permute-start(bf16[32,1536]{1,0:T(8,128)(2,1)} %get-tuple-element.38), channel_id=1, source_target_pairs={{0,64},{16,80},{32,96},{48,112},{64,128},{80,144},{96,160},{112,17... | collective-permute-start | bytes 294920 | tf_op jit(solution)/shard_map/ppermute | solution.py:60
  68.6 10.6 %collective-permute-start.14 = (bf16[32,1536]{1,0:T(8,128)(2,1)}, bf16[32,1536]{1,0:T(8,128)(2,1)S(1)}, u32[]{:S(2)}, u32[]{:S(2)}) collective-permute-start(bf16[32,1536]{1,0:T(8,128)(2,1)} %get-tuple-element.39), channel_id=1, source_target_pairs={{0,160},{16,176},{32,192},{48,208},{64,224},{80,240},{96,0},{112,1... | collective-permute-start | bytes 294920 | tf_op jit(solution)/shard_map/ppermute | solution.py:60
  72.5 12.5 %copy-start.15 = (bf16[32,1536]{1,0:T(8,128)(2,1)}, bf16[32,1536]{1,0:T(8,128)(2,1)S(1)}, u32[]{:S(2)}) copy-start(bf16[32,1536]{1,0:T(8,128)(2,1)S(1)} %collective-permute-done.10.refs_1_) | copy-start | bytes 294916
  72.5 12.1 %collective-permute-start.15 = (bf16[32,1536]{1,0:T(8,128)(2,1)}, bf16[32,1536]{1,0:T(8,128)(2,1)S(1)}, u32[]{:S(2)}, u32[]{:S(2)}) collective-permute-start(bf16[32,1536]{1,0:T(8,128)(2,1)} %get-tuple-element.40), channel_id=1, source_target_pairs={{0,96},{16,112},{32,128},{48,144},{64,160},{80,176},{96,192},{112,... | collective-permute-start | bytes 294920 | tf_op jit(solution)/shard_map/ppermute | solution.py:60
  73.8 0.6 copy-start.16
  74.4 10.5 %collective-permute-start.16 = (bf16[32,1536]{1,0:T(8,128)(2,1)}, bf16[32,1536]{1,0:T(8,128)(2,1)S(1)}, u32[]{:S(2)}, u32[]{:S(2)}) collective-permute-start(bf16[32,1536]{1,0:T(8,128)(2,1)} %get-tuple-element.41), channel_id=1, source_target_pairs={{0,128},{16,144},{32,160},{48,176},{64,192},{80,208},{96,224},{112... | collective-permute-start | bytes 294920 | tf_op jit(solution)/shard_map/ppermute | solution.py:60
  77.8 7.1 %copy-start.17 = (bf16[32,1536]{1,0:T(8,128)(2,1)}, bf16[32,1536]{1,0:T(8,128)(2,1)S(1)}, u32[]{:S(2)}) copy-start(bf16[32,1536]{1,0:T(8,128)(2,1)S(1)} %collective-permute-done.12.refs_3_) | copy-start | bytes 294916
  77.9 7.1 %copy-start.18 = (bf16[32,1536]{1,0:T(8,128)(2,1)}, bf16[32,1536]{1,0:T(8,128)(2,1)S(1)}, u32[]{:S(2)}) copy-start(bf16[32,1536]{1,0:T(8,128)(2,1)S(1)} %collective-permute-done.13.refs_4_) | copy-start | bytes 294916
  79.2 5.7 %copy-start.19 = (bf16[32,1536]{1,0:T(8,128)(2,1)}, bf16[32,1536]{1,0:T(8,128)(2,1)S(1)}, u32[]{:S(2)}) copy-start(bf16[32,1536]{1,0:T(8,128)(2,1)S(1)} %collective-permute-done.14.refs_5_) | copy-start | bytes 294916
  84.5 0.6 copy-start.20
  84.9 0.6 copy-start.21
  88.6 0.9 copy-start.5
  89.9 20.1 %copy-start.4 = (bf16[384,512]{1,0:T(8,128)(2,1)S(1)}, bf16[384,512]{1,0:T(8,128)(2,1)}, u32[]{:S(2)}) copy-start(bf16[384,512]{1,0:T(8,128)(2,1)} %copy-done.3) | copy-start | bytes 1179652
  110.5 1.7 %collective-permute-start.18 = (bf16[192,768]{1,0:T(8,128)(2,1)S(1)}, bf16[192,768]{1,0:T(8,128)(2,1)S(1)}, u32[]{:S(2)}, u32[]{:S(2)}) collective-permute-start(bf16[192,768]{1,0:T(8,128)(2,1)S(1)} %get-tuple-element.44), channel_id=1, source_target_pairs={{0,1},{1,0},{2,3},{3,2},{4,5},{5,4},{6,7},{7,6},{8,9},{9,8},{10,11... | collective-permute-start | bytes 884744 | tf_op jit(solution)/shard_map/ppermute | solution.py:68
  133.1 3.8 %collective-permute-start.19 = (bf16[24,384]{1,0:T(8,128)(2,1)S(1)}, bf16[24,384]{1,0:T(8,128)(2,1)S(1)}, u32[]{:S(2)}, u32[]{:S(2)}) collective-permute-start(bf16[24,384]{1,0:T(8,128)(2,1)S(1)} %get-tuple-element.46), channel_id=1, source_target_pairs={{0,2},{1,3},{2,0},{3,1},{4,6},{5,7},{6,4},{7,5},{8,10},{9,11},{10,... | collective-permute-start | bytes 55304 | tf_op jit(solution)/shard_map/ppermute | solution.py:72
  137.8 20.9 %all-to-all-start.4 = ((bf16[16,2,24,384]{3,2,1,0:T(8,128)(2,1)}), bf16[16,2,24,384]{3,2,1,0:T(8,128)(2,1)S(1)}, u32[]{:S(2)}, u32[]{:S(2)}) async-start(bf16[16,2,24,384]{3,2,1,0:T(8,128)(2,1)} %broadcast_in_dim.8), calls=%async_computation.4 | async-start | bytes 1179648 | tf_op jit(solution)/shard_map/all_to_all | solution.py:363
  141.7 1.3 collective-permute-start.17

commit v13 on v11

--- a/solution.py
+++ b/solution.py
@@ -201,25 +201,30 @@
             out_ref[s, part] = total[row : row + rows, col : col + cols].astype(BF16)
 
 
-def sum_kernel(parts_ref, own_ref, other_ref):
-    for part, out in enumerate((own_ref, other_ref)):
+def sum_kernel(flags, parts_ref, out_ref):
+    totals = []
+    for part in range(2):
         total = parts_ref[0, part].astype(F32)
         for i in range(1, parts_ref.shape[0]):
             total += parts_ref[i, part].astype(F32)
-        out[...] = total.astype(BF16)
-
-
-def paste_kernel(flags, parts_ref, img_ref, txt_ref):
+        totals.append(total)
+    first = flags[0] == 0
+    for i in range(2):
+        out_ref[i] = jnp.where(first, totals[i], totals[1 - i]).astype(BF16)
+
+
+def paste_kernel(parts_ref, img_ref, txt_ref):
     rows, cols = parts_ref.shape[2:]
-    first = flags[0] == 0
     for s in range(8):
         row, col = (s // 2) * rows, (s % 2) * cols
         for kind, out in enumerate((img_ref, txt_ref)):
-            own, other = parts_ref[2 * s + kind, 0], parts_ref[2 * s + kind, 1]
-            out[pl.ds(row, rows), pl.ds(col, cols)] = jnp.where(first, own, other).astype(F32)
-            out[pl.ds(row, rows), pl.ds(2 * cols + col, cols)] = jnp.where(
-                first, other, own
-            ).astype(F32)
+            for h in range(2):
+                place = (pl.ds(row, rows), pl.ds(2 * h * cols + col, cols))
+                out[place] = parts_ref[2 * s + kind, h].astype(F32)
+
+
+def copies_kernel(source, out_ref, sems):
+    wait_all(start_all([(source, out_ref.at[i]) for i in range(out_ref.shape[0])], sems))
 
 
 def shards(img_emb, txt_emb, img_feat_t, txt_feat_t, logit_scale, logit_bias):
@@ -238,7 +243,10 @@
     def over_z(value):
         return lax.all_to_all(value, "dp", 0, 0, tiled=True, axis_index_groups=same_y)
 
-    texts = over_z(jnp.broadcast_to(txt_emb[None], (8, sub, width))).reshape(half, width)
+    copies = local(
+        copies_kernel, ((8, sub, width), BF16), [txt_emb], WHOLE, [ANY], [HBM], [DMA((8,))]
+    )
+    texts = over_z(copies).reshape(half, width)
     mine = jnp.where(y == 0, img_feat_t, txt_feat_t)
     theirs = jnp.where(y == 0, txt_feat_t, img_feat_t)
     came, mine_x, came_x = swap_y(theirs), swap_x(mine), swap_both(theirs)
@@ -339,17 +347,24 @@
     shape = (feats // 4, narrow // 2)
     cut = local(cut_kernel, ((8, 2, *shape), BF16), [kept, swap_core(sent)], 6)
     parts = over_z(cut)
-    own_sum, other_sum = local(sum_kernel, [(shape, BF16)] * 2, [parts], 6)
-    summed = jnp.stack([own_sum, swap_x(other_sum)])
+    summed = local(
+        sum_kernel,
+        ((2, *shape), BF16),
+        [(chip % 2).reshape(1), parts],
+        6,
+        [SMEM, VMEM],
+    )
+    columns = [
+        [16 * d + 4 * q + 2 * k + c for d in range(16) for k in range(2)]
+        for q in range(4)
+        for c in range(2)
+    ]
     weights = lax.all_to_all(
-        jnp.broadcast_to(summed[None], (16, 2, *shape)), "dp", 0, 0, tiled=True
+        jnp.broadcast_to(summed[None], (16, 2, *shape)).reshape(32, *shape),
+        ("dp", "mp"), 0, 0, tiled=True, axis_index_groups=columns,
     )
     img_weight, txt_weight = local(
-        paste_kernel,
-        [((feats, width), F32)] * 2,
-        [(chip % 2).reshape(1), weights],
-        8,
-        [SMEM, VMEM],
+        paste_kernel, [((feats, width), F32)] * 2, [weights.reshape(16, 2, *shape)], 8
     )
 
     extra = grads[:, :, narrow : narrow + 2].astype(F32)

time: 155 us -> 177 us (1.14)
  Pallas kernels: 14.4 us -> 40.1 us
  blocking collectives: 39.7 us -> 19.8 us
  waiting for transfers between devices: 44.7 us -> 56.2 us
  starting transfers between devices: 41.4 us -> 48.5 us
  local copies, waits for them, and re-layouts: 10 us -> 8.06 us
    pallas_call x9 -> x10, Pallas kernels: 14.4 us -> 40.1 us  [local(): pl.pallas_call(kernel, out_shape=shapes, in_specs=specs or [VMEM] * len(o...]
    all_to_all x1 -> x0, blocking collectives: 19.9 us -> none  [over_z(): lax.all_to_all(value, 'dp', 0, 0, tiled=True, axis_index_groups=same_y)]
    all_to_all x1 -> x2, waiting for transfers between devices: 10.7 us -> 23.6 us  [over_z(): lax.all_to_all(value, 'dp', 0, 0, tiled=True, axis_index_groups=same_y)]
    all_to_all x1 -> x2, starting transfers between devices: 8.47 us -> 15.7 us  [over_z(): lax.all_to_all(value, 'dp', 0, 0, tiled=True, axis_index_groups=same_y)]
    ppermute x2 -> x1, waiting for transfers between devices: 4.65 us -> 2.5 us  [swap_x(): return lax.ppermute(value, 'mp', [(m, m ^ 2) for m in range(16)])]
    broadcast_in_dim x2 -> x1, local copies, waits for them, and re-layouts: 2.84 us -> 0.87 us  [shards(): jnp.broadcast_to(summed[None], (16, 2, *shape)).reshape(32, *shape)]
  transfers between devices with their start and end apart: 23 -> 23, of which waited for: 15 -> 15; matrix products, arithmetic and copies ran while one was open for 2% -> 1% of each run, Pallas kernels for 5% -> 4%
where the time goes in v13:
time: 177 us; the launch traced here: 176 us
  waiting for transfers between devices  56.2 us (32%)
  starting transfers between devices  48.5 us (27%)
  Pallas kernels  40.1 us (23%)
  blocking collectives  19.8 us (11%)
  local copies, waits for them, and re-layouts  8.06 us (5%)
  between operations  2.23 us (1%)
    pallas_call x10, Pallas kernels, local(): pl.pallas_call(kernel, out_shape=shapes, in_specs=specs or [VMEM] * len(o...  40.1 us
    all_to_all x2, waiting for transfers between devices, over_z(): lax.all_to_all(value, 'dp', 0, 0, tiled=True, axis_index_groups=same_y)  23.6 us
    all_to_all x1, blocking collectives, over_plane(): lax.all_to_all(value, ('dp', 'mp'), 0, 0, tiled=True, axis_index_groups=p...  19.8 us
    all_to_all x1, waiting for transfers between devices, shards(): lax.all_to_all(jnp.broadcast_to(summed[None], (16, 2, *shape)).reshape(32...  15.9 us
    all_to_all x2, starting transfers between devices, over_z(): lax.all_to_all(value, 'dp', 0, 0, tiled=True, axis_index_groups=same_y)  15.7 us
    ppermute x7, starting transfers between devices, along_z(): lax.ppermute(value, 'dp', [(d, (d + 2 * steps) % 16) for d in range(16)])  14.1 us
    ppermute x7, waiting for transfers between devices, along_z(): lax.ppermute(value, 'dp', [(d, (d + 2 * steps) % 16) for d in range(16)])  7.72 us
    all_to_all x1, starting transfers between devices, over_plane(): lax.all_to_all(value, ('dp', 'mp'), 0, 0, tiled=True, axis_index_groups=p...  7.48 us
  transfers between devices with their start and end apart: 23, of which 15 were waited for; matrix products, arithmetic and copies ran while one was open for 1% of the time, Pallas kernels for 4%

profile of v13, /device:TPU:2, one launch (start us, length us, event | category | flops | bytes accessed | tf_op | source)
XLA Modules:
  0.0 176.3 jit_solution(16690332842581763247)
XLA Ops:
  0.7 25.0 %shard_map.85 = bf16[8,32,1536]{2,1,0:T(8,128)(2,1)} custom-call(bf16[32,1536]{1,0:T(8,128)(2,1)} %refs_8_.1), custom_call_target="tpu_custom_call" | custom-call | tf_op jit(solution)/shard_map/pallas_call | solution.py:23
  25.7 8.5 %all-to-all-start = ((bf16[8,32,1536]{2,1,0:T(8,128)(2,1)}), bf16[8,32,1536]{2,1,0:T(8,128)(2,1)S(1)}, u32[]{:S(2)}, u32[]{:S(2)}) async-start(bf16[8,32,1536]{2,1,0:T(8,128)(2,1)} %shard_map.85), calls=%async_computation | async-start | bytes 1572864 | tf_op jit(solution)/shard_map/all_to_all | solution.py:244
  34.2 0.7 broadcast_select_fusion
  34.8 1.6 collective-permute-start
  36.4 0.4 collective-permute-start.2
  36.8 1.5 collective-permute-start.1
  38.4 1.7 collective-permute-start.8
  40.1 2.5 %collective-permute-done.1.refs_2_ = bf16[96,512]{1,0:T(8,128)(2,1)S(1)} collective-permute-done((bf16[96,512]{1,0:T(8,128)(2,1)S(1)}, bf16[96,512]{1,0:T(8,128)(2,1)S(1)}, u32[]{:S(2)}, u32[]{:S(2)}) %collective-permute-start.1) | collective-permute-done | bytes 98336 | tf_op jit(solution)/shard_map/ppermute | solution.py:71
  42.6 0.5 collective-permute-start.4
  43.1 0.1 collective-permute-start.6
  43.2 0.1 pad_add_fusion.2.flags
  43.3 0.6 collective-permute-done.5.refs_6_
  43.9 0.2 collective-permute-done.4.refs_5_
  44.0 0.4 collective-permute-done.6.refs_7_
  44.4 1.4 shard_map.86.feats_ref
  45.8 0.7 copy-done.3
  46.6 10.7 %all-to-all-done = bf16[8,32,1536]{2,1,0:T(8,128)(2,1)S(1)} async-done(((bf16[8,32,1536]{2,1,0:T(8,128)(2,1)}), bf16[8,32,1536]{2,1,0:T(8,128)(2,1)S(1)}, u32[]{:S(2)}, u32[]{:S(2)}) %all-to-all-start) | async-done | bytes 786464 | tf_op jit(solution)/shard_map/all_to_all | solution.py:244
  57.3 0.1 copy.11.refs_3_
  57.4 0.1 add_multiply_fusion
  57.5 0.1 broadcast_add_fusion.1
  57.6 0.1 iota_add_fusion
  57.7 0.1 add.120.refs_2_
  59.1 0.1 pad_add_fusion.1.refs_1_
  59.1 0.1 pad_maximum_fusion.refs_0_
  59.2 0.2 collective-permute-done.8.refs_7_
  59.4 0.3 collective-permute-done.7.refs_5_
  59.7 5.2 %shard_map.87 = (bf16[16,32,1664]{2,1,0:T(8,128)(2,1)S(1)}, f32[256,1536]{1,0:T(8,128)S(1)}, bf16[256,1536]{1,0:T(8,128)(2,1)S(1)}) custom-call(f32[2]{0:T(128)S(1)} %pad_maximum_fusion.refs_0_, s32[2]{0:T(128)S(1)} %pad_add_fusion.1.refs_1_, s32[1,512]{1,0:T(1,128)S(1)} %add.120.refs_2_, s32[512,1]{1,0:T(8,128)S(1)} %copy.11.refs_3_, ...), custom_call_target="tpu_custom_call" | custom-call | tf_op jit(solution)/shard_map/pallas_call | solution.py:23
  64.9 1.2 copy-done.1
  66.1 1.1 copy-done.2
  67.3 0.1 collective-permute-start.9
  67.4 2.1 %collective-permute-done.9.came_ref = bf16[256,1536]{1,0:T(8,128)(2,1)S(1)} collective-permute-done((bf16[256,1536]{1,0:T(8,128)(2,1)S(1)}, bf16[256,1536]{1,0:T(8,128)(2,1)S(1)}, u32[]{:S(2)}, u32[]{:S(2)}) %collective-permute-start.9) | collective-permute-done | bytes 786464 | tf_op jit(solution)/shard_map/ppermute | solution.py:67
  69.6 0.9 copy-done.6
  70.4 7.5 %all-to-all-start.1 = ((bf16[16,32,1664]{2,1,0:T(8,128)(2,1)}), bf16[16,32,1664]{2,1,0:T(8,128)(2,1)S(1)}, u32[]{:S(2)}, u32[]{:S(2)}) async-start(bf16[16,32,1664]{2,1,0:T(8,128)(2,1)} %copy-done.1), calls=%async_computation.1 | async-start | bytes 3407872 | tf_op jit(solution)/shard_map/all_to_all | solution.py:302
  77.9 2.7 %shard_map.88 = (bf16[32,1536]{1,0:T(8,128)(2,1)}, bf16[32,1536]{1,0:T(8,128)(2,1)}, bf16[32,1536]{1,0:T(8,128)(2,1)}, bf16[32,1536]{1,0:T(8,128)(2,1)}, bf16[32...) custom-call(s32[1]{0:T(128)} %bitcast.10.flags, ...), custom_call_target="tpu_custom_call" | custom-call | tf_op jit(solution)/shard_map/pallas_call | solution.py:23
  80.6 2.6 %collective-permute-start.10 = (bf16[32,1536]{1,0:T(8,128)(2,1)}, bf16[32,1536]{1,0:T(8,128)(2,1)S(1)}, u32[]{:S(2)}, u32[]{:S(2)}) collective-permute-start(bf16[32,1536]{1,0:T(8,128)(2,1)} %get-tuple-element.29), channel_id=1, source_target_pairs={{0,224},{16,240},{32,0},{48,16},{64,32},{80,48},{96,64},{112,80},{... | collective-permute-start | bytes 294920 | tf_op jit(solution)/shard_map/ppermute | solution.py:59
  83.2 2.9 %collective-permute-start.12 = (bf16[32,1536]{1,0:T(8,128)(2,1)}, bf16[32,1536]{1,0:T(8,128)(2,1)S(1)}, u32[]{:S(2)}, u32[]{:S(2)}) collective-permute-start(bf16[32,1536]{1,0:T(8,128)(2,1)} %get-tuple-element.31), channel_id=1, source_target_pairs={{0,192},{16,208},{32,224},{48,240},{64,0},{80,16},{96,32},{112,48}... | collective-permute-start | bytes 294920 | tf_op jit(solution)/shard_map/ppermute | solution.py:59
  86.1 3.8 %collective-permute-start.14 = (bf16[32,1536]{1,0:T(8,128)(2,1)}, bf16[32,1536]{1,0:T(8,128)(2,1)S(1)}, u32[]{:S(2)}, u32[]{:S(2)}) collective-permute-start(bf16[32,1536]{1,0:T(8,128)(2,1)} %get-tuple-element.33), channel_id=1, source_target_pairs={{0,160},{16,176},{32,192},{48,208},{64,224},{80,240},{96,0},{112,1... | collective-permute-start | bytes 294920 | tf_op jit(solution)/shard_map/ppermute | solution.py:59
  89.9 1.3 collective-permute-start.15
  91.2 0.6 copy-done.10
  91.9 3.4 %collective-permute-start.16 = (bf16[32,1536]{1,0:T(8,128)(2,1)}, bf16[32,1536]{1,0:T(8,128)(2,1)S(1)}, u32[]{:S(2)}, u32[]{:S(2)}) collective-permute-start(bf16[32,1536]{1,0:T(8,128)(2,1)} %get-tuple-element.35), channel_id=1, source_target_pairs={{0,128},{16,144},{32,160},{48,176},{64,192},{80,208},{96,224},{112... | collective-permute-start | bytes 294920 | tf_op jit(solution)/shard_map/ppermute | solution.py:59
  95.3 1.4 collective-permute-done.14.refs_5_
  96.8 4.9 %collective-permute-done.15.refs_6_ = bf16[32,1536]{1,0:T(8,128)(2,1)S(1)} collective-permute-done((bf16[32,1536]{1,0:T(8,128)(2,1)}, bf16[32,1536]{1,0:T(8,128)(2,1)S(1)}, u32[]{:S(2)}, u32[]{:S(2)}) %collective-permute-start.15) | collective-permute-done | bytes 98336 | tf_op jit(solution)/shard_map/ppermute | solution.py:59
  101.7 1.3 collective-permute-done.16.refs_7_
  103.1 0.6 copy-done.15
  103.7 3.1 %shard_map.89.d_txt = bf16[32,1536]{1,0:T(8,128)(2,1)} custom-call(bf16[32,1536]{1,0:T(8,128)(2,1)} %get-tuple-element.28.refs_0_, bf16[32,1536]{1,0:T(8,128)(2,1)} %copy-done.9, bf16[32,1536]{1,0:T(8,128)(2,1)} %copy-done.10, bf16[32,1536]{1,0:T(8,128)(2,1)} %copy-done.11, bf16[32,1536]{1,0:T(8,128)(2,1)} %copy-done.12, bf16[32,1536]{1,0:T(8,128)(2,1)} %copy-done.13, ...), custom_call_target="tpu_custom_call" | custom-call | tf_op jit(solution)/shard_map/pallas_call | solution.py:23
  106.8 0.9 copy-done.5
  107.7 0.4 shard_map.90
  108.1 0.1 broadcast_in_dim.4
  108.2 19.8 %all_to_all.25.grads_ref = bf16[16,32,896]{2,1,0:T(8,128)(2,1)S(1)} all-to-all(bf16[16,32,896]{2,1,0:T(8,128)(2,1)S(1)} %bitcast.25), channel_id=1, replica_groups={{0,2,4,6,8,10,12,14,16,18,20,22,24,26,28,30},{1,3,5,7,9,11,13,15,17,19,..., dimensions={0} | all-to-all | bytes 1835008 | tf_op jit(solution)/shard_map/all_to_all | solution.py:302
  128.0 0.5 shard_map.91
  128.5 0.1 collective-permute-start.18
  128.6 1.6 collective-permute-done.18.came_ref
  130.1 0.8 shard_map.92
  130.9 7.3 %all-to-all-start.3 = ((bf16[8,2,24,384]{3,2,1,0:T(8,128)(2,1)}), bf16[8,2,24,384]{3,2,1,0:T(8,128)(2,1)S(1)}, u32[]{:S(2)}, u32[]{:S(2)}) async-start(bf16[8,2,24,384]{3,2,1,0:T(8,128)(2,1)} %shard_map.92), calls=%async_computation.3 | async-start | bytes 589824 | tf_op jit(solution)/shard_map/all_to_all | solution.py:244
  138.2 12.9 %all-to-all-done.3.parts_ref = bf16[8,2,24,384]{3,2,1,0:T(8,128)(2,1)S(1)} async-done(((bf16[8,2,24,384]{3,2,1,0:T(8,128)(2,1)}), bf16[8,2,24,384]{3,2,1,0:T(8,128)(2,1)S(1)}, u32[]{:S(2)}, u32[]{:S(2)}) %all-to-all-start.3) | async-done | bytes 294944 | tf_op jit(solution)/shard_map/all_to_all | solution.py:244
  151.1 0.9 broadcast_in_dim.5
  152.0 5.1 %all-to-all-start.4 = ((bf16[32,24,384]{2,1,0:T(8,128)(2,1)}), bf16[32,24,384]{2,1,0:T(8,128)(2,1)S(1)}, u32[]{:S(2)}, u32[]{:S(2)}) async-start(bf16[32,24,384]{2,1,0:T(8,128)(2,1)} %bitcast.26), calls=%async_computation.4 | async-start | bytes 1179648 | tf_op jit(solution)/shard_map/all_to_all | solution.py:362
  157.1 0.1 slice_add_fusion
  157.3 0.1 fusion
  157.4 0.1 collective-permute-start.17
  157.5 1.1 collective-permute-done.17
  158.6 0.7 select_n.95
  159.3 15.9 %all-to-all-done.4 = bf16[32,24,384]{2,1,0:T(8,128)(2,1)S(1)} async-done(((bf16[32,24,384]{2,1,0:T(8,128)(2,1)}), bf16[32,24,384]{2,1,0:T(8,128)(2,1)S(1)}, u32[]{:S(2)}, u32[]{:S(2)}) %all-to-all-start.4) | async-done | bytes 589856 | tf_op jit(solution)/shard_map/all_to_all | solution.py:362
  175.2 1.1 shard_map.94
  (47 shorter events, 0.3 us)
Async XLA Ops:
  0.6 37.7 %copy-start = (bf16[512,1536]{1,0:T(8,128)(2,1)S(1)}, bf16[512,1536]{1,0:T(8,128)(2,1)}, u32[]{:S(2)}) copy-start(bf16[512,1536]{1,0:T(8,128)(2,1)} %param.6) | copy-start | bytes 4718596
  0.6 33.5 %copy-start.8 = (bf16[96,512]{1,0:T(8,128)(2,1)S(1)}, bf16[96,512]{1,0:T(8,128)(2,1)}, u32[]{:S(2)}) copy-start(bf16[96,512]{1,0:T(8,128)(2,1)} %param.8) | copy-start | bytes 294916
  0.7 33.5 %copy-start.7 = (bf16[96,512]{1,0:T(8,128)(2,1)S(1)}, bf16[96,512]{1,0:T(8,128)(2,1)}, u32[]{:S(2)}) copy-start(bf16[96,512]{1,0:T(8,128)(2,1)} %param.9) | copy-start | bytes 294916
  25.7 31.6 %all-to-all-start = ((bf16[8,32,1536]{2,1,0:T(8,128)(2,1)}), bf16[8,32,1536]{2,1,0:T(8,128)(2,1)S(1)}, u32[]{:S(2)}, u32[]{:S(2)}) async-start(bf16[8,32,1536]{2,1,0:T(8,128)(2,1)} %shard_map.85), calls=%async_computation | async-start | bytes 1572864 | tf_op jit(solution)/shard_map/all_to_all | solution.py:244
  34.8 7.8 %collective-permute-start = (bf16[96,512]{1,0:T(8,128)(2,1)}, bf16[96,512]{1,0:T(8,128)(2,1)S(1)}, u32[]{:S(2)}, u32[]{:S(2)}) collective-permute-start(bf16[96,512]{1,0:T(8,128)(2,1)} %get-tuple-element.41), channel_id=1, source_target_pairs={{0,16},{16,0},{32,48},{48,32},{64,80},{80,64},{96,112},{112,96},{1... | collective-permute-start | bytes 294920 | tf_op jit(solution)/shard_map/ppermute | solution.py:63
  36.4 6.7 %collective-permute-start.2 = (bf16[96,512]{1,0:T(8,128)(2,1)}, bf16[96,512]{1,0:T(8,128)(2,1)S(1)}, u32[]{:S(2)}, u32[]{:S(2)}) collective-permute-start(bf16[96,512]{1,0:T(8,128)(2,1)} %get-tuple-element.41), channel_id=1, source_target_pairs={{0,18},{1,19},{2,16},{3,17},{4,22},{5,23},{6,20},{7,21},{8,26},{9,... | collective-permute-start | bytes 294920 | tf_op jit(solution)/shard_map/ppermute | solution.py:76
  36.8 5.8 %collective-permute-start.1 = (bf16[96,512]{1,0:T(8,128)(2,1)S(1)}, bf16[96,512]{1,0:T(8,128)(2,1)S(1)}, u32[]{:S(2)}, u32[]{:S(2)}) collective-permute-start(bf16[96,512]{1,0:T(8,128)(2,1)S(1)} %get-tuple-element.42.refs_0_), channel_id=1, source_target_pairs={{0,2},{1,3},{2,0},{3,1},{4,6},{5,7},{6,4},{7,5},{8,10},{9,11},{10,... | collective-permute-start | bytes 294920 | tf_op jit(solution)/shard_map/ppermute | solution.py:71
  38.3 5.0 %collective-permute-start.3 = (bf16[96,512]{1,0:T(8,128)(2,1)S(1)}, bf16[96,512]{1,0:T(8,128)(2,1)}, u32[]{:S(2)}, u32[]{:S(2)}) collective-permute-start(bf16[96,512]{1,0:T(8,128)(2,1)S(1)} %get-tuple-element.42.refs_0_), channel_id=1, source_target_pairs={{0,1},{1,0},{2,3},{3,2},{4,5},{5,4},{6,7},{7,6},{8,9},{9,8},{10,11... | collective-permute-start | bytes 294920 | tf_op jit(solution)/shard_map/ppermute | solution.py:67
  38.4 21.0 %collective-permute-start.8 = (bf16[256,1536]{1,0:T(8,128)(2,1)S(1)}, bf16[256,1536]{1,0:T(8,128)(2,1)}, u32[]{:S(2)}, u32[]{:S(2)}) collective-permute-start(bf16[256,1536]{1,0:T(8,128)(2,1)S(1)} %bitcast.22), channel_id=1, source_target_pairs={{0,16},{16,0},{32,48},{48,32},{64,80},{80,64},{96,112},{112,96},{1... | collective-permute-start | bytes 2359304 | tf_op jit(solution)/shard_map/ppermute | solution.py:63
  42.6 1.3 collective-permute-start.5
  42.6 1.5 collective-permute-start.4
  43.1 1.3 collective-permute-start.6
  45.8 0.7 copy-start.3
  57.3 2.4 %collective-permute-start.7 = (bf16[256,1536]{1,0:T(8,128)(2,1)S(1)}, bf16[256,1536]{1,0:T(8,128)(2,1)}, u32[]{:S(2)}, u32[]{:S(2)}) collective-permute-start(bf16[256,1536]{1,0:T(8,128)(2,1)S(1)} %bitcast.20), channel_id=1, source_target_pairs={{0,1},{1,0},{2,3},{3,2},{4,5},{5,4},{6,7},{7,6},{8,9},{9,8},{10,11... | collective-permute-start | bytes 2359304 | tf_op jit(solution)/shard_map/ppermute | solution.py:67
  64.9 1.2 copy-start.1
  66.1 1.1 copy-start.2
  67.3 2.3 %collective-permute-start.9 = (bf16[256,1536]{1,0:T(8,128)(2,1)S(1)}, bf16[256,1536]{1,0:T(8,128)(2,1)S(1)}, u32[]{:S(2)}, u32[]{:S(2)}) collective-permute-start(bf16[256,1536]{1,0:T(8,128)(2,1)S(1)} %get-tuple-element.24), channel_id=1, source_target_pairs={{0,1},{1,0},{2,3},{3,2},{4,5},{5,4},{6,7},{7,6},{8,9},{9,8},{10,11... | collective-permute-start | bytes 2359304 | tf_op jit(solution)/shard_map/ppermute | solution.py:67
  69.6 0.9 copy-start.6
  70.4 36.3 %all-to-all-start.1 = ((bf16[16,32,1664]{2,1,0:T(8,128)(2,1)}), bf16[16,32,1664]{2,1,0:T(8,128)(2,1)S(1)}, u32[]{:S(2)}, u32[]{:S(2)}) async-start(bf16[16,32,1664]{2,1,0:T(8,128)(2,1)} %copy-done.1), calls=%async_computation.1 | async-start | bytes 3407872 | tf_op jit(solution)/shard_map/all_to_all | solution.py:302
  80.6 9.4 %collective-permute-start.10 = (bf16[32,1536]{1,0:T(8,128)(2,1)}, bf16[32,1536]{1,0:T(8,128)(2,1)S(1)}, u32[]{:S(2)}, u32[]{:S(2)}) collective-permute-start(bf16[32,1536]{1,0:T(8,128)(2,1)} %get-tuple-element.29), channel_id=1, source_target_pairs={{0,224},{16,240},{32,0},{48,16},{64,32},{80,48},{96,64},{112,80},{... | collective-permute-start | bytes 294920 | tf_op jit(solution)/shard_map/ppermute | solution.py:59
  83.2 8.1 %collective-permute-start.11 = (bf16[32,1536]{1,0:T(8,128)(2,1)}, bf16[32,1536]{1,0:T(8,128)(2,1)S(1)}, u32[]{:S(2)}, u32[]{:S(2)}) collective-permute-start(bf16[32,1536]{1,0:T(8,128)(2,1)} %get-tuple-element.30), channel_id=1, source_target_pairs={{0,32},{16,48},{32,64},{48,80},{64,96},{80,112},{96,128},{112,144}... | collective-permute-start | bytes 294920 | tf_op jit(solution)/shard_map/ppermute | solution.py:59
  83.2 12.1 %collective-permute-start.12 = (bf16[32,1536]{1,0:T(8,128)(2,1)}, bf16[32,1536]{1,0:T(8,128)(2,1)S(1)}, u32[]{:S(2)}, u32[]{:S(2)}) collective-permute-start(bf16[32,1536]{1,0:T(8,128)(2,1)} %get-tuple-element.31), channel_id=1, source_target_pairs={{0,192},{16,208},{32,224},{48,240},{64,0},{80,16},{96,32},{112,48}... | collective-permute-start | bytes 294920 | tf_op jit(solution)/shard_map/ppermute | solution.py:59
  86.1 9.2 %collective-permute-start.13 = (bf16[32,1536]{1,0:T(8,128)(2,1)}, bf16[32,1536]{1,0:T(8,128)(2,1)S(1)}, u32[]{:S(2)}, u32[]{:S(2)}) collective-permute-start(bf16[32,1536]{1,0:T(8,128)(2,1)} %get-tuple-element.32), channel_id=1, source_target_pairs={{0,64},{16,80},{32,96},{48,112},{64,128},{80,144},{96,160},{112,17... | collective-permute-start | bytes 294920 | tf_op jit(solution)/shard_map/ppermute | solution.py:59
  86.1 10.7 %collective-permute-start.14 = (bf16[32,1536]{1,0:T(8,128)(2,1)}, bf16[32,1536]{1,0:T(8,128)(2,1)S(1)}, u32[]{:S(2)}, u32[]{:S(2)}) collective-permute-start(bf16[32,1536]{1,0:T(8,128)(2,1)} %get-tuple-element.33), channel_id=1, source_target_pairs={{0,160},{16,176},{32,192},{48,208},{64,224},{80,240},{96,0},{112,1... | collective-permute-start | bytes 294920 | tf_op jit(solution)/shard_map/ppermute | solution.py:59
  89.9 13.1 %copy-start.9 = (bf16[32,1536]{1,0:T(8,128)(2,1)}, bf16[32,1536]{1,0:T(8,128)(2,1)S(1)}, u32[]{:S(2)}) copy-start(bf16[32,1536]{1,0:T(8,128)(2,1)S(1)} %collective-permute-done.10.refs_1_) | copy-start | bytes 294916
  89.9 11.8 %collective-permute-start.15 = (bf16[32,1536]{1,0:T(8,128)(2,1)}, bf16[32,1536]{1,0:T(8,128)(2,1)S(1)}, u32[]{:S(2)}, u32[]{:S(2)}) collective-permute-start(bf16[32,1536]{1,0:T(8,128)(2,1)} %get-tuple-element.34), channel_id=1, source_target_pairs={{0,96},{16,112},{32,128},{48,144},{64,160},{80,176},{96,192},{112,... | collective-permute-start | bytes 294920 | tf_op jit(solution)/shard_map/ppermute | solution.py:59
  91.2 0.6 copy-start.10
  91.9 11.2 %collective-permute-start.16 = (bf16[32,1536]{1,0:T(8,128)(2,1)}, bf16[32,1536]{1,0:T(8,128)(2,1)S(1)}, u32[]{:S(2)}, u32[]{:S(2)}) collective-permute-start(bf16[32,1536]{1,0:T(8,128)(2,1)} %get-tuple-element.35), channel_id=1, source_target_pairs={{0,128},{16,144},{32,160},{48,176},{64,192},{80,208},{96,224},{112... | collective-permute-start | bytes 294920 | tf_op jit(solution)/shard_map/ppermute | solution.py:59
  95.3 7.8 %copy-start.11 = (bf16[32,1536]{1,0:T(8,128)(2,1)}, bf16[32,1536]{1,0:T(8,128)(2,1)S(1)}, u32[]{:S(2)}) copy-start(bf16[32,1536]{1,0:T(8,128)(2,1)S(1)} %collective-permute-done.12.refs_3_) | copy-start | bytes 294916
  95.3 7.7 %copy-start.12 = (bf16[32,1536]{1,0:T(8,128)(2,1)}, bf16[32,1536]{1,0:T(8,128)(2,1)S(1)}, u32[]{:S(2)}) copy-start(bf16[32,1536]{1,0:T(8,128)(2,1)S(1)} %collective-permute-done.13.refs_4_) | copy-start | bytes 294916
  96.8 6.3 %copy-start.13 = (bf16[32,1536]{1,0:T(8,128)(2,1)}, bf16[32,1536]{1,0:T(8,128)(2,1)S(1)}, u32[]{:S(2)}) copy-start(bf16[32,1536]{1,0:T(8,128)(2,1)S(1)} %collective-permute-done.14.refs_5_) | copy-start | bytes 294916
  101.7 1.3 copy-start.14
  103.1 0.6 copy-start.15
  106.8 0.9 copy-start.5
  108.1 19.9 %copy-start.4 = (bf16[384,512]{1,0:T(8,128)(2,1)S(1)}, bf16[384,512]{1,0:T(8,128)(2,1)}, u32[]{:S(2)}) copy-start(bf16[384,512]{1,0:T(8,128)(2,1)} %copy-done.3) | copy-start | bytes 1179652
  128.5 1.7 collective-permute-start.18
  130.9 20.1 %all-to-all-start.3 = ((bf16[8,2,24,384]{3,2,1,0:T(8,128)(2,1)}), bf16[8,2,24,384]{3,2,1,0:T(8,128)(2,1)S(1)}, u32[]{:S(2)}, u32[]{:S(2)}) async-start(bf16[8,2,24,384]{3,2,1,0:T(8,128)(2,1)} %shard_map.92), calls=%async_computation.3 | async-start | bytes 589824 | tf_op jit(solution)/shard_map/all_to_all | solution.py:244
  152.0 23.3 %all-to-all-start.4 = ((bf16[32,24,384]{2,1,0:T(8,128)(2,1)}), bf16[32,24,384]{2,1,0:T(8,128)(2,1)S(1)}, u32[]{:S(2)}, u32[]{:S(2)}) async-start(bf16[32,24,384]{2,1,0:T(8,128)(2,1)} %bitcast.26), calls=%async_computation.4 | async-start | bytes 1179648 | tf_op jit(solution)/shard_map/all_to_all | solution.py:362
  157.4 1.3 collective-permute-start.17

commit v14 on v13

--- a/solution.py
+++ b/solution.py
@@ -7,7 +7,6 @@
 
 F32 = jnp.float32
 BF16 = jnp.bfloat16
-LANES = 128
 ALONG = (0, 1, -1, 2, -2, 3, -3, 4)
 VMEM = pl.BlockSpec(memory_space=pltpu.VMEM)
 SMEM = pl.BlockSpec(memory_space=pltpu.SMEM)
@@ -74,19 +73,6 @@
 def swap_both(value):
     pairs = [(16 * d + m, 16 * (d ^ 1) + (m ^ 2)) for d in range(16) for m in range(16)]
     return lax.ppermute(value, ("dp", "mp"), pairs)
-
-
-def loss_columns(losses):
-    high = losses.astype(BF16)
-    low = (losses - high.astype(F32)).astype(BF16)
-    lane = lax.broadcasted_iota(jnp.int32, (losses.shape[0], LANES), 1)
-    zero = jnp.zeros((), BF16)
-    return jnp.where(lane == 0, high, jnp.where(lane == 1, low, zero))
-
-
-def column_loss(extra):
-    values = extra.astype(F32)
-    return values[:, 0:1] + values[:, 1:2]
 
 
 def feature_kernel(flags, *refs):
@@ -107,9 +93,9 @@
 
 
 def tile_kernel(*refs):
-    numbers, places, text_ids, image_ids = refs[0], refs[1], refs[2], refs[3]
-    blocks, own, partner = refs[4:6], refs[6], refs[7]
-    image_out, keep_ref, send_ref, texts, images, slopes = refs[8:]
+    numbers, places, text_ids = refs[0], refs[1], refs[2]
+    blocks, own, partner = refs[3:5], refs[5], refs[6]
+    image_out, keep_ref, send_ref, loss_ref, texts, images, slopes = refs[7:]
     sub, width = image_out.shape[1], own.shape[1]
     scale, bias = numbers[0], numbers[1]
     rows = own.shape[0]
@@ -122,7 +108,9 @@
         logits = scale * lax.dot_general(
             images[place, :], texts[...], (((1,), (1,)), ((), ())), preferred_element_type=F32
         ) + bias
-        match = image_ids[place, :] == text_ids[...]
+        row = lax.broadcasted_iota(jnp.int32, (rows, 1), 0)
+        image_ids = places[2 + part] + (row // sub) * 2 * sub + row % sub
+        match = image_ids == text_ids[...]
         u = jnp.where(match, -logits, logits)
         e = jnp.exp(-jnp.abs(u))
         w = 1.0 + e
@@ -132,11 +120,10 @@
         slope = jnp.where(match, -scale, scale) * (jnp.where(u >= 0.0, 1.0, e) * inverse)
         slopes[place, :] = slope.astype(BF16)
         grad = jnp.dot(slopes[place, :], texts[...], preferred_element_type=F32).astype(BF16)
-        extra = loss_columns(losses)
+        loss_ref[pl.ds(places[part] // 8, 1), :] = losses.reshape(1, rows)
         first = places[part]
         for i in range(pieces):
-            image_out[first + i, :, pl.ds(0, width)] = grad[i * sub : (i + 1) * sub]
-            image_out[first + i, :, pl.ds(width, LANES)] = extra[i * sub : (i + 1) * sub]
+            image_out[first + i] = grad[i * sub : (i + 1) * sub]
     text_grad = lax.dot_general(
         slopes[...], images[...], (((0,), (0,)), ((), ())), preferred_element_type=F32
     )
@@ -146,40 +133,52 @@
 
 
 def join_kernel(flags, keep_ref, came_ref, *refs):
-    outs, stage, sems = refs[:8], refs[8], refs[9]
+    outs, keep, came, stage, keep_sems, came_sems, out_sems = refs[:8], *refs[8:]
     sub = stage.shape[1]
-    for i, steps in enumerate(ALONG):
+    places = []
+    for steps in ALONG:
         owner = lax.rem(flags[0] + (8 - steps), 8)
-        place = pl.ds(pl.multiple_of(owner * sub, sub), sub)
-        stage[i] = (keep_ref[place, :] + came_ref[place, :].astype(F32)).astype(BF16)
-    wait_all(start_all([(stage.at[i], out) for i, out in enumerate(outs)], sems))
+        places.append(pl.ds(pl.multiple_of(owner * sub, sub), sub))
+    keeps = start_all([(keep_ref.at[p], keep.at[i]) for i, p in enumerate(places)], keep_sems)
+    cames = start_all([(came_ref.at[p], came.at[i]) for i, p in enumerate(places)], came_sems)
+    sent = []
+    for i, out in enumerate(outs):
+        keeps[i].wait()
+        cames[i].wait()
+        stage[i] = (keep[i] + came[i].astype(F32)).astype(BF16)
+        copy = pltpu.make_async_copy(stage.at[i], out, out_sems.at[i])
+        copy.start()
+        sent.append(copy)
+    wait_all(sent)
 
 
 def text_kernel(*refs):
-    blocks, raw_txt, out_ref, came, sems = refs[:8], *refs[8:]
-    wait_all(start_all([(block, came.at[i]) for i, block in enumerate(blocks)], sems))
+    blocks, raw_ref, out_ref, came, raw_txt, sems, raw_sem = refs[:8], *refs[8:]
+    load = start_all([(raw_ref, raw_txt)], raw_sem)
+    loads = start_all([(block, came.at[i]) for i, block in enumerate(blocks)], sems)
+    wait_all(load)
+    normed, inverse = normalize(raw_txt[...])
+    loads[0].wait()
     text_grad = came[0].astype(F32)
     for i in range(1, came.shape[0]):
+        loads[i].wait()
         text_grad += came[i].astype(F32)
-    out_ref[...] = through_norm(text_grad, *normalize(raw_txt[...])).astype(BF16)
-
-
-def grad_kernel(pieces, d_txt, raw_img, out_ref):
-    width = raw_img.shape[1]
-    half = width // 2
-    image_grad = pieces[0, :, pl.ds(0, width)].astype(F32)
-    losses = column_loss(pieces[0, :, pl.ds(width, LANES)])
+    out_ref[...] = through_norm(text_grad, normed, inverse).astype(BF16)
+
+
+def grad_kernel(flags, pieces, d_txt_ref, img_ref, out_ref, raw_img, d_txt, sems):
+    sub = raw_img.shape[0]
+    half = raw_img.shape[1] // 2
+    rows = pl.ds(pl.multiple_of(flags[0] * sub, sub), sub)
+    loads = start_all([(img_ref.at[rows], raw_img), (d_txt_ref, d_txt)], sems)
+    image_grad = pieces[0].astype(F32)
     for i in range(1, pieces.shape[0]):
-        image_grad += pieces[i, :, pl.ds(0, width)].astype(F32)
-        losses += column_loss(pieces[i, :, pl.ds(width, LANES)])
+        image_grad += pieces[i].astype(F32)
+    wait_all(loads)
     d_img = through_norm(image_grad, *normalize(raw_img[...])).astype(BF16)
-    extra = loss_columns(losses)
     for h in range(2):
-        place = pl.ds(h * half, half)
-        out_ref[0, h, :, pl.ds(0, half)] = d_img[:, h * half : (h + 1) * half]
-        out_ref[1, h, :, pl.ds(0, half)] = d_txt[:, place]
-        for kind in range(2):
-            out_ref[kind, h, :, pl.ds(half, LANES)] = extra
+        out_ref[0, h] = d_img[:, h * half : (h + 1) * half]
+        out_ref[1, h] = d_txt[:, pl.ds(h * half, half)]
 
 
 def weight_kernel(feats_ref, grads_ref, keep_ref, send_ref):
@@ -223,16 +222,11 @@
                 out[place] = parts_ref[2 * s + kind, h].astype(F32)
 
 
-def copies_kernel(source, out_ref, sems):
-    wait_all(start_all([(source, out_ref.at[i]) for i in range(out_ref.shape[0])], sems))
-
-
 def shards(img_emb, txt_emb, img_feat_t, txt_feat_t, logit_scale, logit_bias):
     rows, width = img_emb.shape
     sub = txt_emb.shape[0]
     half = rows // 2
     feats = img_feat_t.shape[0]
-    full = width + LANES
     dp_index = lax.axis_index("dp").astype(jnp.int32)
     mp_index = lax.axis_index("mp").astype(jnp.int32)
     core, chip = mp_index % 2, mp_index // 2
@@ -243,10 +237,7 @@
     def over_z(value):
         return lax.all_to_all(value, "dp", 0, 0, tiled=True, axis_index_groups=same_y)
 
-    copies = local(
-        copies_kernel, ((8, sub, width), BF16), [txt_emb], WHOLE, [ANY], [HBM], [DMA((8,))]
-    )
-    texts = over_z(copies).reshape(half, width)
+    texts = over_z(jnp.broadcast_to(txt_emb[None], (8, sub, width))).reshape(half, width)
     mine = jnp.where(y == 0, img_feat_t, txt_feat_t)
     theirs = jnp.where(y == 0, txt_feat_t, img_feat_t)
     came, mine_x, came_x = swap_y(theirs), swap_x(mine), swap_both(theirs)
@@ -266,28 +257,30 @@
     cores = jnp.stack([mp_index, mp_index ^ 1])
     text_ids = owners[None, :, None] * rows + cores[:, None, None] * sub
     text_ids = text_ids + jnp.arange(sub, dtype=jnp.int32)[None, None]
-    count = jnp.arange(half, dtype=jnp.int32)
-    in_shard = (count // sub) * 2 * sub + core * sub + count % sub
-    image_ids = jnp.concatenate(
-        [(2 * z + y) * rows + in_shard, (2 * z + 1 - y) * rows + in_shard]
-    )
-    places = jnp.stack([8 * y, 8 * (1 - y)])
+    shard_start = 2 * z * rows + core * sub
+    places = jnp.stack(
+        [8 * y, 8 * (1 - y), shard_start + y * rows, shard_start + (1 - y) * rows]
+    )
     numbers = jnp.concatenate([logit_scale, logit_bias])
-    image_part, keep, send = local(
+    image_part, keep, send, losses = local(
         tile_kernel,
-        [((16, sub, full), BF16), ((half, width), F32), ((half, width), BF16)],
+        [
+            ((16, sub, width), BF16),
+            ((half, width), F32),
+            ((half, width), BF16),
+            ((2, half), F32),
+        ],
         [
             numbers,
             places.astype(jnp.int32),
             text_ids.astype(jnp.int32).reshape(1, rows),
-            image_ids.astype(jnp.int32).reshape(rows, 1),
             texts,
             swap_core(texts),
             own,
             partner,
         ],
         24,
-        [SMEM, SMEM] + [VMEM] * 6,
+        [SMEM, SMEM] + [VMEM] * 5,
         None,
         [pltpu.VMEM((rows, width), BF16)] * 2
         + [pltpu.VMEM((rows, rows), BF16)],
@@ -304,15 +297,21 @@
         )
 
     came_grad = swap_core(send)
-    image_part, came_grad = lax.optimization_barrier((image_part, came_grad))
+    losses = losses + lax.ppermute(losses, "mp", [(m, m ^ 2) for m in range(16)])
+    image_part, came_grad, losses = lax.optimization_barrier((image_part, came_grad, losses))
     text_parts = local(
         join_kernel,
         [((sub, width), BF16)] * 8,
         [z.reshape(1), keep, came_grad],
         WHOLE,
-        [SMEM, VMEM, VMEM],
+        [SMEM, ANY, ANY],
         [HBM] * 8,
-        [pltpu.VMEM((8, sub, width), BF16), DMA((8,))],
+        [
+            pltpu.VMEM((8, sub, width), F32),
+            pltpu.VMEM((8, sub, width), BF16),
+            pltpu.VMEM((8, sub, width), BF16),
+        ]
+        + [DMA((8,))] * 3,
     )
     image_pieces = over_plane(image_part)
     text_came = [text_parts[0]] + [
@@ -323,20 +322,27 @@
         ((sub, width), BF16),
         [*text_came, txt_emb],
         WHOLE,
-        [ANY] * 8 + [VMEM],
+        [ANY] * 9,
         None,
-        [pltpu.VMEM((8, sub, width), BF16), DMA((8,))],
-    )
-    raw_img = lax.dynamic_slice_in_dim(img_emb, (2 * chip + core) * sub, sub, 0)
+        [
+            pltpu.VMEM((8, sub, width), BF16),
+            pltpu.VMEM((sub, width), BF16),
+            DMA((8,)),
+            DMA((1,)),
+        ],
+    )
     narrow = width // 2
     kinds = local(
         grad_kernel,
-        ((2, 2, sub, narrow + LANES), BF16),
-        [image_pieces, d_txt, raw_img],
+        ((2, 2, sub, narrow), BF16),
+        [mp_index.reshape(1), image_pieces, d_txt, img_emb],
         12,
-    )
-    spread = jnp.broadcast_to(kinds[:, None], (2, 4, 2, sub, narrow + LANES))
-    grads = over_plane(spread.reshape(16, sub, narrow + LANES))
+        [SMEM, VMEM, ANY, ANY],
+        None,
+        [pltpu.VMEM((sub, width), BF16), pltpu.VMEM((sub, width), BF16), DMA((2,))],
+    )
+    spread = jnp.broadcast_to(kinds[:, None], (2, 4, 2, sub, narrow))
+    grads = over_plane(spread.reshape(16, sub, narrow))
 
     kept, sent = local(
         weight_kernel,
@@ -347,6 +353,10 @@
     shape = (feats // 4, narrow // 2)
     cut = local(cut_kernel, ((8, 2, *shape), BF16), [kept, swap_core(sent)], 6)
     parts = over_z(cut)
+    for turn in (4, 8):
+        losses = losses + lax.ppermute(losses, "mp", [(m, m ^ turn) for m in range(16)])
+    parts, losses = lax.optimization_barrier((parts, losses))
+    losses = losses + swap_y(losses)
     summed = local(
         sum_kernel,
         ((2, *shape), BF16),
@@ -367,9 +377,7 @@
         paste_kernel, [((feats, width), F32)] * 2, [weights.reshape(16, 2, *shape)], 8
     )
 
-    extra = grads[:, :, narrow : narrow + 2].astype(F32)
-    both_loss = (extra[:, :, 0] + extra[:, :, 1]).reshape(2, 8, sub)
-    own_loss = jnp.where(y == 0, both_loss[0], both_loss[1])
+    own_loss = jnp.where(y == 0, losses[0], losses[1]).reshape(8, sub)
     other_loss = swap_core(own_loss)
     row_loss = jnp.where(
         core == 0, jnp.stack([own_loss, other_loss], 1), jnp.stack([other_loss, own_loss], 1)

time: 177 us -> 153 us (0.86)
  Pallas kernels: 40.1 us -> 14.5 us
  waiting for transfers between devices: 56.2 us -> 46.9 us
  local copies, waits for them, and re-layouts: 8.06 us -> 14.6 us
  starting transfers between devices: 48.5 us -> 54.2 us
  blocking collectives: 19.8 us -> 17.6 us
    pallas_call x10 -> x9, Pallas kernels: 40.1 us -> 14.5 us  [local(): pl.pallas_call(kernel, out_shape=shapes, in_specs=specs or [VMEM] * len(o...]
    all_to_all x2, waiting for transfers between devices: 23.6 us -> 9.88 us  [over_z(): lax.all_to_all(value, 'dp', 0, 0, tiled=True, axis_index_groups=same_y)]
    ppermute x0 -> x3, waiting for transfers between devices: none -> 11.2 us  [the longest x2 8.1 us: shards(): lax.ppermute(losses, 'mp', [(m, m ^ turn) for m in range(16)])]
    all_to_all x1, waiting for transfers between devices: 15.9 us -> 10 us  [shards(): lax.all_to_all(jnp.broadcast_to(summed[None], (16, 2, *shape)).reshape(32...]
    unnamed x32 -> x44, local copies, waits for them, and re-layouts: 6.13 us -> 10.2 us
    ppermute x2 -> x3, waiting for transfers between devices: 0.17 us -> 4.06 us  [swap_y(): return lax.ppermute(value, 'dp', [(d, d ^ 1) for d in range(16)])]
    ppermute x8, waiting for transfers between devices: 6.3 us -> 3.5 us  [swap_core(): return lax.ppermute(value, 'mp', [(m, m ^ 1) for m in range(16)])]
    ppermute x0 -> x3, starting transfers between devices: none -> 2.63 us  [the longest x2 2.08 us: shards(): lax.ppermute(losses, 'mp', [(m, m ^ turn) for m in range(16)])]
  transfers between devices with their start and end apart: 23 -> 27, of which waited for: 15 -> 17; matrix products, arithmetic and copies ran while one was open for 1% -> 2% of each run, Pallas kernels for 4% -> 4%
where the time goes in v14:
time: 153 us; the launch traced here: 152 us
  starting transfers between devices  54.2 us (35%)
  waiting for transfers between devices  46.9 us (31%)
  blocking collectives  17.6 us (12%)
  local copies, waits for them, and re-layouts  14.6 us (10%)
  Pallas kernels  14.5 us (9%)
  between operations  2.16 us (1%)
  other arithmetic  1.81 us (1%)
    all_to_all x1, blocking collectives, over_plane(): lax.all_to_all(value, ('dp', 'mp'), 0, 0, tiled=True, axis_index_groups=p...  17.6 us
    all_to_all x2, starting transfers between devices, over_z(): lax.all_to_all(value, 'dp', 0, 0, tiled=True, axis_index_groups=same_y)  16.6 us
    pallas_call x9, Pallas kernels, local(): pl.pallas_call(kernel, out_shape=shapes, in_specs=specs or [VMEM] * len(o...  14.5 us
    ppermute x7, starting transfers between devices, along_z(): lax.ppermute(value, 'dp', [(d, (d + 2 * steps) % 16) for d in range(16)])  13.9 us
    unnamed x44, local copies, waits for them, and re-layouts  10.2 us
    all_to_all x1, waiting for transfers between devices, shards(): lax.all_to_all(jnp.broadcast_to(summed[None], (16, 2, *shape)).reshape(32...  10 us
    all_to_all x2, waiting for transfers between devices, over_z(): lax.all_to_all(value, 'dp', 0, 0, tiled=True, axis_index_groups=same_y)  9.88 us
    ppermute x2, waiting for transfers between devices, shards(): lax.ppermute(losses, 'mp', [(m, m ^ turn) for m in range(16)])  8.1 us
  transfers between devices with their start and end apart: 27, of which 17 were waited for; matrix products, arithmetic and copies ran while one was open for 2% of the time, Pallas kernels for 4%

profile of v14, /device:TPU:2, one launch (start us, length us, event | category | flops | bytes accessed | tf_op | source)
XLA Modules:
  0.0 151.8 jit_solution(9660009601227662961)
XLA Ops:
  0.7 2.0 %broadcast_in_dim.6 = bf16[8,32,1536]{2,1,0:T(8,128)(2,1)} broadcast(bf16[32,1536]{1,0:T(8,128)(2,1)} %refs_8_.1), dimensions={1,2} | broadcast | bytes 884736 | tf_op jit(solution)/shard_map/broadcast_in_dim | solution.py:240
  2.6 8.5 %all-to-all-start = ((bf16[8,32,1536]{2,1,0:T(8,128)(2,1)}), bf16[8,32,1536]{2,1,0:T(8,128)(2,1)S(1)}, u32[]{:S(2)}, u32[]{:S(2)}) async-start(bf16[8,32,1536]{2,1,0:T(8,128)(2,1)} %broadcast_in_dim.6), calls=%async_computation | async-start | bytes 1572864 | tf_op jit(solution)/shard_map/all_to_all | solution.py:238
  11.1 0.7 broadcast_select_fusion
  11.8 1.5 %collective-permute-start.2 = (bf16[96,512]{1,0:T(8,128)(2,1)}, bf16[96,512]{1,0:T(8,128)(2,1)S(1)}, u32[]{:S(2)}, u32[]{:S(2)}) collective-permute-start(bf16[96,512]{1,0:T(8,128)(2,1)} %get-tuple-element.51), channel_id=1, source_target_pairs={{0,18},{1,19},{2,16},{3,17},{4,22},{5,23},{6,20},{7,21},{8,26},{9,... | collective-permute-start | bytes 294920 | tf_op jit(solution)/shard_map/ppermute | solution.py:75
  13.3 0.4 collective-permute-start
  13.8 1.5 collective-permute-start.1
  15.3 1.7 %collective-permute-start.8 = (bf16[256,1536]{1,0:T(8,128)(2,1)S(1)}, bf16[256,1536]{1,0:T(8,128)(2,1)}, u32[]{:S(2)}, u32[]{:S(2)}) collective-permute-start(bf16[256,1536]{1,0:T(8,128)(2,1)S(1)} %bitcast.24), channel_id=1, source_target_pairs={{0,16},{16,0},{32,48},{48,32},{64,80},{80,64},{96,112},{112,96},{1... | collective-permute-start | bytes 2359304 | tf_op jit(solution)/shard_map/ppermute | solution.py:62
  17.0 0.6 collective-permute-done.2.refs_3_
  17.6 0.6 copy-done.6
  18.2 1.5 %collective-permute-done.refs_1_ = bf16[96,512]{1,0:T(8,128)(2,1)S(1)} collective-permute-done((bf16[96,512]{1,0:T(8,128)(2,1)}, bf16[96,512]{1,0:T(8,128)(2,1)S(1)}, u32[]{:S(2)}, u32[]{:S(2)}) %collective-permute-start) | collective-permute-done | bytes 98336 | tf_op jit(solution)/shard_map/ppermute | solution.py:62
  19.7 0.6 copy-done.8
  20.4 0.5 collective-permute-start.5
  20.9 0.6 copy-done.10
  21.6 0.4 collective-permute-done.5.refs_6_
  22.0 0.9 copy-done.5
  22.9 0.9 copy-done.7
  23.8 0.9 copy-done.9
  24.7 0.9 copy-done.11
  25.6 1.4 shard_map.85.feats_ref
  27.0 7.2 %all-to-all-done = bf16[8,32,1536]{2,1,0:T(8,128)(2,1)S(1)} async-done(((bf16[8,32,1536]{2,1,0:T(8,128)(2,1)}), bf16[8,32,1536]{2,1,0:T(8,128)(2,1)S(1)}, u32[]{:S(2)}, u32[]{:S(2)}) %all-to-all-start) | async-done | bytes 786464 | tf_op jit(solution)/shard_map/all_to_all | solution.py:238
  36.0 0.2 collective-permute-done.8.refs_6_
  36.2 0.4 collective-permute-done.7.refs_4_
  36.6 5.2 %shard_map.86 = (bf16[16,32,1536]{2,1,0:T(8,128)(2,1)S(1)}, f32[256,1536]{1,0:T(8,128)S(1)}, bf16[256,1536]{1,0:T(8,128)(2,1)S(1)}, f32[2,256]{1,0:T(2,128)S(1)}) custom-call(f32[2]{0:T(128)S(1)} %pad_maximum_fusion.refs_0_, s32[4]{0:T(128)S(1)} %pad_add_fusion.1.refs_1_, s32[1,512]{1,0:T(1,128)S(1)} %add.100.refs_2_, bf16[256,1536]{1,0:T(8,128)(2,1)S(1)} %bitcast.23, ...), custom_call_target="tpu_custom_call" | custom-call | tf_op jit(solution)/shard_map/pallas_call | solution.py:22
  41.8 1.2 copy-done.1
  43.0 1.1 copy-done.2
  44.1 0.1 collective-permute-start.9
  44.3 0.5 collective-permute-start.10
  44.8 3.1 %collective-permute-done.10 = f32[2,256]{1,0:T(2,128)S(1)} collective-permute-done((f32[2,256]{1,0:T(2,128)S(1)}, f32[2,256]{1,0:T(2,128)S(1)}, u32[]{:S(2)}, u32[]{:S(2)}) %collective-permute-start.10) | collective-permute-done | bytes 2080 | tf_op jit(solution)/shard_map/ppermute | solution.py:300
  47.9 0.9 copy-done.12
  48.8 7.5 %all-to-all-start.1 = ((bf16[16,32,1536]{2,1,0:T(8,128)(2,1)}), bf16[16,32,1536]{2,1,0:T(8,128)(2,1)S(1)}, u32[]{:S(2)}, u32[]{:S(2)}) async-start(bf16[16,32,1536]{2,1,0:T(8,128)(2,1)} %copy-done.1), calls=%async_computation.1 | async-start | bytes 3145728 | tf_op jit(solution)/shard_map/all_to_all | solution.py:295
  56.3 2.6 %shard_map.87 = (bf16[32,1536]{1,0:T(8,128)(2,1)}, bf16[32,1536]{1,0:T(8,128)(2,1)}, bf16[32,1536]{1,0:T(8,128)(2,1)}, bf16[32,1536]{1,0:T(8,128)(2,1)}, bf16[32...) custom-call(s32[1]{0:T(128)} %bitcast.11.flags, ...), custom_call_target="tpu_custom_call" | custom-call | tf_op jit(solution)/shard_map/pallas_call | solution.py:22
  58.8 2.5 %collective-permute-start.11 = (bf16[32,1536]{1,0:T(8,128)(2,1)}, bf16[32,1536]{1,0:T(8,128)(2,1)S(1)}, u32[]{:S(2)}, u32[]{:S(2)}) collective-permute-start(bf16[32,1536]{1,0:T(8,128)(2,1)} %get-tuple-element.35), channel_id=1, source_target_pairs={{0,224},{16,240},{32,0},{48,16},{64,32},{80,48},{96,64},{112,80},{... | collective-permute-start | bytes 294920 | tf_op jit(solution)/shard_map/ppermute | solution.py:58
  61.3 2.9 %collective-permute-start.13 = (bf16[32,1536]{1,0:T(8,128)(2,1)}, bf16[32,1536]{1,0:T(8,128)(2,1)S(1)}, u32[]{:S(2)}, u32[]{:S(2)}) collective-permute-start(bf16[32,1536]{1,0:T(8,128)(2,1)} %get-tuple-element.37), channel_id=1, source_target_pairs={{0,192},{16,208},{32,224},{48,240},{64,0},{80,16},{96,32},{112,48}... | collective-permute-start | bytes 294920 | tf_op jit(solution)/shard_map/ppermute | solution.py:58
  64.2 3.8 %collective-permute-start.15 = (bf16[32,1536]{1,0:T(8,128)(2,1)}, bf16[32,1536]{1,0:T(8,128)(2,1)S(1)}, u32[]{:S(2)}, u32[]{:S(2)}) collective-permute-start(bf16[32,1536]{1,0:T(8,128)(2,1)} %get-tuple-element.39), channel_id=1, source_target_pairs={{0,160},{16,176},{32,192},{48,208},{64,224},{80,240},{96,0},{112,1... | collective-permute-start | bytes 294920 | tf_op jit(solution)/shard_map/ppermute | solution.py:58
  68.0 1.3 collective-permute-start.16
  69.3 3.4 %collective-permute-start.17 = (bf16[32,1536]{1,0:T(8,128)(2,1)}, bf16[32,1536]{1,0:T(8,128)(2,1)S(1)}, u32[]{:S(2)}, u32[]{:S(2)}) collective-permute-start(bf16[32,1536]{1,0:T(8,128)(2,1)} %get-tuple-element.41), channel_id=1, source_target_pairs={{0,128},{16,144},{32,160},{48,176},{64,192},{80,208},{96,224},{112... | collective-permute-start | bytes 294920 | tf_op jit(solution)/shard_map/ppermute | solution.py:58
  72.8 2.1 %collective-permute-done.14.refs_4_ = bf16[32,1536]{1,0:T(8,128)(2,1)S(1)} collective-permute-done((bf16[32,1536]{1,0:T(8,128)(2,1)}, bf16[32,1536]{1,0:T(8,128)(2,1)S(1)}, u32[]{:S(2)}, u32[]{:S(2)}) %collective-permute-start.14) | collective-permute-done | bytes 98336 | tf_op jit(solution)/shard_map/ppermute | solution.py:58
  74.9 5.4 %collective-permute-done.16.refs_6_ = bf16[32,1536]{1,0:T(8,128)(2,1)S(1)} collective-permute-done((bf16[32,1536]{1,0:T(8,128)(2,1)}, bf16[32,1536]{1,0:T(8,128)(2,1)S(1)}, u32[]{:S(2)}, u32[]{:S(2)}) %collective-permute-start.16) | collective-permute-done | bytes 98336 | tf_op jit(solution)/shard_map/ppermute | solution.py:58
  80.3 0.2 collective-permute-done.17.refs_7_
  80.5 0.4 copy-done.20
  80.9 0.2 copy-done.21
  81.1 2.3 %shard_map.88.d_txt_ref = bf16[32,1536]{1,0:T(8,128)(2,1)} custom-call(bf16[32,1536]{1,0:T(8,128)(2,1)} %get-tuple-element.34.refs_0_, bf16[32,1536]{1,0:T(8,128)(2,1)} %copy-done.15, bf16[32,1536]{1,0:T(8,128)(2,1)} %copy-done.16, bf16[32,1536]{1,0:T(8,128)(2,1)} %copy-done.17, bf16[32,1536]{1,0:T(8,128)(2,1)} %copy-done.18, bf16[32,1536]{1,0:T(8,128)(2,1)} %copy-done.19, ...), custom_call_target="tpu_custom_call" | custom-call | tf_op jit(solution)/shard_map/pallas_call | solution.py:22
  83.5 0.9 copy-done.3
  84.3 0.7 shard_map.89
  85.1 17.6 %all_to_all.25.grads_ref = bf16[16,32,768]{2,1,0:T(8,128)(2,1)S(1)} all-to-all(bf16[16,32,768]{2,1,0:T(8,128)(2,1)S(1)} %bitcast.27), channel_id=1, replica_groups={{0,2,4,6,8,10,12,14,16,18,20,22,24,26,28,30},{1,3,5,7,9,11,13,15,17,19,..., dimensions={0} | all-to-all | bytes 1572864 | tf_op jit(solution)/shard_map/all_to_all | solution.py:295
  102.7 0.5 shard_map.90
  103.3 1.6 %collective-permute-done.18.came_ref = bf16[192,768]{1,0:T(8,128)(2,1)S(1)} collective-permute-done((bf16[192,768]{1,0:T(8,128)(2,1)S(1)}, bf16[192,768]{1,0:T(8,128)(2,1)S(1)}, u32[]{:S(2)}, u32[]{:S(2)}) %collective-permute-start.18) | collective-permute-done | bytes 294944 | tf_op jit(solution)/shard_map/ppermute | solution.py:66
  104.9 0.8 shard_map.91
  105.7 8.1 %all-to-all-start.3 = ((bf16[8,2,24,384]{3,2,1,0:T(8,128)(2,1)}), bf16[8,2,24,384]{3,2,1,0:T(8,128)(2,1)S(1)}, u32[]{:S(2)}, u32[]{:S(2)}) async-start(bf16[8,2,24,384]{3,2,1,0:T(8,128)(2,1)} %shard_map.91), calls=%async_computation.3 | async-start | bytes 589824 | tf_op jit(solution)/shard_map/all_to_all | solution.py:238
  113.8 1.2 collective-permute-start.19
  115.0 3.9 %collective-permute-done.19 = f32[2,256]{1,0:T(2,128)S(1)} collective-permute-done((f32[2,256]{1,0:T(2,128)S(1)}, f32[2,256]{1,0:T(2,128)S(1)}, u32[]{:S(2)}, u32[]{:S(2)}) %collective-permute-start.19) | collective-permute-done | bytes 2080 | tf_op jit(solution)/shard_map/ppermute | solution.py:357
  118.9 0.9 collective-permute-start.20
  119.7 4.2 %collective-permute-done.20 = f32[2,256]{1,0:T(2,128)S(1)} collective-permute-done((f32[2,256]{1,0:T(2,128)S(1)}, f32[2,256]{1,0:T(2,128)S(1)}, u32[]{:S(2)}, u32[]{:S(2)}) %collective-permute-start.20) | collective-permute-done | bytes 2080 | tf_op jit(solution)/shard_map/ppermute | solution.py:357
  124.0 2.7 %all-to-all-done.3.parts_ref = bf16[8,2,24,384]{3,2,1,0:T(8,128)(2,1)S(1)} async-done(((bf16[8,2,24,384]{3,2,1,0:T(8,128)(2,1)}), bf16[8,2,24,384]{3,2,1,0:T(8,128)(2,1)S(1)}, u32[]{:S(2)}, u32[]{:S(2)}) %all-to-all-start.3) | async-done | bytes 294944 | tf_op jit(solution)/shard_map/all_to_all | solution.py:238
  126.7 0.9 broadcast_in_dim.8
  127.6 6.1 %all-to-all-start.4 = ((bf16[32,24,384]{2,1,0:T(8,128)(2,1)}), bf16[32,24,384]{2,1,0:T(8,128)(2,1)S(1)}, u32[]{:S(2)}, u32[]{:S(2)}) async-start(bf16[32,24,384]{2,1,0:T(8,128)(2,1)} %bitcast.16), calls=%async_computation.4 | async-start | bytes 1179648 | tf_op jit(solution)/shard_map/all_to_all | solution.py:372
  133.7 1.6 %collective-permute-start.21 = (f32[2,256]{1,0:T(2,128)S(1)}, f32[2,256]{1,0:T(2,128)S(1)}, u32[]{:S(2)}, u32[]{:S(2)}) collective-permute-start(f32[2,256]{1,0:T(2,128)S(1)} %add.104), channel_id=1, source_target_pairs={{0,16},{16,0},{32,48},{48,32},{64,80},{80,64},{96,112},{112,96},{1... | collective-permute-start | bytes 6152 | tf_op jit(solution)/shard_map/ppermute | solution.py:62
  135.3 2.3 %collective-permute-done.21 = f32[2,256]{1,0:T(2,128)S(1)} collective-permute-done((f32[2,256]{1,0:T(2,128)S(1)}, f32[2,256]{1,0:T(2,128)S(1)}, u32[]{:S(2)}, u32[]{:S(2)}) %collective-permute-start.21) | collective-permute-done | bytes 2080 | tf_op jit(solution)/shard_map/ppermute | solution.py:62
  137.6 0.5 broadcast.87
  138.1 0.7 fusion
  139.0 1.1 collective-permute-done.22
  140.1 0.7 select_n.84
  140.7 10.0 %all-to-all-done.4 = bf16[32,24,384]{2,1,0:T(8,128)(2,1)S(1)} async-done(((bf16[32,24,384]{2,1,0:T(8,128)(2,1)}), bf16[32,24,384]{2,1,0:T(8,128)(2,1)S(1)}, u32[]{:S(2)}, u32[]{:S(2)}) %all-to-all-start.4) | async-done | bytes 589856 | tf_op jit(solution)/shard_map/all_to_all | solution.py:372
  150.7 1.1 shard_map.93
  (67 shorter events, 1.1 us)
Async XLA Ops:
  0.6 10.5 %copy-start.13 = (bf16[96,512]{1,0:T(8,128)(2,1)S(1)}, bf16[96,512]{1,0:T(8,128)(2,1)}, u32[]{:S(2)}) copy-start(bf16[96,512]{1,0:T(8,128)(2,1)} %param.9) | copy-start | bytes 294916
  0.6 10.5 %copy-start.14 = (bf16[96,512]{1,0:T(8,128)(2,1)S(1)}, bf16[96,512]{1,0:T(8,128)(2,1)}, u32[]{:S(2)}) copy-start(bf16[96,512]{1,0:T(8,128)(2,1)} %param.8) | copy-start | bytes 294916
  0.7 14.6 %copy-start = (bf16[512,1536]{1,0:T(8,128)(2,1)S(1)}, bf16[512,1536]{1,0:T(8,128)(2,1)}, u32[]{:S(2)}) copy-start(bf16[512,1536]{1,0:T(8,128)(2,1)} %img_ref.1) | copy-start | bytes 4718596
  2.6 31.6 %all-to-all-start = ((bf16[8,32,1536]{2,1,0:T(8,128)(2,1)}), bf16[8,32,1536]{2,1,0:T(8,128)(2,1)S(1)}, u32[]{:S(2)}, u32[]{:S(2)}) async-start(bf16[8,32,1536]{2,1,0:T(8,128)(2,1)} %broadcast_in_dim.6), calls=%async_computation | async-start | bytes 1572864 | tf_op jit(solution)/shard_map/all_to_all | solution.py:238
  11.8 9.8 %copy-start.4 = (bf16[96,512]{1,0:T(8,128)(2,1)}, bf16[96,512]{1,0:T(8,128)(2,1)S(1)}, u32[]{:S(2)}) copy-start(bf16[96,512]{1,0:T(8,128)(2,1)S(1)} %get-tuple-element.52.refs_0_) | copy-start | bytes 294916
  11.8 5.8 %collective-permute-start.2 = (bf16[96,512]{1,0:T(8,128)(2,1)}, bf16[96,512]{1,0:T(8,128)(2,1)S(1)}, u32[]{:S(2)}, u32[]{:S(2)}) collective-permute-start(bf16[96,512]{1,0:T(8,128)(2,1)} %get-tuple-element.51), channel_id=1, source_target_pairs={{0,18},{1,19},{2,16},{3,17},{4,22},{5,23},{6,20},{7,21},{8,26},{9,... | collective-permute-start | bytes 294920 | tf_op jit(solution)/shard_map/ppermute | solution.py:75
  13.3 6.4 %collective-permute-start = (bf16[96,512]{1,0:T(8,128)(2,1)}, bf16[96,512]{1,0:T(8,128)(2,1)S(1)}, u32[]{:S(2)}, u32[]{:S(2)}) collective-permute-start(bf16[96,512]{1,0:T(8,128)(2,1)} %get-tuple-element.51), channel_id=1, source_target_pairs={{0,16},{16,0},{32,48},{48,32},{64,80},{80,64},{96,112},{112,96},{1... | collective-permute-start | bytes 294920 | tf_op jit(solution)/shard_map/ppermute | solution.py:62
  13.8 7.2 %collective-permute-start.3 = (bf16[96,512]{1,0:T(8,128)(2,1)S(1)}, bf16[96,512]{1,0:T(8,128)(2,1)S(1)}, u32[]{:S(2)}, u32[]{:S(2)}) collective-permute-start(bf16[96,512]{1,0:T(8,128)(2,1)S(1)} %get-tuple-element.52.refs_0_), channel_id=1, source_target_pairs={{0,1},{1,0},{2,3},{3,2},{4,5},{5,4},{6,7},{7,6},{8,9},{9,8},{10,11... | collective-permute-start | bytes 294920 | tf_op jit(solution)/shard_map/ppermute | solution.py:66
  13.8 6.6 %collective-permute-start.1 = (bf16[96,512]{1,0:T(8,128)(2,1)S(1)}, bf16[96,512]{1,0:T(8,128)(2,1)}, u32[]{:S(2)}, u32[]{:S(2)}) collective-permute-start(bf16[96,512]{1,0:T(8,128)(2,1)S(1)} %get-tuple-element.52.refs_0_), channel_id=1, source_target_pairs={{0,2},{1,3},{2,0},{3,1},{4,6},{5,7},{6,4},{7,5},{8,10},{9,11},{10,... | collective-permute-start | bytes 294920 | tf_op jit(solution)/shard_map/ppermute | solution.py:70
  15.3 20.9 %collective-permute-start.8 = (bf16[256,1536]{1,0:T(8,128)(2,1)S(1)}, bf16[256,1536]{1,0:T(8,128)(2,1)}, u32[]{:S(2)}, u32[]{:S(2)}) collective-permute-start(bf16[256,1536]{1,0:T(8,128)(2,1)S(1)} %bitcast.24), channel_id=1, source_target_pairs={{0,16},{16,0},{32,48},{48,32},{64,80},{80,64},{96,112},{112,96},{1... | collective-permute-start | bytes 2359304 | tf_op jit(solution)/shard_map/ppermute | solution.py:62
  17.6 4.0 %collective-permute-start.6 = (bf16[96,512]{1,0:T(8,128)(2,1)S(1)}, bf16[96,512]{1,0:T(8,128)(2,1)S(1)}, u32[]{:S(2)}, u32[]{:S(2)}) collective-permute-start(bf16[96,512]{1,0:T(8,128)(2,1)S(1)} %collective-permute-done.2.refs_3_), channel_id=1, source_target_pairs={{0,1},{1,0},{2,3},{3,2},{4,5},{5,4},{6,7},{7,6},{8,9},{9,8},{10,11... | collective-permute-start | bytes 294920 | tf_op jit(solution)/shard_map/ppermute | solution.py:66
  17.6 0.6 copy-start.6
  19.7 1.9 %collective-permute-start.4 = (bf16[96,512]{1,0:T(8,128)(2,1)S(1)}, bf16[96,512]{1,0:T(8,128)(2,1)S(1)}, u32[]{:S(2)}, u32[]{:S(2)}) collective-permute-start(bf16[96,512]{1,0:T(8,128)(2,1)S(1)} %collective-permute-done.refs_1_), channel_id=1, source_target_pairs={{0,1},{1,0},{2,3},{3,2},{4,5},{5,4},{6,7},{7,6},{8,9},{9,8},{10,11... | collective-permute-start | bytes 294920 | tf_op jit(solution)/shard_map/ppermute | solution.py:66
  19.7 0.6 copy-start.8
  20.4 1.7 %collective-permute-start.5 = (bf16[96,512]{1,0:T(8,128)(2,1)}, bf16[96,512]{1,0:T(8,128)(2,1)S(1)}, u32[]{:S(2)}, u32[]{:S(2)}) collective-permute-start(bf16[96,512]{1,0:T(8,128)(2,1)} %collective-permute-done.1.refs_2_), channel_id=1, source_target_pairs={{0,1},{1,0},{2,3},{3,2},{4,5},{5,4},{6,7},{7,6},{8,9},{9,8},{10,11... | collective-permute-start | bytes 294920 | tf_op jit(solution)/shard_map/ppermute | solution.py:66
  20.9 0.6 copy-start.10
  22.0 0.9 copy-start.5
  22.9 0.9 copy-start.7
  23.8 0.9 copy-start.9
  24.7 0.9 copy-start.11
  34.2 2.4 %collective-permute-start.7 = (bf16[256,1536]{1,0:T(8,128)(2,1)S(1)}, bf16[256,1536]{1,0:T(8,128)(2,1)}, u32[]{:S(2)}, u32[]{:S(2)}) collective-permute-start(bf16[256,1536]{1,0:T(8,128)(2,1)S(1)} %bitcast.22), channel_id=1, source_target_pairs={{0,1},{1,0},{2,3},{3,2},{4,5},{5,4},{6,7},{7,6},{8,9},{9,8},{10,11... | collective-permute-start | bytes 2359304 | tf_op jit(solution)/shard_map/ppermute | solution.py:66
  41.8 1.2 copy-start.1
  43.0 1.1 copy-start.2
  44.1 3.7 %collective-permute-start.9 = (bf16[256,1536]{1,0:T(8,128)(2,1)S(1)}, bf16[256,1536]{1,0:T(8,128)(2,1)S(1)}, u32[]{:S(2)}, u32[]{:S(2)}) collective-permute-start(bf16[256,1536]{1,0:T(8,128)(2,1)S(1)} %get-tuple-element.29), channel_id=1, source_target_pairs={{0,1},{1,0},{2,3},{3,2},{4,5},{5,4},{6,7},{7,6},{8,9},{9,8},{10,11... | collective-permute-start | bytes 2359304 | tf_op jit(solution)/shard_map/ppermute | solution.py:66
  44.3 3.6 %collective-permute-start.10 = (f32[2,256]{1,0:T(2,128)S(1)}, f32[2,256]{1,0:T(2,128)S(1)}, u32[]{:S(2)}, u32[]{:S(2)}) collective-permute-start(f32[2,256]{1,0:T(2,128)S(1)} %get-tuple-element.30), channel_id=1, source_target_pairs={{0,2},{1,3},{2,0},{3,1},{4,6},{5,7},{6,4},{7,5},{8,10},{9,11},{10,... | collective-permute-start | bytes 6152 | tf_op jit(solution)/shard_map/ppermute | solution.py:300
  47.9 0.9 copy-start.12
  48.8 34.7 %all-to-all-start.1 = ((bf16[16,32,1536]{2,1,0:T(8,128)(2,1)}), bf16[16,32,1536]{2,1,0:T(8,128)(2,1)S(1)}, u32[]{:S(2)}, u32[]{:S(2)}) async-start(bf16[16,32,1536]{2,1,0:T(8,128)(2,1)} %copy-done.1), calls=%async_computation.1 | async-start | bytes 3145728 | tf_op jit(solution)/shard_map/all_to_all | solution.py:295
  58.8 9.2 %collective-permute-start.11 = (bf16[32,1536]{1,0:T(8,128)(2,1)}, bf16[32,1536]{1,0:T(8,128)(2,1)S(1)}, u32[]{:S(2)}, u32[]{:S(2)}) collective-permute-start(bf16[32,1536]{1,0:T(8,128)(2,1)} %get-tuple-element.35), channel_id=1, source_target_pairs={{0,224},{16,240},{32,0},{48,16},{64,32},{80,48},{96,64},{112,80},{... | collective-permute-start | bytes 294920 | tf_op jit(solution)/shard_map/ppermute | solution.py:58
  61.3 8.0 %collective-permute-start.12 = (bf16[32,1536]{1,0:T(8,128)(2,1)}, bf16[32,1536]{1,0:T(8,128)(2,1)S(1)}, u32[]{:S(2)}, u32[]{:S(2)}) collective-permute-start(bf16[32,1536]{1,0:T(8,128)(2,1)} %get-tuple-element.36), channel_id=1, source_target_pairs={{0,32},{16,48},{32,64},{48,80},{64,96},{80,112},{96,128},{112,144}... | collective-permute-start | bytes 294920 | tf_op jit(solution)/shard_map/ppermute | solution.py:58
  61.3 11.5 %collective-permute-start.13 = (bf16[32,1536]{1,0:T(8,128)(2,1)}, bf16[32,1536]{1,0:T(8,128)(2,1)S(1)}, u32[]{:S(2)}, u32[]{:S(2)}) collective-permute-start(bf16[32,1536]{1,0:T(8,128)(2,1)} %get-tuple-element.37), channel_id=1, source_target_pairs={{0,192},{16,208},{32,224},{48,240},{64,0},{80,16},{96,32},{112,48}... | collective-permute-start | bytes 294920 | tf_op jit(solution)/shard_map/ppermute | solution.py:58
  64.2 10.7 %collective-permute-start.14 = (bf16[32,1536]{1,0:T(8,128)(2,1)}, bf16[32,1536]{1,0:T(8,128)(2,1)S(1)}, u32[]{:S(2)}, u32[]{:S(2)}) collective-permute-start(bf16[32,1536]{1,0:T(8,128)(2,1)} %get-tuple-element.38), channel_id=1, source_target_pairs={{0,64},{16,80},{32,96},{48,112},{64,128},{80,144},{96,160},{112,17... | collective-permute-start | bytes 294920 | tf_op jit(solution)/shard_map/ppermute | solution.py:58
  64.2 10.7 %collective-permute-start.15 = (bf16[32,1536]{1,0:T(8,128)(2,1)}, bf16[32,1536]{1,0:T(8,128)(2,1)S(1)}, u32[]{:S(2)}, u32[]{:S(2)}) collective-permute-start(bf16[32,1536]{1,0:T(8,128)(2,1)} %get-tuple-element.39), channel_id=1, source_target_pairs={{0,160},{16,176},{32,192},{48,208},{64,224},{80,240},{96,0},{112,1... | collective-permute-start | bytes 294920 | tf_op jit(solution)/shard_map/ppermute | solution.py:58
  68.0 12.5 %copy-start.15 = (bf16[32,1536]{1,0:T(8,128)(2,1)}, bf16[32,1536]{1,0:T(8,128)(2,1)S(1)}, u32[]{:S(2)}) copy-start(bf16[32,1536]{1,0:T(8,128)(2,1)S(1)} %collective-permute-done.11.refs_1_) | copy-start | bytes 294916
  68.0 12.2 %collective-permute-start.16 = (bf16[32,1536]{1,0:T(8,128)(2,1)}, bf16[32,1536]{1,0:T(8,128)(2,1)S(1)}, u32[]{:S(2)}, u32[]{:S(2)}) collective-permute-start(bf16[32,1536]{1,0:T(8,128)(2,1)} %get-tuple-element.40), channel_id=1, source_target_pairs={{0,96},{16,112},{32,128},{48,144},{64,160},{80,176},{96,192},{112,... | collective-permute-start | bytes 294920 | tf_op jit(solution)/shard_map/ppermute | solution.py:58
  69.3 11.2 %copy-start.16 = (bf16[32,1536]{1,0:T(8,128)(2,1)}, bf16[32,1536]{1,0:T(8,128)(2,1)S(1)}, u32[]{:S(2)}) copy-start(bf16[32,1536]{1,0:T(8,128)(2,1)S(1)} %collective-permute-done.12.refs_2_) | copy-start | bytes 294916
  69.3 11.2 %collective-permute-start.17 = (bf16[32,1536]{1,0:T(8,128)(2,1)}, bf16[32,1536]{1,0:T(8,128)(2,1)S(1)}, u32[]{:S(2)}, u32[]{:S(2)}) collective-permute-start(bf16[32,1536]{1,0:T(8,128)(2,1)} %get-tuple-element.41), channel_id=1, source_target_pairs={{0,128},{16,144},{32,160},{48,176},{64,192},{80,208},{96,224},{112... | collective-permute-start | bytes 294920 | tf_op jit(solution)/shard_map/ppermute | solution.py:58
  72.8 7.7 %copy-start.17 = (bf16[32,1536]{1,0:T(8,128)(2,1)}, bf16[32,1536]{1,0:T(8,128)(2,1)S(1)}, u32[]{:S(2)}) copy-start(bf16[32,1536]{1,0:T(8,128)(2,1)S(1)} %collective-permute-done.13.refs_3_) | copy-start | bytes 294916
  74.9 5.6 %copy-start.18 = (bf16[32,1536]{1,0:T(8,128)(2,1)}, bf16[32,1536]{1,0:T(8,128)(2,1)S(1)}, u32[]{:S(2)}) copy-start(bf16[32,1536]{1,0:T(8,128)(2,1)S(1)} %collective-permute-done.14.refs_4_) | copy-start | bytes 294916
  74.9 5.7 %copy-start.19 = (bf16[32,1536]{1,0:T(8,128)(2,1)}, bf16[32,1536]{1,0:T(8,128)(2,1)S(1)}, u32[]{:S(2)}) copy-start(bf16[32,1536]{1,0:T(8,128)(2,1)S(1)} %collective-permute-done.15.refs_5_) | copy-start | bytes 294916
  80.3 0.6 copy-start.20
  80.5 0.6 copy-start.21
  83.4 0.9 copy-start.3
  103.2 1.7 %collective-permute-start.18 = (bf16[192,768]{1,0:T(8,128)(2,1)S(1)}, bf16[192,768]{1,0:T(8,128)(2,1)S(1)}, u32[]{:S(2)}, u32[]{:S(2)}) collective-permute-start(bf16[192,768]{1,0:T(8,128)(2,1)S(1)} %get-tuple-element.43), channel_id=1, source_target_pairs={{0,1},{1,0},{2,3},{3,2},{4,5},{5,4},{6,7},{7,6},{8,9},{9,8},{10,11... | collective-permute-start | bytes 884744 | tf_op jit(solution)/shard_map/ppermute | solution.py:66
  105.7 21.0 %all-to-all-start.3 = ((bf16[8,2,24,384]{3,2,1,0:T(8,128)(2,1)}), bf16[8,2,24,384]{3,2,1,0:T(8,128)(2,1)S(1)}, u32[]{:S(2)}, u32[]{:S(2)}) async-start(bf16[8,2,24,384]{3,2,1,0:T(8,128)(2,1)} %shard_map.91), calls=%async_computation.3 | async-start | bytes 589824 | tf_op jit(solution)/shard_map/all_to_all | solution.py:238
  113.8 5.1 %collective-permute-start.19 = (f32[2,256]{1,0:T(2,128)S(1)}, f32[2,256]{1,0:T(2,128)S(1)}, u32[]{:S(2)}, u32[]{:S(2)}) collective-permute-start(f32[2,256]{1,0:T(2,128)S(1)} %add.102), channel_id=1, source_target_pairs={{0,4},{1,5},{2,6},{3,7},{4,0},{5,1},{6,2},{7,3},{8,12},{9,13},{10,... | collective-permute-start | bytes 6152 | tf_op jit(solution)/shard_map/ppermute | solution.py:357
  118.9 5.1 %collective-permute-start.20 = (f32[2,256]{1,0:T(2,128)S(1)}, f32[2,256]{1,0:T(2,128)S(1)}, u32[]{:S(2)}, u32[]{:S(2)}) collective-permute-start(f32[2,256]{1,0:T(2,128)S(1)} %add.103), channel_id=1, source_target_pairs={{0,8},{1,9},{2,10},{3,11},{4,12},{5,13},{6,14},{7,15},{8,0},{9,1},... | collective-permute-start | bytes 6152 | tf_op jit(solution)/shard_map/ppermute | solution.py:357
  127.6 23.2 %all-to-all-start.4 = ((bf16[32,24,384]{2,1,0:T(8,128)(2,1)}), bf16[32,24,384]{2,1,0:T(8,128)(2,1)S(1)}, u32[]{:S(2)}, u32[]{:S(2)}) async-start(bf16[32,24,384]{2,1,0:T(8,128)(2,1)} %bitcast.16), calls=%async_computation.4 | async-start | bytes 1179648 | tf_op jit(solution)/shard_map/all_to_all | solution.py:372
  133.7 3.9 %collective-permute-start.21 = (f32[2,256]{1,0:T(2,128)S(1)}, f32[2,256]{1,0:T(2,128)S(1)}, u32[]{:S(2)}, u32[]{:S(2)}) collective-permute-start(f32[2,256]{1,0:T(2,128)S(1)} %add.104), channel_id=1, source_target_pairs={{0,16},{16,0},{32,48},{48,32},{64,80},{80,64},{96,112},{112,96},{1... | collective-permute-start | bytes 6152 | tf_op jit(solution)/shard_map/ppermute | solution.py:62
  138.8 1.2 collective-permute-start.22

commit v15 on v14

--- a/solution.py
+++ b/solution.py
@@ -279,7 +279,7 @@
             own,
             partner,
         ],
-        24,
+        50,
         [SMEM, SMEM] + [VMEM] * 5,
         None,
         [pltpu.VMEM((rows, width), BF16)] * 2

time: 153 us -> 151 us (0.987)
  local copies, waits for them, and re-layouts: 14.6 us -> 12.3 us
    unnamed x44 -> x40, local copies, waits for them, and re-layouts: 10.2 us -> 7.91 us
where the time goes in v15:
time: 151 us
  starting transfers between devices  54.2 us (36%)
  waiting for transfers between devices  46.9 us (31%)
  blocking collectives  17.6 us (12%)
  Pallas kernels  15.6 us (10%)
  local copies, waits for them, and re-layouts  12.3 us (8%)
  between operations  2.15 us (1%)
  other arithmetic  1.81 us (1%)
    all_to_all x1, blocking collectives, over_plane(): lax.all_to_all(value, ('dp', 'mp'), 0, 0, tiled=True, axis_index_groups=p...  17.6 us
    all_to_all x2, starting transfers between devices, over_z(): lax.all_to_all(value, 'dp', 0, 0, tiled=True, axis_index_groups=same_y)  16.5 us
    pallas_call x9, Pallas kernels, local(): pl.pallas_call(kernel, out_shape=shapes, in_specs=specs or [VMEM] * len(o...  15.6 us
    ppermute x7, starting transfers between devices, along_z(): lax.ppermute(value, 'dp', [(d, (d + 2 * steps) % 16) for d in range(16)])  13.9 us
    all_to_all x1, waiting for transfers between devices, shards(): lax.all_to_all(jnp.broadcast_to(summed[None], (16, 2, *shape)).reshape(32...  10 us
    all_to_all x2, waiting for transfers between devices, over_z(): lax.all_to_all(value, 'dp', 0, 0, tiled=True, axis_index_groups=same_y)  9.88 us
    ppermute x2, waiting for transfers between devices, shards(): lax.ppermute(losses, 'mp', [(m, m ^ turn) for m in range(16)])  8.1 us
    unnamed x40, local copies, waits for them, and re-layouts  7.91 us
  transfers between devices with their start and end apart: 27, of which 17 were waited for; matrix products, arithmetic and copies ran while one was open for 2% of the time, Pallas kernels for 4%

profile of v15, /device:TPU:2, one launch (start us, length us, event | category | flops | bytes accessed | tf_op | source)
XLA Modules:
  0.0 150.6 jit_solution(17300585056802782239)
XLA Ops:
  0.7 2.0 %broadcast_in_dim.6 = bf16[8,32,1536]{2,1,0:T(8,128)(2,1)} broadcast(bf16[32,1536]{1,0:T(8,128)(2,1)} %refs_8_.1), dimensions={1,2} | broadcast | bytes 884736 | tf_op jit(solution)/shard_map/broadcast_in_dim | solution.py:240
  2.6 8.5 %all-to-all-start = ((bf16[8,32,1536]{2,1,0:T(8,128)(2,1)}), bf16[8,32,1536]{2,1,0:T(8,128)(2,1)S(1)}, u32[]{:S(2)}, u32[]{:S(2)}) async-start(bf16[8,32,1536]{2,1,0:T(8,128)(2,1)} %broadcast_in_dim.6), calls=%async_computation | async-start | bytes 1572864 | tf_op jit(solution)/shard_map/all_to_all | solution.py:238
  11.1 0.7 broadcast_select_fusion
  11.8 1.5 %collective-permute-start.2 = (bf16[96,512]{1,0:T(8,128)(2,1)}, bf16[96,512]{1,0:T(8,128)(2,1)S(1)}, u32[]{:S(2)}, u32[]{:S(2)}) collective-permute-start(bf16[96,512]{1,0:T(8,128)(2,1)} %get-tuple-element.51), channel_id=1, source_target_pairs={{0,18},{1,19},{2,16},{3,17},{4,22},{5,23},{6,20},{7,21},{8,26},{9,... | collective-permute-start | bytes 294920 | tf_op jit(solution)/shard_map/ppermute | solution.py:75
  13.3 0.4 collective-permute-start
  13.8 1.5 collective-permute-start.1
  15.3 1.7 %collective-permute-start.8 = (bf16[256,1536]{1,0:T(8,128)(2,1)S(1)}, bf16[256,1536]{1,0:T(8,128)(2,1)}, u32[]{:S(2)}, u32[]{:S(2)}) collective-permute-start(bf16[256,1536]{1,0:T(8,128)(2,1)S(1)} %bitcast.24), channel_id=1, source_target_pairs={{0,16},{16,0},{32,48},{48,32},{64,80},{80,64},{96,112},{112,96},{1... | collective-permute-start | bytes 2359304 | tf_op jit(solution)/shard_map/ppermute | solution.py:62
  17.0 0.6 collective-permute-done.2.refs_3_
  17.6 0.6 copy-done.4
  18.2 1.5 %collective-permute-done.refs_1_ = bf16[96,512]{1,0:T(8,128)(2,1)S(1)} collective-permute-done((bf16[96,512]{1,0:T(8,128)(2,1)}, bf16[96,512]{1,0:T(8,128)(2,1)S(1)}, u32[]{:S(2)}, u32[]{:S(2)}) %collective-permute-start) | collective-permute-done | bytes 98336 | tf_op jit(solution)/shard_map/ppermute | solution.py:62
  19.7 0.6 copy-done.6
  20.4 0.5 collective-permute-start.5
  21.0 0.6 copy-done.8
  21.6 0.4 collective-permute-done.5.refs_6_
  22.0 0.9 copy-done.3
  22.9 0.9 copy-done.5
  23.8 0.9 copy-done.7
  24.7 0.9 copy-done.9
  25.6 1.4 shard_map.85.feats_ref
  27.0 7.2 %all-to-all-done = bf16[8,32,1536]{2,1,0:T(8,128)(2,1)S(1)} async-done(((bf16[8,32,1536]{2,1,0:T(8,128)(2,1)}), bf16[8,32,1536]{2,1,0:T(8,128)(2,1)S(1)}, u32[]{:S(2)}, u32[]{:S(2)}) %all-to-all-start) | async-done | bytes 786464 | tf_op jit(solution)/shard_map/all_to_all | solution.py:238
  35.8 0.1 add.100.refs_2_
  36.0 0.2 collective-permute-done.8.refs_6_
  36.2 0.4 collective-permute-done.7.refs_4_
  36.6 6.2 %shard_map.86 = (bf16[16,32,1536]{2,1,0:T(8,128)(2,1)}, f32[256,1536]{1,0:T(8,128)}, bf16[256,1536]{1,0:T(8,128)(2,1)S(1)}, f32[2,256]{1,0:T(2,128)S(1)}) custom-call(f32[2]{0:T(128)S(1)} %pad_maximum_fusion.refs_0_, s32[4]{0:T(128)S(1)} %pad_add_fusion.1.refs_1_, s32[1,512]{1,0:T(1,128)S(1)} %add.100.refs_2_, bf16[256,1536]{1,0:T(8,128)(2,1)S(1)} %bitcast.23, ...), custom_call_target="tpu_custom_call" | custom-call | tf_op jit(solution)/shard_map/pallas_call | solution.py:22
  42.9 0.1 collective-permute-start.9
  43.0 0.6 collective-permute-start.10
  43.6 3.1 %collective-permute-done.10 = f32[2,256]{1,0:T(2,128)S(1)} collective-permute-done((f32[2,256]{1,0:T(2,128)S(1)}, f32[2,256]{1,0:T(2,128)S(1)}, u32[]{:S(2)}, u32[]{:S(2)}) %collective-permute-start.10) | collective-permute-done | bytes 2080 | tf_op jit(solution)/shard_map/ppermute | solution.py:300
  46.6 0.9 copy-done.10
  47.5 7.5 %all-to-all-start.1 = ((bf16[16,32,1536]{2,1,0:T(8,128)(2,1)}), bf16[16,32,1536]{2,1,0:T(8,128)(2,1)S(1)}, u32[]{:S(2)}, u32[]{:S(2)}) async-start(bf16[16,32,1536]{2,1,0:T(8,128)(2,1)} %get-tuple-element.31), calls=%async_computation.1 | async-start | bytes 3145728 | tf_op jit(solution)/shard_map/all_to_all | solution.py:295
  55.0 2.6 %shard_map.87 = (bf16[32,1536]{1,0:T(8,128)(2,1)}, bf16[32,1536]{1,0:T(8,128)(2,1)}, bf16[32,1536]{1,0:T(8,128)(2,1)}, bf16[32,1536]{1,0:T(8,128)(2,1)}, bf16[32...) custom-call(s32[1]{0:T(128)} %bitcast.11.flags, ...), custom_call_target="tpu_custom_call" | custom-call | tf_op jit(solution)/shard_map/pallas_call | solution.py:22
  57.5 2.5 %collective-permute-start.11 = (bf16[32,1536]{1,0:T(8,128)(2,1)}, bf16[32,1536]{1,0:T(8,128)(2,1)S(1)}, u32[]{:S(2)}, u32[]{:S(2)}) collective-permute-start(bf16[32,1536]{1,0:T(8,128)(2,1)} %get-tuple-element.35), channel_id=1, source_target_pairs={{0,224},{16,240},{32,0},{48,16},{64,32},{80,48},{96,64},{112,80},{... | collective-permute-start | bytes 294920 | tf_op jit(solution)/shard_map/ppermute | solution.py:58
  60.0 2.9 %collective-permute-start.13 = (bf16[32,1536]{1,0:T(8,128)(2,1)}, bf16[32,1536]{1,0:T(8,128)(2,1)S(1)}, u32[]{:S(2)}, u32[]{:S(2)}) collective-permute-start(bf16[32,1536]{1,0:T(8,128)(2,1)} %get-tuple-element.37), channel_id=1, source_target_pairs={{0,192},{16,208},{32,224},{48,240},{64,0},{80,16},{96,32},{112,48}... | collective-permute-start | bytes 294920 | tf_op jit(solution)/shard_map/ppermute | solution.py:58
  62.9 3.8 %collective-permute-start.15 = (bf16[32,1536]{1,0:T(8,128)(2,1)}, bf16[32,1536]{1,0:T(8,128)(2,1)S(1)}, u32[]{:S(2)}, u32[]{:S(2)}) collective-permute-start(bf16[32,1536]{1,0:T(8,128)(2,1)} %get-tuple-element.39), channel_id=1, source_target_pairs={{0,160},{16,176},{32,192},{48,208},{64,224},{80,240},{96,0},{112,1... | collective-permute-start | bytes 294920 | tf_op jit(solution)/shard_map/ppermute | solution.py:58
  66.7 1.3 collective-permute-start.16
  68.0 3.4 %collective-permute-start.17 = (bf16[32,1536]{1,0:T(8,128)(2,1)}, bf16[32,1536]{1,0:T(8,128)(2,1)S(1)}, u32[]{:S(2)}, u32[]{:S(2)}) collective-permute-start(bf16[32,1536]{1,0:T(8,128)(2,1)} %get-tuple-element.41), channel_id=1, source_target_pairs={{0,128},{16,144},{32,160},{48,176},{64,192},{80,208},{96,224},{112... | collective-permute-start | bytes 294920 | tf_op jit(solution)/shard_map/ppermute | solution.py:58
  71.5 2.1 %collective-permute-done.14.refs_4_ = bf16[32,1536]{1,0:T(8,128)(2,1)S(1)} collective-permute-done((bf16[32,1536]{1,0:T(8,128)(2,1)}, bf16[32,1536]{1,0:T(8,128)(2,1)S(1)}, u32[]{:S(2)}, u32[]{:S(2)}) %collective-permute-start.14) | collective-permute-done | bytes 98336 | tf_op jit(solution)/shard_map/ppermute | solution.py:58
  73.6 5.4 %collective-permute-done.16.refs_6_ = bf16[32,1536]{1,0:T(8,128)(2,1)S(1)} collective-permute-done((bf16[32,1536]{1,0:T(8,128)(2,1)}, bf16[32,1536]{1,0:T(8,128)(2,1)S(1)}, u32[]{:S(2)}, u32[]{:S(2)}) %collective-permute-start.16) | collective-permute-done | bytes 98336 | tf_op jit(solution)/shard_map/ppermute | solution.py:58
  79.0 0.2 collective-permute-done.17.refs_7_
  79.3 0.3 copy-done.18
  79.6 0.3 copy-done.19
  79.9 2.3 %shard_map.88.d_txt_ref = bf16[32,1536]{1,0:T(8,128)(2,1)} custom-call(bf16[32,1536]{1,0:T(8,128)(2,1)} %get-tuple-element.34.refs_0_, bf16[32,1536]{1,0:T(8,128)(2,1)} %copy-done.13, bf16[32,1536]{1,0:T(8,128)(2,1)} %copy-done.14, bf16[32,1536]{1,0:T(8,128)(2,1)} %copy-done.15, bf16[32,1536]{1,0:T(8,128)(2,1)} %copy-done.16, bf16[32,1536]{1,0:T(8,128)(2,1)} %copy-done.17, ...), custom_call_target="tpu_custom_call" | custom-call | tf_op jit(solution)/shard_map/pallas_call | solution.py:22
  82.2 0.9 copy-done.1
  83.1 0.7 shard_map.89
  83.9 17.6 %all_to_all.25.grads_ref = bf16[16,32,768]{2,1,0:T(8,128)(2,1)S(1)} all-to-all(bf16[16,32,768]{2,1,0:T(8,128)(2,1)S(1)} %bitcast.27), channel_id=1, replica_groups={{0,2,4,6,8,10,12,14,16,18,20,22,24,26,28,30},{1,3,5,7,9,11,13,15,17,19,..., dimensions={0} | all-to-all | bytes 1572864 | tf_op jit(solution)/shard_map/all_to_all | solution.py:295
  101.5 0.5 shard_map.90
  102.0 0.1 collective-permute-start.18
  102.1 1.6 %collective-permute-done.18.came_ref = bf16[192,768]{1,0:T(8,128)(2,1)S(1)} collective-permute-done((bf16[192,768]{1,0:T(8,128)(2,1)S(1)}, bf16[192,768]{1,0:T(8,128)(2,1)S(1)}, u32[]{:S(2)}, u32[]{:S(2)}) %collective-permute-start.18) | collective-permute-done | bytes 294944 | tf_op jit(solution)/shard_map/ppermute | solution.py:66
  103.7 0.8 shard_map.91
  104.4 8.1 %all-to-all-start.3 = ((bf16[8,2,24,384]{3,2,1,0:T(8,128)(2,1)}), bf16[8,2,24,384]{3,2,1,0:T(8,128)(2,1)S(1)}, u32[]{:S(2)}, u32[]{:S(2)}) async-start(bf16[8,2,24,384]{3,2,1,0:T(8,128)(2,1)} %shard_map.91), calls=%async_computation.3 | async-start | bytes 589824 | tf_op jit(solution)/shard_map/all_to_all | solution.py:238
  112.5 1.2 collective-permute-start.19
  113.7 3.9 %collective-permute-done.19 = f32[2,256]{1,0:T(2,128)S(1)} collective-permute-done((f32[2,256]{1,0:T(2,128)S(1)}, f32[2,256]{1,0:T(2,128)S(1)}, u32[]{:S(2)}, u32[]{:S(2)}) %collective-permute-start.19) | collective-permute-done | bytes 2080 | tf_op jit(solution)/shard_map/ppermute | solution.py:357
  117.6 0.9 collective-permute-start.20
  118.5 4.2 %collective-permute-done.20 = f32[2,256]{1,0:T(2,128)S(1)} collective-permute-done((f32[2,256]{1,0:T(2,128)S(1)}, f32[2,256]{1,0:T(2,128)S(1)}, u32[]{:S(2)}, u32[]{:S(2)}) %collective-permute-start.20) | collective-permute-done | bytes 2080 | tf_op jit(solution)/shard_map/ppermute | solution.py:357
  122.7 2.7 %all-to-all-done.3.parts_ref = bf16[8,2,24,384]{3,2,1,0:T(8,128)(2,1)S(1)} async-done(((bf16[8,2,24,384]{3,2,1,0:T(8,128)(2,1)}), bf16[8,2,24,384]{3,2,1,0:T(8,128)(2,1)S(1)}, u32[]{:S(2)}, u32[]{:S(2)}) %all-to-all-start.3) | async-done | bytes 294944 | tf_op jit(solution)/shard_map/all_to_all | solution.py:238
  125.4 0.9 broadcast_in_dim.8
  126.3 6.1 %all-to-all-start.4 = ((bf16[32,24,384]{2,1,0:T(8,128)(2,1)}), bf16[32,24,384]{2,1,0:T(8,128)(2,1)S(1)}, u32[]{:S(2)}, u32[]{:S(2)}) async-start(bf16[32,24,384]{2,1,0:T(8,128)(2,1)} %bitcast.16), calls=%async_computation.4 | async-start | bytes 1179648 | tf_op jit(solution)/shard_map/all_to_all | solution.py:372
  132.4 1.6 %collective-permute-start.21 = (f32[2,256]{1,0:T(2,128)S(1)}, f32[2,256]{1,0:T(2,128)S(1)}, u32[]{:S(2)}, u32[]{:S(2)}) collective-permute-start(f32[2,256]{1,0:T(2,128)S(1)} %add.104), channel_id=1, source_target_pairs={{0,16},{16,0},{32,48},{48,32},{64,80},{80,64},{96,112},{112,96},{1... | collective-permute-start | bytes 6152 | tf_op jit(solution)/shard_map/ppermute | solution.py:62
  134.0 2.3 %collective-permute-done.21 = f32[2,256]{1,0:T(2,128)S(1)} collective-permute-done((f32[2,256]{1,0:T(2,128)S(1)}, f32[2,256]{1,0:T(2,128)S(1)}, u32[]{:S(2)}, u32[]{:S(2)}) %collective-permute-start.21) | collective-permute-done | bytes 2080 | tf_op jit(solution)/shard_map/ppermute | solution.py:62
  136.3 0.5 broadcast.87
  136.8 0.7 fusion
  137.7 1.1 collective-permute-done.22
  138.8 0.7 select_n.84
  139.5 10.0 %all-to-all-done.4 = bf16[32,24,384]{2,1,0:T(8,128)(2,1)S(1)} async-done(((bf16[32,24,384]{2,1,0:T(8,128)(2,1)}), bf16[32,24,384]{2,1,0:T(8,128)(2,1)S(1)}, u32[]{:S(2)}, u32[]{:S(2)}) %all-to-all-start.4) | async-done | bytes 589856 | tf_op jit(solution)/shard_map/all_to_all | solution.py:372
  149.5 1.1 shard_map.93
  (63 shorter events, 1.0 us)
Async XLA Ops:
  0.6 10.5 %copy-start.11 = (bf16[96,512]{1,0:T(8,128)(2,1)S(1)}, bf16[96,512]{1,0:T(8,128)(2,1)}, u32[]{:S(2)}) copy-start(bf16[96,512]{1,0:T(8,128)(2,1)} %param.9) | copy-start | bytes 294916
  0.6 10.5 %copy-start.12 = (bf16[96,512]{1,0:T(8,128)(2,1)S(1)}, bf16[96,512]{1,0:T(8,128)(2,1)}, u32[]{:S(2)}) copy-start(bf16[96,512]{1,0:T(8,128)(2,1)} %param.8) | copy-start | bytes 294916
  0.7 14.6 %copy-start = (bf16[512,1536]{1,0:T(8,128)(2,1)S(1)}, bf16[512,1536]{1,0:T(8,128)(2,1)}, u32[]{:S(2)}) copy-start(bf16[512,1536]{1,0:T(8,128)(2,1)} %img_ref.1) | copy-start | bytes 4718596
  2.6 31.6 %all-to-all-start = ((bf16[8,32,1536]{2,1,0:T(8,128)(2,1)}), bf16[8,32,1536]{2,1,0:T(8,128)(2,1)S(1)}, u32[]{:S(2)}, u32[]{:S(2)}) async-start(bf16[8,32,1536]{2,1,0:T(8,128)(2,1)} %broadcast_in_dim.6), calls=%async_computation | async-start | bytes 1572864 | tf_op jit(solution)/shard_map/all_to_all | solution.py:238
  11.8 9.8 %copy-start.2 = (bf16[96,512]{1,0:T(8,128)(2,1)}, bf16[96,512]{1,0:T(8,128)(2,1)S(1)}, u32[]{:S(2)}) copy-start(bf16[96,512]{1,0:T(8,128)(2,1)S(1)} %get-tuple-element.52.refs_0_) | copy-start | bytes 294916
  11.8 5.8 %collective-permute-start.2 = (bf16[96,512]{1,0:T(8,128)(2,1)}, bf16[96,512]{1,0:T(8,128)(2,1)S(1)}, u32[]{:S(2)}, u32[]{:S(2)}) collective-permute-start(bf16[96,512]{1,0:T(8,128)(2,1)} %get-tuple-element.51), channel_id=1, source_target_pairs={{0,18},{1,19},{2,16},{3,17},{4,22},{5,23},{6,20},{7,21},{8,26},{9,... | collective-permute-start | bytes 294920 | tf_op jit(solution)/shard_map/ppermute | solution.py:75
  13.3 6.4 %collective-permute-start = (bf16[96,512]{1,0:T(8,128)(2,1)}, bf16[96,512]{1,0:T(8,128)(2,1)S(1)}, u32[]{:S(2)}, u32[]{:S(2)}) collective-permute-start(bf16[96,512]{1,0:T(8,128)(2,1)} %get-tuple-element.51), channel_id=1, source_target_pairs={{0,16},{16,0},{32,48},{48,32},{64,80},{80,64},{96,112},{112,96},{1... | collective-permute-start | bytes 294920 | tf_op jit(solution)/shard_map/ppermute | solution.py:62
  13.8 7.2 %collective-permute-start.3 = (bf16[96,512]{1,0:T(8,128)(2,1)S(1)}, bf16[96,512]{1,0:T(8,128)(2,1)S(1)}, u32[]{:S(2)}, u32[]{:S(2)}) collective-permute-start(bf16[96,512]{1,0:T(8,128)(2,1)S(1)} %get-tuple-element.52.refs_0_), channel_id=1, source_target_pairs={{0,1},{1,0},{2,3},{3,2},{4,5},{5,4},{6,7},{7,6},{8,9},{9,8},{10,11... | collective-permute-start | bytes 294920 | tf_op jit(solution)/shard_map/ppermute | solution.py:66
  13.8 6.6 %collective-permute-start.1 = (bf16[96,512]{1,0:T(8,128)(2,1)S(1)}, bf16[96,512]{1,0:T(8,128)(2,1)}, u32[]{:S(2)}, u32[]{:S(2)}) collective-permute-start(bf16[96,512]{1,0:T(8,128)(2,1)S(1)} %get-tuple-element.52.refs_0_), channel_id=1, source_target_pairs={{0,2},{1,3},{2,0},{3,1},{4,6},{5,7},{6,4},{7,5},{8,10},{9,11},{10,... | collective-permute-start | bytes 294920 | tf_op jit(solution)/shard_map/ppermute | solution.py:70
  15.3 20.9 %collective-permute-start.8 = (bf16[256,1536]{1,0:T(8,128)(2,1)S(1)}, bf16[256,1536]{1,0:T(8,128)(2,1)}, u32[]{:S(2)}, u32[]{:S(2)}) collective-permute-start(bf16[256,1536]{1,0:T(8,128)(2,1)S(1)} %bitcast.24), channel_id=1, source_target_pairs={{0,16},{16,0},{32,48},{48,32},{64,80},{80,64},{96,112},{112,96},{1... | collective-permute-start | bytes 2359304 | tf_op jit(solution)/shard_map/ppermute | solution.py:62
  17.6 4.0 %collective-permute-start.6 = (bf16[96,512]{1,0:T(8,128)(2,1)S(1)}, bf16[96,512]{1,0:T(8,128)(2,1)S(1)}, u32[]{:S(2)}, u32[]{:S(2)}) collective-permute-start(bf16[96,512]{1,0:T(8,128)(2,1)S(1)} %collective-permute-done.2.refs_3_), channel_id=1, source_target_pairs={{0,1},{1,0},{2,3},{3,2},{4,5},{5,4},{6,7},{7,6},{8,9},{9,8},{10,11... | collective-permute-start | bytes 294920 | tf_op jit(solution)/shard_map/ppermute | solution.py:66
  17.6 0.6 copy-start.4
  19.7 1.9 %collective-permute-start.4 = (bf16[96,512]{1,0:T(8,128)(2,1)S(1)}, bf16[96,512]{1,0:T(8,128)(2,1)S(1)}, u32[]{:S(2)}, u32[]{:S(2)}) collective-permute-start(bf16[96,512]{1,0:T(8,128)(2,1)S(1)} %collective-permute-done.refs_1_), channel_id=1, source_target_pairs={{0,1},{1,0},{2,3},{3,2},{4,5},{5,4},{6,7},{7,6},{8,9},{9,8},{10,11... | collective-permute-start | bytes 294920 | tf_op jit(solution)/shard_map/ppermute | solution.py:66
  19.7 0.6 copy-start.6
  20.4 1.7 %collective-permute-start.5 = (bf16[96,512]{1,0:T(8,128)(2,1)}, bf16[96,512]{1,0:T(8,128)(2,1)S(1)}, u32[]{:S(2)}, u32[]{:S(2)}) collective-permute-start(bf16[96,512]{1,0:T(8,128)(2,1)} %collective-permute-done.1.refs_2_), channel_id=1, source_target_pairs={{0,1},{1,0},{2,3},{3,2},{4,5},{5,4},{6,7},{7,6},{8,9},{9,8},{10,11... | collective-permute-start | bytes 294920 | tf_op jit(solution)/shard_map/ppermute | solution.py:66
  21.0 0.6 copy-start.8
  22.0 0.9 copy-start.3
  22.9 0.9 copy-start.5
  23.8 0.9 copy-start.7
  24.7 0.9 copy-start.9
  34.2 2.4 %collective-permute-start.7 = (bf16[256,1536]{1,0:T(8,128)(2,1)S(1)}, bf16[256,1536]{1,0:T(8,128)(2,1)}, u32[]{:S(2)}, u32[]{:S(2)}) collective-permute-start(bf16[256,1536]{1,0:T(8,128)(2,1)S(1)} %bitcast.22), channel_id=1, source_target_pairs={{0,1},{1,0},{2,3},{3,2},{4,5},{5,4},{6,7},{7,6},{8,9},{9,8},{10,11... | collective-permute-start | bytes 2359304 | tf_op jit(solution)/shard_map/ppermute | solution.py:66
  42.9 3.7 %collective-permute-start.9 = (bf16[256,1536]{1,0:T(8,128)(2,1)S(1)}, bf16[256,1536]{1,0:T(8,128)(2,1)S(1)}, u32[]{:S(2)}, u32[]{:S(2)}) collective-permute-start(bf16[256,1536]{1,0:T(8,128)(2,1)S(1)} %get-tuple-element.29), channel_id=1, source_target_pairs={{0,1},{1,0},{2,3},{3,2},{4,5},{5,4},{6,7},{7,6},{8,9},{9,8},{10,11... | collective-permute-start | bytes 2359304 | tf_op jit(solution)/shard_map/ppermute | solution.py:66
  43.0 3.6 %collective-permute-start.10 = (f32[2,256]{1,0:T(2,128)S(1)}, f32[2,256]{1,0:T(2,128)S(1)}, u32[]{:S(2)}, u32[]{:S(2)}) collective-permute-start(f32[2,256]{1,0:T(2,128)S(1)} %get-tuple-element.30), channel_id=1, source_target_pairs={{0,2},{1,3},{2,0},{3,1},{4,6},{5,7},{6,4},{7,5},{8,10},{9,11},{10,... | collective-permute-start | bytes 6152 | tf_op jit(solution)/shard_map/ppermute | solution.py:300
  46.6 0.9 copy-start.10
  47.5 34.7 %all-to-all-start.1 = ((bf16[16,32,1536]{2,1,0:T(8,128)(2,1)}), bf16[16,32,1536]{2,1,0:T(8,128)(2,1)S(1)}, u32[]{:S(2)}, u32[]{:S(2)}) async-start(bf16[16,32,1536]{2,1,0:T(8,128)(2,1)} %get-tuple-element.31), calls=%async_computation.1 | async-start | bytes 3145728 | tf_op jit(solution)/shard_map/all_to_all | solution.py:295
  57.5 9.2 %collective-permute-start.11 = (bf16[32,1536]{1,0:T(8,128)(2,1)}, bf16[32,1536]{1,0:T(8,128)(2,1)S(1)}, u32[]{:S(2)}, u32[]{:S(2)}) collective-permute-start(bf16[32,1536]{1,0:T(8,128)(2,1)} %get-tuple-element.35), channel_id=1, source_target_pairs={{0,224},{16,240},{32,0},{48,16},{64,32},{80,48},{96,64},{112,80},{... | collective-permute-start | bytes 294920 | tf_op jit(solution)/shard_map/ppermute | solution.py:58
  60.0 8.0 %collective-permute-start.12 = (bf16[32,1536]{1,0:T(8,128)(2,1)}, bf16[32,1536]{1,0:T(8,128)(2,1)S(1)}, u32[]{:S(2)}, u32[]{:S(2)}) collective-permute-start(bf16[32,1536]{1,0:T(8,128)(2,1)} %get-tuple-element.36), channel_id=1, source_target_pairs={{0,32},{16,48},{32,64},{48,80},{64,96},{80,112},{96,128},{112,144}... | collective-permute-start | bytes 294920 | tf_op jit(solution)/shard_map/ppermute | solution.py:58
  60.0 11.5 %collective-permute-start.13 = (bf16[32,1536]{1,0:T(8,128)(2,1)}, bf16[32,1536]{1,0:T(8,128)(2,1)S(1)}, u32[]{:S(2)}, u32[]{:S(2)}) collective-permute-start(bf16[32,1536]{1,0:T(8,128)(2,1)} %get-tuple-element.37), channel_id=1, source_target_pairs={{0,192},{16,208},{32,224},{48,240},{64,0},{80,16},{96,32},{112,48}... | collective-permute-start | bytes 294920 | tf_op jit(solution)/shard_map/ppermute | solution.py:58
  62.9 10.6 %collective-permute-start.14 = (bf16[32,1536]{1,0:T(8,128)(2,1)}, bf16[32,1536]{1,0:T(8,128)(2,1)S(1)}, u32[]{:S(2)}, u32[]{:S(2)}) collective-permute-start(bf16[32,1536]{1,0:T(8,128)(2,1)} %get-tuple-element.38), channel_id=1, source_target_pairs={{0,64},{16,80},{32,96},{48,112},{64,128},{80,144},{96,160},{112,17... | collective-permute-start | bytes 294920 | tf_op jit(solution)/shard_map/ppermute | solution.py:58
  62.9 10.6 %collective-permute-start.15 = (bf16[32,1536]{1,0:T(8,128)(2,1)}, bf16[32,1536]{1,0:T(8,128)(2,1)S(1)}, u32[]{:S(2)}, u32[]{:S(2)}) collective-permute-start(bf16[32,1536]{1,0:T(8,128)(2,1)} %get-tuple-element.39), channel_id=1, source_target_pairs={{0,160},{16,176},{32,192},{48,208},{64,224},{80,240},{96,0},{112,1... | collective-permute-start | bytes 294920 | tf_op jit(solution)/shard_map/ppermute | solution.py:58
  66.7 12.5 %copy-start.13 = (bf16[32,1536]{1,0:T(8,128)(2,1)}, bf16[32,1536]{1,0:T(8,128)(2,1)S(1)}, u32[]{:S(2)}) copy-start(bf16[32,1536]{1,0:T(8,128)(2,1)S(1)} %collective-permute-done.11.refs_1_) | copy-start | bytes 294916
  66.7 12.2 %collective-permute-start.16 = (bf16[32,1536]{1,0:T(8,128)(2,1)}, bf16[32,1536]{1,0:T(8,128)(2,1)S(1)}, u32[]{:S(2)}, u32[]{:S(2)}) collective-permute-start(bf16[32,1536]{1,0:T(8,128)(2,1)} %get-tuple-element.40), channel_id=1, source_target_pairs={{0,96},{16,112},{32,128},{48,144},{64,160},{80,176},{96,192},{112,... | collective-permute-start | bytes 294920 | tf_op jit(solution)/shard_map/ppermute | solution.py:58
  68.0 11.2 %copy-start.14 = (bf16[32,1536]{1,0:T(8,128)(2,1)}, bf16[32,1536]{1,0:T(8,128)(2,1)S(1)}, u32[]{:S(2)}) copy-start(bf16[32,1536]{1,0:T(8,128)(2,1)S(1)} %collective-permute-done.12.refs_2_) | copy-start | bytes 294916
  68.0 11.2 %collective-permute-start.17 = (bf16[32,1536]{1,0:T(8,128)(2,1)}, bf16[32,1536]{1,0:T(8,128)(2,1)S(1)}, u32[]{:S(2)}, u32[]{:S(2)}) collective-permute-start(bf16[32,1536]{1,0:T(8,128)(2,1)} %get-tuple-element.41), channel_id=1, source_target_pairs={{0,128},{16,144},{32,160},{48,176},{64,192},{80,208},{96,224},{112... | collective-permute-start | bytes 294920 | tf_op jit(solution)/shard_map/ppermute | solution.py:58
  71.5 7.8 %copy-start.15 = (bf16[32,1536]{1,0:T(8,128)(2,1)}, bf16[32,1536]{1,0:T(8,128)(2,1)S(1)}, u32[]{:S(2)}) copy-start(bf16[32,1536]{1,0:T(8,128)(2,1)S(1)} %collective-permute-done.13.refs_3_) | copy-start | bytes 294916
  73.6 5.7 %copy-start.16 = (bf16[32,1536]{1,0:T(8,128)(2,1)}, bf16[32,1536]{1,0:T(8,128)(2,1)S(1)}, u32[]{:S(2)}) copy-start(bf16[32,1536]{1,0:T(8,128)(2,1)S(1)} %collective-permute-done.14.refs_4_) | copy-start | bytes 294916
  73.6 5.7 %copy-start.17 = (bf16[32,1536]{1,0:T(8,128)(2,1)}, bf16[32,1536]{1,0:T(8,128)(2,1)S(1)}, u32[]{:S(2)}) copy-start(bf16[32,1536]{1,0:T(8,128)(2,1)S(1)} %collective-permute-done.15.refs_5_) | copy-start | bytes 294916
  79.0 0.6 copy-start.18
  79.2 0.6 copy-start.19
  82.2 0.9 copy-start.1
  102.0 1.7 %collective-permute-start.18 = (bf16[192,768]{1,0:T(8,128)(2,1)S(1)}, bf16[192,768]{1,0:T(8,128)(2,1)S(1)}, u32[]{:S(2)}, u32[]{:S(2)}) collective-permute-start(bf16[192,768]{1,0:T(8,128)(2,1)S(1)} %get-tuple-element.43), channel_id=1, source_target_pairs={{0,1},{1,0},{2,3},{3,2},{4,5},{5,4},{6,7},{7,6},{8,9},{9,8},{10,11... | collective-permute-start | bytes 884744 | tf_op jit(solution)/shard_map/ppermute | solution.py:66
  104.4 21.0 %all-to-all-start.3 = ((bf16[8,2,24,384]{3,2,1,0:T(8,128)(2,1)}), bf16[8,2,24,384]{3,2,1,0:T(8,128)(2,1)S(1)}, u32[]{:S(2)}, u32[]{:S(2)}) async-start(bf16[8,2,24,384]{3,2,1,0:T(8,128)(2,1)} %shard_map.91), calls=%async_computation.3 | async-start | bytes 589824 | tf_op jit(solution)/shard_map/all_to_all | solution.py:238
  112.5 5.1 %collective-permute-start.19 = (f32[2,256]{1,0:T(2,128)S(1)}, f32[2,256]{1,0:T(2,128)S(1)}, u32[]{:S(2)}, u32[]{:S(2)}) collective-permute-start(f32[2,256]{1,0:T(2,128)S(1)} %add.102), channel_id=1, source_target_pairs={{0,4},{1,5},{2,6},{3,7},{4,0},{5,1},{6,2},{7,3},{8,12},{9,13},{10,... | collective-permute-start | bytes 6152 | tf_op jit(solution)/shard_map/ppermute | solution.py:357
  117.6 5.1 %collective-permute-start.20 = (f32[2,256]{1,0:T(2,128)S(1)}, f32[2,256]{1,0:T(2,128)S(1)}, u32[]{:S(2)}, u32[]{:S(2)}) collective-permute-start(f32[2,256]{1,0:T(2,128)S(1)} %add.103), channel_id=1, source_target_pairs={{0,8},{1,9},{2,10},{3,11},{4,12},{5,13},{6,14},{7,15},{8,0},{9,1},... | collective-permute-start | bytes 6152 | tf_op jit(solution)/shard_map/ppermute | solution.py:357
  126.3 23.2 %all-to-all-start.4 = ((bf16[32,24,384]{2,1,0:T(8,128)(2,1)}), bf16[32,24,384]{2,1,0:T(8,128)(2,1)S(1)}, u32[]{:S(2)}, u32[]{:S(2)}) async-start(bf16[32,24,384]{2,1,0:T(8,128)(2,1)} %bitcast.16), calls=%async_computation.4 | async-start | bytes 1179648 | tf_op jit(solution)/shard_map/all_to_all | solution.py:372
  132.4 3.9 %collective-permute-start.21 = (f32[2,256]{1,0:T(2,128)S(1)}, f32[2,256]{1,0:T(2,128)S(1)}, u32[]{:S(2)}, u32[]{:S(2)}) collective-permute-start(f32[2,256]{1,0:T(2,128)S(1)} %add.104), channel_id=1, source_target_pairs={{0,16},{16,0},{32,48},{48,32},{64,80},{80,64},{96,112},{112,96},{1... | collective-permute-start | bytes 6152 | tf_op jit(solution)/shard_map/ppermute | solution.py:62
  137.6 1.2 collective-permute-start.22

commit v16 on v15

--- a/solution.py
+++ b/solution.py
@@ -297,8 +297,7 @@
         )
 
     came_grad = swap_core(send)
-    losses = losses + lax.ppermute(losses, "mp", [(m, m ^ 2) for m in range(16)])
-    image_part, came_grad, losses = lax.optimization_barrier((image_part, came_grad, losses))
+    image_part, came_grad = lax.optimization_barrier((image_part, came_grad))
     text_parts = local(
         join_kernel,
         [((sub, width), BF16)] * 8,
@@ -353,9 +352,10 @@
     shape = (feats // 4, narrow // 2)
     cut = local(cut_kernel, ((8, 2, *shape), BF16), [kept, swap_core(sent)], 6)
     parts = over_z(cut)
-    for turn in (4, 8):
+    for turn in (2, 4):
         losses = losses + lax.ppermute(losses, "mp", [(m, m ^ turn) for m in range(16)])
     parts, losses = lax.optimization_barrier((parts, losses))
+    losses = losses + lax.ppermute(losses, "mp", [(m, m ^ 8) for m in range(16)])
     losses = losses + swap_y(losses)
     summed = local(
         sum_kernel,

time: 151 us -> 150 us (level)
  waiting for transfers between devices: 46.9 us -> 45.2 us
    all_to_all x1, waiting for transfers between devices: 10 us -> 6.03 us  [shards(): lax.all_to_all(jnp.broadcast_to(summed[None], (16, 2, *shape)).reshape(32...]
    ppermute x8, waiting for transfers between devices: 3.5 us -> 5.66 us  [swap_core(): return lax.ppermute(value, 'mp', [(m, m ^ 1) for m in range(16)])]
    ppermute x2, waiting for transfers between devices: 8.1 us -> 5.99 us  [shards(): lax.ppermute(losses, 'mp', [(m, m ^ turn) for m in range(16)])]
  transfers between devices with their start and end apart: 27 -> 27, of which waited for: 17 -> 18; matrix products, arithmetic and copies ran while one was open for 2% -> 2% of each run, Pallas kernels for 4% -> 4%
where the time goes in v16:
time: 150 us
  starting transfers between devices  54.6 us (36%)
  waiting for transfers between devices  45.2 us (30%)
  blocking collectives  18 us (12%)
  Pallas kernels  15.6 us (10%)
  local copies, waits for them, and re-layouts  12.3 us (8%)
  between operations  2.16 us (1%)
  other arithmetic  1.81 us (1%)
    all_to_all x1, blocking collectives, over_plane(): lax.all_to_all(value, ('dp', 'mp'), 0, 0, tiled=True, axis_index_groups=p...  18 us
    all_to_all x2, starting transfers between devices, over_z(): lax.all_to_all(value, 'dp', 0, 0, tiled=True, axis_index_groups=same_y)  15.9 us
    pallas_call x9, Pallas kernels, local(): pl.pallas_call(kernel, out_shape=shapes, in_specs=specs or [VMEM] * len(o...  15.6 us
    ppermute x7, starting transfers between devices, along_z(): lax.ppermute(value, 'dp', [(d, (d + 2 * steps) % 16) for d in range(16)])  14.1 us
    all_to_all x2, waiting for transfers between devices, over_z(): lax.all_to_all(value, 'dp', 0, 0, tiled=True, axis_index_groups=same_y)  11.4 us
    ppermute x7, waiting for transfers between devices, along_z(): lax.ppermute(value, 'dp', [(d, (d + 2 * steps) % 16) for d in range(16)])  8.38 us
    unnamed x40, local copies, waits for them, and re-layouts  7.91 us
    all_to_all x1, starting transfers between devices, over_plane(): lax.all_to_all(value, ('dp', 'mp'), 0, 0, tiled=True, axis_index_groups=p...  7.48 us
  transfers between devices with their start and end apart: 27, of which 18 were waited for; matrix products, arithmetic and copies ran while one was open for 2% of the time, Pallas kernels for 4%

profile of v16, /device:TPU:2, one launch (start us, length us, event | category | flops | bytes accessed | tf_op | source)
XLA Modules:
  0.0 149.6 jit_solution(8840188848755849309)
XLA Ops:
  0.7 2.0 %broadcast_in_dim.6 = bf16[8,32,1536]{2,1,0:T(8,128)(2,1)} broadcast(bf16[32,1536]{1,0:T(8,128)(2,1)} %refs_8_.1), dimensions={1,2} | broadcast | bytes 884736 | tf_op jit(solution)/shard_map/broadcast_in_dim | solution.py:240
  2.6 8.5 %all-to-all-start = ((bf16[8,32,1536]{2,1,0:T(8,128)(2,1)}), bf16[8,32,1536]{2,1,0:T(8,128)(2,1)S(1)}, u32[]{:S(2)}, u32[]{:S(2)}) async-start(bf16[8,32,1536]{2,1,0:T(8,128)(2,1)} %broadcast_in_dim.6), calls=%async_computation | async-start | bytes 1572864 | tf_op jit(solution)/shard_map/all_to_all | solution.py:238
  11.1 0.7 broadcast_select_fusion
  11.8 1.5 %collective-permute-start.2 = (bf16[96,512]{1,0:T(8,128)(2,1)}, bf16[96,512]{1,0:T(8,128)(2,1)S(1)}, u32[]{:S(2)}, u32[]{:S(2)}) collective-permute-start(bf16[96,512]{1,0:T(8,128)(2,1)} %get-tuple-element.49), channel_id=1, source_target_pairs={{0,18},{1,19},{2,16},{3,17},{4,22},{5,23},{6,20},{7,21},{8,26},{9,... | collective-permute-start | bytes 294920 | tf_op jit(solution)/shard_map/ppermute | solution.py:75
  13.3 0.4 collective-permute-start
  13.8 1.5 collective-permute-start.1
  15.3 1.7 %collective-permute-start.8 = (bf16[256,1536]{1,0:T(8,128)(2,1)S(1)}, bf16[256,1536]{1,0:T(8,128)(2,1)}, u32[]{:S(2)}, u32[]{:S(2)}) collective-permute-start(bf16[256,1536]{1,0:T(8,128)(2,1)S(1)} %bitcast.24), channel_id=1, source_target_pairs={{0,16},{16,0},{32,48},{48,32},{64,80},{80,64},{96,112},{112,96},{1... | collective-permute-start | bytes 2359304 | tf_op jit(solution)/shard_map/ppermute | solution.py:62
  17.0 0.6 collective-permute-done.2.refs_3_
  17.6 0.6 copy-done.4
  18.2 1.5 %collective-permute-done.refs_1_ = bf16[96,512]{1,0:T(8,128)(2,1)S(1)} collective-permute-done((bf16[96,512]{1,0:T(8,128)(2,1)}, bf16[96,512]{1,0:T(8,128)(2,1)S(1)}, u32[]{:S(2)}, u32[]{:S(2)}) %collective-permute-start) | collective-permute-done | bytes 98336 | tf_op jit(solution)/shard_map/ppermute | solution.py:62
  19.7 0.6 copy-done.6
  20.4 0.5 collective-permute-start.5
  21.0 0.6 copy-done.8
  21.6 0.4 collective-permute-done.5.refs_6_
  22.0 0.9 copy-done.3
  22.9 0.9 copy-done.5
  23.8 0.9 copy-done.7
  24.7 0.9 copy-done.9
  25.6 1.4 shard_map.85.feats_ref
  27.0 7.2 %all-to-all-done = bf16[8,32,1536]{2,1,0:T(8,128)(2,1)S(1)} async-done(((bf16[8,32,1536]{2,1,0:T(8,128)(2,1)}), bf16[8,32,1536]{2,1,0:T(8,128)(2,1)S(1)}, u32[]{:S(2)}, u32[]{:S(2)}) %all-to-all-start) | async-done | bytes 786464 | tf_op jit(solution)/shard_map/all_to_all | solution.py:238
  35.8 0.1 add.100.refs_2_
  36.0 0.2 collective-permute-done.8.refs_6_
  36.2 0.4 collective-permute-done.7.refs_4_
  36.6 6.2 %shard_map.86 = (bf16[16,32,1536]{2,1,0:T(8,128)(2,1)}, f32[256,1536]{1,0:T(8,128)}, bf16[256,1536]{1,0:T(8,128)(2,1)S(1)}, f32[2,256]{1,0:T(2,128)S(1)}) custom-call(f32[2]{0:T(128)S(1)} %pad_maximum_fusion.refs_0_, s32[4]{0:T(128)S(1)} %pad_add_fusion.1.refs_1_, s32[1,512]{1,0:T(1,128)S(1)} %add.100.refs_2_, bf16[256,1536]{1,0:T(8,128)(2,1)S(1)} %bitcast.23, ...), custom_call_target="tpu_custom_call" | custom-call | tf_op jit(solution)/shard_map/pallas_call | solution.py:22
  42.9 0.1 collective-permute-start.9
  43.0 2.2 %collective-permute-done.9.came_ref = bf16[256,1536]{1,0:T(8,128)(2,1)S(1)} collective-permute-done((bf16[256,1536]{1,0:T(8,128)(2,1)S(1)}, bf16[256,1536]{1,0:T(8,128)(2,1)S(1)}, u32[]{:S(2)}, u32[]{:S(2)}) %collective-permute-start.9) | collective-permute-done | bytes 786464 | tf_op jit(solution)/shard_map/ppermute | solution.py:66
  45.2 0.9 copy-done.10
  46.0 7.5 %all-to-all-start.1 = ((bf16[16,32,1536]{2,1,0:T(8,128)(2,1)}), bf16[16,32,1536]{2,1,0:T(8,128)(2,1)S(1)}, u32[]{:S(2)}, u32[]{:S(2)}) async-start(bf16[16,32,1536]{2,1,0:T(8,128)(2,1)} %get-tuple-element.29), calls=%async_computation.1 | async-start | bytes 3145728 | tf_op jit(solution)/shard_map/all_to_all | solution.py:295
  53.5 2.6 %shard_map.87 = (bf16[32,1536]{1,0:T(8,128)(2,1)}, bf16[32,1536]{1,0:T(8,128)(2,1)}, bf16[32,1536]{1,0:T(8,128)(2,1)}, bf16[32,1536]{1,0:T(8,128)(2,1)}, bf16[32...) custom-call(s32[1]{0:T(128)} %bitcast.11.flags, ...), custom_call_target="tpu_custom_call" | custom-call | tf_op jit(solution)/shard_map/pallas_call | solution.py:22
  56.1 2.6 %collective-permute-start.10 = (bf16[32,1536]{1,0:T(8,128)(2,1)}, bf16[32,1536]{1,0:T(8,128)(2,1)S(1)}, u32[]{:S(2)}, u32[]{:S(2)}) collective-permute-start(bf16[32,1536]{1,0:T(8,128)(2,1)} %get-tuple-element.33), channel_id=1, source_target_pairs={{0,224},{16,240},{32,0},{48,16},{64,32},{80,48},{96,64},{112,80},{... | collective-permute-start | bytes 294920 | tf_op jit(solution)/shard_map/ppermute | solution.py:58
  58.7 2.9 %collective-permute-start.12 = (bf16[32,1536]{1,0:T(8,128)(2,1)}, bf16[32,1536]{1,0:T(8,128)(2,1)S(1)}, u32[]{:S(2)}, u32[]{:S(2)}) collective-permute-start(bf16[32,1536]{1,0:T(8,128)(2,1)} %get-tuple-element.35), channel_id=1, source_target_pairs={{0,192},{16,208},{32,224},{48,240},{64,0},{80,16},{96,32},{112,48}... | collective-permute-start | bytes 294920 | tf_op jit(solution)/shard_map/ppermute | solution.py:58
  61.6 3.8 %collective-permute-start.14 = (bf16[32,1536]{1,0:T(8,128)(2,1)}, bf16[32,1536]{1,0:T(8,128)(2,1)S(1)}, u32[]{:S(2)}, u32[]{:S(2)}) collective-permute-start(bf16[32,1536]{1,0:T(8,128)(2,1)} %get-tuple-element.37), channel_id=1, source_target_pairs={{0,160},{16,176},{32,192},{48,208},{64,224},{80,240},{96,0},{112,1... | collective-permute-start | bytes 294920 | tf_op jit(solution)/shard_map/ppermute | solution.py:58
  65.4 1.3 collective-permute-start.15
  66.7 3.4 %collective-permute-start.16 = (bf16[32,1536]{1,0:T(8,128)(2,1)}, bf16[32,1536]{1,0:T(8,128)(2,1)S(1)}, u32[]{:S(2)}, u32[]{:S(2)}) collective-permute-start(bf16[32,1536]{1,0:T(8,128)(2,1)} %get-tuple-element.39), channel_id=1, source_target_pairs={{0,128},{16,144},{32,160},{48,176},{64,192},{80,208},{96,224},{112... | collective-permute-start | bytes 294920 | tf_op jit(solution)/shard_map/ppermute | solution.py:58
  70.2 2.1 %collective-permute-done.14.refs_5_ = bf16[32,1536]{1,0:T(8,128)(2,1)S(1)} collective-permute-done((bf16[32,1536]{1,0:T(8,128)(2,1)}, bf16[32,1536]{1,0:T(8,128)(2,1)S(1)}, u32[]{:S(2)}, u32[]{:S(2)}) %collective-permute-start.14) | collective-permute-done | bytes 98336 | tf_op jit(solution)/shard_map/ppermute | solution.py:58
  72.3 5.0 %collective-permute-done.15.refs_6_ = bf16[32,1536]{1,0:T(8,128)(2,1)S(1)} collective-permute-done((bf16[32,1536]{1,0:T(8,128)(2,1)}, bf16[32,1536]{1,0:T(8,128)(2,1)S(1)}, u32[]{:S(2)}, u32[]{:S(2)}) %collective-permute-start.15) | collective-permute-done | bytes 98336 | tf_op jit(solution)/shard_map/ppermute | solution.py:58
  77.3 1.3 collective-permute-done.16.refs_7_
  78.6 0.6 copy-done.19
  79.2 2.3 %shard_map.88.d_txt_ref = bf16[32,1536]{1,0:T(8,128)(2,1)} custom-call(bf16[32,1536]{1,0:T(8,128)(2,1)} %get-tuple-element.32.refs_0_, bf16[32,1536]{1,0:T(8,128)(2,1)} %copy-done.13, bf16[32,1536]{1,0:T(8,128)(2,1)} %copy-done.14, bf16[32,1536]{1,0:T(8,128)(2,1)} %copy-done.15, bf16[32,1536]{1,0:T(8,128)(2,1)} %copy-done.16, bf16[32,1536]{1,0:T(8,128)(2,1)} %copy-done.17, ...), custom_call_target="tpu_custom_call" | custom-call | tf_op jit(solution)/shard_map/pallas_call | solution.py:22
  81.5 0.9 copy-done.1
  82.4 0.7 shard_map.89
  83.2 18.0 %all_to_all.25.grads_ref = bf16[16,32,768]{2,1,0:T(8,128)(2,1)S(1)} all-to-all(bf16[16,32,768]{2,1,0:T(8,128)(2,1)S(1)} %bitcast.27), channel_id=1, replica_groups={{0,2,4,6,8,10,12,14,16,18,20,22,24,26,28,30},{1,3,5,7,9,11,13,15,17,19,..., dimensions={0} | all-to-all | bytes 1572864 | tf_op jit(solution)/shard_map/all_to_all | solution.py:295
  101.2 0.5 shard_map.90
  101.7 0.1 collective-permute-start.17
  101.8 1.6 %collective-permute-done.17.came_ref = bf16[192,768]{1,0:T(8,128)(2,1)S(1)} collective-permute-done((bf16[192,768]{1,0:T(8,128)(2,1)S(1)}, bf16[192,768]{1,0:T(8,128)(2,1)S(1)}, u32[]{:S(2)}, u32[]{:S(2)}) %collective-permute-start.17) | collective-permute-done | bytes 294944 | tf_op jit(solution)/shard_map/ppermute | solution.py:66
  103.4 0.8 shard_map.91
  104.2 7.4 %all-to-all-start.3 = ((bf16[8,2,24,384]{3,2,1,0:T(8,128)(2,1)}), bf16[8,2,24,384]{3,2,1,0:T(8,128)(2,1)S(1)}, u32[]{:S(2)}, u32[]{:S(2)}) async-start(bf16[8,2,24,384]{3,2,1,0:T(8,128)(2,1)} %shard_map.91), calls=%async_computation.3 | async-start | bytes 589824 | tf_op jit(solution)/shard_map/all_to_all | solution.py:238
  111.6 1.5 collective-permute-start.18
  113.1 2.1 %collective-permute-done.18 = f32[2,256]{1,0:T(2,128)S(1)} collective-permute-done((f32[2,256]{1,0:T(2,128)S(1)}, f32[2,256]{1,0:T(2,128)S(1)}, u32[]{:S(2)}, u32[]{:S(2)}) %collective-permute-start.18) | collective-permute-done | bytes 2080 | tf_op jit(solution)/shard_map/ppermute | solution.py:356
  115.2 1.2 collective-permute-start.19
  116.4 3.9 %collective-permute-done.19 = f32[2,256]{1,0:T(2,128)S(1)} collective-permute-done((f32[2,256]{1,0:T(2,128)S(1)}, f32[2,256]{1,0:T(2,128)S(1)}, u32[]{:S(2)}, u32[]{:S(2)}) %collective-permute-start.19) | collective-permute-done | bytes 2080 | tf_op jit(solution)/shard_map/ppermute | solution.py:356
  120.3 4.2 %all-to-all-done.3.parts_ref = bf16[8,2,24,384]{3,2,1,0:T(8,128)(2,1)S(1)} async-done(((bf16[8,2,24,384]{3,2,1,0:T(8,128)(2,1)}), bf16[8,2,24,384]{3,2,1,0:T(8,128)(2,1)S(1)}, u32[]{:S(2)}, u32[]{:S(2)}) %all-to-all-start.3) | async-done | bytes 294944 | tf_op jit(solution)/shard_map/all_to_all | solution.py:238
  124.5 0.9 broadcast_in_dim.8
  125.4 5.0 %all-to-all-start.4 = ((bf16[32,24,384]{2,1,0:T(8,128)(2,1)}), bf16[32,24,384]{2,1,0:T(8,128)(2,1)S(1)}, u32[]{:S(2)}, u32[]{:S(2)}) async-start(bf16[32,24,384]{2,1,0:T(8,128)(2,1)} %bitcast.16), calls=%async_computation.4 | async-start | bytes 1179648 | tf_op jit(solution)/shard_map/all_to_all | solution.py:372
  130.4 2.1 %collective-permute-start.20 = (f32[2,256]{1,0:T(2,128)S(1)}, f32[2,256]{1,0:T(2,128)S(1)}, u32[]{:S(2)}, u32[]{:S(2)}) collective-permute-start(f32[2,256]{1,0:T(2,128)S(1)} %add.103), channel_id=1, source_target_pairs={{0,8},{1,9},{2,10},{3,11},{4,12},{5,13},{6,14},{7,15},{8,0},{9,1},... | collective-permute-start | bytes 6152 | tf_op jit(solution)/shard_map/ppermute | solution.py:358
  132.5 3.1 %collective-permute-done.20 = f32[2,256]{1,0:T(2,128)S(1)} collective-permute-done((f32[2,256]{1,0:T(2,128)S(1)}, f32[2,256]{1,0:T(2,128)S(1)}, u32[]{:S(2)}, u32[]{:S(2)}) %collective-permute-start.20) | collective-permute-done | bytes 2080 | tf_op jit(solution)/shard_map/ppermute | solution.py:358
  135.6 1.5 collective-permute-start.21
  137.1 2.3 %collective-permute-done.21 = f32[2,256]{1,0:T(2,128)S(1)} collective-permute-done((f32[2,256]{1,0:T(2,128)S(1)}, f32[2,256]{1,0:T(2,128)S(1)}, u32[]{:S(2)}, u32[]{:S(2)}) %collective-permute-start.21) | collective-permute-done | bytes 2080 | tf_op jit(solution)/shard_map/ppermute | solution.py:62
  139.4 0.5 broadcast.87
  139.9 0.7 fusion
  140.8 1.1 collective-permute-done.22
  141.9 0.7 select_n.84
  142.5 6.0 %all-to-all-done.4 = bf16[32,24,384]{2,1,0:T(8,128)(2,1)S(1)} async-done(((bf16[32,24,384]{2,1,0:T(8,128)(2,1)}), bf16[32,24,384]{2,1,0:T(8,128)(2,1)S(1)}, u32[]{:S(2)}, u32[]{:S(2)}) %all-to-all-start.4) | async-done | bytes 589856 | tf_op jit(solution)/shard_map/all_to_all | solution.py:372
  148.6 1.1 shard_map.93
  (63 shorter events, 1.0 us)
Async XLA Ops:
  0.6 10.5 %copy-start.11 = (bf16[96,512]{1,0:T(8,128)(2,1)S(1)}, bf16[96,512]{1,0:T(8,128)(2,1)}, u32[]{:S(2)}) copy-start(bf16[96,512]{1,0:T(8,128)(2,1)} %param.9) | copy-start | bytes 294916
  0.6 10.5 %copy-start.12 = (bf16[96,512]{1,0:T(8,128)(2,1)S(1)}, bf16[96,512]{1,0:T(8,128)(2,1)}, u32[]{:S(2)}) copy-start(bf16[96,512]{1,0:T(8,128)(2,1)} %param.8) | copy-start | bytes 294916
  0.7 14.6 %copy-start = (bf16[512,1536]{1,0:T(8,128)(2,1)S(1)}, bf16[512,1536]{1,0:T(8,128)(2,1)}, u32[]{:S(2)}) copy-start(bf16[512,1536]{1,0:T(8,128)(2,1)} %img_ref.1) | copy-start | bytes 4718596
  2.6 31.6 %all-to-all-start = ((bf16[8,32,1536]{2,1,0:T(8,128)(2,1)}), bf16[8,32,1536]{2,1,0:T(8,128)(2,1)S(1)}, u32[]{:S(2)}, u32[]{:S(2)}) async-start(bf16[8,32,1536]{2,1,0:T(8,128)(2,1)} %broadcast_in_dim.6), calls=%async_computation | async-start | bytes 1572864 | tf_op jit(solution)/shard_map/all_to_all | solution.py:238
  11.8 9.8 %copy-start.2 = (bf16[96,512]{1,0:T(8,128)(2,1)}, bf16[96,512]{1,0:T(8,128)(2,1)S(1)}, u32[]{:S(2)}) copy-start(bf16[96,512]{1,0:T(8,128)(2,1)S(1)} %get-tuple-element.50.refs_0_) | copy-start | bytes 294916
  11.8 5.8 %collective-permute-start.2 = (bf16[96,512]{1,0:T(8,128)(2,1)}, bf16[96,512]{1,0:T(8,128)(2,1)S(1)}, u32[]{:S(2)}, u32[]{:S(2)}) collective-permute-start(bf16[96,512]{1,0:T(8,128)(2,1)} %get-tuple-element.49), channel_id=1, source_target_pairs={{0,18},{1,19},{2,16},{3,17},{4,22},{5,23},{6,20},{7,21},{8,26},{9,... | collective-permute-start | bytes 294920 | tf_op jit(solution)/shard_map/ppermute | solution.py:75
  13.3 6.4 %collective-permute-start = (bf16[96,512]{1,0:T(8,128)(2,1)}, bf16[96,512]{1,0:T(8,128)(2,1)S(1)}, u32[]{:S(2)}, u32[]{:S(2)}) collective-permute-start(bf16[96,512]{1,0:T(8,128)(2,1)} %get-tuple-element.49), channel_id=1, source_target_pairs={{0,16},{16,0},{32,48},{48,32},{64,80},{80,64},{96,112},{112,96},{1... | collective-permute-start | bytes 294920 | tf_op jit(solution)/shard_map/ppermute | solution.py:62
  13.8 7.2 %collective-permute-start.3 = (bf16[96,512]{1,0:T(8,128)(2,1)S(1)}, bf16[96,512]{1,0:T(8,128)(2,1)S(1)}, u32[]{:S(2)}, u32[]{:S(2)}) collective-permute-start(bf16[96,512]{1,0:T(8,128)(2,1)S(1)} %get-tuple-element.50.refs_0_), channel_id=1, source_target_pairs={{0,1},{1,0},{2,3},{3,2},{4,5},{5,4},{6,7},{7,6},{8,9},{9,8},{10,11... | collective-permute-start | bytes 294920 | tf_op jit(solution)/shard_map/ppermute | solution.py:66
  13.8 6.6 %collective-permute-start.1 = (bf16[96,512]{1,0:T(8,128)(2,1)S(1)}, bf16[96,512]{1,0:T(8,128)(2,1)}, u32[]{:S(2)}, u32[]{:S(2)}) collective-permute-start(bf16[96,512]{1,0:T(8,128)(2,1)S(1)} %get-tuple-element.50.refs_0_), channel_id=1, source_target_pairs={{0,2},{1,3},{2,0},{3,1},{4,6},{5,7},{6,4},{7,5},{8,10},{9,11},{10,... | collective-permute-start | bytes 294920 | tf_op jit(solution)/shard_map/ppermute | solution.py:70
  15.3 20.9 %collective-permute-start.8 = (bf16[256,1536]{1,0:T(8,128)(2,1)S(1)}, bf16[256,1536]{1,0:T(8,128)(2,1)}, u32[]{:S(2)}, u32[]{:S(2)}) collective-permute-start(bf16[256,1536]{1,0:T(8,128)(2,1)S(1)} %bitcast.24), channel_id=1, source_target_pairs={{0,16},{16,0},{32,48},{48,32},{64,80},{80,64},{96,112},{112,96},{1... | collective-permute-start | bytes 2359304 | tf_op jit(solution)/shard_map/ppermute | solution.py:62
  17.6 4.0 %collective-permute-start.6 = (bf16[96,512]{1,0:T(8,128)(2,1)S(1)}, bf16[96,512]{1,0:T(8,128)(2,1)S(1)}, u32[]{:S(2)}, u32[]{:S(2)}) collective-permute-start(bf16[96,512]{1,0:T(8,128)(2,1)S(1)} %collective-permute-done.2.refs_3_), channel_id=1, source_target_pairs={{0,1},{1,0},{2,3},{3,2},{4,5},{5,4},{6,7},{7,6},{8,9},{9,8},{10,11... | collective-permute-start | bytes 294920 | tf_op jit(solution)/shard_map/ppermute | solution.py:66
  17.6 0.6 copy-start.4
  19.7 1.9 %collective-permute-start.4 = (bf16[96,512]{1,0:T(8,128)(2,1)S(1)}, bf16[96,512]{1,0:T(8,128)(2,1)S(1)}, u32[]{:S(2)}, u32[]{:S(2)}) collective-permute-start(bf16[96,512]{1,0:T(8,128)(2,1)S(1)} %collective-permute-done.refs_1_), channel_id=1, source_target_pairs={{0,1},{1,0},{2,3},{3,2},{4,5},{5,4},{6,7},{7,6},{8,9},{9,8},{10,11... | collective-permute-start | bytes 294920 | tf_op jit(solution)/shard_map/ppermute | solution.py:66
  19.7 0.6 copy-start.6
  20.4 1.7 %collective-permute-start.5 = (bf16[96,512]{1,0:T(8,128)(2,1)}, bf16[96,512]{1,0:T(8,128)(2,1)S(1)}, u32[]{:S(2)}, u32[]{:S(2)}) collective-permute-start(bf16[96,512]{1,0:T(8,128)(2,1)} %collective-permute-done.1.refs_2_), channel_id=1, source_target_pairs={{0,1},{1,0},{2,3},{3,2},{4,5},{5,4},{6,7},{7,6},{8,9},{9,8},{10,11... | collective-permute-start | bytes 294920 | tf_op jit(solution)/shard_map/ppermute | solution.py:66
  21.0 0.6 copy-start.8
  22.0 0.9 copy-start.3
  22.9 0.9 copy-start.5
  23.8 0.9 copy-start.7
  24.7 0.9 copy-start.9
  34.2 2.4 %collective-permute-start.7 = (bf16[256,1536]{1,0:T(8,128)(2,1)S(1)}, bf16[256,1536]{1,0:T(8,128)(2,1)}, u32[]{:S(2)}, u32[]{:S(2)}) collective-permute-start(bf16[256,1536]{1,0:T(8,128)(2,1)S(1)} %bitcast.22), channel_id=1, source_target_pairs={{0,1},{1,0},{2,3},{3,2},{4,5},{5,4},{6,7},{7,6},{8,9},{9,8},{10,11... | collective-permute-start | bytes 2359304 | tf_op jit(solution)/shard_map/ppermute | solution.py:66
  42.9 2.3 %collective-permute-start.9 = (bf16[256,1536]{1,0:T(8,128)(2,1)S(1)}, bf16[256,1536]{1,0:T(8,128)(2,1)S(1)}, u32[]{:S(2)}, u32[]{:S(2)}) collective-permute-start(bf16[256,1536]{1,0:T(8,128)(2,1)S(1)} %get-tuple-element.28), channel_id=1, source_target_pairs={{0,1},{1,0},{2,3},{3,2},{4,5},{5,4},{6,7},{7,6},{8,9},{9,8},{10,11... | collective-permute-start | bytes 2359304 | tf_op jit(solution)/shard_map/ppermute | solution.py:66
  45.2 0.9 copy-start.10
  46.0 35.5 %all-to-all-start.1 = ((bf16[16,32,1536]{2,1,0:T(8,128)(2,1)}), bf16[16,32,1536]{2,1,0:T(8,128)(2,1)S(1)}, u32[]{:S(2)}, u32[]{:S(2)}) async-start(bf16[16,32,1536]{2,1,0:T(8,128)(2,1)} %get-tuple-element.29), calls=%async_computation.1 | async-start | bytes 3145728 | tf_op jit(solution)/shard_map/all_to_all | solution.py:295
  56.1 9.3 %collective-permute-start.10 = (bf16[32,1536]{1,0:T(8,128)(2,1)}, bf16[32,1536]{1,0:T(8,128)(2,1)S(1)}, u32[]{:S(2)}, u32[]{:S(2)}) collective-permute-start(bf16[32,1536]{1,0:T(8,128)(2,1)} %get-tuple-element.33), channel_id=1, source_target_pairs={{0,224},{16,240},{32,0},{48,16},{64,32},{80,48},{96,64},{112,80},{... | collective-permute-start | bytes 294920 | tf_op jit(solution)/shard_map/ppermute | solution.py:58
  58.7 8.0 %collective-permute-start.11 = (bf16[32,1536]{1,0:T(8,128)(2,1)}, bf16[32,1536]{1,0:T(8,128)(2,1)S(1)}, u32[]{:S(2)}, u32[]{:S(2)}) collective-permute-start(bf16[32,1536]{1,0:T(8,128)(2,1)} %get-tuple-element.34), channel_id=1, source_target_pairs={{0,32},{16,48},{32,64},{48,80},{64,96},{80,112},{96,128},{112,144}... | collective-permute-start | bytes 294920 | tf_op jit(solution)/shard_map/ppermute | solution.py:58
  58.7 11.5 %collective-permute-start.12 = (bf16[32,1536]{1,0:T(8,128)(2,1)}, bf16[32,1536]{1,0:T(8,128)(2,1)S(1)}, u32[]{:S(2)}, u32[]{:S(2)}) collective-permute-start(bf16[32,1536]{1,0:T(8,128)(2,1)} %get-tuple-element.35), channel_id=1, source_target_pairs={{0,192},{16,208},{32,224},{48,240},{64,0},{80,16},{96,32},{112,48}... | collective-permute-start | bytes 294920 | tf_op jit(solution)/shard_map/ppermute | solution.py:58
  61.6 8.6 %collective-permute-start.13 = (bf16[32,1536]{1,0:T(8,128)(2,1)}, bf16[32,1536]{1,0:T(8,128)(2,1)S(1)}, u32[]{:S(2)}, u32[]{:S(2)}) collective-permute-start(bf16[32,1536]{1,0:T(8,128)(2,1)} %get-tuple-element.36), channel_id=1, source_target_pairs={{0,64},{16,80},{32,96},{48,112},{64,128},{80,144},{96,160},{112,17... | collective-permute-start | bytes 294920 | tf_op jit(solution)/shard_map/ppermute | solution.py:58
  61.6 10.7 %collective-permute-start.14 = (bf16[32,1536]{1,0:T(8,128)(2,1)}, bf16[32,1536]{1,0:T(8,128)(2,1)S(1)}, u32[]{:S(2)}, u32[]{:S(2)}) collective-permute-start(bf16[32,1536]{1,0:T(8,128)(2,1)} %get-tuple-element.37), channel_id=1, source_target_pairs={{0,160},{16,176},{32,192},{48,208},{64,224},{80,240},{96,0},{112,1... | collective-permute-start | bytes 294920 | tf_op jit(solution)/shard_map/ppermute | solution.py:58
  65.4 13.1 %copy-start.13 = (bf16[32,1536]{1,0:T(8,128)(2,1)}, bf16[32,1536]{1,0:T(8,128)(2,1)S(1)}, u32[]{:S(2)}) copy-start(bf16[32,1536]{1,0:T(8,128)(2,1)S(1)} %collective-permute-done.10.refs_1_) | copy-start | bytes 294916
  65.4 11.9 %collective-permute-start.15 = (bf16[32,1536]{1,0:T(8,128)(2,1)}, bf16[32,1536]{1,0:T(8,128)(2,1)S(1)}, u32[]{:S(2)}, u32[]{:S(2)}) collective-permute-start(bf16[32,1536]{1,0:T(8,128)(2,1)} %get-tuple-element.38), channel_id=1, source_target_pairs={{0,96},{16,112},{32,128},{48,144},{64,160},{80,176},{96,192},{112,... | collective-permute-start | bytes 294920 | tf_op jit(solution)/shard_map/ppermute | solution.py:58
  66.7 11.9 %copy-start.14 = (bf16[32,1536]{1,0:T(8,128)(2,1)}, bf16[32,1536]{1,0:T(8,128)(2,1)S(1)}, u32[]{:S(2)}) copy-start(bf16[32,1536]{1,0:T(8,128)(2,1)S(1)} %collective-permute-done.11.refs_2_) | copy-start | bytes 294916
  66.7 11.8 %collective-permute-start.16 = (bf16[32,1536]{1,0:T(8,128)(2,1)}, bf16[32,1536]{1,0:T(8,128)(2,1)S(1)}, u32[]{:S(2)}, u32[]{:S(2)}) collective-permute-start(bf16[32,1536]{1,0:T(8,128)(2,1)} %get-tuple-element.39), channel_id=1, source_target_pairs={{0,128},{16,144},{32,160},{48,176},{64,192},{80,208},{96,224},{112... | collective-permute-start | bytes 294920 | tf_op jit(solution)/shard_map/ppermute | solution.py:58
  70.2 8.4 %copy-start.15 = (bf16[32,1536]{1,0:T(8,128)(2,1)}, bf16[32,1536]{1,0:T(8,128)(2,1)S(1)}, u32[]{:S(2)}) copy-start(bf16[32,1536]{1,0:T(8,128)(2,1)S(1)} %collective-permute-done.12.refs_3_) | copy-start | bytes 294916
  70.2 8.4 %copy-start.16 = (bf16[32,1536]{1,0:T(8,128)(2,1)}, bf16[32,1536]{1,0:T(8,128)(2,1)S(1)}, u32[]{:S(2)}) copy-start(bf16[32,1536]{1,0:T(8,128)(2,1)S(1)} %collective-permute-done.13.refs_4_) | copy-start | bytes 294916
  72.3 6.3 %copy-start.17 = (bf16[32,1536]{1,0:T(8,128)(2,1)}, bf16[32,1536]{1,0:T(8,128)(2,1)S(1)}, u32[]{:S(2)}) copy-start(bf16[32,1536]{1,0:T(8,128)(2,1)S(1)} %collective-permute-done.14.refs_5_) | copy-start | bytes 294916
  77.3 1.3 copy-start.18
  78.6 0.6 copy-start.19
  81.5 0.9 copy-start.1
  101.7 1.7 %collective-permute-start.17 = (bf16[192,768]{1,0:T(8,128)(2,1)S(1)}, bf16[192,768]{1,0:T(8,128)(2,1)S(1)}, u32[]{:S(2)}, u32[]{:S(2)}) collective-permute-start(bf16[192,768]{1,0:T(8,128)(2,1)S(1)} %get-tuple-element.41), channel_id=1, source_target_pairs={{0,1},{1,0},{2,3},{3,2},{4,5},{5,4},{6,7},{7,6},{8,9},{9,8},{10,11... | collective-permute-start | bytes 884744 | tf_op jit(solution)/shard_map/ppermute | solution.py:66
  104.2 20.3 %all-to-all-start.3 = ((bf16[8,2,24,384]{3,2,1,0:T(8,128)(2,1)}), bf16[8,2,24,384]{3,2,1,0:T(8,128)(2,1)S(1)}, u32[]{:S(2)}, u32[]{:S(2)}) async-start(bf16[8,2,24,384]{3,2,1,0:T(8,128)(2,1)} %shard_map.91), calls=%async_computation.3 | async-start | bytes 589824 | tf_op jit(solution)/shard_map/all_to_all | solution.py:238
  111.6 3.6 %collective-permute-start.18 = (f32[2,256]{1,0:T(2,128)S(1)}, f32[2,256]{1,0:T(2,128)S(1)}, u32[]{:S(2)}, u32[]{:S(2)}) collective-permute-start(f32[2,256]{1,0:T(2,128)S(1)} %get-tuple-element.42), channel_id=1, source_target_pairs={{0,2},{1,3},{2,0},{3,1},{4,6},{5,7},{6,4},{7,5},{8,10},{9,11},{10,... | collective-permute-start | bytes 6152 | tf_op jit(solution)/shard_map/ppermute | solution.py:356
  115.2 5.1 %collective-permute-start.19 = (f32[2,256]{1,0:T(2,128)S(1)}, f32[2,256]{1,0:T(2,128)S(1)}, u32[]{:S(2)}, u32[]{:S(2)}) collective-permute-start(f32[2,256]{1,0:T(2,128)S(1)} %add.102), channel_id=1, source_target_pairs={{0,4},{1,5},{2,6},{3,7},{4,0},{5,1},{6,2},{7,3},{8,12},{9,13},{10,... | collective-permute-start | bytes 6152 | tf_op jit(solution)/shard_map/ppermute | solution.py:356
  125.4 23.2 %all-to-all-start.4 = ((bf16[32,24,384]{2,1,0:T(8,128)(2,1)}), bf16[32,24,384]{2,1,0:T(8,128)(2,1)S(1)}, u32[]{:S(2)}, u32[]{:S(2)}) async-start(bf16[32,24,384]{2,1,0:T(8,128)(2,1)} %bitcast.16), calls=%async_computation.4 | async-start | bytes 1179648 | tf_op jit(solution)/shard_map/all_to_all | solution.py:372
  130.4 5.2 %collective-permute-start.20 = (f32[2,256]{1,0:T(2,128)S(1)}, f32[2,256]{1,0:T(2,128)S(1)}, u32[]{:S(2)}, u32[]{:S(2)}) collective-permute-start(f32[2,256]{1,0:T(2,128)S(1)} %add.103), channel_id=1, source_target_pairs={{0,8},{1,9},{2,10},{3,11},{4,12},{5,13},{6,14},{7,15},{8,0},{9,1},... | collective-permute-start | bytes 6152 | tf_op jit(solution)/shard_map/ppermute | solution.py:358
  135.6 3.8 %collective-permute-start.21 = (f32[2,256]{1,0:T(2,128)S(1)}, f32[2,256]{1,0:T(2,128)S(1)}, u32[]{:S(2)}, u32[]{:S(2)}) collective-permute-start(f32[2,256]{1,0:T(2,128)S(1)} %add.104), channel_id=1, source_target_pairs={{0,16},{16,0},{32,48},{48,32},{64,80},{80,64},{96,112},{112,96},{1... | collective-permute-start | bytes 6152 | tf_op jit(solution)/shard_map/ppermute | solution.py:62
  140.6 1.2 collective-permute-start.22
